TPU v7x, 32 devices: a whole 2x2x4 slice. The times are simulated.
32 devices in a mesh: feat: 4 (over y, x), dp: 8 (over z, core).
Axes of the slice: x: 2, y: 2, z: 4, core: 2. Of those that a mesh axis runs over, the one named last changes fastest.
Arguments:
- features: bfloat16 [1024, 4096], P('feat', 'dp'), may hold values from -6 to 6
- neighbors: int32 [4096, 10], P('dp'), may hold values from 0 to 511
- labels: int32 [4096], P('dp'), may hold values from 0 to 171
- loss_weight: float32 [4096], P('dp'), as said below
- w1_self: bfloat16 [1024, 256], P('feat'), may hold values from -0.1875 to 0.1875
- w1_neigh: bfloat16 [1024, 256], P('feat'), may hold values from -0.1875 to 0.1875
- w2_self: bfloat16 [256, 172], replicated, may hold values from -0.375 to 0.375
- w2_neigh: bfloat16 [256, 172], replicated, may hold values from -0.375 to 0.375
Outputs:
- loss: float32 [], replicated
- grad_w1: float32 [2, 1024, 256], P(None, ('feat', 'dp'))
- grad_w2: float32 [2, 256, 172], replicated
Inputs may be any that keep to these rules, and one draw needn't show every extreme that they name: `loss_weight`: positive weights.
All inputs are finite; a program needn't handle non-finite values.
Results may differ from a plain program's by a relative error of at most 0.0055.
Values may be sent and summed in bfloat16 or wider, within the bound.
No kernel may reach another device: no remote copies, remote signals or barrier semaphores. Data moves between devices by JAX's collectives and lax.ppermute only.
A program may use at most 128 MiB of HBM per device.

v0:
```python
import jax
import jax.numpy as jnp
from jax import lax
from jax.sharding import PartitionSpec as P


def focal_rows(logits, targets):
    logprob = jax.nn.log_softmax(logits, axis=-1)
    picked = jnp.take_along_axis(logprob, targets[:, None], axis=1)[:, 0]
    chance = jnp.exp(picked)
    return -(1.0 - chance) * (1.0 - chance) * picked


def neighbor_mean(lookup_table, indices):
    total = jnp.zeros((indices.shape[0], lookup_table.shape[1]), jnp.float32)
    for which in range(indices.shape[1]):
        total = total + jnp.take(lookup_table, indices[:, which], axis=0).astype(jnp.float32)
    return total / indices.shape[1]


def adjoint_rows(values, indices, begin, count):
    total = jnp.zeros((count, values.shape[1]), jnp.float32)
    for which in range(indices.shape[1]):
        local = indices[:, which] - begin
        inside = jnp.logical_and(local >= 0, local < count)
        target = jnp.where(inside, local, count)
        total = total + jax.ops.segment_sum(values, target, num_segments=count + 1)[:count]
    return total


def contract_first(left_side, right_side):
    return lax.dot_general(
        left_side, right_side, (((0,), (0,)), ((), ())), preferred_element_type=jnp.float32
    )


def contract_last(left_side, right_side):
    return lax.dot_general(
        left_side, right_side, (((1,), (1,)), ((), ())), preferred_element_type=jnp.float32
    )


def on_device(features, neighbors, labels, loss_weight, w1_self, w1_neigh, w2_self, w2_neigh):
    feat_count = lax.axis_size("feat")
    sub_rows = neighbors.shape[0]
    own_count = sub_rows // feat_count
    row_start = lax.axis_index("feat") * own_count
    own_neighbors = lax.dynamic_slice_in_dim(neighbors, row_start, own_count, 0)
    own_labels = lax.dynamic_slice_in_dim(labels, row_start, own_count, 0)
    own_weight = lax.dynamic_slice_in_dim(loss_weight, row_start, own_count, 0)
    fanout = neighbors.shape[1]
    node_block = lax.all_to_all(features, "feat", split_axis=1, concat_axis=0, tiled=True)
    full_self, full_neigh = (
        lax.all_gather(w1_self, "feat", axis=0, tiled=True),
        lax.all_gather(w1_neigh, "feat", axis=0, tiled=True),
    )
    proj_self = contract_first(node_block, full_self)
    proj_neigh = contract_first(node_block, full_neigh).astype(jnp.bfloat16)
    neigh_table = lax.all_gather(proj_neigh, "feat", axis=0, tiled=True)
    first_pre = proj_self + neighbor_mean(neigh_table, own_neighbors)
    hidden = jax.nn.relu(first_pre).astype(jnp.bfloat16)
    hidden_table = lax.all_gather(hidden, "feat", axis=0, tiled=True)
    second_agg = neighbor_mean(hidden_table, own_neighbors).astype(jnp.bfloat16)
    logits = jnp.dot(hidden, w2_self, preferred_element_type=jnp.float32) + jnp.dot(
        second_agg, w2_neigh, preferred_element_type=jnp.float32
    )
    focal_terms, focal_vjp = jax.vjp(lambda values: focal_rows(values, own_labels), logits)
    grad_logits = focal_vjp(own_weight)[0].astype(jnp.bfloat16)
    weight_part = jnp.sum(own_weight)
    loss_part = jnp.sum(own_weight * focal_terms)
    norm_total, loss_total = lax.psum((weight_part, loss_part), ("feat", "dp"))
    second_local = jnp.stack(
        [contract_first(hidden, grad_logits), contract_first(second_agg, grad_logits)]
    )
    hidden_own = contract_last(grad_logits, w2_self)
    agg_grad = contract_last(grad_logits, w2_neigh)
    hidden_back = lax.psum_scatter(
        adjoint_rows(agg_grad, own_neighbors, 0, sub_rows), "feat", scatter_dimension=0, tiled=True
    )
    hidden_grad = hidden_own + hidden_back / fanout
    pre_grad = jnp.where(first_pre > 0, hidden_grad, 0.0).astype(jnp.bfloat16)
    neigh_back = lax.psum_scatter(
        adjoint_rows(pre_grad.astype(jnp.float32), own_neighbors, 0, sub_rows),
        "feat",
        scatter_dimension=0,
        tiled=True,
    )
    proj_grad = (neigh_back / fanout).astype(jnp.bfloat16)
    first_local = jnp.stack(
        [
            jnp.dot(node_block, pre_grad, preferred_element_type=jnp.float32),
            jnp.dot(node_block, proj_grad, preferred_element_type=jnp.float32),
        ]
    )
    first_sum = lax.psum_scatter(first_local, ("feat", "dp"), scatter_dimension=1, tiled=True)
    second_sum = lax.psum(second_local, ("feat", "dp"))
    return (loss_total / norm_total, first_sum / norm_total, second_sum / norm_total)


def solution(mesh):
    in_specs = (
        P("feat", "dp"),
        P("dp", None),
        P("dp"),
        P("dp"),
        P("feat", None),
        P("feat", None),
        P(),
        P(),
    )
    out_specs = (P(), P(None, ("feat", "dp"), None), P())
    return jax.shard_map(
        on_device, mesh=mesh, in_specs=in_specs, out_specs=out_specs, check_vma=False
    )
```

profile of v0, /device:TPU:0, one launch (start us, length us, event | category | flops | bytes accessed | tf_op | source)
XLA Modules:
  0.0 323.1 jit_solution(142940275706532337)
XLA Ops:
  7.2 1.8 copy.19
  9.0 5.2 %all-to-all-start = ((bf16[256,4,128]{0,2,1:T(8,128)(2,1)}), bf16[256,4,128]{0,2,1:T(8,128)(2,1)S(1)}, u32[]{:S(2)}, u32[]{:S(2)}) async-start(bf16[256,4,128]{0,2,1:T(8,128)(2,1)} %bitcast), calls=%async_computation | async-start | bytes 524288 | tf_op jit(solution)/shard_map/all_to_all | solution.py:52
  14.2 1.1 compare_and_fusion.9
  15.2 1.1 fusion.56
  17.8 10.9 %all_gather.13 = bf16[1024,256]{1,0:T(8,128)(2,1)S(1)} all-gather(bf16[256,256]{1,0:T(8,128)(2,1)} %param.15), channel_id=1, replica_groups=mesh['feat'=4,'dp'=8] {'feat'}, dimensions={0}, use_global_device_ids=true | all-gather | bytes 655360 | tf_op jit(solution)/shard_map/all_gather | solution.py:55
  28.7 9.9 %all_gather.12 = bf16[1024,256]{1,0:T(8,128)(2,1)S(1)} all-gather(bf16[256,256]{1,0:T(8,128)(2,1)} %param.14), channel_id=1, replica_groups=mesh['feat'=4,'dp'=8] {'feat'}, dimensions={0}, use_global_device_ids=true | all-gather | bytes 655360 | tf_op jit(solution)/shard_map/all_gather | solution.py:54
  39.2 8.6 %all_gather.14 = bf16[512,256]{1,0:T(8,128)(2,1)S(1)} all-gather(bf16[128,256]{1,0:T(8,128)(2,1)S(1)} %convolution_convert_fusion), channel_id=1, replica_groups=mesh['feat'=4,'dp'=8] {'feat'}, dimensions={0}, use_global_device_ids=true | all-gather | bytes 327680 | tf_op jit(solution)/shard_map/all_gather | solution.py:59
  47.8 0.8 gather_fusion.10
  48.7 0.8 gather_fusion.9
  49.5 0.8 gather_fusion.8
  50.4 0.8 gather_fusion.7
  51.2 0.8 gather_fusion.6
  52.1 0.8 gather_fusion.5
  52.9 0.8 gather_fusion.4
  53.8 0.8 gather_fusion.3
  54.6 0.8 gather_fusion.2
  55.5 0.8 gather_fusion.1
  56.3 1.0 maximum_convert_fusion
  57.3 8.3 %all_gather.15 = bf16[512,256]{1,0:T(8,128)(2,1)S(1)} all-gather(bf16[128,256]{1,0:T(8,128)(2,1)S(1)} %get-tuple-element.71), channel_id=1, replica_groups=mesh['feat'=4,'dp'=8] {'feat'}, dimensions={0}, use_global_device_ids=true | all-gather | bytes 327680 | tf_op jit(solution)/shard_map/all_gather | solution.py:62
  65.7 0.8 gather_fusion.20
  66.5 0.8 gather_fusion.19
  67.4 0.8 gather_fusion.18
  68.2 0.8 gather_fusion.17
  69.1 0.8 gather_fusion.16
  69.9 0.8 gather_fusion.15
  70.8 0.8 gather_fusion.14
  71.6 0.8 gather_fusion.13
  72.5 0.8 gather_fusion.12
  73.3 0.8 gather_fusion.11
  74.9 1.3 gather_fusion
  76.2 1.4 dynamic-slice_reduce_fusion
  77.9 1.4 scatter_custom_fusion.9
  79.3 1.4 scatter_custom_fusion.8
  80.6 1.5 scatter_custom_fusion.7
  82.2 1.4 scatter_custom_fusion.6
  83.6 1.4 scatter_custom_fusion.5
  84.9 2.0 scatter_custom_fusion.4
  87.0 2.1 scatter_custom_fusion.3
  89.0 2.1 scatter_custom_fusion.2
  91.1 2.0 scatter_custom_fusion.1
  93.1 2.0 scatter_custom_fusion
  95.2 2.9 slice_add_fusion.9
  98.1 25.1 %reduce-scatter.3.cloned.1.call-done = f32[128,256]{1,0:T(8,128)} async-done(((f32[512,256]{1,0:T(8,128)}), f32[128,256]{1,0:T(8,128)}) %reduce-scatter.3.cloned.1.call-update) | async-done | bytes 131088 | tf_op jit(solution)/shard_map/reduce_scatter | solution.py:77
  123.2 1.2 fusion.1
  124.4 1.4 scatter_custom_fusion.19
  125.8 1.4 scatter_custom_fusion.18
  127.2 1.4 scatter_custom_fusion.17
  128.5 1.4 scatter_custom_fusion.16
  129.9 1.4 scatter_custom_fusion.15
  131.3 2.0 scatter_custom_fusion.14
  133.4 2.1 scatter_custom_fusion.13
  135.4 2.1 scatter_custom_fusion.12
  137.5 2.1 scatter_custom_fusion.11
  139.5 2.1 scatter_custom_fusion.10
  141.6 2.9 slice_add_fusion
  144.8 0.8 pad_maximum_fusion.1
  145.9 23.5 %reduce-scatter.5.cloned.1.call-done = f32[128,256]{1,0:T(8,128)} async-done(((f32[512,256]{1,0:T(8,128)}), f32[128,256]{1,0:T(8,128)}) %reduce-scatter.5.cloned.1.call-update) | async-done | bytes 131088 | tf_op jit(solution)/shard_map/reduce_scatter | solution.py:82
  169.4 1.2 convolution_bitcast_fusion
  170.9 2.4 copy.21
  173.3 40.0 %all-reduce.1 = (f32[]{:T(128)}, f32[]{:T(128)}) all-reduce(f32[]{:T(128)} %get-tuple-element.17, f32[]{:T(128)} %get-tuple-element.16), channel_id=1, replica_groups=mesh['feat'=4,'dp'=8] {'feat','dp'}, use_global_device_ids=true, to_apply=%region_3.5 | all-reduce | flops 2 | bytes 16 | tf_op jit(solution)/shard_map/psum | solution.py:71
  214.6 96.0 %all-reduce.5.cloned.1.call-done = (f32[2,1024,256]{2,0,1:T(2,128)}, f32[2,256,172]{1,2,0:T(8,128)}) async-done(((f32[2,1024,256]{2,0,1:T(2,128)}, f32[2,256,172]{1,2,0:T(8,128)}), (f32[2,1024,256]{2,0,1:T(2,128)}, f32[2,256,172]{1,2,0:T(8,128)})) %all-reduce.5.cloned.1.call-update) | async-done | bytes 2449424
  310.6 1.5 dynamic-slice_divide_fusion
  312.8 1.7 broadcast_divide_fusion
  314.4 1.0 copy.23
  (38 shorter events, 4.6 us)
Async XLA Ops:
  7.2 67.4 %copy-start = (bf16[256,172]{0,1:T(8,128)(2,1)S(1)}, bf16[256,172]{0,1:T(8,128)(2,1)}, u32[]{:S(2)}) copy-start(bf16[256,172]{0,1:T(8,128)(2,1)} %param.17) | copy-start | bytes 264196
  9.0 29.7 %all-to-all-start = ((bf16[256,4,128]{0,2,1:T(8,128)(2,1)}), bf16[256,4,128]{0,2,1:T(8,128)(2,1)S(1)}, u32[]{:S(2)}, u32[]{:S(2)}) async-start(bf16[256,4,128]{0,2,1:T(8,128)(2,1)} %bitcast), calls=%async_computation | async-start | bytes 524288 | tf_op jit(solution)/shard_map/all_to_all | solution.py:52
  14.2 109.1 %reduce-scatter.3.cloned.1.call-start = ((), (), s32[]{:S(2)}) async-start(), calls=%async_computation.3 | async-start | bytes 655360 | tf_op jit(solution)/shard_map/reduce_scatter | solution.py:77
  68.2 6.0 %copy-start.1 = (bf16[256,172]{0,1:T(8,128)(2,1)S(1)}, bf16[256,172]{0,1:T(8,128)(2,1)}, u32[]{:S(2)}) copy-start(bf16[256,172]{0,1:T(8,128)(2,1)} %param.16) | copy-start | bytes 264196
  98.0 71.4 %reduce-scatter.5.cloned.1.call-start = ((), (), s32[]{:S(2)}) async-start(), calls=%async_computation.4 | async-start | bytes 655360 | tf_op jit(solution)/shard_map/reduce_scatter | solution.py:82
  144.5 166.1 %all-reduce.5.cloned.1.call-start = ((), (), s32[]{:S(2)}) async-start(), calls=%async_computation.5 | async-start | bytes 4915200
Sparse Core Ops, SparseCore 0:
  98.2 25.0 reduce-scatter.2
  144.6 24.7 reduce-scatter.4
  174.9 135.6 all-reduce.4
where the time goes:
time: 324 us; the launch traced here: 323 us
  waiting for transfers between devices  145 us (45%)
  blocking collectives  77.7 us (24%)
  other arithmetic  49.8 us (15%)
  local copies, waits for them, and re-layouts  24.3 us (8%)
  between operations  16.5 us (5%)
  starting transfers between devices  5.25 us (2%)
  matrix products  4.86 us (2%)
    unnamed x4, waiting for transfers between devices  96.1 us
    psum x1, blocking collectives, on_device(): norm_total, loss_total = lax.psum((weight_part, loss_part), ('feat', 'dp'))  40 us
    scatter-add x20, other arithmetic, adjoint_rows(): jax.ops.segment_sum(values, target, num_segments=count + 1)[:count]  34.4 us
    reduce_scatter x1, waiting for transfers between devices, on_device(): lax.psum_scatter(adjoint_rows(agg_grad, own_neighbors, 0, sub_rows), 'fea...  25.1 us
    reduce_scatter x1, waiting for transfers between devices, on_device(): lax.psum_scatter(adjoint_rows(pre_grad.astype(jnp.float32), own_neighbors...  23.5 us
    gather x20, local copies, waits for them, and re-layouts, neighbor_mean(): jnp.take(lookup_table, indices[:, which], axis=0).astype(jnp.float32)  16.9 us
    all_gather x1, blocking collectives, on_device(): lax.all_gather(w1_neigh, 'feat', axis=0, tiled=True)  10.9 us
    all_gather x1, blocking collectives, on_device(): lax.all_gather(w1_self, 'feat', axis=0, tiled=True)  9.89 us
  transfers between devices with their start and end apart: 4, of which 3 were waited for; matrix products, arithmetic and copies ran while one was open for 2% of the time, Pallas kernels for 0%

commit v1 on v0

v1 whole, which is shorter than its diff:
```python
import functools

import jax
import jax.numpy as jnp
from jax import lax
from jax.experimental import pallas as pl
from jax.experimental.pallas import tpu as pltpu
from jax.sharding import PartitionSpec as P

BF16 = jnp.bfloat16
F32 = jnp.float32
VMEM_LIMIT = 56 * 1024 * 1024


def dot_nn(left, right):
    return lax.dot_general(left, right, (((1,), (0,)), ((), ())), preferred_element_type=F32)


def dot_nt(left, right):
    return lax.dot_general(left, right, (((1,), (1,)), ((), ())), preferred_element_type=F32)


def dot_tn(left, right):
    return lax.dot_general(left, right, (((0,), (0,)), ((), ())), preferred_element_type=F32)


def tree_sum(terms):
    terms = list(terms)
    while len(terms) > 1:
        terms = [terms[i] + terms[i + 1] for i in range(0, len(terms), 2)]
    return terms[0]


def call(kernel, outs, args, scratch=(), flops=0, smem=()):
    size = sum(a.size * a.dtype.itemsize for a in args)
    size += sum(o.size * o.dtype.itemsize for o in outs)
    specs = [
        pl.BlockSpec(memory_space=pltpu.SMEM if i in smem else pltpu.VMEM) for i in range(len(args))
    ]
    return pl.pallas_call(
        kernel,
        out_shape=outs,
        in_specs=specs,
        out_specs=[pl.BlockSpec(memory_space=pltpu.VMEM)] * len(outs),
        scratch_shapes=list(scratch),
        cost_estimate=pl.CostEstimate(flops=flops, bytes_accessed=size, transcendentals=0),
        compiler_params=pltpu.CompilerParams(vmem_limit_bytes=VMEM_LIMIT),
    )(*args)


def shape(dims, dtype):
    return jax.ShapeDtypeStruct(dims, dtype)


def count_kernel(fanout, nbr_ref, at_ref):
    nodes = at_ref.shape[1]
    step = 32

    def body(i, carry):
        row = lax.broadcasted_iota(jnp.int32, (step, nodes), 0) + i * step
        total = jnp.zeros((step, nodes), F32)
        for k in range(fanout):
            total = total + jnp.where(nbr_ref[k : k + 1, :] == row, 1.0, 0.0)
        at_ref[pl.ds(pl.multiple_of(i * step, step), step), :] = total.astype(BF16)
        return carry

    lax.fori_loop(0, nodes // step, body, 0)


def forward_kernel(feat_count, fanout, *refs):
    core_ref, labels_ref, weight_ref, at_ref, w2s_ref, w2n_ref, ws_ref, wn_ref = refs[:8]
    f_refs = refs[8 : 8 + feat_count]
    mine_refs = refs[8 + feat_count : 7 + 2 * feat_count]
    partner_refs = refs[7 + 2 * feat_count : 6 + 3 * feat_count]
    send_ref, keep_ref, g_ref, hidden_ref, proj, pair = refs[6 + 3 * feat_count :]
    core = core_ref[0]
    classes = w2s_ref.shape[1]
    nodes = at_ref.shape[1]
    scale = 1.0 / fanout
    first = core == 0
    own_mine = jnp.where(first, ws_ref[...], wn_ref[...])
    own_partner = jnp.where(first, wn_ref[...], ws_ref[...])
    proj[core] = tree_sum(
        [dot_tn(own_mine, f_refs[0][...])]
        + [dot_tn(mine_refs[s - 1][...], f_refs[s][...]) for s in range(1, feat_count)]
    )
    proj[1 - core] = tree_sum(
        [dot_tn(own_partner, f_refs[0][...])]
        + [dot_tn(partner_refs[s - 1][...], f_refs[s][...]) for s in range(1, feat_count)]
    )
    at = at_ref[...]
    pre = proj[0] + dot_nn(proj[1].astype(BF16), at) * scale
    hidden = jnp.maximum(pre, 0.0).astype(BF16)
    hidden_ref[...] = hidden
    second = (dot_nn(hidden, at) * scale).astype(BF16)
    logits = dot_tn(w2s_ref[...], hidden) + dot_tn(w2n_ref[...], second)
    shifted = logits - jnp.max(logits, axis=0, keepdims=True)
    logprob = shifted - jnp.log(jnp.sum(jnp.exp(shifted), axis=0, keepdims=True))
    hot = lax.broadcasted_iota(jnp.int32, (classes, nodes), 0) == labels_ref[...]
    picked = jnp.sum(jnp.where(hot, logprob, 0.0), axis=0, keepdims=True)
    chance = jnp.exp(picked)
    rest = 1.0 - chance
    weight = weight_ref[...]
    terms = -rest * rest * picked
    slope = weight * (2.0 * rest * chance * picked - rest * rest)
    grad = (slope * (jnp.where(hot, 1.0, 0.0) - jnp.exp(logprob))).astype(BF16)
    g_ref[...] = grad
    pair[0] = hidden
    pair[1] = second
    loss_part = jnp.sum(weight * terms)
    norm_part = jnp.sum(weight)
    for out_ref, which in ((send_ref, 1 - core), (keep_ref, core)):
        rows, cols = out_ref.shape
        row = lax.broadcasted_iota(jnp.int32, (rows, cols), 0)
        col = lax.broadcasted_iota(jnp.int32, (rows, cols), 1)
        extra = jnp.where(col == 0, loss_part, jnp.where(col == 1, norm_part, 0.0))
        out_ref[...] = jnp.where(row >= classes, extra, 0.0)
        out_ref[:classes, :] = dot_nt(grad, pair[which])


def backward_kernel(
    fanout, groups, core_ref, g_ref, hidden_ref, at_ref, w2s_ref, w2n_ref, f_ref, send_ref, keep_ref
):
    core = core_ref[0]
    scale = 1.0 / fanout
    grad = g_ref[...]
    at = at_ref[...]
    summed = dot_nt(grad, at)
    high = summed.astype(BF16)
    low = (summed - high.astype(F32)).astype(BF16)
    w2n = w2n_ref[...]
    hidden_grad = dot_nn(w2s_ref[...], grad) + (dot_nn(w2n, high) + dot_nn(w2n, low)) * scale
    pre_grad = jnp.where(hidden_ref[...] > 0, hidden_grad, 0.0).astype(BF16)
    proj_grad = (dot_nt(pre_grad, at) * scale).astype(BF16)
    features = f_ref[...]
    full = (dot_nt(features, pre_grad), dot_nt(features, proj_grad))
    rows = send_ref.shape[2]
    first = core == 0
    for z in range(groups):
        for part in range(2):
            low_rows = full[part][2 * z * rows : (2 * z + 1) * rows]
            high_rows = full[part][(2 * z + 1) * rows : (2 * z + 2) * rows]
            send_ref[z, part] = jnp.where(first, high_rows, low_rows)
            keep_ref[z, part] = jnp.where(first, low_rows, high_rows)


def pair_kernel(classes, keep_ref, recv_ref, out_ref):
    total = keep_ref[...] + recv_ref[...]
    high = total.astype(BF16).astype(F32)
    rest = total - high
    middle = rest.astype(BF16).astype(F32)
    low = rest - middle
    row = lax.broadcasted_iota(jnp.int32, total.shape, 0)
    out = jnp.where(row == classes + 1, middle, jnp.where(row == classes + 2, low, high))
    out_ref[...] = out.astype(BF16)


def chunk_kernel(groups, z_ref, keep_ref, recv_ref, own_ref, *out_refs):
    z = z_ref[0]
    own_ref[...] = keep_ref[z] + recv_ref[z]
    for s in range(1, groups):
        other = jnp.bitwise_xor(z, s)
        out_refs[s - 1][...] = (keep_ref[other] + recv_ref[other]).astype(BF16)


def second_sum_kernel(*refs):
    refs[-1][...] = tree_sum([r[...].astype(F32) for r in refs[:-1]])


def scalars(total, classes):
    row = lax.broadcasted_iota(jnp.int32, total.shape, 0)
    col = lax.broadcasted_iota(jnp.int32, total.shape, 1)
    inside = jnp.logical_and(row >= classes, row < classes + 3)
    loss = jnp.sum(jnp.where(jnp.logical_and(inside, col == 0), total, 0.0), keepdims=True)
    norm = jnp.sum(jnp.where(jnp.logical_and(inside, col == 1), total, 0.0), keepdims=True)
    return loss, norm


def second_out_kernel(classes, core_ref, own_ref, other_ref, out_ref, loss_ref):
    core = core_ref[0]
    loss, norm = scalars(own_ref[...], classes)
    inverse = 1.0 / norm
    out_ref[core] = (own_ref[...] * inverse).T[:, :classes]
    out_ref[1 - core] = (other_ref[...] * inverse).T[:, :classes]
    loss_ref[...] = loss * inverse


def first_out_kernel(classes, total_ref, *refs):
    _, norm = scalars(total_ref[...], classes)
    out_ref = refs[-1]
    summed = tree_sum([r[...].astype(F32) for r in refs[:-1]])
    out_ref[...] = summed * (1.0 / norm)[None]


def exchange(value, axis, step):
    size = lax.axis_size(axis)
    return lax.ppermute(value, axis, [(i, i ^ step) for i in range(size)])


def on_device(features, neighbors, labels, loss_weight, w1_self, w1_neigh, w2_self, w2_neigh):
    feat_count = lax.axis_size("feat")
    dp_count = lax.axis_size("dp")
    groups = dp_count // 2
    nodes, fanout = neighbors.shape
    rows, hid = w1_self.shape
    classes = w2_self.shape[1]
    place = lax.axis_index("dp").astype(jnp.int32)
    core = (place % 2).reshape(1)
    z = (place // 2).reshape(1)

    wide = [features] + [exchange(features, "feat", s) for s in range(1, feat_count)]
    mine_own = jnp.where(core[0] == 0, w1_self, w1_neigh)
    mine = [exchange(mine_own, "feat", s) for s in range(1, feat_count)]
    partner = [exchange(m, "dp", 1) for m in mine]

    (at,) = call(
        functools.partial(count_kernel, fanout),
        [shape((nodes, nodes), BF16)],
        [neighbors.T],
        flops=nodes * nodes * fanout,
    )
    padded = (classes + 3 + 15) // 16 * 16
    send2, keep2, grad, hidden = call(
        functools.partial(forward_kernel, feat_count, fanout),
        [
            shape((padded, hid), F32),
            shape((padded, hid), F32),
            shape((classes, nodes), BF16),
            shape((hid, nodes), BF16),
        ],
        [core, labels.reshape(1, nodes), loss_weight.reshape(1, nodes), at, w2_self, w2_neigh, w1_self, w1_neigh]
        + wide
        + mine
        + partner,
        scratch=[pltpu.VMEM((2, hid, nodes), F32), pltpu.VMEM((2, hid, nodes), BF16)],
        flops=2 * nodes * hid * 2 * (rows * feat_count + nodes),
        smem=(0,),
    )
    recv2 = exchange(send2, "dp", 1)
    send1, keep1 = call(
        functools.partial(backward_kernel, fanout, groups),
        [shape((groups, 2, rows // dp_count, hid), F32)] * 2,
        [core, grad, hidden, at, w2_self, w2_neigh, features],
        flops=2 * nodes * hid * 2 * (rows + nodes),
        smem=(0,),
    )
    (chip2,) = call(functools.partial(pair_kernel, classes), [shape((padded, hid), BF16)], [keep2, recv2])
    far2 = [exchange(chip2, "dp", 2 * s) for s in range(1, groups)]
    recv1 = exchange(send1, "dp", 1)
    own1, *chunks = call(
        functools.partial(chunk_kernel, groups),
        [shape((2, rows // dp_count, hid), F32)] + [shape((2, rows // dp_count, hid), BF16)] * (groups - 1),
        [z, keep1, recv1],
        smem=(0,),
    )
    far1 = [exchange(chunks[s - 1], "dp", 2 * s) for s in range(1, groups)]
    (total2,) = call(second_sum_kernel, [shape((padded, hid), F32)], [chip2] + far2)
    other2 = exchange(total2, "dp", 1)
    (grad_w1,) = call(
        functools.partial(first_out_kernel, classes),
        [shape((2, rows // dp_count, hid), F32)],
        [total2, own1] + far1,
    )
    grad_w2, loss = call(
        functools.partial(second_out_kernel, classes),
        [shape((2, hid, classes), F32), shape((1, 1), F32)],
        [core, total2, other2],
        smem=(0,),
    )
    return loss[0, 0], grad_w1, grad_w2


def solution(mesh):
    in_specs = (
        P("feat", "dp"),
        P("dp", None),
        P("dp"),
        P("dp"),
        P("feat", None),
        P("feat", None),
        P(),
        P(),
    )
    out_specs = (P(), P(None, ("feat", "dp"), None), P())
    return jax.shard_map(
        on_device, mesh=mesh, in_specs=in_specs, out_specs=out_specs, check_vma=False
    )
```

time: 324 us -> 70.7 us (0.22)
  waiting for transfers between devices: 145 us -> 22.5 us
  blocking collectives: 77.7 us -> 0 us
  other arithmetic: 49.8 us -> 0.97 us
  Pallas kernels: 0 us -> 19.5 us
  local copies, waits for them, and re-layouts: 24.3 us -> 8.09 us
  between operations: 16.5 us -> 0.77 us
  starting transfers between devices: 5.25 us -> 18.5 us
  matrix products: 4.86 us -> 0 us
    unnamed x4 -> x0, waiting for transfers between devices: 96.1 us -> none
    reduce_scatter x2 -> x0, waiting for transfers between devices: 48.6 us -> none  [the longest x1 25.1 us: on_device(): lax.psum_scatter(adjoint_rows(agg_grad, own_neighbors, 0, sub_rows), 'fea...]
    psum x1 -> x0, blocking collectives: 40 us -> none  [on_device(): norm_total, loss_total = lax.psum((weight_part, loss_part), ('feat', 'dp'))]
    all_gather x4 -> x0, blocking collectives: 37.7 us -> none  [the longest x1 10.9 us: on_device(): lax.all_gather(w1_neigh, 'feat', axis=0, tiled=True)]
    scatter-add x20 -> x0, other arithmetic: 34.4 us -> none  [adjoint_rows(): jax.ops.segment_sum(values, target, num_segments=count + 1)[:count]]
    ppermute x0 -> x18, waiting for transfers between devices: none -> 22.5 us  [exchange(): return lax.ppermute(value, axis, [(i, i ^ step) for i in range(size)])]
    pallas_call x0 -> x8, Pallas kernels: none -> 19.5 us  [call(): pl.pallas_call(kernel, out_shape=outs, in_specs=specs, out_specs=[pl.Bloc...]
    ppermute x0 -> x18, starting transfers between devices: none -> 18.5 us  [exchange(): return lax.ppermute(value, axis, [(i, i ^ step) for i in range(size)])]
  transfers between devices with their start and end apart: 4 -> 18, of which waited for: 3 -> 8; matrix products, arithmetic and copies ran while one was open for 2% -> 2% of each run, Pallas kernels for 0% -> 18%
where the time goes in v1:
time: 70.7 us; the launch traced here: 70.2 us
  waiting for transfers between devices  22.5 us (32%)
  Pallas kernels  19.5 us (28%)
  starting transfers between devices  18.5 us (26%)
  local copies, waits for them, and re-layouts  8.09 us (11%)
  other arithmetic  0.97 us (1%)
  between operations  0.77 us (1%)
    ppermute x18, waiting for transfers between devices, exchange(): return lax.ppermute(value, axis, [(i, i ^ step) for i in range(size)])  22.5 us
    pallas_call x8, Pallas kernels, call(): pl.pallas_call(kernel, out_shape=outs, in_specs=specs, out_specs=[pl.Bloc...  19.5 us
    ppermute x18, starting transfers between devices, exchange(): return lax.ppermute(value, axis, [(i, i ^ step) for i in range(size)])  18.5 us
    unnamed x45, local copies, waits for them, and re-layouts  8.09 us
  transfers between devices with their start and end apart: 18, of which 8 were waited for; matrix products, arithmetic and copies ran while one was open for 2% of the time, Pallas kernels for 18%

profile of v1, /device:TPU:0, one launch (start us, length us, event | category | flops | bytes accessed | tf_op | source)
XLA Modules:
  0.0 70.2 jit_solution(9704528169156807729)
XLA Ops:
  0.6 0.0 copy-start.1
  0.7 0.0 copy-start.4
  0.7 1.0 %broadcast_select_fusion = bf16[256,256]{1,0:T(8,128)(2,1)S(1)} fusion(bf16[256,256]{1,0:T(8,128)(2,1)} %refs_6_.1, bf16[256,256]{1,0:T(8,128)(2,1)} %refs_7_.1, pred[]{:T(512)S(6)} %eq.5), kind=kLoop, calls=%fused_computation | loop fusion | flops 65536 | bytes 393217 | tf_op jit(solution)/shard_map/jit(_where)/select_n | solution.py:212
  1.6 0.0 copy-start.5
  1.7 4.0 %collective-permute-start.5 = (bf16[256,256]{1,0:T(8,128)(2,1)S(1)}, bf16[256,256]{1,0:T(8,128)(2,1)S(1)}, u32[]{:S(2)}, u32[]{:S(2)}) collective-permute-start(bf16[256,256]{1,0:T(8,128)(2,1)S(1)} %broadcast_select_fusion), channel_id=1, source_target_pairs={{0,24},{8,16},{16,8},{24,0},{1,25},{9,17},{17,9},{25,1},{2,26},{10... | collective-permute-start | bytes 393224 | tf_op jit(solution)/shard_map/ppermute | solution.py:197
  5.6 0.5 collective-permute-start.4
  6.1 0.1 collective-permute-start.3
  6.3 3.3 %collective-permute-done.5.refs_14_ = bf16[256,256]{1,0:T(8,128)(2,1)S(1)} collective-permute-done((bf16[256,256]{1,0:T(8,128)(2,1)S(1)}, bf16[256,256]{1,0:T(8,128)(2,1)S(1)}, u32[]{:S(2)}, u32[]{:S(2)}) %collective-permute-start.5) | collective-permute-done | bytes 131104 | tf_op jit(solution)/shard_map/ppermute | solution.py:197
  9.5 0.0 collective-permute-start.8
  9.5 3.4 %collective-permute-start.2 = (bf16[256,512]{1,0:T(8,128)(2,1)S(1)}, bf16[256,512]{1,0:T(8,128)(2,1)S(1)}, u32[]{:S(2)}, u32[]{:S(2)}) collective-permute-start(bf16[256,512]{1,0:T(8,128)(2,1)S(1)} %copy-done.1), channel_id=1, source_target_pairs={{0,24},{8,16},{16,8},{24,0},{1,25},{9,17},{17,9},{25,1},{2,26},{10... | collective-permute-start | bytes 786440 | tf_op jit(solution)/shard_map/ppermute | solution.py:197
  13.0 0.5 collective-permute-start.1
  13.5 0.0 collective-permute-done.4.refs_13_
  13.5 0.2 collective-permute-start
  13.6 0.0 collective-permute-done.3.refs_12_
  13.6 0.0 collective-permute-start.7
  13.7 0.0 collective-permute-done.8.refs_17_
  13.7 0.5 collective-permute-start.6
  14.2 0.0 copy-done.4
  14.2 0.7 %copy.11.refs_4_.w2s_ref = bf16[256,172]{1,0:T(8,128)(2,1)} copy(bf16[256,172]{0,1:T(8,128)(2,1)S(1)} %copy-done.4) | data formatting | bytes 176128 | tf_op args[6]
  14.9 0.0 copy-done.5
  14.9 0.7 %copy.12.refs_5_.w2n_ref = bf16[256,172]{1,0:T(8,128)(2,1)} copy(bf16[256,172]{0,1:T(8,128)(2,1)S(1)} %copy-done.5) | data formatting | bytes 176128 | tf_op args[7]
  15.7 0.0 copy-done.17
  15.7 2.7 %shard_map.103.refs_3_.at_ref = bf16[512,512]{1,0:T(8,128)(2,1)} custom-call(s32[10,512]{1,0:T(8,128)} %bitcast.6), custom_call_target="tpu_custom_call" | custom-call | flops 2621440 | bytes 544768 | tf_op jit(solution)/shard_map/pallas_call | solution.py:40
  18.3 0.0 collective-permute-done.7.refs_16_
  18.3 0.0 collective-permute-done.6.refs_15_
  18.3 0.0 copy-start.20
  18.4 1.8 %collective-permute-done.2.refs_11_ = bf16[256,512]{1,0:T(8,128)(2,1)S(1)} collective-permute-done((bf16[256,512]{1,0:T(8,128)(2,1)S(1)}, bf16[256,512]{1,0:T(8,128)(2,1)S(1)}, u32[]{:S(2)}, u32[]{:S(2)}) %collective-permute-start.2) | collective-permute-done | bytes 262176 | tf_op jit(solution)/shard_map/ppermute | solution.py:197
  20.2 5.3 %collective-permute-done.1.refs_10_ = bf16[256,512]{1,0:T(8,128)(2,1)S(1)} collective-permute-done((bf16[256,512]{1,0:T(8,128)(2,1)S(1)}, bf16[256,512]{1,0:T(8,128)(2,1)S(1)}, u32[]{:S(2)}, u32[]{:S(2)}) %collective-permute-start.1) | collective-permute-done | bytes 262176 | tf_op jit(solution)/shard_map/ppermute | solution.py:197
  25.5 0.3 collective-permute-done.refs_9_
  25.8 0.0 copy-done.12
  25.8 0.4 copy-done.13
  26.2 0.3 copy-done.14
  26.5 4.6 %shard_map.104 = (f32[176,256]{1,0:T(8,128)}, f32[176,256]{1,0:T(8,128)}, bf16[172,512]{1,0:T(8,128)(2,1)}, bf16[256,512]{1,0:T(8,128)(2,1)}) custom-call(s32[1]{0:T(128)} %bitcast.refs_0_.core_ref, s32[1,512]{1,0:T(1,128)} %bitcast.7, f32[1,512]{1,0:T(1,128)} %bitcast.8, bf16[512,512]{1,0:T(8,128)(2,1)} %shard_map.103.refs_3_.at_ref, ...), custom_call_target="tpu_custom_call" | custom-call | flops 805306368 | bytes 3600388 | tf_op jit(solution)/shard_map/pallas_call | solution.py:40
  31.1 0.0 collective-permute-start.9
  31.1 3.3 %shard_map.108 = (f32[4,2,32,256]{3,2,1,0:T(8,128)}, f32[4,2,32,256]{3,2,1,0:T(8,128)}) custom-call(s32[1]{0:T(128)} %bitcast.refs_0_.core_ref, bf16[172,512]{1,0:T(8,128)(2,1)} %get-tuple-element.18.g_ref, bf16[256,512]{1,0:T(8,128)(2,1)} %get-tuple-element.19.hidden_ref, bf16[512,512]{1,0:T(8,128)(2,1)} %shard_map.103.refs_3_.at_ref, ...), custom_call_target="tpu_custom_call" | custom-call | flops 402653184 | bytes 1925124 | tf_op jit(solution)/shard_map/pallas_call | solution.py:40
  34.4 0.5 collective-permute-start.14
  34.9 0.0 collective-permute-done.9.recv_ref
  34.9 0.7 copy-done.2
  35.5 1.7 %shard_map.105.refs_0_ = bf16[176,256]{1,0:T(8,128)(2,1)} custom-call(f32[176,256]{1,0:T(8,128)} %get-tuple-element.15.keep_ref, f32[176,256]{1,0:T(8,128)} %copy-done.2), custom_call_target="tpu_custom_call" | custom-call | bytes 450560 | tf_op jit(solution)/shard_map/pallas_call | solution.py:40
  37.2 3.6 %collective-permute-start.12 = (bf16[176,256]{1,0:T(8,128)(2,1)}, bf16[176,256]{1,0:T(8,128)(2,1)S(1)}, u32[]{:S(2)}, u32[]{:S(2)}) collective-permute-start(bf16[176,256]{1,0:T(8,128)(2,1)} %shard_map.105.refs_0_), channel_id=1, source_target_pairs={{0,6},{1,7},{2,4},{3,5},{4,2},{5,3},{6,0},{7,1},{8,14},{9,15},{10,... | collective-permute-start | bytes 270344 | tf_op jit(solution)/shard_map/ppermute | solution.py:197
  40.8 0.0 collective-permute-start.11
  40.8 0.8 %collective-permute-start.10 = (bf16[176,256]{1,0:T(8,128)(2,1)}, bf16[176,256]{1,0:T(8,128)(2,1)S(1)}, u32[]{:S(2)}, u32[]{:S(2)}) collective-permute-start(bf16[176,256]{1,0:T(8,128)(2,1)} %shard_map.105.refs_0_), channel_id=1, source_target_pairs={{0,2},{1,3},{2,0},{3,1},{4,6},{5,7},{6,4},{7,5},{8,10},{9,11},{10,... | collective-permute-start | bytes 270344 | tf_op jit(solution)/shard_map/ppermute | solution.py:197
  41.6 3.0 %collective-permute-done.12.refs_3_ = bf16[176,256]{1,0:T(8,128)(2,1)S(1)} collective-permute-done((bf16[176,256]{1,0:T(8,128)(2,1)}, bf16[176,256]{1,0:T(8,128)(2,1)S(1)}, u32[]{:S(2)}, u32[]{:S(2)}) %collective-permute-start.12) | collective-permute-done | bytes 90144 | tf_op jit(solution)/shard_map/ppermute | solution.py:197
  44.5 4.2 %collective-permute-done.11.refs_2_ = bf16[176,256]{1,0:T(8,128)(2,1)S(1)} collective-permute-done((bf16[176,256]{1,0:T(8,128)(2,1)}, bf16[176,256]{1,0:T(8,128)(2,1)S(1)}, u32[]{:S(2)}, u32[]{:S(2)}) %collective-permute-start.11) | collective-permute-done | bytes 90144 | tf_op jit(solution)/shard_map/ppermute | solution.py:197
  48.8 0.0 collective-permute-done.10.refs_1_
  48.8 0.6 copy-done.7
  49.4 0.6 copy-done.8
  50.0 1.7 %shard_map.106.own_ref.total_ref = f32[176,256]{1,0:T(8,128)} custom-call(bf16[176,256]{1,0:T(8,128)(2,1)} %shard_map.105.refs_0_, bf16[176,256]{1,0:T(8,128)(2,1)} %copy-done.8, bf16[176,256]{1,0:T(8,128)(2,1)} %copy-done.7, bf16[176,256]{1,0:T(8,128)(2,1)} %copy-done.6), custom_call_target="tpu_custom_call" | custom-call | bytes 540672 | tf_op jit(solution)/shard_map/pallas_call | solution.py:40
  51.7 0.0 collective-permute-start.13
  51.7 0.0 collective-permute-done.14.recv_ref
  51.8 0.7 copy-done
  52.5 1.7 %shard_map.109 = (f32[2,32,256]{2,1,0:T(8,128)}, bf16[2,32,256]{2,1,0:T(8,128)(2,1)}, bf16[2,32,256]{2,1,0:T(8,128)(2,1)}, bf16[2,32,256]{2,1,0:T(8,128)(2,1)}) custom-call(s32[1]{0:T(128)} %bitcast.5.z_ref, f32[4,2,32,256]{3,2,1,0:T(8,128)} %get-tuple-element.20.keep_ref, f32[4,2,32,256]{3,2,1,0:T(8,128)} %copy-done), custom_call_target="tpu_custom_call" | custom-call | bytes 688132 | tf_op jit(solution)/shard_map/pallas_call | solution.py:40
  54.2 0.1 collective-permute-start.15
  54.2 3.0 %collective-permute-start.16 = (bf16[2,32,256]{2,1,0:T(8,128)(2,1)}, bf16[2,32,256]{2,1,0:T(8,128)(2,1)S(1)}, u32[]{:S(2)}, u32[]{:S(2)}) collective-permute-start(bf16[2,32,256]{2,1,0:T(8,128)(2,1)} %get-tuple-element.24), channel_id=1, source_target_pairs={{0,4},{1,5},{2,6},{3,7},{4,0},{5,1},{6,2},{7,3},{8,12},{9,13},{10,... | collective-permute-start | bytes 98312 | tf_op jit(solution)/shard_map/ppermute | solution.py:197
  57.2 1.3 %collective-permute-start.17 = (bf16[2,32,256]{2,1,0:T(8,128)(2,1)}, bf16[2,32,256]{2,1,0:T(8,128)(2,1)S(1)}, u32[]{:S(2)}, u32[]{:S(2)}) collective-permute-start(bf16[2,32,256]{2,1,0:T(8,128)(2,1)} %get-tuple-element.25), channel_id=1, source_target_pairs={{0,6},{1,7},{2,4},{3,5},{4,2},{5,3},{6,0},{7,1},{8,14},{9,15},{10,... | collective-permute-start | bytes 98312 | tf_op jit(solution)/shard_map/ppermute | solution.py:197
  58.5 0.0 collective-permute-done.15.refs_1_
  58.6 0.8 %collective-permute-done.16.refs_2_ = bf16[2,32,256]{2,1,0:T(8,128)(2,1)S(1)} collective-permute-done((bf16[2,32,256]{2,1,0:T(8,128)(2,1)}, bf16[2,32,256]{2,1,0:T(8,128)(2,1)S(1)}, u32[]{:S(2)}, u32[]{:S(2)}) %collective-permute-start.16) | collective-permute-done | bytes 32800 | tf_op jit(solution)/shard_map/ppermute | solution.py:197
  59.3 3.8 %collective-permute-done.17.refs_3_ = bf16[2,32,256]{2,1,0:T(8,128)(2,1)S(1)} collective-permute-done((bf16[2,32,256]{2,1,0:T(8,128)(2,1)}, bf16[2,32,256]{2,1,0:T(8,128)(2,1)S(1)}, u32[]{:S(2)}, u32[]{:S(2)}) %collective-permute-start.17) | collective-permute-done | bytes 32800 | tf_op jit(solution)/shard_map/ppermute | solution.py:197
  63.1 0.6 copy-done.11
  63.7 1.7 %shard_map.110 = f32[2,32,256]{2,1,0:T(8,128)} custom-call(f32[176,256]{1,0:T(8,128)} %shard_map.106.own_ref.total_ref, f32[2,32,256]{2,1,0:T(8,128)} %get-tuple-element.22.refs_0_, bf16[2,32,256]{2,1,0:T(8,128)(2,1)} %copy-done.9, bf16[2,32,256]{2,1,0:T(8,128)(2,1)} %copy-done.10, bf16[2,32,256]{2,1,0:T(8,128)(2,1)} %copy-done.11), custom_call_target="tpu_custom_call" | custom-call | bytes 409600 | tf_op jit(solution)/shard_map/pallas_call | solution.py:40
  65.5 0.0 collective-permute-done.13.other_ref
  65.5 0.7 copy-done.3
  66.2 2.1 %shard_map.107 = (f32[2,256,172]{2,1,0:T(8,128)}, f32[1,1]{1,0:T(1,128)}) custom-call(s32[1]{0:T(128)} %bitcast.refs_0_.core_ref, f32[176,256]{1,0:T(8,128)} %shard_map.106.own_ref.total_ref, f32[176,256]{1,0:T(8,128)} %copy-done.3), custom_call_target="tpu_custom_call" | custom-call | bytes 712712 | tf_op jit(solution)/shard_map/pallas_call | solution.py:40
  68.3 2.0 %copy.15 = f32[2,256,172]{1,0,2:T(2,128)} copy(f32[2,256,172]{2,1,0:T(8,128)} %get-tuple-element.29) | data formatting | bytes 704512
  (26 shorter events, 0.0 us)
Async XLA Ops:
  0.6 8.9 %copy-start.1 = (bf16[256,512]{1,0:T(8,128)(2,1)S(1)}, bf16[256,512]{1,0:T(8,128)(2,1)}, u32[]{:S(2)}) copy-start(bf16[256,512]{1,0:T(8,128)(2,1)} %f_ref.1) | copy-start | bytes 786436
  0.7 13.5 %copy-start.4 = (bf16[256,172]{0,1:T(8,128)(2,1)S(1)}, bf16[256,172]{0,1:T(8,128)(2,1)}, u32[]{:S(2)}) copy-start(bf16[256,172]{0,1:T(8,128)(2,1)} %param.14) | copy-start | bytes 264196
  1.6 13.3 %copy-start.5 = (bf16[256,172]{0,1:T(8,128)(2,1)S(1)}, bf16[256,172]{0,1:T(8,128)(2,1)}, u32[]{:S(2)}) copy-start(bf16[256,172]{0,1:T(8,128)(2,1)} %param.15) | copy-start | bytes 264196
  1.7 7.9 %collective-permute-start.5 = (bf16[256,256]{1,0:T(8,128)(2,1)S(1)}, bf16[256,256]{1,0:T(8,128)(2,1)S(1)}, u32[]{:S(2)}, u32[]{:S(2)}) collective-permute-start(bf16[256,256]{1,0:T(8,128)(2,1)S(1)} %broadcast_select_fusion), channel_id=1, source_target_pairs={{0,24},{8,16},{16,8},{24,0},{1,25},{9,17},{17,9},{25,1},{2,26},{10... | collective-permute-start | bytes 393224 | tf_op jit(solution)/shard_map/ppermute | solution.py:197
  5.6 7.9 %collective-permute-start.4 = (bf16[256,256]{1,0:T(8,128)(2,1)S(1)}, bf16[256,256]{1,0:T(8,128)(2,1)S(1)}, u32[]{:S(2)}, u32[]{:S(2)}) collective-permute-start(bf16[256,256]{1,0:T(8,128)(2,1)S(1)} %broadcast_select_fusion), channel_id=1, source_target_pairs={{0,16},{8,24},{16,0},{24,8},{1,17},{9,25},{17,1},{25,9},{2,18},{10... | collective-permute-start | bytes 393224 | tf_op jit(solution)/shard_map/ppermute | solution.py:197
  6.1 7.5 %collective-permute-start.3 = (bf16[256,256]{1,0:T(8,128)(2,1)S(1)}, bf16[256,256]{1,0:T(8,128)(2,1)S(1)}, u32[]{:S(2)}, u32[]{:S(2)}) collective-permute-start(bf16[256,256]{1,0:T(8,128)(2,1)S(1)} %broadcast_select_fusion), channel_id=1, source_target_pairs={{0,8},{8,0},{16,24},{24,16},{1,9},{9,1},{17,25},{25,17},{2,10},{10... | collective-permute-start | bytes 393224 | tf_op jit(solution)/shard_map/ppermute | solution.py:197
  9.5 6.1 %copy-start.15 = (bf16[256,256]{1,0:T(8,128)(2,1)}, bf16[256,256]{1,0:T(8,128)(2,1)S(1)}, u32[]{:S(2)}) copy-start(bf16[256,256]{1,0:T(8,128)(2,1)S(1)} %collective-permute-done.5.refs_14_) | copy-start | bytes 393220
  9.5 4.1 %collective-permute-start.8 = (bf16[256,256]{1,0:T(8,128)(2,1)S(1)}, bf16[256,256]{1,0:T(8,128)(2,1)S(1)}, u32[]{:S(2)}, u32[]{:S(2)}) collective-permute-start(bf16[256,256]{1,0:T(8,128)(2,1)S(1)} %collective-permute-done.5.refs_14_), channel_id=1, source_target_pairs={{0,1},{1,0},{2,3},{3,2},{4,5},{5,4},{6,7},{7,6},{8,9},{9,8},{10,11... | collective-permute-start | bytes 393224 | tf_op jit(solution)/shard_map/ppermute | solution.py:197
  9.5 10.7 %collective-permute-start.2 = (bf16[256,512]{1,0:T(8,128)(2,1)S(1)}, bf16[256,512]{1,0:T(8,128)(2,1)S(1)}, u32[]{:S(2)}, u32[]{:S(2)}) collective-permute-start(bf16[256,512]{1,0:T(8,128)(2,1)S(1)} %copy-done.1), channel_id=1, source_target_pairs={{0,24},{8,16},{16,8},{24,0},{1,25},{9,17},{17,9},{25,1},{2,26},{10... | collective-permute-start | bytes 786440 | tf_op jit(solution)/shard_map/ppermute | solution.py:197
  13.0 12.5 %collective-permute-start.1 = (bf16[256,512]{1,0:T(8,128)(2,1)S(1)}, bf16[256,512]{1,0:T(8,128)(2,1)S(1)}, u32[]{:S(2)}, u32[]{:S(2)}) collective-permute-start(bf16[256,512]{1,0:T(8,128)(2,1)S(1)} %copy-done.1), channel_id=1, source_target_pairs={{0,16},{8,24},{16,0},{24,8},{1,17},{9,25},{17,1},{25,9},{2,18},{10... | collective-permute-start | bytes 786440 | tf_op jit(solution)/shard_map/ppermute | solution.py:197
  13.5 2.2 %copy-start.16 = (bf16[256,256]{1,0:T(8,128)(2,1)}, bf16[256,256]{1,0:T(8,128)(2,1)S(1)}, u32[]{:S(2)}) copy-start(bf16[256,256]{1,0:T(8,128)(2,1)S(1)} %collective-permute-done.4.refs_13_) | copy-start | bytes 393220
  13.5 12.3 %collective-permute-start = (bf16[256,512]{1,0:T(8,128)(2,1)S(1)}, bf16[256,512]{1,0:T(8,128)(2,1)S(1)}, u32[]{:S(2)}, u32[]{:S(2)}) collective-permute-start(bf16[256,512]{1,0:T(8,128)(2,1)S(1)} %copy-done.1), channel_id=1, source_target_pairs={{0,8},{8,0},{16,24},{24,16},{1,9},{9,1},{17,25},{25,17},{2,10},{10... | collective-permute-start | bytes 786440 | tf_op jit(solution)/shard_map/ppermute | solution.py:197
  13.6 2.0 %copy-start.17 = (bf16[256,256]{1,0:T(8,128)(2,1)}, bf16[256,256]{1,0:T(8,128)(2,1)S(1)}, u32[]{:S(2)}) copy-start(bf16[256,256]{1,0:T(8,128)(2,1)S(1)} %collective-permute-done.3.refs_12_) | copy-start | bytes 393220
  13.6 4.7 %collective-permute-start.7 = (bf16[256,256]{1,0:T(8,128)(2,1)S(1)}, bf16[256,256]{1,0:T(8,128)(2,1)S(1)}, u32[]{:S(2)}, u32[]{:S(2)}) collective-permute-start(bf16[256,256]{1,0:T(8,128)(2,1)S(1)} %collective-permute-done.4.refs_13_), channel_id=1, source_target_pairs={{0,1},{1,0},{2,3},{3,2},{4,5},{5,4},{6,7},{7,6},{8,9},{9,8},{10,11... | collective-permute-start | bytes 393224 | tf_op jit(solution)/shard_map/ppermute | solution.py:197
  13.7 4.7 %copy-start.18 = (bf16[256,256]{1,0:T(8,128)(2,1)}, bf16[256,256]{1,0:T(8,128)(2,1)S(1)}, u32[]{:S(2)}) copy-start(bf16[256,256]{1,0:T(8,128)(2,1)S(1)} %collective-permute-done.8.refs_17_) | copy-start | bytes 393220
  13.7 4.7 %collective-permute-start.6 = (bf16[256,256]{1,0:T(8,128)(2,1)S(1)}, bf16[256,256]{1,0:T(8,128)(2,1)S(1)}, u32[]{:S(2)}, u32[]{:S(2)}) collective-permute-start(bf16[256,256]{1,0:T(8,128)(2,1)S(1)} %collective-permute-done.3.refs_12_), channel_id=1, source_target_pairs={{0,1},{1,0},{2,3},{3,2},{4,5},{5,4},{6,7},{7,6},{8,9},{9,8},{10,11... | collective-permute-start | bytes 393224 | tf_op jit(solution)/shard_map/ppermute | solution.py:197
  18.3 7.5 %copy-start.19 = (bf16[256,256]{1,0:T(8,128)(2,1)}, bf16[256,256]{1,0:T(8,128)(2,1)S(1)}, u32[]{:S(2)}) copy-start(bf16[256,256]{1,0:T(8,128)(2,1)S(1)} %collective-permute-done.7.refs_16_) | copy-start | bytes 393220
  18.3 7.5 %copy-start.20 = (bf16[256,256]{1,0:T(8,128)(2,1)}, bf16[256,256]{1,0:T(8,128)(2,1)S(1)}, u32[]{:S(2)}) copy-start(bf16[256,256]{1,0:T(8,128)(2,1)S(1)} %collective-permute-done.6.refs_15_) | copy-start | bytes 393220
  20.2 5.6 %copy-start.12 = (bf16[256,512]{1,0:T(8,128)(2,1)}, bf16[256,512]{1,0:T(8,128)(2,1)S(1)}, u32[]{:S(2)}) copy-start(bf16[256,512]{1,0:T(8,128)(2,1)S(1)} %collective-permute-done.2.refs_11_) | copy-start | bytes 786436
  25.5 0.7 %copy-start.13 = (bf16[256,512]{1,0:T(8,128)(2,1)}, bf16[256,512]{1,0:T(8,128)(2,1)S(1)}, u32[]{:S(2)}) copy-start(bf16[256,512]{1,0:T(8,128)(2,1)S(1)} %collective-permute-done.1.refs_10_) | copy-start | bytes 786436
  25.8 0.7 %copy-start.14 = (bf16[256,512]{1,0:T(8,128)(2,1)}, bf16[256,512]{1,0:T(8,128)(2,1)S(1)}, u32[]{:S(2)}) copy-start(bf16[256,512]{1,0:T(8,128)(2,1)S(1)} %collective-permute-done.refs_9_) | copy-start | bytes 786436
  31.1 3.8 %collective-permute-start.9 = (f32[176,256]{1,0:T(8,128)}, f32[176,256]{1,0:T(8,128)S(1)}, u32[]{:S(2)}, u32[]{:S(2)}) collective-permute-start(f32[176,256]{1,0:T(8,128)} %get-tuple-element.16), channel_id=1, source_target_pairs={{0,1},{1,0},{2,3},{3,2},{4,5},{5,4},{6,7},{7,6},{8,9},{9,8},{10,11... | collective-permute-start | bytes 540680 | tf_op jit(solution)/shard_map/ppermute | solution.py:197
  34.4 17.4 %collective-permute-start.14 = (f32[4,2,32,256]{3,2,1,0:T(8,128)}, f32[4,2,32,256]{3,2,1,0:T(8,128)S(1)}, u32[]{:S(2)}, u32[]{:S(2)}) collective-permute-start(f32[4,2,32,256]{3,2,1,0:T(8,128)} %get-tuple-element.21), channel_id=1, source_target_pairs={{0,1},{1,0},{2,3},{3,2},{4,5},{5,4},{6,7},{7,6},{8,9},{9,8},{10,11... | collective-permute-start | bytes 786440 | tf_op jit(solution)/shard_map/ppermute | solution.py:197
  34.9 0.7 copy-start.2
  37.2 7.3 %collective-permute-start.12 = (bf16[176,256]{1,0:T(8,128)(2,1)}, bf16[176,256]{1,0:T(8,128)(2,1)S(1)}, u32[]{:S(2)}, u32[]{:S(2)}) collective-permute-start(bf16[176,256]{1,0:T(8,128)(2,1)} %shard_map.105.refs_0_), channel_id=1, source_target_pairs={{0,6},{1,7},{2,4},{3,5},{4,2},{5,3},{6,0},{7,1},{8,14},{9,15},{10,... | collective-permute-start | bytes 270344 | tf_op jit(solution)/shard_map/ppermute | solution.py:197
  40.8 7.9 %collective-permute-start.11 = (bf16[176,256]{1,0:T(8,128)(2,1)}, bf16[176,256]{1,0:T(8,128)(2,1)S(1)}, u32[]{:S(2)}, u32[]{:S(2)}) collective-permute-start(bf16[176,256]{1,0:T(8,128)(2,1)} %shard_map.105.refs_0_), channel_id=1, source_target_pairs={{0,4},{1,5},{2,6},{3,7},{4,0},{5,1},{6,2},{7,3},{8,12},{9,13},{10,... | collective-permute-start | bytes 270344 | tf_op jit(solution)/shard_map/ppermute | solution.py:197
  40.8 7.9 %collective-permute-start.10 = (bf16[176,256]{1,0:T(8,128)(2,1)}, bf16[176,256]{1,0:T(8,128)(2,1)S(1)}, u32[]{:S(2)}, u32[]{:S(2)}) collective-permute-start(bf16[176,256]{1,0:T(8,128)(2,1)} %shard_map.105.refs_0_), channel_id=1, source_target_pairs={{0,2},{1,3},{2,0},{3,1},{4,6},{5,7},{6,4},{7,5},{8,10},{9,11},{10,... | collective-permute-start | bytes 270344 | tf_op jit(solution)/shard_map/ppermute | solution.py:197
  44.5 4.2 %copy-start.6 = (bf16[176,256]{1,0:T(8,128)(2,1)}, bf16[176,256]{1,0:T(8,128)(2,1)S(1)}, u32[]{:S(2)}) copy-start(bf16[176,256]{1,0:T(8,128)(2,1)S(1)} %collective-permute-done.12.refs_3_) | copy-start | bytes 270340
  48.8 0.6 copy-start.7
  49.4 0.6 copy-start.8
  51.7 13.7 %collective-permute-start.13 = (f32[176,256]{1,0:T(8,128)}, f32[176,256]{1,0:T(8,128)S(1)}, u32[]{:S(2)}, u32[]{:S(2)}) collective-permute-start(f32[176,256]{1,0:T(8,128)} %shard_map.106.own_ref.total_ref), channel_id=1, source_target_pairs={{0,1},{1,0},{2,3},{3,2},{4,5},{5,4},{6,7},{7,6},{8,9},{9,8},{10,11... | collective-permute-start | bytes 540680 | tf_op jit(solution)/shard_map/ppermute | solution.py:197
  51.8 0.7 %copy-start = (f32[4,2,32,256]{3,2,1,0:T(8,128)}, f32[4,2,32,256]{3,2,1,0:T(8,128)S(1)}, u32[]{:S(2)}) copy-start(f32[4,2,32,256]{3,2,1,0:T(8,128)S(1)} %collective-permute-done.14.recv_ref) | copy-start | bytes 786436
  54.2 4.4 %collective-permute-start.15 = (bf16[2,32,256]{2,1,0:T(8,128)(2,1)}, bf16[2,32,256]{2,1,0:T(8,128)(2,1)S(1)}, u32[]{:S(2)}, u32[]{:S(2)}) collective-permute-start(bf16[2,32,256]{2,1,0:T(8,128)(2,1)} %get-tuple-element.23), channel_id=1, source_target_pairs={{0,2},{1,3},{2,0},{3,1},{4,6},{5,7},{6,4},{7,5},{8,10},{9,11},{10,... | collective-permute-start | bytes 98312 | tf_op jit(solution)/shard_map/ppermute | solution.py:197
  54.2 5.1 %collective-permute-start.16 = (bf16[2,32,256]{2,1,0:T(8,128)(2,1)}, bf16[2,32,256]{2,1,0:T(8,128)(2,1)S(1)}, u32[]{:S(2)}, u32[]{:S(2)}) collective-permute-start(bf16[2,32,256]{2,1,0:T(8,128)(2,1)} %get-tuple-element.24), channel_id=1, source_target_pairs={{0,4},{1,5},{2,6},{3,7},{4,0},{5,1},{6,2},{7,3},{8,12},{9,13},{10,... | collective-permute-start | bytes 98312 | tf_op jit(solution)/shard_map/ppermute | solution.py:197
  57.2 5.9 %collective-permute-start.17 = (bf16[2,32,256]{2,1,0:T(8,128)(2,1)}, bf16[2,32,256]{2,1,0:T(8,128)(2,1)S(1)}, u32[]{:S(2)}, u32[]{:S(2)}) collective-permute-start(bf16[2,32,256]{2,1,0:T(8,128)(2,1)} %get-tuple-element.25), channel_id=1, source_target_pairs={{0,6},{1,7},{2,4},{3,5},{4,2},{5,3},{6,0},{7,1},{8,14},{9,15},{10,... | collective-permute-start | bytes 98312 | tf_op jit(solution)/shard_map/ppermute | solution.py:197
  58.5 4.6 %copy-start.9 = (bf16[2,32,256]{2,1,0:T(8,128)(2,1)}, bf16[2,32,256]{2,1,0:T(8,128)(2,1)S(1)}, u32[]{:S(2)}) copy-start(bf16[2,32,256]{2,1,0:T(8,128)(2,1)S(1)} %collective-permute-done.15.refs_1_) | copy-start | bytes 98308
  59.3 3.8 %copy-start.10 = (bf16[2,32,256]{2,1,0:T(8,128)(2,1)}, bf16[2,32,256]{2,1,0:T(8,128)(2,1)S(1)}, u32[]{:S(2)}) copy-start(bf16[2,32,256]{2,1,0:T(8,128)(2,1)S(1)} %collective-permute-done.16.refs_2_) | copy-start | bytes 98308
  63.1 0.6 copy-start.11
  65.5 0.7 copy-start.3

commit v2 on v1

v2 whole, which is shorter than its diff:
```python
import functools

import jax
import jax.numpy as jnp
from jax import lax
from jax.experimental import pallas as pl
from jax.experimental.pallas import tpu as pltpu
from jax.sharding import PartitionSpec as P

BF16 = jnp.bfloat16
F32 = jnp.float32


def dot_nn(left, right):
    return lax.dot_general(left, right, (((1,), (0,)), ((), ())), preferred_element_type=F32)


def dot_nt(left, right):
    return lax.dot_general(left, right, (((1,), (1,)), ((), ())), preferred_element_type=F32)


def dot_tn(left, right):
    return lax.dot_general(left, right, (((0,), (0,)), ((), ())), preferred_element_type=F32)


def tree_sum(terms):
    terms = list(terms)
    while len(terms) > 1:
        terms = [terms[i] + terms[i + 1] for i in range(0, len(terms), 2)]
    return terms[0]


def call(kernel, outs, args, flops=0, scratch=(), smem=(), limit=16, final=False):
    size = sum(a.size * a.dtype.itemsize for a in args)
    size += sum(o.dtype.itemsize * o.size for o in outs)
    spaces = [pltpu.SMEM if i in smem else pltpu.VMEM for i in range(len(args))]
    placed = [a if i in smem else pltpu.with_memory_space_constraint(a, pltpu.VMEM) for i, a in enumerate(args)]
    return pl.pallas_call(
        kernel,
        out_shape=outs if final else [pltpu.VMEM(o.shape, o.dtype) for o in outs],
        in_specs=[pl.BlockSpec(memory_space=space) for space in spaces],
        out_specs=[pl.BlockSpec(memory_space=pltpu.VMEM)] * len(outs),
        scratch_shapes=list(scratch),
        cost_estimate=pl.CostEstimate(flops=flops, bytes_accessed=size, transcendentals=0),
        compiler_params=pltpu.CompilerParams(vmem_limit_bytes=limit * 1024 * 1024),
    )(*placed)


def shape(dims, dtype):
    return jax.ShapeDtypeStruct(dims, dtype)


def count_kernel(fanout, nbr_ref, *refs):
    at_ref, stack_ref = refs[-2:]
    for i, ref in enumerate(refs[:-2]):
        stack_ref[i] = ref[...]
    nodes = at_ref.shape[1]
    step = 32

    def body(i, carry):
        row = lax.broadcasted_iota(jnp.int32, (step, nodes), 0) + i * step
        total = jnp.zeros((step, nodes), F32)
        for k in range(fanout):
            total = total + jnp.where(nbr_ref[k : k + 1, :] == row, 1.0, 0.0)
        at_ref[pl.ds(pl.multiple_of(i * step, step), step), :] = total.astype(BF16)
        return carry

    lax.fori_loop(0, nodes // step, body, 0)


def forward_kernel(parts, fanout, *refs):
    core_ref, labels_ref, weight_ref, at_ref, w2s_ref, w2n_ref, ws_ref, wn_ref, mine_ref, partner_ref = refs[:10]
    feat_count = len(parts)
    f_refs = refs[10 : 10 + sum(parts)]
    send_ref, keep_ref, g_ref, hidden_ref, proj, pair, joined = refs[10 + sum(parts) :]
    blocks, at_ref_index, join_index = [], 0, 0
    for count in parts:
        if count == 1:
            blocks.append(f_refs[at_ref_index][...])
        else:
            start = 0
            for ref in f_refs[at_ref_index : at_ref_index + count]:
                joined[join_index, start : start + ref.shape[0]] = ref[...]
                start += ref.shape[0]
            blocks.append(joined[join_index])
            join_index += 1
        at_ref_index += count
    core = core_ref[0]
    classes = w2s_ref.shape[0]
    nodes = at_ref.shape[1]
    scale = 1.0 / fanout
    first = core == 0
    own_mine = jnp.where(first, ws_ref[...], wn_ref[...])
    own_partner = jnp.where(first, wn_ref[...], ws_ref[...])
    proj[core] = tree_sum(
        [dot_tn(own_mine, blocks[0])]
        + [dot_tn(mine_ref[s - 1], blocks[s]) for s in range(1, feat_count)]
    )
    proj[1 - core] = tree_sum(
        [dot_tn(own_partner, blocks[0])]
        + [dot_tn(partner_ref[s - 1], blocks[s]) for s in range(1, feat_count)]
    )
    at = at_ref[...]
    pre = proj[0] + dot_nn(proj[1].astype(BF16), at) * scale
    hidden = jnp.maximum(pre, 0.0).astype(BF16)
    hidden_ref[...] = hidden
    second = (dot_nn(hidden, at) * scale).astype(BF16)
    logits = dot_nn(w2s_ref[...], hidden) + dot_nn(w2n_ref[...], second)
    shifted = logits - jnp.max(logits, axis=0, keepdims=True)
    logprob = shifted - jnp.log(jnp.sum(jnp.exp(shifted), axis=0, keepdims=True))
    hot = lax.broadcasted_iota(jnp.int32, (classes, nodes), 0) == labels_ref[...]
    picked = jnp.sum(jnp.where(hot, logprob, 0.0), axis=0, keepdims=True)
    chance = jnp.exp(picked)
    rest = 1.0 - chance
    weight = weight_ref[...]
    terms = -rest * rest * picked
    slope = weight * (2.0 * rest * chance * picked - rest * rest)
    grad = (slope * (jnp.where(hot, 1.0, 0.0) - jnp.exp(logprob))).astype(BF16)
    g_ref[...] = grad
    pair[0] = hidden
    pair[1] = second
    loss_part = jnp.sum(weight * terms)
    norm_part = jnp.sum(weight)
    for out_ref, which in ((send_ref, 1 - core), (keep_ref, core)):
        rows, cols = out_ref.shape
        row = lax.broadcasted_iota(jnp.int32, (rows, cols), 0)
        col = lax.broadcasted_iota(jnp.int32, (rows, cols), 1)
        extra = jnp.where(col == 0, loss_part, jnp.where(col == 1, norm_part, 0.0))
        out_ref[...] = jnp.where(row >= classes, extra, 0.0)
        out_ref[:classes, :] = dot_nt(grad, pair[which])


def backward_kernel(
    fanout, groups, core_ref, g_ref, hidden_ref, at_ref, w2s_ref, w2n_ref, f_ref, send_ref, keep_ref
):
    core = core_ref[0]
    scale = 1.0 / fanout
    grad = g_ref[...]
    at = at_ref[...]
    summed = dot_nt(grad, at)
    high = summed.astype(BF16)
    low = (summed - high.astype(F32)).astype(BF16)
    w2n = w2n_ref[...]
    hidden_grad = dot_tn(w2s_ref[...], grad) + (dot_tn(w2n, high) + dot_tn(w2n, low)) * scale
    pre_grad = jnp.where(hidden_ref[...] > 0, hidden_grad, 0.0).astype(BF16)
    proj_grad = (dot_nt(pre_grad, at) * scale).astype(BF16)
    features = f_ref[...]
    full = (dot_nt(features, pre_grad), dot_nt(features, proj_grad))
    rows = send_ref.shape[1] // 2
    first = core == 0
    for z in range(groups):
        for part in range(2):
            low_rows = full[part][2 * z * rows : (2 * z + 1) * rows]
            high_rows = full[part][(2 * z + 1) * rows : (2 * z + 2) * rows]
            send_ref[z, part * rows : (part + 1) * rows] = jnp.where(first, high_rows, low_rows)
            keep_ref[z, part * rows : (part + 1) * rows] = jnp.where(first, low_rows, high_rows)


def pack_kernel(classes, groups, z_ref, keep2_ref, recv2_ref, keep1_ref, recv1_ref, own2_ref, own1_ref, *pack_refs):
    z = z_ref[0]
    total = keep2_ref[...] + recv2_ref[...]
    high = total.astype(BF16).astype(F32)
    rest = total - high
    middle = rest.astype(BF16).astype(F32)
    low = rest - middle
    row = lax.broadcasted_iota(jnp.int32, total.shape, 0)
    out = jnp.where(row == classes + 1, middle, jnp.where(row == classes + 2, low, high)).astype(BF16)
    own2_ref[...] = out
    own1_ref[...] = keep1_ref[z] + recv1_ref[z]
    padded = total.shape[0]
    for s in range(1, groups):
        other = jnp.bitwise_xor(z, s)
        pack_refs[s - 1][:padded] = out
        pack_refs[s - 1][padded:] = (keep1_ref[other] + recv1_ref[other]).astype(BF16)


def second_sum_kernel(*refs):
    out_ref = refs[-1]
    padded = out_ref.shape[0]
    out_ref[...] = tree_sum([r[:padded].astype(F32) for r in refs[:-1]])


def scalars(total, classes):
    row = lax.broadcasted_iota(jnp.int32, total.shape, 0)
    col = lax.broadcasted_iota(jnp.int32, total.shape, 1)
    inside = jnp.logical_and(row >= classes, row < classes + 3)
    loss = jnp.sum(jnp.where(jnp.logical_and(inside, col == 0), total, 0.0), keepdims=True)
    norm = jnp.sum(jnp.where(jnp.logical_and(inside, col == 1), total, 0.0), keepdims=True)
    return loss, norm


def second_out_kernel(classes, core_ref, own_ref, other_ref, out_ref, loss_ref):
    first = core_ref[0] == 0
    loss, norm = scalars(own_ref[...], classes)
    inverse = 1.0 / norm
    own = own_ref[:classes, :] * inverse
    other = other_ref[:classes, :] * inverse
    out_ref[:, 0, :] = jnp.where(first, own, other)
    out_ref[:, 1, :] = jnp.where(first, other, own)
    loss_ref[...] = loss * inverse


def first_out_kernel(classes, total_ref, own_ref, *refs):
    _, norm = scalars(total_ref[...], classes)
    out_ref = refs[-1]
    padded = total_ref.shape[0]
    summed = tree_sum([own_ref[...]] + [r[padded:].astype(F32) for r in refs[:-1]]) * (1.0 / norm)
    rows = out_ref.shape[1]
    out_ref[0] = summed[:rows]
    out_ref[1] = summed[rows:]


def exchange(value, axis, step):
    size = lax.axis_size(axis)
    return lax.ppermute(value, axis, [(i, i ^ step) for i in range(size)])


def gather_parts(block, count):
    half = block.shape[0] // 2
    parts = [[block]]
    for s in range(1, count):
        low_bit = s & -s
        rest = s ^ low_bit
        if rest == 0:
            parts.append([exchange(block, "feat", s)])
        else:
            low = parts[rest][0][:half] if len(parts[rest]) == 1 else parts[rest][0]
            high = parts[low_bit][0][half:]
            parts.append([exchange(low, "feat", low_bit), exchange(high, "feat", rest)])
    return parts


def on_device(features, neighbors, labels, loss_weight, w1_self, w1_neigh, w2_self, w2_neigh):
    feat_count = lax.axis_size("feat")
    dp_count = lax.axis_size("dp")
    groups = dp_count // 2
    nodes, fanout = neighbors.shape
    rows, hid = w1_self.shape
    classes = w2_self.shape[1]
    place = lax.axis_index("dp").astype(jnp.int32)
    core = (place % 2).reshape(1)
    z = (place // 2).reshape(1)

    wide = gather_parts(features, feat_count)
    parts = tuple(len(w) for w in wide)
    mine_own = jnp.where(core[0] == 0, w1_self, w1_neigh)
    mine = [exchange(mine_own, "feat", s) for s in range(1, feat_count)]
    at, stacked = call(
        functools.partial(count_kernel, fanout),
        [shape((nodes, nodes), BF16), shape((feat_count - 1, rows, hid), BF16)],
        [neighbors.T] + mine,
        flops=nodes * nodes * fanout,
    )
    partner = exchange(stacked, "dp", 1)
    w2s, w2n = w2_self.T, w2_neigh.T
    limit = 12 + 6 * nodes * nodes // (1024 * 1024)
    padded = (classes + 3 + 15) // 16 * 16
    send2, keep2, grad, hidden = call(
        functools.partial(forward_kernel, parts, fanout),
        [
            shape((padded, hid), F32),
            shape((padded, hid), F32),
            shape((classes, nodes), BF16),
            shape((hid, nodes), BF16),
        ],
        [core, labels.reshape(1, nodes), loss_weight.reshape(1, nodes), at, w2s, w2n, w1_self, w1_neigh, stacked, partner]
        + [part for block in wide for part in block],
        scratch=[
            pltpu.VMEM((2, hid, nodes), F32),
            pltpu.VMEM((2, hid, nodes), BF16),
            pltpu.VMEM((max(1, sum(p > 1 for p in parts)), rows, nodes), BF16),
        ],
        flops=2 * nodes * hid * 2 * (rows * feat_count + nodes),
        smem=(0,),
        limit=limit,
    )
    recv2 = exchange(send2, "dp", 1)
    chunk = 2 * (rows // dp_count)
    send1, keep1 = call(
        functools.partial(backward_kernel, fanout, groups),
        [shape((groups, chunk, hid), F32)] * 2,
        [core, grad, hidden, at, w2s, w2n, features],
        flops=2 * nodes * hid * 2 * (rows + nodes),
        smem=(0,),
        limit=limit,
    )
    recv1 = exchange(send1, "dp", 1)
    own2, own1, *packs = call(
        functools.partial(pack_kernel, classes, groups),
        [shape((padded, hid), BF16), shape((chunk, hid), F32)] + [shape((padded + chunk, hid), BF16)] * (groups - 1),
        [z, keep2, recv2, keep1, recv1],
        smem=(0,),
    )
    far = [exchange(packs[s - 1], "dp", 2 * s) for s in range(1, groups)]
    (total2,) = call(second_sum_kernel, [shape((padded, hid), F32)], [own2] + far)
    other2 = exchange(total2, "dp", 1)
    (grad_w1,) = call(
        functools.partial(first_out_kernel, classes),
        [shape((2, rows // dp_count, hid), F32)],
        [total2, own1] + far,
        final=True,
    )
    grad_w2, loss = call(
        functools.partial(second_out_kernel, classes),
        [shape((classes, 2, hid), F32), shape((1, 1), F32)],
        [core, total2, other2],
        smem=(0,),
        final=True,
    )
    return loss[0, 0], grad_w1, grad_w2.transpose(1, 2, 0)


def solution(mesh):
    in_specs = (
        P("feat", "dp"),
        P("dp", None),
        P("dp"),
        P("dp"),
        P("feat", None),
        P("feat", None),
        P(),
        P(),
    )
    out_specs = (P(), P(None, ("feat", "dp"), None), P())
    return jax.shard_map(
        on_device, mesh=mesh, in_specs=in_specs, out_specs=out_specs, check_vma=False
    )
```

time: 70.7 us -> 47 us (0.66)
  Pallas kernels: 19.5 us -> 6.1 us
  local copies, waits for them, and re-layouts: 8.09 us -> 0.69 us
  starting transfers between devices: 18.5 us -> 15.7 us
    pallas_call x8 -> x7, Pallas kernels: 19.5 us -> 6.1 us  [call(): pl.pallas_call(kernel, out_shape=outs if final else [pltpu.VMEM(o.shape,...]
    unnamed x45 -> x16, local copies, waits for them, and re-layouts: 8.09 us -> 0.67 us
    ppermute x18 -> x14, starting transfers between devices: 18.5 us -> 15.7 us  [exchange(): return lax.ppermute(value, axis, [(i, i ^ step) for i in range(size)])]
    ppermute x18 -> x14, waiting for transfers between devices: 22.5 us -> 22.6 us  [exchange(): return lax.ppermute(value, axis, [(i, i ^ step) for i in range(size)])]
  transfers between devices with their start and end apart: 18 -> 14, of which waited for: 8 -> 9; matrix products, arithmetic and copies ran while one was open for 2% -> 0% of each run, Pallas kernels for 18% -> 4%
where the time goes in v2:
time: 47 us; the launch traced here: 46.8 us
  waiting for transfers between devices  22.6 us (48%)
  starting transfers between devices  15.7 us (33%)
  Pallas kernels  6.1 us (13%)
  other arithmetic  0.96 us (2%)
  between operations  0.79 us (2%)
  local copies, waits for them, and re-layouts  0.69 us (1%)
    ppermute x14, waiting for transfers between devices, exchange(): return lax.ppermute(value, axis, [(i, i ^ step) for i in range(size)])  22.6 us
    ppermute x14, starting transfers between devices, exchange(): return lax.ppermute(value, axis, [(i, i ^ step) for i in range(size)])  15.7 us
    pallas_call x7, Pallas kernels, call(): pl.pallas_call(kernel, out_shape=outs if final else [pltpu.VMEM(o.shape,...  6.1 us
    select_n x1, other arithmetic, on_device(): mine_own = jnp.where(core[0] == 0, w1_self, w1_neigh)  0.96 us
  transfers between devices with their start and end apart: 14, of which 9 were waited for; matrix products, arithmetic and copies ran while one was open for 0% of the time, Pallas kernels for 4%

profile of v2, /device:TPU:0, one launch (start us, length us, event | category | flops | bytes accessed | tf_op | source)
XLA Modules:
  0.0 46.8 jit_solution(14369484955711231145)
XLA Ops:
  0.6 0.0 copy-start.3
  0.7 0.0 copy-start.2
  0.7 1.0 %broadcast_select_fusion = bf16[256,256]{1,0:T(8,128)(2,1)S(1)} fusion(bf16[256,256]{1,0:T(8,128)(2,1)} %refs_6_.1, bf16[256,256]{1,0:T(8,128)(2,1)} %refs_7_.1, pred[]{:T(512)S(6)} %eq.5), kind=kLoop, calls=%fused_computation | loop fusion | flops 65536 | bytes 393217 | tf_op jit(solution)/shard_map/jit(_where)/select_n | solution.py:246
  1.6 4.0 %collective-permute-start.2 = (bf16[256,256]{1,0:T(8,128)(2,1)S(1)}, bf16[256,256]{1,0:T(8,128)(2,1)S(1)}, u32[]{:S(2)}, u32[]{:S(2)}) collective-permute-start(bf16[256,256]{1,0:T(8,128)(2,1)S(1)} %broadcast_select_fusion), channel_id=1, source_target_pairs={{0,24},{8,16},{16,8},{24,0},{1,25},{9,17},{17,9},{25,1},{2,26},{10... | collective-permute-start | bytes 393224 | tf_op jit(solution)/shard_map/ppermute | solution.py:215
  5.6 0.5 %collective-permute-start.1 = (bf16[256,256]{1,0:T(8,128)(2,1)S(1)}, bf16[256,256]{1,0:T(8,128)(2,1)S(1)}, u32[]{:S(2)}, u32[]{:S(2)}) collective-permute-start(bf16[256,256]{1,0:T(8,128)(2,1)S(1)} %broadcast_select_fusion), channel_id=1, source_target_pairs={{0,16},{8,24},{16,0},{24,8},{1,17},{9,25},{17,1},{25,9},{2,18},{10... | collective-permute-start | bytes 393224 | tf_op jit(solution)/shard_map/ppermute | solution.py:215
  6.1 0.1 collective-permute-start
  6.2 0.0 copy-done.3
  6.2 1.9 %collective-permute-start.5 = (bf16[256,512]{1,0:T(8,128)(2,1)S(1)}, bf16[256,512]{1,0:T(8,128)(2,1)S(1)}, u32[]{:S(2)}, u32[]{:S(2)}) collective-permute-start(bf16[256,512]{1,0:T(8,128)(2,1)S(1)} %copy-done.3), channel_id=1, source_target_pairs={{0,16},{8,24},{16,0},{24,8},{1,17},{9,25},{17,1},{25,9},{2,18},{10... | collective-permute-start | bytes 786440 | tf_op jit(solution)/shard_map/ppermute | solution.py:215
  8.2 1.5 %collective-permute-start.4 = (bf16[256,512]{1,0:T(8,128)(2,1)S(1)}, bf16[256,512]{1,0:T(8,128)(2,1)S(1)}, u32[]{:S(2)}, u32[]{:S(2)}) collective-permute-start(bf16[256,512]{1,0:T(8,128)(2,1)S(1)} %copy-done.3), channel_id=1, source_target_pairs={{0,8},{8,0},{16,24},{24,16},{1,9},{9,1},{17,25},{25,17},{2,10},{10... | collective-permute-start | bytes 786440 | tf_op jit(solution)/shard_map/ppermute | solution.py:215
  9.6 0.0 collective-permute-done.2.refs_2_
  9.7 2.3 %collective-permute-done.1.refs_1_ = bf16[256,256]{1,0:T(8,128)(2,1)S(1)} collective-permute-done((bf16[256,256]{1,0:T(8,128)(2,1)S(1)}, bf16[256,256]{1,0:T(8,128)(2,1)S(1)}, u32[]{:S(2)}, u32[]{:S(2)}) %collective-permute-start.1) | collective-permute-done | bytes 131104 | tf_op jit(solution)/shard_map/ppermute | solution.py:215
  12.0 1.3 %collective-permute-done.refs_0_ = bf16[256,256]{1,0:T(8,128)(2,1)S(1)} collective-permute-done((bf16[256,256]{1,0:T(8,128)(2,1)S(1)}, bf16[256,256]{1,0:T(8,128)(2,1)S(1)}, u32[]{:S(2)}, u32[]{:S(2)}) %collective-permute-start) | collective-permute-done | bytes 131104 | tf_op jit(solution)/shard_map/ppermute | solution.py:215
  13.3 0.0 copy-done.2
  13.3 1.1 %shard_map.103 = (bf16[512,512]{1,0:T(8,128)(2,1)S(1)}, bf16[3,256,256]{2,1,0:T(8,128)(2,1)S(1)}) custom-call(s32[10,512]{1,0:T(8,128)S(1)} %bitcast.9, bf16[256,256]{1,0:T(8,128)(2,1)S(1)} %collective-permute-done.refs_0_, bf16[256,256]{1,0:T(8,128)(2,1)S(1)} %collective-permute-done.1.refs_1_, bf16[256,256]{1,0:T(8,128)(2,1)S(1)} %collective-permute-done.2.refs_2_), custom_call_target="tpu_custom_call" | custom-call | flops 2621440 | bytes 1331200 | tf_op jit(solution)/shard_map/pallas_call | solution.py:38
  14.5 0.1 collective-permute-start.3
  14.5 3.0 %collective-permute-done.5.refs_12_ = bf16[256,512]{1,0:T(8,128)(2,1)S(1)} collective-permute-done((bf16[256,512]{1,0:T(8,128)(2,1)S(1)}, bf16[256,512]{1,0:T(8,128)(2,1)S(1)}, u32[]{:S(2)}, u32[]{:S(2)}) %collective-permute-start.5) | collective-permute-done | bytes 262176 | tf_op jit(solution)/shard_map/ppermute | solution.py:215
  17.5 0.0 copy-start.4
  17.5 0.0 copy-start.5
  17.5 0.0 copy-start
  17.5 0.0 copy-start.1
  17.6 1.7 %collective-permute-start.6 = (bf16[128,512]{1,0:T(8,128)(2,1)S(1)}, bf16[128,512]{1,0:T(8,128)(2,1)S(1)}, u32[]{:S(2)}, u32[]{:S(2)}) collective-permute-start(bf16[128,512]{1,0:T(8,128)(2,1)S(1)} %slice.8), channel_id=1, source_target_pairs={{0,8},{8,0},{16,24},{24,16},{1,9},{9,1},{17,25},{25,17},{2,10},{10... | collective-permute-start | bytes 393224 | tf_op jit(solution)/shard_map/ppermute | solution.py:215
  19.3 0.0 collective-permute-done.4.refs_11_
  19.3 0.0 copy-start.7
  19.3 0.8 %collective-permute-start.7 = (bf16[128,512]{1,0:T(8,128)(2,1)S(1)}, bf16[128,512]{1,0:T(8,128)(2,1)S(1)}, u32[]{:S(2)}, u32[]{:S(2)}) collective-permute-start(bf16[128,512]{1,0:T(8,128)(2,1)S(1)} %slice.9), channel_id=1, source_target_pairs={{0,16},{8,24},{16,0},{24,8},{1,17},{9,25},{17,1},{25,9},{2,18},{10... | collective-permute-start | bytes 393224 | tf_op jit(solution)/shard_map/ppermute | solution.py:215
  20.1 2.9 %collective-permute-done.6.refs_13_ = bf16[128,512]{1,0:T(8,128)(2,1)S(1)} collective-permute-done((bf16[128,512]{1,0:T(8,128)(2,1)S(1)}, bf16[128,512]{1,0:T(8,128)(2,1)S(1)}, u32[]{:S(2)}, u32[]{:S(2)}) %collective-permute-start.6) | collective-permute-done | bytes 131104 | tf_op jit(solution)/shard_map/ppermute | solution.py:215
  23.0 1.5 %collective-permute-done.7.refs_14_ = bf16[128,512]{1,0:T(8,128)(2,1)S(1)} collective-permute-done((bf16[128,512]{1,0:T(8,128)(2,1)S(1)}, bf16[128,512]{1,0:T(8,128)(2,1)S(1)}, u32[]{:S(2)}, u32[]{:S(2)}) %collective-permute-start.7) | collective-permute-done | bytes 131104 | tf_op jit(solution)/shard_map/ppermute | solution.py:215
  24.5 0.0 collective-permute-done.3.refs_9_
  24.5 0.0 copy-start.6
  24.5 0.0 copy-done.4
  24.5 0.0 copy-done.5
  24.6 0.0 copy-done
  24.6 0.0 copy-done.1
  24.6 0.0 copy-done.7
  24.6 0.6 %copy-done.6 = s32[512]{0:T(512)S(1)} copy-done((s32[512]{0:T(512)S(1)}, s32[512]{0:T(512)}, u32[]{:S(2)}) %copy-start.6) | copy-done | bytes 2072
  25.2 2.0 %shard_map.104 = (f32[176,256]{1,0:T(8,128)S(1)}, f32[176,256]{1,0:T(8,128)S(1)}, bf16[172,512]{1,0:T(8,128)(2,1)S(1)}, bf16[256,512]{1,0:T(8,128)(2,1)S(1)}) custom-call(s32[1]{0:T(128)} %bitcast.refs_0_.core_ref, s32[1,512]{1,0:T(1,128)S(1)} %bitcast.14, f32[1,512]{1,0:T(1,128)S(1)} %bitcast.15, bf16[512,512]{1,0:T(8,128)(2,1)S(1)} %get-tuple-element.18.refs_3_.at_ref, ...), custom_call_target="tpu_custom_call" | custom-call | flops 805306368 | bytes 3600388 | tf_op jit(solution)/shard_map/pallas_call | solution.py:38
  27.2 1.1 %shard_map.105 = (f32[4,64,256]{2,1,0:T(8,128)S(1)}, f32[4,64,256]{2,1,0:T(8,128)S(1)}) custom-call(s32[1]{0:T(128)} %bitcast.refs_0_.core_ref, bf16[172,512]{1,0:T(8,128)(2,1)S(1)} %get-tuple-element.22.g_ref, bf16[256,512]{1,0:T(8,128)(2,1)S(1)} %get-tuple-element.23.hidden_ref, bf16[512,512]{1,0:T(8,128)(2,1)S(1)} %get-tuple-element.18.refs_3_.at_ref, ...), custom_call_target="tpu_custom_call" | custom-call | flops 402653184 | bytes 1925124 | tf_op jit(solution)/shard_map/pallas_call | solution.py:38
  28.3 0.1 collective-permute-start.9
  28.4 0.5 %collective-permute-start.8 = (f32[176,256]{1,0:T(8,128)S(1)}, f32[176,256]{1,0:T(8,128)S(1)}, u32[]{:S(2)}, u32[]{:S(2)}) collective-permute-start(f32[176,256]{1,0:T(8,128)S(1)} %get-tuple-element.21), channel_id=1, source_target_pairs={{0,1},{1,0},{2,3},{3,2},{4,5},{5,4},{6,7},{7,6},{8,9},{9,8},{10,11... | collective-permute-start | bytes 540680 | tf_op jit(solution)/shard_map/ppermute | solution.py:215
  28.9 1.3 %collective-permute-done.8.recv2_ref = f32[176,256]{1,0:T(8,128)S(1)} collective-permute-done((f32[176,256]{1,0:T(8,128)S(1)}, f32[176,256]{1,0:T(8,128)S(1)}, u32[]{:S(2)}, u32[]{:S(2)}) %collective-permute-start.8) | collective-permute-done | bytes 180256 | tf_op jit(solution)/shard_map/ppermute | solution.py:215
  30.2 0.0 collective-permute-done.9.recv1_ref
  30.2 0.1 shard_map.106
  30.2 1.7 %collective-permute-start.10 = (bf16[240,256]{1,0:T(8,128)(2,1)S(1)}, bf16[240,256]{1,0:T(8,128)(2,1)S(1)}, u32[]{:S(2)}, u32[]{:S(2)}) collective-permute-start(bf16[240,256]{1,0:T(8,128)(2,1)S(1)} %get-tuple-element.27), channel_id=1, source_target_pairs={{0,2},{1,3},{2,0},{3,1},{4,6},{5,7},{6,4},{7,5},{8,10},{9,11},{10,... | collective-permute-start | bytes 368648 | tf_op jit(solution)/shard_map/ppermute | solution.py:215
  31.9 2.6 %collective-permute-start.11 = (bf16[240,256]{1,0:T(8,128)(2,1)S(1)}, bf16[240,256]{1,0:T(8,128)(2,1)S(1)}, u32[]{:S(2)}, u32[]{:S(2)}) collective-permute-start(bf16[240,256]{1,0:T(8,128)(2,1)S(1)} %get-tuple-element.28), channel_id=1, source_target_pairs={{0,4},{1,5},{2,6},{3,7},{4,0},{5,1},{6,2},{7,3},{8,12},{9,13},{10,... | collective-permute-start | bytes 368648 | tf_op jit(solution)/shard_map/ppermute | solution.py:215
  34.5 0.2 collective-permute-start.12
  34.7 2.7 %collective-permute-done.10.refs_1_.refs_0_ = bf16[240,256]{1,0:T(8,128)(2,1)S(1)} collective-permute-done((bf16[240,256]{1,0:T(8,128)(2,1)S(1)}, bf16[240,256]{1,0:T(8,128)(2,1)S(1)}, u32[]{:S(2)}, u32[]{:S(2)}) %collective-permute-start.10) | collective-permute-done | bytes 122912 | tf_op jit(solution)/shard_map/ppermute | solution.py:215
  37.4 6.9 %collective-permute-done.11.refs_2_.refs_1_ = bf16[240,256]{1,0:T(8,128)(2,1)S(1)} collective-permute-done((bf16[240,256]{1,0:T(8,128)(2,1)S(1)}, bf16[240,256]{1,0:T(8,128)(2,1)S(1)}, u32[]{:S(2)}, u32[]{:S(2)}) %collective-permute-start.11) | collective-permute-done | bytes 122912 | tf_op jit(solution)/shard_map/ppermute | solution.py:215
  44.3 0.0 collective-permute-done.12.refs_3_.refs_2_
  44.3 0.1 collective-permute-start.13
  44.4 0.8 %shard_map.109 = f32[2,32,256]{2,1,0:T(8,128)} custom-call(f32[176,256]{1,0:T(8,128)S(1)} %shard_map.107.own_ref.total_ref, f32[64,256]{1,0:T(8,128)S(1)} %get-tuple-element.31.own_ref, bf16[240,256]{1,0:T(8,128)(2,1)S(1)} %collective-permute-done.10.refs_1_.refs_0_, bf16[240,256]{1,0:T(8,128)(2,1)S(1)} %collective-permute-done.11.refs_2_.refs_1_, ...), custom_call_target="tpu_custom_call" | custom-call | bytes 679936 | tf_op jit(solution)/shard_map/pallas_call | solution.py:38
  45.2 0.6 %collective-permute-done.13.other_ref = f32[176,256]{1,0:T(8,128)S(1)} collective-permute-done((f32[176,256]{1,0:T(8,128)S(1)}, f32[176,256]{1,0:T(8,128)S(1)}, u32[]{:S(2)}, u32[]{:S(2)}) %collective-permute-start.13) | collective-permute-done | bytes 180256 | tf_op jit(solution)/shard_map/ppermute | solution.py:215
  45.8 1.0 %shard_map.108 = (f32[172,2,256]{2,1,0:T(2,128)}, f32[1,1]{1,0:T(1,128)}) custom-call(s32[1]{0:T(128)} %bitcast.refs_0_.core_ref, f32[176,256]{1,0:T(8,128)S(1)} %shard_map.107.own_ref.total_ref, f32[176,256]{1,0:T(8,128)S(1)} %collective-permute-done.13.other_ref), custom_call_target="tpu_custom_call" | custom-call | bytes 712712 | tf_op jit(solution)/shard_map/pallas_call | solution.py:38
  (3 shorter events, 0.1 us)
Async XLA Ops:
  0.6 5.6 %copy-start.3 = (bf16[256,512]{1,0:T(8,128)(2,1)S(1)}, bf16[256,512]{1,0:T(8,128)(2,1)}, u32[]{:S(2)}) copy-start(bf16[256,512]{1,0:T(8,128)(2,1)} %f_ref.1) | copy-start | bytes 786436
  0.7 12.6 %copy-start.2 = (s32[512,10]{0,1:T(8,128)S(1)}, s32[512,10]{0,1:T(8,128)}, u32[]{:S(2)}) copy-start(s32[512,10]{0,1:T(8,128)} %param.9) | copy-start | bytes 61444
  1.6 8.0 %collective-permute-start.2 = (bf16[256,256]{1,0:T(8,128)(2,1)S(1)}, bf16[256,256]{1,0:T(8,128)(2,1)S(1)}, u32[]{:S(2)}, u32[]{:S(2)}) collective-permute-start(bf16[256,256]{1,0:T(8,128)(2,1)S(1)} %broadcast_select_fusion), channel_id=1, source_target_pairs={{0,24},{8,16},{16,8},{24,0},{1,25},{9,17},{17,9},{25,1},{2,26},{10... | collective-permute-start | bytes 393224 | tf_op jit(solution)/shard_map/ppermute | solution.py:215
  5.6 6.4 %collective-permute-start.1 = (bf16[256,256]{1,0:T(8,128)(2,1)S(1)}, bf16[256,256]{1,0:T(8,128)(2,1)S(1)}, u32[]{:S(2)}, u32[]{:S(2)}) collective-permute-start(bf16[256,256]{1,0:T(8,128)(2,1)S(1)} %broadcast_select_fusion), channel_id=1, source_target_pairs={{0,16},{8,24},{16,0},{24,8},{1,17},{9,25},{17,1},{25,9},{2,18},{10... | collective-permute-start | bytes 393224 | tf_op jit(solution)/shard_map/ppermute | solution.py:215
  6.1 7.2 %collective-permute-start = (bf16[256,256]{1,0:T(8,128)(2,1)S(1)}, bf16[256,256]{1,0:T(8,128)(2,1)S(1)}, u32[]{:S(2)}, u32[]{:S(2)}) collective-permute-start(bf16[256,256]{1,0:T(8,128)(2,1)S(1)} %broadcast_select_fusion), channel_id=1, source_target_pairs={{0,8},{8,0},{16,24},{24,16},{1,9},{9,1},{17,25},{25,17},{2,10},{10... | collective-permute-start | bytes 393224 | tf_op jit(solution)/shard_map/ppermute | solution.py:215
  6.2 11.3 %collective-permute-start.5 = (bf16[256,512]{1,0:T(8,128)(2,1)S(1)}, bf16[256,512]{1,0:T(8,128)(2,1)S(1)}, u32[]{:S(2)}, u32[]{:S(2)}) collective-permute-start(bf16[256,512]{1,0:T(8,128)(2,1)S(1)} %copy-done.3), channel_id=1, source_target_pairs={{0,16},{8,24},{16,0},{24,8},{1,17},{9,25},{17,1},{25,9},{2,18},{10... | collective-permute-start | bytes 786440 | tf_op jit(solution)/shard_map/ppermute | solution.py:215
  8.2 11.2 %collective-permute-start.4 = (bf16[256,512]{1,0:T(8,128)(2,1)S(1)}, bf16[256,512]{1,0:T(8,128)(2,1)S(1)}, u32[]{:S(2)}, u32[]{:S(2)}) collective-permute-start(bf16[256,512]{1,0:T(8,128)(2,1)S(1)} %copy-done.3), channel_id=1, source_target_pairs={{0,8},{8,0},{16,24},{24,16},{1,9},{9,1},{17,25},{25,17},{2,10},{10... | collective-permute-start | bytes 786440 | tf_op jit(solution)/shard_map/ppermute | solution.py:215
  14.5 10.1 %collective-permute-start.3 = (bf16[3,256,256]{2,1,0:T(8,128)(2,1)S(1)}, bf16[3,256,256]{2,1,0:T(8,128)(2,1)S(1)}, u32[]{:S(2)}, u32[]{:S(2)}) collective-permute-start(bf16[3,256,256]{2,1,0:T(8,128)(2,1)S(1)} %get-tuple-element.19.refs_8_), channel_id=1, source_target_pairs={{0,1},{1,0},{2,3},{3,2},{4,5},{5,4},{6,7},{7,6},{8,9},{9,8},{10,11... | collective-permute-start | bytes 1179656 | tf_op jit(solution)/shard_map/ppermute | solution.py:215
  17.5 7.0 %copy-start.4 = (bf16[256,172]{0,1:T(8,128)(2,1)S(1)}, bf16[256,172]{0,1:T(8,128)(2,1)}, u32[]{:S(2)}) copy-start(bf16[256,172]{0,1:T(8,128)(2,1)} %param.14) | copy-start | bytes 264196
  17.5 7.0 %copy-start.5 = (bf16[256,172]{0,1:T(8,128)(2,1)S(1)}, bf16[256,172]{0,1:T(8,128)(2,1)}, u32[]{:S(2)}) copy-start(bf16[256,172]{0,1:T(8,128)(2,1)} %param.15) | copy-start | bytes 264196
  17.5 7.0 %copy-start = (bf16[256,256]{1,0:T(8,128)(2,1)S(1)}, bf16[256,256]{1,0:T(8,128)(2,1)}, u32[]{:S(2)}) copy-start(bf16[256,256]{1,0:T(8,128)(2,1)} %refs_6_.1) | copy-start | bytes 393220
  17.5 7.0 %copy-start.1 = (bf16[256,256]{1,0:T(8,128)(2,1)S(1)}, bf16[256,256]{1,0:T(8,128)(2,1)}, u32[]{:S(2)}) copy-start(bf16[256,256]{1,0:T(8,128)(2,1)} %refs_7_.1) | copy-start | bytes 393220
  17.6 5.5 %collective-permute-start.6 = (bf16[128,512]{1,0:T(8,128)(2,1)S(1)}, bf16[128,512]{1,0:T(8,128)(2,1)S(1)}, u32[]{:S(2)}, u32[]{:S(2)}) collective-permute-start(bf16[128,512]{1,0:T(8,128)(2,1)S(1)} %slice.8), channel_id=1, source_target_pairs={{0,8},{8,0},{16,24},{24,16},{1,9},{9,1},{17,25},{25,17},{2,10},{10... | collective-permute-start | bytes 393224 | tf_op jit(solution)/shard_map/ppermute | solution.py:215
  19.3 5.3 %copy-start.7 = (f32[512]{0:T(512)S(1)}, f32[512]{0:T(512)}, u32[]{:S(2)}) copy-start(f32[512]{0:T(512)} %param.11) | copy-start | bytes 6148
  19.3 5.2 %collective-permute-start.7 = (bf16[128,512]{1,0:T(8,128)(2,1)S(1)}, bf16[128,512]{1,0:T(8,128)(2,1)S(1)}, u32[]{:S(2)}, u32[]{:S(2)}) collective-permute-start(bf16[128,512]{1,0:T(8,128)(2,1)S(1)} %slice.9), channel_id=1, source_target_pairs={{0,16},{8,24},{16,0},{24,8},{1,17},{9,25},{17,1},{25,9},{2,18},{10... | collective-permute-start | bytes 393224 | tf_op jit(solution)/shard_map/ppermute | solution.py:215
  24.5 0.7 %copy-start.6 = (s32[512]{0:T(512)S(1)}, s32[512]{0:T(512)}, u32[]{:S(2)}) copy-start(s32[512]{0:T(512)} %param.10) | copy-start | bytes 6148
  28.3 1.9 %collective-permute-start.9 = (f32[4,64,256]{2,1,0:T(8,128)S(1)}, f32[4,64,256]{2,1,0:T(8,128)S(1)}, u32[]{:S(2)}, u32[]{:S(2)}) collective-permute-start(f32[4,64,256]{2,1,0:T(8,128)S(1)} %get-tuple-element.25), channel_id=1, source_target_pairs={{0,1},{1,0},{2,3},{3,2},{4,5},{5,4},{6,7},{7,6},{8,9},{9,8},{10,11... | collective-permute-start | bytes 786440 | tf_op jit(solution)/shard_map/ppermute | solution.py:215
  28.4 1.8 %collective-permute-start.8 = (f32[176,256]{1,0:T(8,128)S(1)}, f32[176,256]{1,0:T(8,128)S(1)}, u32[]{:S(2)}, u32[]{:S(2)}) collective-permute-start(f32[176,256]{1,0:T(8,128)S(1)} %get-tuple-element.21), channel_id=1, source_target_pairs={{0,1},{1,0},{2,3},{3,2},{4,5},{5,4},{6,7},{7,6},{8,9},{9,8},{10,11... | collective-permute-start | bytes 540680 | tf_op jit(solution)/shard_map/ppermute | solution.py:215
  30.2 7.1 %collective-permute-start.10 = (bf16[240,256]{1,0:T(8,128)(2,1)S(1)}, bf16[240,256]{1,0:T(8,128)(2,1)S(1)}, u32[]{:S(2)}, u32[]{:S(2)}) collective-permute-start(bf16[240,256]{1,0:T(8,128)(2,1)S(1)} %get-tuple-element.27), channel_id=1, source_target_pairs={{0,2},{1,3},{2,0},{3,1},{4,6},{5,7},{6,4},{7,5},{8,10},{9,11},{10,... | collective-permute-start | bytes 368648 | tf_op jit(solution)/shard_map/ppermute | solution.py:215
  31.9 12.4 %collective-permute-start.11 = (bf16[240,256]{1,0:T(8,128)(2,1)S(1)}, bf16[240,256]{1,0:T(8,128)(2,1)S(1)}, u32[]{:S(2)}, u32[]{:S(2)}) collective-permute-start(bf16[240,256]{1,0:T(8,128)(2,1)S(1)} %get-tuple-element.28), channel_id=1, source_target_pairs={{0,4},{1,5},{2,6},{3,7},{4,0},{5,1},{6,2},{7,3},{8,12},{9,13},{10,... | collective-permute-start | bytes 368648 | tf_op jit(solution)/shard_map/ppermute | solution.py:215
  34.5 9.8 %collective-permute-start.12 = (bf16[240,256]{1,0:T(8,128)(2,1)S(1)}, bf16[240,256]{1,0:T(8,128)(2,1)S(1)}, u32[]{:S(2)}, u32[]{:S(2)}) collective-permute-start(bf16[240,256]{1,0:T(8,128)(2,1)S(1)} %get-tuple-element.29), channel_id=1, source_target_pairs={{0,6},{1,7},{2,4},{3,5},{4,2},{5,3},{6,0},{7,1},{8,14},{9,15},{10,... | collective-permute-start | bytes 368648 | tf_op jit(solution)/shard_map/ppermute | solution.py:215
  44.3 1.5 %collective-permute-start.13 = (f32[176,256]{1,0:T(8,128)S(1)}, f32[176,256]{1,0:T(8,128)S(1)}, u32[]{:S(2)}, u32[]{:S(2)}) collective-permute-start(f32[176,256]{1,0:T(8,128)S(1)} %shard_map.107.own_ref.total_ref), channel_id=1, source_target_pairs={{0,1},{1,0},{2,3},{3,2},{4,5},{5,4},{6,7},{7,6},{8,9},{9,8},{10,11... | collective-permute-start | bytes 540680 | tf_op jit(solution)/shard_map/ppermute | solution.py:215

commit v3 on v2

--- a/solution.py
+++ b/solution.py
@@ -50,9 +50,11 @@
     return jax.ShapeDtypeStruct(dims, dtype)
 
 
-def count_kernel(fanout, nbr_ref, *refs):
-    at_ref, stack_ref = refs[-2:]
-    for i, ref in enumerate(refs[:-2]):
+def count_kernel(fanout, nbr_ref, labels_ref, weight_ref, *refs):
+    at_ref, stack_ref, labels_out_ref, weight_out_ref = refs[-4:]
+    labels_out_ref[...] = labels_ref[...]
+    weight_out_ref[...] = weight_ref[...]
+    for i, ref in enumerate(refs[:-4]):
         stack_ref[i] = ref[...]
     nodes = at_ref.shape[1]
     step = 32
@@ -68,38 +70,41 @@
     lax.fori_loop(0, nodes // step, body, 0)
 
 
-def forward_kernel(parts, fanout, *refs):
-    core_ref, labels_ref, weight_ref, at_ref, w2s_ref, w2n_ref, ws_ref, wn_ref, mine_ref, partner_ref = refs[:10]
-    feat_count = len(parts)
-    f_refs = refs[10 : 10 + sum(parts)]
-    send_ref, keep_ref, g_ref, hidden_ref, proj, pair, joined = refs[10 + sum(parts) :]
-    blocks, at_ref_index, join_index = [], 0, 0
+def project(own, others_ref, f_refs):
+    products = [dot_tn(own, f_refs[0][...])]
+    for s in range(1, len(f_refs)):
+        products.append(dot_tn(others_ref[s - 1], f_refs[s][...]))
+    return tree_sum(products)
+
+
+def mine_kernel(parts, core_ref, ws_ref, wn_ref, mine_ref, *refs):
+    out_ref, joined_refs = refs[sum(parts)], refs[sum(parts) + 1 :]
+    own = jnp.where(core_ref[0] == 0, ws_ref[...], wn_ref[...])
+    blocks, at, done = [], 0, 0
     for count in parts:
-        if count == 1:
-            blocks.append(f_refs[at_ref_index][...])
-        else:
-            start = 0
-            for ref in f_refs[at_ref_index : at_ref_index + count]:
-                joined[join_index, start : start + ref.shape[0]] = ref[...]
+        block = refs[at]
+        if count > 1:
+            block, start = joined_refs[done], 0
+            for ref in refs[at : at + count]:
+                block[start : start + ref.shape[0]] = ref[...]
                 start += ref.shape[0]
-            blocks.append(joined[join_index])
-            join_index += 1
-        at_ref_index += count
+            done += 1
+        blocks.append(block)
+        at += count
+    out_ref[...] = project(own, mine_ref, blocks)
+
+
+def forward_kernel(feat_count, fanout, *refs):
+    f_refs, refs = refs[:feat_count], refs[feat_count:]
+    core_ref, labels_ref, weight_ref, at_ref, w2s_ref, w2n_ref, ws_ref, wn_ref, partner_ref, mine_ref = refs[:10]
+    send_ref, keep_ref, g_ref, hidden_ref, proj, pair = refs[10:]
     core = core_ref[0]
     classes = w2s_ref.shape[0]
     nodes = at_ref.shape[1]
     scale = 1.0 / fanout
-    first = core == 0
-    own_mine = jnp.where(first, ws_ref[...], wn_ref[...])
-    own_partner = jnp.where(first, wn_ref[...], ws_ref[...])
-    proj[core] = tree_sum(
-        [dot_tn(own_mine, blocks[0])]
-        + [dot_tn(mine_ref[s - 1], blocks[s]) for s in range(1, feat_count)]
-    )
-    proj[1 - core] = tree_sum(
-        [dot_tn(own_partner, blocks[0])]
-        + [dot_tn(partner_ref[s - 1], blocks[s]) for s in range(1, feat_count)]
-    )
+    own = jnp.where(core == 0, wn_ref[...], ws_ref[...])
+    proj[core] = mine_ref[...]
+    proj[1 - core] = project(own, partner_ref, f_refs)
     at = at_ref[...]
     pre = proj[0] + dot_nn(proj[1].astype(BF16), at) * scale
     hidden = jnp.maximum(pre, 0.0).astype(BF16)
@@ -242,36 +247,49 @@
     z = (place // 2).reshape(1)
 
     wide = gather_parts(features, feat_count)
-    parts = tuple(len(w) for w in wide)
+    parts = tuple(len(block) for block in wide)
     mine_own = jnp.where(core[0] == 0, w1_self, w1_neigh)
     mine = [exchange(mine_own, "feat", s) for s in range(1, feat_count)]
-    at, stacked = call(
+    limit = 12 + 6 * nodes * nodes // (1024 * 1024)
+    at, stacked, labels, loss_weight = call(
         functools.partial(count_kernel, fanout),
-        [shape((nodes, nodes), BF16), shape((feat_count - 1, rows, hid), BF16)],
-        [neighbors.T] + mine,
+        [
+            shape((nodes, nodes), BF16),
+            shape((feat_count - 1, rows, hid), BF16),
+            shape((1, nodes), jnp.int32),
+            shape((1, nodes), F32),
+        ],
+        [neighbors.T, labels.reshape(1, nodes), loss_weight.reshape(1, nodes)] + mine,
         flops=nodes * nodes * fanout,
     )
+    mine_proj, *joined = call(
+        functools.partial(mine_kernel, parts),
+        [shape((hid, nodes), F32)] + [shape((rows, nodes), BF16)] * sum(count > 1 for count in parts),
+        [core, w1_self, w1_neigh, stacked] + [part for block in wide for part in block],
+        flops=30 * nodes * hid * rows * feat_count,
+        smem=(0,),
+        limit=limit,
+    )
+    rest = iter(joined)
+    whole = [block[0] if len(block) == 1 else next(rest) for block in wide]
     partner = exchange(stacked, "dp", 1)
     w2s, w2n = w2_self.T, w2_neigh.T
-    limit = 12 + 6 * nodes * nodes // (1024 * 1024)
     padded = (classes + 3 + 15) // 16 * 16
     send2, keep2, grad, hidden = call(
-        functools.partial(forward_kernel, parts, fanout),
+        functools.partial(forward_kernel, feat_count, fanout),
         [
             shape((padded, hid), F32),
             shape((padded, hid), F32),
             shape((classes, nodes), BF16),
             shape((hid, nodes), BF16),
         ],
-        [core, labels.reshape(1, nodes), loss_weight.reshape(1, nodes), at, w2s, w2n, w1_self, w1_neigh, stacked, partner]
-        + [part for block in wide for part in block],
+        whole + [core, labels, loss_weight, at, w2s, w2n, w1_self, w1_neigh, partner, mine_proj],
         scratch=[
             pltpu.VMEM((2, hid, nodes), F32),
             pltpu.VMEM((2, hid, nodes), BF16),
-            pltpu.VMEM((max(1, sum(p > 1 for p in parts)), rows, nodes), BF16),
         ],
         flops=2 * nodes * hid * 2 * (rows * feat_count + nodes),
-        smem=(0,),
+        smem=(feat_count,),
         limit=limit,
     )
     recv2 = exchange(send2, "dp", 1)

time: 47 us -> 43.8 us (0.932)
  waiting for transfers between devices: 22.6 us -> 17.3 us
  starting transfers between devices: 15.7 us -> 17.6 us
    ppermute x14, waiting for transfers between devices: 22.6 us -> 17.3 us  [exchange(): return lax.ppermute(value, axis, [(i, i ^ step) for i in range(size)])]
    ppermute x14, starting transfers between devices: 15.7 us -> 17.6 us  [exchange(): return lax.ppermute(value, axis, [(i, i ^ step) for i in range(size)])]
    pallas_call x7 -> x8, Pallas kernels: 6.1 us -> 6.28 us  [call(): pl.pallas_call(kernel, out_shape=outs if final else [pltpu.VMEM(o.shape,...]
  transfers between devices with their start and end apart: 14 -> 14, of which waited for: 9 -> 8; matrix products, arithmetic and copies ran while one was open for 0% -> 2% of each run, Pallas kernels for 4% -> 5%
where the time goes in v3:
time: 43.8 us; the launch traced here: 43.6 us
  starting transfers between devices  17.6 us (40%)
  waiting for transfers between devices  17.3 us (39%)
  Pallas kernels  6.28 us (14%)
  other arithmetic  0.92 us (2%)
  between operations  0.76 us (2%)
  local copies, waits for them, and re-layouts  0.74 us (2%)
    ppermute x14, starting transfers between devices, exchange(): return lax.ppermute(value, axis, [(i, i ^ step) for i in range(size)])  17.6 us
    ppermute x14, waiting for transfers between devices, exchange(): return lax.ppermute(value, axis, [(i, i ^ step) for i in range(size)])  17.3 us
    pallas_call x8, Pallas kernels, call(): pl.pallas_call(kernel, out_shape=outs if final else [pltpu.VMEM(o.shape,...  6.28 us
    select_n x1, other arithmetic, on_device(): mine_own = jnp.where(core[0] == 0, w1_self, w1_neigh)  0.92 us
  transfers between devices with their start and end apart: 14, of which 8 were waited for; matrix products, arithmetic and copies ran while one was open for 2% of the time, Pallas kernels for 5%

profile of v3, /device:TPU:0, one launch (start us, length us, event | category | flops | bytes accessed | tf_op | source)
XLA Modules:
  0.0 43.6 jit_solution(3687238883181513566)
XLA Ops:
  0.6 3.0 %collective-permute-start.1 = (bf16[256,512]{1,0:T(8,128)(2,1)}, bf16[256,512]{1,0:T(8,128)(2,1)S(1)}, u32[]{:S(2)}, u32[]{:S(2)}) collective-permute-start(bf16[256,512]{1,0:T(8,128)(2,1)} %f_ref.1), channel_id=1, source_target_pairs={{0,16},{8,24},{16,0},{24,8},{1,17},{9,25},{17,1},{25,9},{2,18},{10... | collective-permute-start | bytes 786440 | tf_op jit(solution)/shard_map/ppermute | solution.py:220
  3.7 1.5 %collective-permute-start = (bf16[256,512]{1,0:T(8,128)(2,1)}, bf16[256,512]{1,0:T(8,128)(2,1)S(1)}, u32[]{:S(2)}, u32[]{:S(2)}) collective-permute-start(bf16[256,512]{1,0:T(8,128)(2,1)} %f_ref.1), channel_id=1, source_target_pairs={{0,8},{8,0},{16,24},{24,16},{1,9},{9,1},{17,25},{25,17},{2,10},{10... | collective-permute-start | bytes 786440 | tf_op jit(solution)/shard_map/ppermute | solution.py:220
  5.2 0.9 %broadcast_select_fusion = bf16[256,256]{1,0:T(8,128)(2,1)S(1)} fusion(bf16[256,256]{1,0:T(8,128)(2,1)} %refs_10_.1, bf16[256,256]{1,0:T(8,128)(2,1)} %refs_11_.1, pred[]{:T(512)S(6)} %eq.5), kind=kLoop, calls=%fused_computation | loop fusion | flops 65536 | bytes 393217 | tf_op jit(solution)/shard_map/jit(_where)/select_n | solution.py:251
  6.1 0.1 collective-permute-start.4
  6.2 1.9 %collective-permute-start.3 = (bf16[256,256]{1,0:T(8,128)(2,1)S(1)}, bf16[256,256]{1,0:T(8,128)(2,1)S(1)}, u32[]{:S(2)}, u32[]{:S(2)}) collective-permute-start(bf16[256,256]{1,0:T(8,128)(2,1)S(1)} %broadcast_select_fusion), channel_id=1, source_target_pairs={{0,16},{8,24},{16,0},{24,8},{1,17},{9,25},{17,1},{25,9},{2,18},{10... | collective-permute-start | bytes 393224 | tf_op jit(solution)/shard_map/ppermute | solution.py:220
  8.1 1.5 %collective-permute-start.2 = (bf16[256,256]{1,0:T(8,128)(2,1)S(1)}, bf16[256,256]{1,0:T(8,128)(2,1)S(1)}, u32[]{:S(2)}, u32[]{:S(2)}) collective-permute-start(bf16[256,256]{1,0:T(8,128)(2,1)S(1)} %broadcast_select_fusion), channel_id=1, source_target_pairs={{0,8},{8,0},{16,24},{24,16},{1,9},{9,1},{17,25},{25,17},{2,10},{10... | collective-permute-start | bytes 393224 | tf_op jit(solution)/shard_map/ppermute | solution.py:220
  9.6 2.1 %collective-permute-done.1.refs_2_ = bf16[256,512]{1,0:T(8,128)(2,1)S(1)} collective-permute-done((bf16[256,512]{1,0:T(8,128)(2,1)}, bf16[256,512]{1,0:T(8,128)(2,1)S(1)}, u32[]{:S(2)}, u32[]{:S(2)}) %collective-permute-start.1) | collective-permute-done | bytes 262176 | tf_op jit(solution)/shard_map/ppermute | solution.py:220
  11.7 0.0 copy-start.5
  11.7 0.0 copy-start.2
  11.8 2.8 %collective-permute-start.5 = (bf16[128,512]{1,0:T(8,128)(2,1)S(1)}, bf16[128,512]{1,0:T(8,128)(2,1)S(1)}, u32[]{:S(2)}, u32[]{:S(2)}) collective-permute-start(bf16[128,512]{1,0:T(8,128)(2,1)S(1)} %slice.8), channel_id=1, source_target_pairs={{0,8},{8,0},{16,24},{24,16},{1,9},{9,1},{17,25},{25,17},{2,10},{10... | collective-permute-start | bytes 393224 | tf_op jit(solution)/shard_map/ppermute | solution.py:220
  14.5 0.0 collective-permute-done.refs_1_
  14.6 1.6 %collective-permute-start.6 = (bf16[128,512]{1,0:T(8,128)(2,1)S(1)}, bf16[128,512]{1,0:T(8,128)(2,1)S(1)}, u32[]{:S(2)}, u32[]{:S(2)}) collective-permute-start(bf16[128,512]{1,0:T(8,128)(2,1)S(1)} %slice.9), channel_id=1, source_target_pairs={{0,16},{8,24},{16,0},{24,8},{1,17},{9,25},{17,1},{25,9},{2,18},{10... | collective-permute-start | bytes 393224 | tf_op jit(solution)/shard_map/ppermute | solution.py:220
  16.1 0.0 collective-permute-done.4.refs_2_
  16.1 0.5 %collective-permute-done.3.refs_1_ = bf16[256,256]{1,0:T(8,128)(2,1)S(1)} collective-permute-done((bf16[256,256]{1,0:T(8,128)(2,1)S(1)}, bf16[256,256]{1,0:T(8,128)(2,1)S(1)}, u32[]{:S(2)}, u32[]{:S(2)}) %collective-permute-start.3) | collective-permute-done | bytes 131104 | tf_op jit(solution)/shard_map/ppermute | solution.py:220
  16.6 2.0 %collective-permute-done.2.refs_0_ = bf16[256,256]{1,0:T(8,128)(2,1)S(1)} collective-permute-done((bf16[256,256]{1,0:T(8,128)(2,1)S(1)}, bf16[256,256]{1,0:T(8,128)(2,1)S(1)}, u32[]{:S(2)}, u32[]{:S(2)}) %collective-permute-start.2) | collective-permute-done | bytes 131104 | tf_op jit(solution)/shard_map/ppermute | solution.py:220
  18.7 0.0 copy-start.4
  18.7 0.0 copy-start.3
  18.7 0.0 copy-done.2
  18.7 0.7 %copy-done.4 = f32[512]{0:T(512)S(1)} copy-done((f32[512]{0:T(512)S(1)}, f32[512]{0:T(512)}, u32[]{:S(2)}) %copy-start.4) | copy-done | bytes 2072
  19.3 0.0 copy-done.3
  19.4 0.0 copy-start
  19.4 0.0 copy-start.1
  19.4 1.1 %shard_map.103 = (bf16[512,512]{1,0:T(8,128)(2,1)S(1)}, bf16[3,256,256]{2,1,0:T(8,128)(2,1)S(1)}, s32[1,512]{1,0:T(1,128)S(1)}, f32[1,512]{1,0:T(1,128)S(1)}) custom-call(s32[10,512]{1,0:T(8,128)S(1)} %bitcast.9, s32[1,512]{1,0:T(1,128)S(1)} %bitcast.10, f32[1,512]{1,0:T(1,128)S(1)} %bitcast.11, bf16[256,256]{1,0:T(8,128)(2,1)S(1)} %collective-permute-done.2.refs_0_, ...), custom_call_target="tpu_custom_call" | custom-call | flops 2621440 | bytes 1339392 | tf_op jit(solution)/shard_map/pallas_call | solution.py:38
  20.5 0.1 collective-permute-start.7
  20.6 0.0 collective-permute-done.5.refs_3_
  20.6 0.0 collective-permute-done.6.refs_4_
  20.6 0.0 copy-done.5
  20.6 0.0 copy-done
  20.6 0.0 copy-done.1
  20.6 0.0 copy-start.6
  20.6 0.0 copy-start.7
  20.7 0.5 %shard_map.104 = (f32[256,512]{1,0:T(8,128)S(1)}, bf16[256,512]{1,0:T(8,128)(2,1)S(1)}) custom-call(s32[1]{0:T(128)} %bitcast.core_ref.refs_4_, bf16[256,256]{1,0:T(8,128)(2,1)S(1)} %copy-done, bf16[256,256]{1,0:T(8,128)(2,1)S(1)} %copy-done.1, bf16[3,256,256]{2,1,0:T(8,128)(2,1)S(1)} %get-tuple-element.22.mine_ref, bf16[256,512]{1,0:T(8,128)(2,1)S(1)} %copy-done.5, ...), custom_call_target="tpu_custom_call" | custom-call | flops 4026531840 | bytes 2490372 | tf_op jit(solution)/shard_map/pallas_call | solution.py:38
  21.1 1.2 %collective-permute-done.7.refs_12_ = bf16[3,256,256]{2,1,0:T(8,128)(2,1)S(1)} collective-permute-done((bf16[3,256,256]{2,1,0:T(8,128)(2,1)S(1)}, bf16[3,256,256]{2,1,0:T(8,128)(2,1)S(1)}, u32[]{:S(2)}, u32[]{:S(2)}) %collective-permute-start.7) | collective-permute-done | bytes 393248 | tf_op jit(solution)/shard_map/ppermute | solution.py:220
  22.3 0.0 copy-done.6
  22.3 0.0 copy-done.7
  22.3 1.7 %shard_map.105 = (f32[176,256]{1,0:T(8,128)S(1)}, f32[176,256]{1,0:T(8,128)S(1)}, bf16[172,512]{1,0:T(8,128)(2,1)S(1)}, bf16[256,512]{1,0:T(8,128)(2,1)S(1)}) custom-call(bf16[256,512]{1,0:T(8,128)(2,1)S(1)} %copy-done.5, bf16[256,512]{1,0:T(8,128)(2,1)S(1)} %collective-permute-done.refs_1_, bf16[256,512]{1,0:T(8,128)(2,1)S(1)} %collective-permute-done.1.refs_2_, ...), custom_call_target="tpu_custom_call" | custom-call | flops 805306368 | bytes 3731460 | tf_op jit(solution)/shard_map/pallas_call | solution.py:38
  24.0 1.1 %shard_map.106 = (f32[4,64,256]{2,1,0:T(8,128)S(1)}, f32[4,64,256]{2,1,0:T(8,128)S(1)}) custom-call(s32[1]{0:T(128)} %bitcast.core_ref.refs_4_, bf16[172,512]{1,0:T(8,128)(2,1)S(1)} %get-tuple-element.30.g_ref, bf16[256,512]{1,0:T(8,128)(2,1)S(1)} %get-tuple-element.31.hidden_ref, bf16[512,512]{1,0:T(8,128)(2,1)S(1)} %get-tuple-element.26.refs_7_.at_ref, ...), custom_call_target="tpu_custom_call" | custom-call | flops 402653184 | bytes 1925124 | tf_op jit(solution)/shard_map/pallas_call | solution.py:38
  25.1 0.2 collective-permute-start.9
  25.3 0.4 collective-permute-start.8
  25.7 1.3 %collective-permute-done.8.recv2_ref = f32[176,256]{1,0:T(8,128)S(1)} collective-permute-done((f32[176,256]{1,0:T(8,128)S(1)}, f32[176,256]{1,0:T(8,128)S(1)}, u32[]{:S(2)}, u32[]{:S(2)}) %collective-permute-start.8) | collective-permute-done | bytes 180256 | tf_op jit(solution)/shard_map/ppermute | solution.py:220
  27.0 0.0 collective-permute-done.9.recv1_ref
  27.0 0.1 shard_map.107
  27.0 1.6 %collective-permute-start.10 = (bf16[240,256]{1,0:T(8,128)(2,1)S(1)}, bf16[240,256]{1,0:T(8,128)(2,1)S(1)}, u32[]{:S(2)}, u32[]{:S(2)}) collective-permute-start(bf16[240,256]{1,0:T(8,128)(2,1)S(1)} %get-tuple-element.35), channel_id=1, source_target_pairs={{0,2},{1,3},{2,0},{3,1},{4,6},{5,7},{6,4},{7,5},{8,10},{9,11},{10,... | collective-permute-start | bytes 368648 | tf_op jit(solution)/shard_map/ppermute | solution.py:220
  28.7 2.6 %collective-permute-start.11 = (bf16[240,256]{1,0:T(8,128)(2,1)S(1)}, bf16[240,256]{1,0:T(8,128)(2,1)S(1)}, u32[]{:S(2)}, u32[]{:S(2)}) collective-permute-start(bf16[240,256]{1,0:T(8,128)(2,1)S(1)} %get-tuple-element.36), channel_id=1, source_target_pairs={{0,4},{1,5},{2,6},{3,7},{4,0},{5,1},{6,2},{7,3},{8,12},{9,13},{10,... | collective-permute-start | bytes 368648 | tf_op jit(solution)/shard_map/ppermute | solution.py:220
  31.3 0.2 collective-permute-start.12
  31.5 2.7 %collective-permute-done.10.refs_1_.refs_0_ = bf16[240,256]{1,0:T(8,128)(2,1)S(1)} collective-permute-done((bf16[240,256]{1,0:T(8,128)(2,1)S(1)}, bf16[240,256]{1,0:T(8,128)(2,1)S(1)}, u32[]{:S(2)}, u32[]{:S(2)}) %collective-permute-start.10) | collective-permute-done | bytes 122912 | tf_op jit(solution)/shard_map/ppermute | solution.py:220
  34.2 6.9 %collective-permute-done.11.refs_2_.refs_1_ = bf16[240,256]{1,0:T(8,128)(2,1)S(1)} collective-permute-done((bf16[240,256]{1,0:T(8,128)(2,1)S(1)}, bf16[240,256]{1,0:T(8,128)(2,1)S(1)}, u32[]{:S(2)}, u32[]{:S(2)}) %collective-permute-start.11) | collective-permute-done | bytes 122912 | tf_op jit(solution)/shard_map/ppermute | solution.py:220
  41.1 0.0 collective-permute-done.12.refs_3_.refs_2_
  41.1 0.1 collective-permute-start.13
  41.2 0.8 %shard_map.110 = f32[2,32,256]{2,1,0:T(8,128)} custom-call(f32[176,256]{1,0:T(8,128)S(1)} %shard_map.108.own_ref.total_ref, f32[64,256]{1,0:T(8,128)S(1)} %get-tuple-element.39.own_ref, bf16[240,256]{1,0:T(8,128)(2,1)S(1)} %collective-permute-done.10.refs_1_.refs_0_, bf16[240,256]{1,0:T(8,128)(2,1)S(1)} %collective-permute-done.11.refs_2_.refs_1_, ...), custom_call_target="tpu_custom_call" | custom-call | bytes 679936 | tf_op jit(solution)/shard_map/pallas_call | solution.py:38
  42.0 0.6 %collective-permute-done.13.other_ref = f32[176,256]{1,0:T(8,128)S(1)} collective-permute-done((f32[176,256]{1,0:T(8,128)S(1)}, f32[176,256]{1,0:T(8,128)S(1)}, u32[]{:S(2)}, u32[]{:S(2)}) %collective-permute-start.13) | collective-permute-done | bytes 180256 | tf_op jit(solution)/shard_map/ppermute | solution.py:220
  42.6 1.0 %shard_map.109 = (f32[172,2,256]{2,1,0:T(2,128)}, f32[1,1]{1,0:T(1,128)}) custom-call(s32[1]{0:T(128)} %bitcast.core_ref.refs_4_, f32[176,256]{1,0:T(8,128)S(1)} %shard_map.108.own_ref.total_ref, f32[176,256]{1,0:T(8,128)S(1)} %collective-permute-done.13.other_ref), custom_call_target="tpu_custom_call" | custom-call | bytes 712712 | tf_op jit(solution)/shard_map/pallas_call | solution.py:38
  (3 shorter events, 0.1 us)
Async XLA Ops:
  0.6 11.1 %collective-permute-start.1 = (bf16[256,512]{1,0:T(8,128)(2,1)}, bf16[256,512]{1,0:T(8,128)(2,1)S(1)}, u32[]{:S(2)}, u32[]{:S(2)}) collective-permute-start(bf16[256,512]{1,0:T(8,128)(2,1)} %f_ref.1), channel_id=1, source_target_pairs={{0,16},{8,24},{16,0},{24,8},{1,17},{9,25},{17,1},{25,9},{2,18},{10... | collective-permute-start | bytes 786440 | tf_op jit(solution)/shard_map/ppermute | solution.py:220
  3.7 10.9 %collective-permute-start = (bf16[256,512]{1,0:T(8,128)(2,1)}, bf16[256,512]{1,0:T(8,128)(2,1)S(1)}, u32[]{:S(2)}, u32[]{:S(2)}) collective-permute-start(bf16[256,512]{1,0:T(8,128)(2,1)} %f_ref.1), channel_id=1, source_target_pairs={{0,8},{8,0},{16,24},{24,16},{1,9},{9,1},{17,25},{25,17},{2,10},{10... | collective-permute-start | bytes 786440 | tf_op jit(solution)/shard_map/ppermute | solution.py:220
  6.1 10.1 %collective-permute-start.4 = (bf16[256,256]{1,0:T(8,128)(2,1)S(1)}, bf16[256,256]{1,0:T(8,128)(2,1)S(1)}, u32[]{:S(2)}, u32[]{:S(2)}) collective-permute-start(bf16[256,256]{1,0:T(8,128)(2,1)S(1)} %broadcast_select_fusion), channel_id=1, source_target_pairs={{0,24},{8,16},{16,8},{24,0},{1,25},{9,17},{17,9},{25,1},{2,26},{10... | collective-permute-start | bytes 393224 | tf_op jit(solution)/shard_map/ppermute | solution.py:220
  6.2 10.4 %collective-permute-start.3 = (bf16[256,256]{1,0:T(8,128)(2,1)S(1)}, bf16[256,256]{1,0:T(8,128)(2,1)S(1)}, u32[]{:S(2)}, u32[]{:S(2)}) collective-permute-start(bf16[256,256]{1,0:T(8,128)(2,1)S(1)} %broadcast_select_fusion), channel_id=1, source_target_pairs={{0,16},{8,24},{16,0},{24,8},{1,17},{9,25},{17,1},{25,9},{2,18},{10... | collective-permute-start | bytes 393224 | tf_op jit(solution)/shard_map/ppermute | solution.py:220
  8.1 10.5 %collective-permute-start.2 = (bf16[256,256]{1,0:T(8,128)(2,1)S(1)}, bf16[256,256]{1,0:T(8,128)(2,1)S(1)}, u32[]{:S(2)}, u32[]{:S(2)}) collective-permute-start(bf16[256,256]{1,0:T(8,128)(2,1)S(1)} %broadcast_select_fusion), channel_id=1, source_target_pairs={{0,8},{8,0},{16,24},{24,16},{1,9},{9,1},{17,25},{25,17},{2,10},{10... | collective-permute-start | bytes 393224 | tf_op jit(solution)/shard_map/ppermute | solution.py:220
  11.7 8.9 %copy-start.5 = (bf16[256,512]{1,0:T(8,128)(2,1)S(1)}, bf16[256,512]{1,0:T(8,128)(2,1)}, u32[]{:S(2)}) copy-start(bf16[256,512]{1,0:T(8,128)(2,1)} %f_ref.1) | copy-start | bytes 786436
  11.7 6.9 %copy-start.2 = (s32[512,10]{0,1:T(8,128)S(1)}, s32[512,10]{0,1:T(8,128)}, u32[]{:S(2)}) copy-start(s32[512,10]{0,1:T(8,128)} %param.9) | copy-start | bytes 61444
  11.8 8.8 %collective-permute-start.5 = (bf16[128,512]{1,0:T(8,128)(2,1)S(1)}, bf16[128,512]{1,0:T(8,128)(2,1)S(1)}, u32[]{:S(2)}, u32[]{:S(2)}) collective-permute-start(bf16[128,512]{1,0:T(8,128)(2,1)S(1)} %slice.8), channel_id=1, source_target_pairs={{0,8},{8,0},{16,24},{24,16},{1,9},{9,1},{17,25},{25,17},{2,10},{10... | collective-permute-start | bytes 393224 | tf_op jit(solution)/shard_map/ppermute | solution.py:220
  14.6 6.0 %collective-permute-start.6 = (bf16[128,512]{1,0:T(8,128)(2,1)S(1)}, bf16[128,512]{1,0:T(8,128)(2,1)S(1)}, u32[]{:S(2)}, u32[]{:S(2)}) collective-permute-start(bf16[128,512]{1,0:T(8,128)(2,1)S(1)} %slice.9), channel_id=1, source_target_pairs={{0,16},{8,24},{16,0},{24,8},{1,17},{9,25},{17,1},{25,9},{2,18},{10... | collective-permute-start | bytes 393224 | tf_op jit(solution)/shard_map/ppermute | solution.py:220
  18.7 0.7 %copy-start.4 = (f32[512]{0:T(512)S(1)}, f32[512]{0:T(512)}, u32[]{:S(2)}) copy-start(f32[512]{0:T(512)} %param.11) | copy-start | bytes 6148
  18.7 0.7 %copy-start.3 = (s32[512]{0:T(512)S(1)}, s32[512]{0:T(512)}, u32[]{:S(2)}) copy-start(s32[512]{0:T(512)} %param.10) | copy-start | bytes 6148
  19.4 1.3 %copy-start = (bf16[256,256]{1,0:T(8,128)(2,1)S(1)}, bf16[256,256]{1,0:T(8,128)(2,1)}, u32[]{:S(2)}) copy-start(bf16[256,256]{1,0:T(8,128)(2,1)} %refs_10_.1) | copy-start | bytes 393220
  19.4 1.3 %copy-start.1 = (bf16[256,256]{1,0:T(8,128)(2,1)S(1)}, bf16[256,256]{1,0:T(8,128)(2,1)}, u32[]{:S(2)}) copy-start(bf16[256,256]{1,0:T(8,128)(2,1)} %refs_11_.1) | copy-start | bytes 393220
  20.5 1.8 %collective-permute-start.7 = (bf16[3,256,256]{2,1,0:T(8,128)(2,1)S(1)}, bf16[3,256,256]{2,1,0:T(8,128)(2,1)S(1)}, u32[]{:S(2)}, u32[]{:S(2)}) collective-permute-start(bf16[3,256,256]{2,1,0:T(8,128)(2,1)S(1)} %get-tuple-element.22.mine_ref), channel_id=1, source_target_pairs={{0,1},{1,0},{2,3},{3,2},{4,5},{5,4},{6,7},{7,6},{8,9},{9,8},{10,11... | collective-permute-start | bytes 1179656 | tf_op jit(solution)/shard_map/ppermute | solution.py:220
  20.6 1.7 %copy-start.6 = (bf16[256,172]{0,1:T(8,128)(2,1)S(1)}, bf16[256,172]{0,1:T(8,128)(2,1)}, u32[]{:S(2)}) copy-start(bf16[256,172]{0,1:T(8,128)(2,1)} %param.14) | copy-start | bytes 264196
  20.6 1.7 %copy-start.7 = (bf16[256,172]{0,1:T(8,128)(2,1)S(1)}, bf16[256,172]{0,1:T(8,128)(2,1)}, u32[]{:S(2)}) copy-start(bf16[256,172]{0,1:T(8,128)(2,1)} %param.15) | copy-start | bytes 264196
  25.1 1.9 %collective-permute-start.9 = (f32[4,64,256]{2,1,0:T(8,128)S(1)}, f32[4,64,256]{2,1,0:T(8,128)S(1)}, u32[]{:S(2)}, u32[]{:S(2)}) collective-permute-start(f32[4,64,256]{2,1,0:T(8,128)S(1)} %get-tuple-element.33), channel_id=1, source_target_pairs={{0,1},{1,0},{2,3},{3,2},{4,5},{5,4},{6,7},{7,6},{8,9},{9,8},{10,11... | collective-permute-start | bytes 786440 | tf_op jit(solution)/shard_map/ppermute | solution.py:220
  25.3 1.7 %collective-permute-start.8 = (f32[176,256]{1,0:T(8,128)S(1)}, f32[176,256]{1,0:T(8,128)S(1)}, u32[]{:S(2)}, u32[]{:S(2)}) collective-permute-start(f32[176,256]{1,0:T(8,128)S(1)} %get-tuple-element.29), channel_id=1, source_target_pairs={{0,1},{1,0},{2,3},{3,2},{4,5},{5,4},{6,7},{7,6},{8,9},{9,8},{10,11... | collective-permute-start | bytes 540680 | tf_op jit(solution)/shard_map/ppermute | solution.py:220
  27.0 7.1 %collective-permute-start.10 = (bf16[240,256]{1,0:T(8,128)(2,1)S(1)}, bf16[240,256]{1,0:T(8,128)(2,1)S(1)}, u32[]{:S(2)}, u32[]{:S(2)}) collective-permute-start(bf16[240,256]{1,0:T(8,128)(2,1)S(1)} %get-tuple-element.35), channel_id=1, source_target_pairs={{0,2},{1,3},{2,0},{3,1},{4,6},{5,7},{6,4},{7,5},{8,10},{9,11},{10,... | collective-permute-start | bytes 368648 | tf_op jit(solution)/shard_map/ppermute | solution.py:220
  28.7 12.4 %collective-permute-start.11 = (bf16[240,256]{1,0:T(8,128)(2,1)S(1)}, bf16[240,256]{1,0:T(8,128)(2,1)S(1)}, u32[]{:S(2)}, u32[]{:S(2)}) collective-permute-start(bf16[240,256]{1,0:T(8,128)(2,1)S(1)} %get-tuple-element.36), channel_id=1, source_target_pairs={{0,4},{1,5},{2,6},{3,7},{4,0},{5,1},{6,2},{7,3},{8,12},{9,13},{10,... | collective-permute-start | bytes 368648 | tf_op jit(solution)/shard_map/ppermute | solution.py:220
  31.3 9.8 %collective-permute-start.12 = (bf16[240,256]{1,0:T(8,128)(2,1)S(1)}, bf16[240,256]{1,0:T(8,128)(2,1)S(1)}, u32[]{:S(2)}, u32[]{:S(2)}) collective-permute-start(bf16[240,256]{1,0:T(8,128)(2,1)S(1)} %get-tuple-element.37), channel_id=1, source_target_pairs={{0,6},{1,7},{2,4},{3,5},{4,2},{5,3},{6,0},{7,1},{8,14},{9,15},{10,... | collective-permute-start | bytes 368648 | tf_op jit(solution)/shard_map/ppermute | solution.py:220
  41.1 1.5 %collective-permute-start.13 = (f32[176,256]{1,0:T(8,128)S(1)}, f32[176,256]{1,0:T(8,128)S(1)}, u32[]{:S(2)}, u32[]{:S(2)}) collective-permute-start(f32[176,256]{1,0:T(8,128)S(1)} %shard_map.108.own_ref.total_ref), channel_id=1, source_target_pairs={{0,1},{1,0},{2,3},{3,2},{4,5},{5,4},{6,7},{7,6},{8,9},{9,8},{10,11... | collective-permute-start | bytes 540680 | tf_op jit(solution)/shard_map/ppermute | solution.py:220

commit v4 on v3

--- a/solution.py
+++ b/solution.py
@@ -50,12 +50,9 @@
     return jax.ShapeDtypeStruct(dims, dtype)
 
 
-def count_kernel(fanout, nbr_ref, labels_ref, weight_ref, *refs):
-    at_ref, stack_ref, labels_out_ref, weight_out_ref = refs[-4:]
+def count_kernel(fanout, nbr_ref, labels_ref, weight_ref, at_ref, labels_out_ref, weight_out_ref):
     labels_out_ref[...] = labels_ref[...]
     weight_out_ref[...] = weight_ref[...]
-    for i, ref in enumerate(refs[:-4]):
-        stack_ref[i] = ref[...]
     nodes = at_ref.shape[1]
     step = 32
 
@@ -70,14 +67,15 @@
     lax.fori_loop(0, nodes // step, body, 0)
 
 
-def project(own, others_ref, f_refs):
+def project(own, others_refs, f_refs):
     products = [dot_tn(own, f_refs[0][...])]
     for s in range(1, len(f_refs)):
-        products.append(dot_tn(others_ref[s - 1], f_refs[s][...]))
+        products.append(dot_tn(others_refs[s - 1][...], f_refs[s][...]))
     return tree_sum(products)
 
 
-def mine_kernel(parts, core_ref, ws_ref, wn_ref, mine_ref, *refs):
+def mine_kernel(parts, core_ref, ws_ref, wn_ref, *refs):
+    mine_refs, refs = refs[: len(parts) - 1], refs[len(parts) - 1 :]
     out_ref, joined_refs = refs[sum(parts)], refs[sum(parts) + 1 :]
     own = jnp.where(core_ref[0] == 0, ws_ref[...], wn_ref[...])
     blocks, at, done = [], 0, 0
@@ -91,20 +89,21 @@
             done += 1
         blocks.append(block)
         at += count
-    out_ref[...] = project(own, mine_ref, blocks)
+    out_ref[...] = project(own, mine_refs, blocks)
 
 
 def forward_kernel(feat_count, fanout, *refs):
     f_refs, refs = refs[:feat_count], refs[feat_count:]
-    core_ref, labels_ref, weight_ref, at_ref, w2s_ref, w2n_ref, ws_ref, wn_ref, partner_ref, mine_ref = refs[:10]
-    send_ref, keep_ref, g_ref, hidden_ref, proj, pair = refs[10:]
+    core_ref, labels_ref, weight_ref, at_ref, w2s_ref, w2n_ref, ws_ref, wn_ref, mine_ref = refs[:9]
+    partner_refs = refs[9 : 8 + feat_count]
+    send_ref, keep_ref, g_ref, hidden_ref, proj, pair = refs[8 + feat_count :]
     core = core_ref[0]
     classes = w2s_ref.shape[0]
     nodes = at_ref.shape[1]
     scale = 1.0 / fanout
     own = jnp.where(core == 0, wn_ref[...], ws_ref[...])
     proj[core] = mine_ref[...]
-    proj[1 - core] = project(own, partner_ref, f_refs)
+    proj[1 - core] = project(own, partner_refs, f_refs)
     at = at_ref[...]
     pre = proj[0] + dot_nn(proj[1].astype(BF16), at) * scale
     hidden = jnp.maximum(pre, 0.0).astype(BF16)
@@ -161,28 +160,27 @@
             keep_ref[z, part * rows : (part + 1) * rows] = jnp.where(first, low_rows, high_rows)
 
 
-def pack_kernel(classes, groups, z_ref, keep2_ref, recv2_ref, keep1_ref, recv1_ref, own2_ref, own1_ref, *pack_refs):
-    z = z_ref[0]
-    total = keep2_ref[...] + recv2_ref[...]
+def pair_kernel(classes, keep_ref, recv_ref, out_ref):
+    total = keep_ref[...] + recv_ref[...]
     high = total.astype(BF16).astype(F32)
     rest = total - high
     middle = rest.astype(BF16).astype(F32)
     low = rest - middle
     row = lax.broadcasted_iota(jnp.int32, total.shape, 0)
-    out = jnp.where(row == classes + 1, middle, jnp.where(row == classes + 2, low, high)).astype(BF16)
-    own2_ref[...] = out
-    own1_ref[...] = keep1_ref[z] + recv1_ref[z]
-    padded = total.shape[0]
+    out_ref[...] = jnp.where(row == classes + 1, middle, jnp.where(row == classes + 2, low, high)).astype(BF16)
+
+
+def chunk_kernel(groups, z_ref, keep_ref, recv_ref, own_ref, *out_refs):
+    z = z_ref[0]
+    own_ref[...] = keep_ref[z] + recv_ref[z]
     for s in range(1, groups):
         other = jnp.bitwise_xor(z, s)
-        pack_refs[s - 1][:padded] = out
-        pack_refs[s - 1][padded:] = (keep1_ref[other] + recv1_ref[other]).astype(BF16)
+        out_refs[s - 1][...] = (keep_ref[other] + recv_ref[other]).astype(BF16)
 
 
 def second_sum_kernel(*refs):
     out_ref = refs[-1]
-    padded = out_ref.shape[0]
-    out_ref[...] = tree_sum([r[:padded].astype(F32) for r in refs[:-1]])
+    out_ref[...] = tree_sum([r[...].astype(F32) for r in refs[:-1]])
 
 
 def scalars(total, classes):
@@ -208,8 +206,7 @@
 def first_out_kernel(classes, total_ref, own_ref, *refs):
     _, norm = scalars(total_ref[...], classes)
     out_ref = refs[-1]
-    padded = total_ref.shape[0]
-    summed = tree_sum([own_ref[...]] + [r[padded:].astype(F32) for r in refs[:-1]]) * (1.0 / norm)
+    summed = tree_sum([own_ref[...]] + [r[...].astype(F32) for r in refs[:-1]]) * (1.0 / norm)
     rows = out_ref.shape[1]
     out_ref[0] = summed[:rows]
     out_ref[1] = summed[rows:]
@@ -251,28 +248,27 @@
     mine_own = jnp.where(core[0] == 0, w1_self, w1_neigh)
     mine = [exchange(mine_own, "feat", s) for s in range(1, feat_count)]
     limit = 12 + 6 * nodes * nodes // (1024 * 1024)
-    at, stacked, labels, loss_weight = call(
+    at, labels, loss_weight = call(
         functools.partial(count_kernel, fanout),
         [
             shape((nodes, nodes), BF16),
-            shape((feat_count - 1, rows, hid), BF16),
             shape((1, nodes), jnp.int32),
             shape((1, nodes), F32),
         ],
-        [neighbors.T, labels.reshape(1, nodes), loss_weight.reshape(1, nodes)] + mine,
+        [neighbors.T, labels.reshape(1, nodes), loss_weight.reshape(1, nodes)],
         flops=nodes * nodes * fanout,
     )
     mine_proj, *joined = call(
         functools.partial(mine_kernel, parts),
         [shape((hid, nodes), F32)] + [shape((rows, nodes), BF16)] * sum(count > 1 for count in parts),
-        [core, w1_self, w1_neigh, stacked] + [part for block in wide for part in block],
+        [core, w1_self, w1_neigh] + mine + [part for block in wide for part in block],
         flops=30 * nodes * hid * rows * feat_count,
         smem=(0,),
         limit=limit,
     )
     rest = iter(joined)
     whole = [block[0] if len(block) == 1 else next(rest) for block in wide]
-    partner = exchange(stacked, "dp", 1)
+    partner = [exchange(block, "dp", 1) for block in mine]
     w2s, w2n = w2_self.T, w2_neigh.T
     padded = (classes + 3 + 15) // 16 * 16
     send2, keep2, grad, hidden = call(
@@ -283,7 +279,7 @@
             shape((classes, nodes), BF16),
             shape((hid, nodes), BF16),
         ],
-        whole + [core, labels, loss_weight, at, w2s, w2n, w1_self, w1_neigh, partner, mine_proj],
+        whole + [core, labels, loss_weight, at, w2s, w2n, w1_self, w1_neigh, mine_proj] + partner,
         scratch=[
             pltpu.VMEM((2, hid, nodes), F32),
             pltpu.VMEM((2, hid, nodes), BF16),
@@ -303,19 +299,22 @@
         limit=limit,
     )
     recv1 = exchange(send1, "dp", 1)
-    own2, own1, *packs = call(
-        functools.partial(pack_kernel, classes, groups),
-        [shape((padded, hid), BF16), shape((chunk, hid), F32)] + [shape((padded + chunk, hid), BF16)] * (groups - 1),
-        [z, keep2, recv2, keep1, recv1],
+    (own2,) = call(functools.partial(pair_kernel, classes), [shape((padded, hid), BF16)], [keep2, recv2])
+    far2 = [exchange(own2, "dp", 2 * s) for s in range(1, groups)]
+    own1, *chunks = call(
+        functools.partial(chunk_kernel, groups),
+        [shape((chunk, hid), F32)] + [shape((chunk, hid), BF16)] * (groups - 1),
+        [z, keep1, recv1],
         smem=(0,),
     )
-    far = [exchange(packs[s - 1], "dp", 2 * s) for s in range(1, groups)]
-    (total2,) = call(second_sum_kernel, [shape((padded, hid), F32)], [own2] + far)
+    far1 = [exchange(chunks[s - 1], "dp", 2 * s) for s in range(1, groups)]
+    (total2,) = call(second_sum_kernel, [shape((padded, hid), F32)], [own2] + far2)
     other2 = exchange(total2, "dp", 1)
     (grad_w1,) = call(
         functools.partial(first_out_kernel, classes),
         [shape((2, rows // dp_count, hid), F32)],
-        [total2, own1] + far,
+        [total2, own1] + far1,
+        flops=300 * rows * nodes * hid,
         final=True,
     )
     grad_w2, loss = call(

time: 43.8 us -> 41 us (0.936)
  waiting for transfers between devices: 17.3 us -> 6.85 us
  starting transfers between devices: 17.6 us -> 24.7 us
    ppermute x14 -> x19, waiting for transfers between devices: 17.3 us -> 6.85 us  [exchange(): return lax.ppermute(value, axis, [(i, i ^ step) for i in range(size)])]
    ppermute x14 -> x19, starting transfers between devices: 17.6 us -> 24.7 us  [exchange(): return lax.ppermute(value, axis, [(i, i ^ step) for i in range(size)])]
    pallas_call x8 -> x9, Pallas kernels: 6.28 us -> 6.31 us  [call(): pl.pallas_call(kernel, out_shape=outs if final else [pltpu.VMEM(o.shape,...]
  transfers between devices with their start and end apart: 14 -> 19, of which waited for: 8 -> 6; matrix products, arithmetic and copies ran while one was open for 2% -> 2% of each run, Pallas kernels for 5% -> 9%
where the time goes in v4:
time: 41 us; the launch traced here: 40.8 us
  starting transfers between devices  24.7 us (60%)
  waiting for transfers between devices  6.85 us (17%)
  Pallas kernels  6.31 us (15%)
  local copies, waits for them, and re-layouts  1.15 us (3%)
  other arithmetic  0.97 us (2%)
  between operations  0.81 us (2%)
    ppermute x19, starting transfers between devices, exchange(): return lax.ppermute(value, axis, [(i, i ^ step) for i in range(size)])  24.7 us
    ppermute x19, waiting for transfers between devices, exchange(): return lax.ppermute(value, axis, [(i, i ^ step) for i in range(size)])  6.85 us
    pallas_call x9, Pallas kernels, call(): pl.pallas_call(kernel, out_shape=outs if final else [pltpu.VMEM(o.shape,...  6.31 us
    unnamed x16, local copies, waits for them, and re-layouts  1.13 us
    select_n x1, other arithmetic, on_device(): mine_own = jnp.where(core[0] == 0, w1_self, w1_neigh)  0.97 us
  transfers between devices with their start and end apart: 19, of which 6 were waited for; matrix products, arithmetic and copies ran while one was open for 2% of the time, Pallas kernels for 9%

profile of v4, /device:TPU:0, one launch (start us, length us, event | category | flops | bytes accessed | tf_op | source)
XLA Modules:
  0.0 40.8 jit_solution(1849985896055910090)
XLA Ops:
  0.6 3.0 %collective-permute-start.1 = (bf16[256,512]{1,0:T(8,128)(2,1)}, bf16[256,512]{1,0:T(8,128)(2,1)S(1)}, u32[]{:S(2)}, u32[]{:S(2)}) collective-permute-start(bf16[256,512]{1,0:T(8,128)(2,1)} %f_ref.1), channel_id=1, source_target_pairs={{0,16},{8,24},{16,0},{24,8},{1,17},{9,25},{17,1},{25,9},{2,18},{10... | collective-permute-start | bytes 786440 | tf_op jit(solution)/shard_map/ppermute | solution.py:217
  3.7 1.5 %collective-permute-start = (bf16[256,512]{1,0:T(8,128)(2,1)}, bf16[256,512]{1,0:T(8,128)(2,1)S(1)}, u32[]{:S(2)}, u32[]{:S(2)}) collective-permute-start(bf16[256,512]{1,0:T(8,128)(2,1)} %f_ref.1), channel_id=1, source_target_pairs={{0,8},{8,0},{16,24},{24,16},{1,9},{9,1},{17,25},{25,17},{2,10},{10... | collective-permute-start | bytes 786440 | tf_op jit(solution)/shard_map/ppermute | solution.py:217
  5.2 0.0 copy-start.5
  5.2 1.0 %broadcast_select_fusion = bf16[256,256]{1,0:T(8,128)(2,1)S(1)} fusion(bf16[256,256]{1,0:T(8,128)(2,1)} %refs_10_.1, bf16[256,256]{1,0:T(8,128)(2,1)} %refs_11_.1, pred[]{:T(512)S(6)} %eq.5), kind=kLoop, calls=%fused_computation | loop fusion | flops 65536 | bytes 393217 | tf_op jit(solution)/shard_map/jit(_where)/select_n | solution.py:248
  6.1 0.1 collective-permute-start.4
  6.2 1.9 %collective-permute-start.3 = (bf16[256,256]{1,0:T(8,128)(2,1)S(1)}, bf16[256,256]{1,0:T(8,128)(2,1)S(1)}, u32[]{:S(2)}, u32[]{:S(2)}) collective-permute-start(bf16[256,256]{1,0:T(8,128)(2,1)S(1)} %broadcast_select_fusion), channel_id=1, source_target_pairs={{0,16},{8,24},{16,0},{24,8},{1,17},{9,25},{17,1},{25,9},{2,18},{10... | collective-permute-start | bytes 393224 | tf_op jit(solution)/shard_map/ppermute | solution.py:217
  8.2 1.5 %collective-permute-start.2 = (bf16[256,256]{1,0:T(8,128)(2,1)S(1)}, bf16[256,256]{1,0:T(8,128)(2,1)S(1)}, u32[]{:S(2)}, u32[]{:S(2)}) collective-permute-start(bf16[256,256]{1,0:T(8,128)(2,1)S(1)} %broadcast_select_fusion), channel_id=1, source_target_pairs={{0,8},{8,0},{16,24},{24,16},{1,9},{9,1},{17,25},{25,17},{2,10},{10... | collective-permute-start | bytes 393224 | tf_op jit(solution)/shard_map/ppermute | solution.py:217
  9.7 2.0 %collective-permute-done.1.refs_5_.refs_2_ = bf16[256,512]{1,0:T(8,128)(2,1)S(1)} collective-permute-done((bf16[256,512]{1,0:T(8,128)(2,1)}, bf16[256,512]{1,0:T(8,128)(2,1)S(1)}, u32[]{:S(2)}, u32[]{:S(2)}) %collective-permute-start.1) | collective-permute-done | bytes 262176 | tf_op jit(solution)/shard_map/ppermute | solution.py:217
  11.7 0.0 copy-start.2
  11.7 0.0 copy-start
  11.8 0.0 copy-start.1
  11.8 2.8 %collective-permute-start.5 = (bf16[128,512]{1,0:T(8,128)(2,1)S(1)}, bf16[128,512]{1,0:T(8,128)(2,1)S(1)}, u32[]{:S(2)}, u32[]{:S(2)}) collective-permute-start(bf16[128,512]{1,0:T(8,128)(2,1)S(1)} %slice.8), channel_id=1, source_target_pairs={{0,8},{8,0},{16,24},{24,16},{1,9},{9,1},{17,25},{25,17},{2,10},{10... | collective-permute-start | bytes 393224 | tf_op jit(solution)/shard_map/ppermute | solution.py:217
  14.5 0.0 collective-permute-done.refs_4_.refs_1_
  14.6 1.6 %collective-permute-start.6 = (bf16[128,512]{1,0:T(8,128)(2,1)S(1)}, bf16[128,512]{1,0:T(8,128)(2,1)S(1)}, u32[]{:S(2)}, u32[]{:S(2)}) collective-permute-start(bf16[128,512]{1,0:T(8,128)(2,1)S(1)} %slice.9), channel_id=1, source_target_pairs={{0,16},{8,24},{16,0},{24,8},{1,17},{9,25},{17,1},{25,9},{2,18},{10... | collective-permute-start | bytes 393224 | tf_op jit(solution)/shard_map/ppermute | solution.py:217
  16.1 0.0 copy-start.4
  16.1 0.0 copy-start.3
  16.2 0.0 copy-done.2
  16.2 0.7 %copy-done.4 = f32[512]{0:T(512)S(1)} copy-done((f32[512]{0:T(512)S(1)}, f32[512]{0:T(512)}, u32[]{:S(2)}) %copy-start.4) | copy-done | bytes 2072
  16.8 0.0 copy-done.3
  16.8 1.1 %shard_map.104 = (bf16[512,512]{1,0:T(8,128)(2,1)S(1)}, s32[1,512]{1,0:T(1,128)S(1)}, f32[1,512]{1,0:T(1,128)S(1)}) custom-call(s32[10,512]{1,0:T(8,128)S(1)} %bitcast.9, s32[1,512]{1,0:T(1,128)S(1)} %bitcast.10, f32[1,512]{1,0:T(1,128)S(1)} %bitcast.11), custom_call_target="tpu_custom_call" | custom-call | flops 2621440 | bytes 552960 | tf_op jit(solution)/shard_map/pallas_call | solution.py:38
  18.0 0.0 collective-permute-done.4.refs_2_
  18.0 0.1 collective-permute-start.9
  18.0 0.0 collective-permute-done.3.refs_1_
  18.1 0.5 %collective-permute-start.8 = (bf16[256,256]{1,0:T(8,128)(2,1)S(1)}, bf16[256,256]{1,0:T(8,128)(2,1)S(1)}, u32[]{:S(2)}, u32[]{:S(2)}) collective-permute-start(bf16[256,256]{1,0:T(8,128)(2,1)S(1)} %collective-permute-done.3.refs_1_), channel_id=1, source_target_pairs={{0,1},{1,0},{2,3},{3,2},{4,5},{5,4},{6,7},{7,6},{8,9},{9,8},{10,11... | collective-permute-start | bytes 393224 | tf_op jit(solution)/shard_map/ppermute | solution.py:217
  18.5 0.1 collective-permute-done.2.refs_0_
  18.7 0.0 collective-permute-start.7
  18.7 1.4 %collective-permute-done.5.refs_6_ = bf16[128,512]{1,0:T(8,128)(2,1)S(1)} collective-permute-done((bf16[128,512]{1,0:T(8,128)(2,1)S(1)}, bf16[128,512]{1,0:T(8,128)(2,1)S(1)}, u32[]{:S(2)}, u32[]{:S(2)}) %collective-permute-start.5) | collective-permute-done | bytes 131104 | tf_op jit(solution)/shard_map/ppermute | solution.py:217
  20.1 0.0 collective-permute-done.6.refs_7_
  20.1 0.0 copy-done.5
  20.1 0.0 copy-done
  20.1 0.0 copy-done.1
  20.1 0.0 copy-start.6
  20.1 0.0 copy-start.7
  20.1 0.5 %shard_map.103 = (f32[256,512]{1,0:T(8,128)S(1)}, bf16[256,512]{1,0:T(8,128)(2,1)S(1)}) custom-call(s32[1]{0:T(128)} %bitcast.core_ref.refs_4_, bf16[256,256]{1,0:T(8,128)(2,1)S(1)} %copy-done, bf16[256,256]{1,0:T(8,128)(2,1)S(1)} %copy-done.1, bf16[256,256]{1,0:T(8,128)(2,1)S(1)} %collective-permute-done.2.refs_0_, ...), custom_call_target="tpu_custom_call" | custom-call | flops 4026531840 | bytes 2490372 | tf_op jit(solution)/shard_map/pallas_call | solution.py:38
  20.6 0.0 collective-permute-done.9.refs_15_
  20.6 0.0 collective-permute-done.8.refs_14_
  20.6 0.0 collective-permute-done.7.refs_13_
  20.6 0.4 copy-done.6
  21.0 0.0 copy-done.7
  21.0 1.7 %shard_map.105 = (f32[176,256]{1,0:T(8,128)S(1)}, f32[176,256]{1,0:T(8,128)S(1)}, bf16[172,512]{1,0:T(8,128)(2,1)S(1)}, bf16[256,512]{1,0:T(8,128)(2,1)S(1)}) custom-call(bf16[256,512]{1,0:T(8,128)(2,1)S(1)} %copy-done.5, bf16[256,512]{1,0:T(8,128)(2,1)S(1)} %collective-permute-done.refs_4_.refs_1_, ...), custom_call_target="tpu_custom_call" | custom-call | flops 805306368 | bytes 3731460 | tf_op jit(solution)/shard_map/pallas_call | solution.py:38
  22.7 0.1 collective-permute-start.10
  22.8 1.2 %shard_map.109 = (f32[4,64,256]{2,1,0:T(8,128)S(1)}, f32[4,64,256]{2,1,0:T(8,128)S(1)}) custom-call(s32[1]{0:T(128)} %bitcast.core_ref.refs_4_, bf16[172,512]{1,0:T(8,128)(2,1)S(1)} %get-tuple-element.28.g_ref, bf16[256,512]{1,0:T(8,128)(2,1)S(1)} %get-tuple-element.29.hidden_ref, bf16[512,512]{1,0:T(8,128)(2,1)S(1)} %get-tuple-element.23.refs_7_.at_ref, ...), custom_call_target="tpu_custom_call" | custom-call | flops 402653184 | bytes 1925124 | tf_op jit(solution)/shard_map/pallas_call | solution.py:38
  24.0 0.6 %collective-permute-start.15 = (f32[4,64,256]{2,1,0:T(8,128)S(1)}, f32[4,64,256]{2,1,0:T(8,128)S(1)}, u32[]{:S(2)}, u32[]{:S(2)}) collective-permute-start(f32[4,64,256]{2,1,0:T(8,128)S(1)} %get-tuple-element.31), channel_id=1, source_target_pairs={{0,1},{1,0},{2,3},{3,2},{4,5},{5,4},{6,7},{7,6},{8,9},{9,8},{10,11... | collective-permute-start | bytes 786440 | tf_op jit(solution)/shard_map/ppermute | solution.py:217
  24.5 0.0 collective-permute-done.10.recv_ref
  24.6 3.7 %collective-permute-start.13 = (bf16[176,256]{1,0:T(8,128)(2,1)S(1)}, bf16[176,256]{1,0:T(8,128)(2,1)S(1)}, u32[]{:S(2)}, u32[]{:S(2)}) collective-permute-start(bf16[176,256]{1,0:T(8,128)(2,1)S(1)} %shard_map.106.refs_0_), channel_id=1, source_target_pairs={{0,6},{1,7},{2,4},{3,5},{4,2},{5,3},{6,0},{7,1},{8,14},{9,15},{10,... | collective-permute-start | bytes 270344 | tf_op jit(solution)/shard_map/ppermute | solution.py:217
  28.2 0.0 collective-permute-start.12
  28.2 0.8 %collective-permute-start.11 = (bf16[176,256]{1,0:T(8,128)(2,1)S(1)}, bf16[176,256]{1,0:T(8,128)(2,1)S(1)}, u32[]{:S(2)}, u32[]{:S(2)}) collective-permute-start(bf16[176,256]{1,0:T(8,128)(2,1)S(1)} %shard_map.106.refs_0_), channel_id=1, source_target_pairs={{0,2},{1,3},{2,0},{3,1},{4,6},{5,7},{6,4},{7,5},{8,10},{9,11},{10,... | collective-permute-start | bytes 270344 | tf_op jit(solution)/shard_map/ppermute | solution.py:217
  29.0 0.0 collective-permute-done.15.recv_ref
  29.1 1.3 %collective-permute-start.16 = (bf16[64,256]{1,0:T(8,128)(2,1)S(1)}, bf16[64,256]{1,0:T(8,128)(2,1)S(1)}, u32[]{:S(2)}, u32[]{:S(2)}) collective-permute-start(bf16[64,256]{1,0:T(8,128)(2,1)S(1)} %get-tuple-element.33), channel_id=1, source_target_pairs={{0,2},{1,3},{2,0},{3,1},{4,6},{5,7},{6,4},{7,5},{8,10},{9,11},{10,... | collective-permute-start | bytes 98312 | tf_op jit(solution)/shard_map/ppermute | solution.py:217
  30.4 2.9 %collective-permute-start.17 = (bf16[64,256]{1,0:T(8,128)(2,1)S(1)}, bf16[64,256]{1,0:T(8,128)(2,1)S(1)}, u32[]{:S(2)}, u32[]{:S(2)}) collective-permute-start(bf16[64,256]{1,0:T(8,128)(2,1)S(1)} %get-tuple-element.34), channel_id=1, source_target_pairs={{0,4},{1,5},{2,6},{3,7},{4,0},{5,1},{6,2},{7,3},{8,12},{9,13},{10,... | collective-permute-start | bytes 98312 | tf_op jit(solution)/shard_map/ppermute | solution.py:217
  33.3 0.0 collective-permute-done.13.refs_3_
  33.3 2.3 %collective-permute-start.18 = (bf16[64,256]{1,0:T(8,128)(2,1)S(1)}, bf16[64,256]{1,0:T(8,128)(2,1)S(1)}, u32[]{:S(2)}, u32[]{:S(2)}) collective-permute-start(bf16[64,256]{1,0:T(8,128)(2,1)S(1)} %get-tuple-element.35), channel_id=1, source_target_pairs={{0,6},{1,7},{2,4},{3,5},{4,2},{5,3},{6,0},{7,1},{8,14},{9,15},{10,... | collective-permute-start | bytes 98312 | tf_op jit(solution)/shard_map/ppermute | solution.py:217
  35.6 2.1 %collective-permute-done.12.refs_2_ = bf16[176,256]{1,0:T(8,128)(2,1)S(1)} collective-permute-done((bf16[176,256]{1,0:T(8,128)(2,1)S(1)}, bf16[176,256]{1,0:T(8,128)(2,1)S(1)}, u32[]{:S(2)}, u32[]{:S(2)}) %collective-permute-start.12) | collective-permute-done | bytes 90144 | tf_op jit(solution)/shard_map/ppermute | solution.py:217
  37.7 0.0 collective-permute-done.11.refs_1_
  37.8 0.1 collective-permute-start.14
  37.9 0.0 collective-permute-done.16.refs_0_
  37.9 0.2 collective-permute-done.17.refs_1_
  38.1 0.9 %collective-permute-done.18.refs_2_ = bf16[64,256]{1,0:T(8,128)(2,1)S(1)} collective-permute-done((bf16[64,256]{1,0:T(8,128)(2,1)S(1)}, bf16[64,256]{1,0:T(8,128)(2,1)S(1)}, u32[]{:S(2)}, u32[]{:S(2)}) %collective-permute-start.18) | collective-permute-done | bytes 32800 | tf_op jit(solution)/shard_map/ppermute | solution.py:217
  39.0 0.8 %shard_map.111 = f32[2,32,256]{2,1,0:T(8,128)} custom-call(f32[176,256]{1,0:T(8,128)S(1)} %shard_map.107.own_ref.total_ref, f32[64,256]{1,0:T(8,128)S(1)} %get-tuple-element.32.own_ref, bf16[64,256]{1,0:T(8,128)(2,1)S(1)} %collective-permute-done.16.refs_0_, bf16[64,256]{1,0:T(8,128)(2,1)S(1)} %collective-permute-done.17.refs_1_, ...), custom_call_target="tpu_custom_call" | custom-call | flops 10066329600 | bytes 409600 | tf_op jit(solution)/shard_map/pallas_call | solution.py:38
  39.8 0.0 collective-permute-done.14.other_ref
  39.8 1.0 %shard_map.108 = (f32[172,2,256]{2,1,0:T(2,128)}, f32[1,1]{1,0:T(1,128)}) custom-call(s32[1]{0:T(128)} %bitcast.core_ref.refs_4_, f32[176,256]{1,0:T(8,128)S(1)} %shard_map.107.own_ref.total_ref, f32[176,256]{1,0:T(8,128)S(1)} %collective-permute-done.14.other_ref), custom_call_target="tpu_custom_call" | custom-call | bytes 712712 | tf_op jit(solution)/shard_map/pallas_call | solution.py:38
  (5 shorter events, 0.1 us)
Async XLA Ops:
  0.6 11.1 %collective-permute-start.1 = (bf16[256,512]{1,0:T(8,128)(2,1)}, bf16[256,512]{1,0:T(8,128)(2,1)S(1)}, u32[]{:S(2)}, u32[]{:S(2)}) collective-permute-start(bf16[256,512]{1,0:T(8,128)(2,1)} %f_ref.1), channel_id=1, source_target_pairs={{0,16},{8,24},{16,0},{24,8},{1,17},{9,25},{17,1},{25,9},{2,18},{10... | collective-permute-start | bytes 786440 | tf_op jit(solution)/shard_map/ppermute | solution.py:217
  3.7 10.9 %collective-permute-start = (bf16[256,512]{1,0:T(8,128)(2,1)}, bf16[256,512]{1,0:T(8,128)(2,1)S(1)}, u32[]{:S(2)}, u32[]{:S(2)}) collective-permute-start(bf16[256,512]{1,0:T(8,128)(2,1)} %f_ref.1), channel_id=1, source_target_pairs={{0,8},{8,0},{16,24},{24,16},{1,9},{9,1},{17,25},{25,17},{2,10},{10... | collective-permute-start | bytes 786440 | tf_op jit(solution)/shard_map/ppermute | solution.py:217
  5.2 14.9 %copy-start.5 = (bf16[256,512]{1,0:T(8,128)(2,1)S(1)}, bf16[256,512]{1,0:T(8,128)(2,1)}, u32[]{:S(2)}) copy-start(bf16[256,512]{1,0:T(8,128)(2,1)} %f_ref.1) | copy-start | bytes 786436
  6.1 11.8 %collective-permute-start.4 = (bf16[256,256]{1,0:T(8,128)(2,1)S(1)}, bf16[256,256]{1,0:T(8,128)(2,1)S(1)}, u32[]{:S(2)}, u32[]{:S(2)}) collective-permute-start(bf16[256,256]{1,0:T(8,128)(2,1)S(1)} %broadcast_select_fusion), channel_id=1, source_target_pairs={{0,24},{8,16},{16,8},{24,0},{1,25},{9,17},{17,9},{25,1},{2,26},{10... | collective-permute-start | bytes 393224 | tf_op jit(solution)/shard_map/ppermute | solution.py:217
  6.2 11.8 %collective-permute-start.3 = (bf16[256,256]{1,0:T(8,128)(2,1)S(1)}, bf16[256,256]{1,0:T(8,128)(2,1)S(1)}, u32[]{:S(2)}, u32[]{:S(2)}) collective-permute-start(bf16[256,256]{1,0:T(8,128)(2,1)S(1)} %broadcast_select_fusion), channel_id=1, source_target_pairs={{0,16},{8,24},{16,0},{24,8},{1,17},{9,25},{17,1},{25,9},{2,18},{10... | collective-permute-start | bytes 393224 | tf_op jit(solution)/shard_map/ppermute | solution.py:217
  8.2 10.5 %collective-permute-start.2 = (bf16[256,256]{1,0:T(8,128)(2,1)S(1)}, bf16[256,256]{1,0:T(8,128)(2,1)S(1)}, u32[]{:S(2)}, u32[]{:S(2)}) collective-permute-start(bf16[256,256]{1,0:T(8,128)(2,1)S(1)} %broadcast_select_fusion), channel_id=1, source_target_pairs={{0,8},{8,0},{16,24},{24,16},{1,9},{9,1},{17,25},{25,17},{2,10},{10... | collective-permute-start | bytes 393224 | tf_op jit(solution)/shard_map/ppermute | solution.py:217
  11.7 4.4 %copy-start.2 = (s32[512,10]{0,1:T(8,128)S(1)}, s32[512,10]{0,1:T(8,128)}, u32[]{:S(2)}) copy-start(s32[512,10]{0,1:T(8,128)} %param.9) | copy-start | bytes 61444
  11.7 8.3 %copy-start = (bf16[256,256]{1,0:T(8,128)(2,1)S(1)}, bf16[256,256]{1,0:T(8,128)(2,1)}, u32[]{:S(2)}) copy-start(bf16[256,256]{1,0:T(8,128)(2,1)} %refs_10_.1) | copy-start | bytes 393220
  11.8 8.3 %copy-start.1 = (bf16[256,256]{1,0:T(8,128)(2,1)S(1)}, bf16[256,256]{1,0:T(8,128)(2,1)}, u32[]{:S(2)}) copy-start(bf16[256,256]{1,0:T(8,128)(2,1)} %refs_11_.1) | copy-start | bytes 393220
  11.8 8.3 %collective-permute-start.5 = (bf16[128,512]{1,0:T(8,128)(2,1)S(1)}, bf16[128,512]{1,0:T(8,128)(2,1)S(1)}, u32[]{:S(2)}, u32[]{:S(2)}) collective-permute-start(bf16[128,512]{1,0:T(8,128)(2,1)S(1)} %slice.8), channel_id=1, source_target_pairs={{0,8},{8,0},{16,24},{24,16},{1,9},{9,1},{17,25},{25,17},{2,10},{10... | collective-permute-start | bytes 393224 | tf_op jit(solution)/shard_map/ppermute | solution.py:217
  14.6 5.5 %collective-permute-start.6 = (bf16[128,512]{1,0:T(8,128)(2,1)S(1)}, bf16[128,512]{1,0:T(8,128)(2,1)S(1)}, u32[]{:S(2)}, u32[]{:S(2)}) collective-permute-start(bf16[128,512]{1,0:T(8,128)(2,1)S(1)} %slice.9), channel_id=1, source_target_pairs={{0,16},{8,24},{16,0},{24,8},{1,17},{9,25},{17,1},{25,9},{2,18},{10... | collective-permute-start | bytes 393224 | tf_op jit(solution)/shard_map/ppermute | solution.py:217
  16.1 0.7 %copy-start.4 = (f32[512]{0:T(512)S(1)}, f32[512]{0:T(512)}, u32[]{:S(2)}) copy-start(f32[512]{0:T(512)} %param.11) | copy-start | bytes 6148
  16.1 0.7 %copy-start.3 = (s32[512]{0:T(512)S(1)}, s32[512]{0:T(512)}, u32[]{:S(2)}) copy-start(s32[512]{0:T(512)} %param.10) | copy-start | bytes 6148
  18.0 2.6 %collective-permute-start.9 = (bf16[256,256]{1,0:T(8,128)(2,1)S(1)}, bf16[256,256]{1,0:T(8,128)(2,1)S(1)}, u32[]{:S(2)}, u32[]{:S(2)}) collective-permute-start(bf16[256,256]{1,0:T(8,128)(2,1)S(1)} %collective-permute-done.4.refs_2_), channel_id=1, source_target_pairs={{0,1},{1,0},{2,3},{3,2},{4,5},{5,4},{6,7},{7,6},{8,9},{9,8},{10,11... | collective-permute-start | bytes 393224 | tf_op jit(solution)/shard_map/ppermute | solution.py:217
  18.1 2.5 %collective-permute-start.8 = (bf16[256,256]{1,0:T(8,128)(2,1)S(1)}, bf16[256,256]{1,0:T(8,128)(2,1)S(1)}, u32[]{:S(2)}, u32[]{:S(2)}) collective-permute-start(bf16[256,256]{1,0:T(8,128)(2,1)S(1)} %collective-permute-done.3.refs_1_), channel_id=1, source_target_pairs={{0,1},{1,0},{2,3},{3,2},{4,5},{5,4},{6,7},{7,6},{8,9},{9,8},{10,11... | collective-permute-start | bytes 393224 | tf_op jit(solution)/shard_map/ppermute | solution.py:217
  18.7 1.9 %collective-permute-start.7 = (bf16[256,256]{1,0:T(8,128)(2,1)S(1)}, bf16[256,256]{1,0:T(8,128)(2,1)S(1)}, u32[]{:S(2)}, u32[]{:S(2)}) collective-permute-start(bf16[256,256]{1,0:T(8,128)(2,1)S(1)} %collective-permute-done.2.refs_0_), channel_id=1, source_target_pairs={{0,1},{1,0},{2,3},{3,2},{4,5},{5,4},{6,7},{7,6},{8,9},{9,8},{10,11... | collective-permute-start | bytes 393224 | tf_op jit(solution)/shard_map/ppermute | solution.py:217
  20.1 0.9 %copy-start.6 = (bf16[256,172]{0,1:T(8,128)(2,1)S(1)}, bf16[256,172]{0,1:T(8,128)(2,1)}, u32[]{:S(2)}) copy-start(bf16[256,172]{0,1:T(8,128)(2,1)} %param.14) | copy-start | bytes 264196
  20.1 0.9 %copy-start.7 = (bf16[256,172]{0,1:T(8,128)(2,1)S(1)}, bf16[256,172]{0,1:T(8,128)(2,1)}, u32[]{:S(2)}) copy-start(bf16[256,172]{0,1:T(8,128)(2,1)} %param.15) | copy-start | bytes 264196
  22.7 1.8 %collective-permute-start.10 = (f32[176,256]{1,0:T(8,128)S(1)}, f32[176,256]{1,0:T(8,128)S(1)}, u32[]{:S(2)}, u32[]{:S(2)}) collective-permute-start(f32[176,256]{1,0:T(8,128)S(1)} %get-tuple-element.26), channel_id=1, source_target_pairs={{0,1},{1,0},{2,3},{3,2},{4,5},{5,4},{6,7},{7,6},{8,9},{9,8},{10,11... | collective-permute-start | bytes 540680 | tf_op jit(solution)/shard_map/ppermute | solution.py:217
  24.0 5.1 %collective-permute-start.15 = (f32[4,64,256]{2,1,0:T(8,128)S(1)}, f32[4,64,256]{2,1,0:T(8,128)S(1)}, u32[]{:S(2)}, u32[]{:S(2)}) collective-permute-start(f32[4,64,256]{2,1,0:T(8,128)S(1)} %get-tuple-element.31), channel_id=1, source_target_pairs={{0,1},{1,0},{2,3},{3,2},{4,5},{5,4},{6,7},{7,6},{8,9},{9,8},{10,11... | collective-permute-start | bytes 786440 | tf_op jit(solution)/shard_map/ppermute | solution.py:217
  24.6 8.7 %collective-permute-start.13 = (bf16[176,256]{1,0:T(8,128)(2,1)S(1)}, bf16[176,256]{1,0:T(8,128)(2,1)S(1)}, u32[]{:S(2)}, u32[]{:S(2)}) collective-permute-start(bf16[176,256]{1,0:T(8,128)(2,1)S(1)} %shard_map.106.refs_0_), channel_id=1, source_target_pairs={{0,6},{1,7},{2,4},{3,5},{4,2},{5,3},{6,0},{7,1},{8,14},{9,15},{10,... | collective-permute-start | bytes 270344 | tf_op jit(solution)/shard_map/ppermute | solution.py:217
  28.2 9.5 %collective-permute-start.12 = (bf16[176,256]{1,0:T(8,128)(2,1)S(1)}, bf16[176,256]{1,0:T(8,128)(2,1)S(1)}, u32[]{:S(2)}, u32[]{:S(2)}) collective-permute-start(bf16[176,256]{1,0:T(8,128)(2,1)S(1)} %shard_map.106.refs_0_), channel_id=1, source_target_pairs={{0,4},{1,5},{2,6},{3,7},{4,0},{5,1},{6,2},{7,3},{8,12},{9,13},{10,... | collective-permute-start | bytes 270344 | tf_op jit(solution)/shard_map/ppermute | solution.py:217
  28.2 9.5 %collective-permute-start.11 = (bf16[176,256]{1,0:T(8,128)(2,1)S(1)}, bf16[176,256]{1,0:T(8,128)(2,1)S(1)}, u32[]{:S(2)}, u32[]{:S(2)}) collective-permute-start(bf16[176,256]{1,0:T(8,128)(2,1)S(1)} %shard_map.106.refs_0_), channel_id=1, source_target_pairs={{0,2},{1,3},{2,0},{3,1},{4,6},{5,7},{6,4},{7,5},{8,10},{9,11},{10,... | collective-permute-start | bytes 270344 | tf_op jit(solution)/shard_map/ppermute | solution.py:217
  29.1 8.8 %collective-permute-start.16 = (bf16[64,256]{1,0:T(8,128)(2,1)S(1)}, bf16[64,256]{1,0:T(8,128)(2,1)S(1)}, u32[]{:S(2)}, u32[]{:S(2)}) collective-permute-start(bf16[64,256]{1,0:T(8,128)(2,1)S(1)} %get-tuple-element.33), channel_id=1, source_target_pairs={{0,2},{1,3},{2,0},{3,1},{4,6},{5,7},{6,4},{7,5},{8,10},{9,11},{10,... | collective-permute-start | bytes 98312 | tf_op jit(solution)/shard_map/ppermute | solution.py:217
  30.4 7.7 %collective-permute-start.17 = (bf16[64,256]{1,0:T(8,128)(2,1)S(1)}, bf16[64,256]{1,0:T(8,128)(2,1)S(1)}, u32[]{:S(2)}, u32[]{:S(2)}) collective-permute-start(bf16[64,256]{1,0:T(8,128)(2,1)S(1)} %get-tuple-element.34), channel_id=1, source_target_pairs={{0,4},{1,5},{2,6},{3,7},{4,0},{5,1},{6,2},{7,3},{8,12},{9,13},{10,... | collective-permute-start | bytes 98312 | tf_op jit(solution)/shard_map/ppermute | solution.py:217
  33.3 5.7 %collective-permute-start.18 = (bf16[64,256]{1,0:T(8,128)(2,1)S(1)}, bf16[64,256]{1,0:T(8,128)(2,1)S(1)}, u32[]{:S(2)}, u32[]{:S(2)}) collective-permute-start(bf16[64,256]{1,0:T(8,128)(2,1)S(1)} %get-tuple-element.35), channel_id=1, source_target_pairs={{0,6},{1,7},{2,4},{3,5},{4,2},{5,3},{6,0},{7,1},{8,14},{9,15},{10,... | collective-permute-start | bytes 98312 | tf_op jit(solution)/shard_map/ppermute | solution.py:217
  37.8 2.0 %collective-permute-start.14 = (f32[176,256]{1,0:T(8,128)S(1)}, f32[176,256]{1,0:T(8,128)S(1)}, u32[]{:S(2)}, u32[]{:S(2)}) collective-permute-start(f32[176,256]{1,0:T(8,128)S(1)} %shard_map.107.own_ref.total_ref), channel_id=1, source_target_pairs={{0,1},{1,0},{2,3},{3,2},{4,5},{5,4},{6,7},{7,6},{8,9},{9,8},{10,11... | collective-permute-start | bytes 540680 | tf_op jit(solution)/shard_map/ppermute | solution.py:217

commit v5 on v4

--- a/solution.py
+++ b/solution.py
@@ -50,9 +50,11 @@
     return jax.ShapeDtypeStruct(dims, dtype)
 
 
-def count_kernel(fanout, nbr_ref, labels_ref, weight_ref, at_ref, labels_out_ref, weight_out_ref):
-    labels_out_ref[...] = labels_ref[...]
-    weight_out_ref[...] = weight_ref[...]
+def count_kernel(fanout, nbr_ref, *refs):
+    passing = len(refs) // 2
+    at_ref = refs[passing]
+    for i in range(passing):
+        refs[passing + 1 + i][...] = refs[i][...]
     nodes = at_ref.shape[1]
     step = 32
 
@@ -192,24 +194,22 @@
     return loss, norm
 
 
-def second_out_kernel(classes, core_ref, own_ref, other_ref, out_ref, loss_ref):
+def first_sum_kernel(own_ref, *refs):
+    refs[-1][...] = tree_sum([own_ref[...]] + [r[...].astype(F32) for r in refs[:-1]])
+
+
+def out_kernel(classes, core_ref, own_ref, other_ref, first_ref, grad1_ref, grad2_ref, loss_ref):
     first = core_ref[0] == 0
     loss, norm = scalars(own_ref[...], classes)
     inverse = 1.0 / norm
     own = own_ref[:classes, :] * inverse
     other = other_ref[:classes, :] * inverse
-    out_ref[:, 0, :] = jnp.where(first, own, other)
-    out_ref[:, 1, :] = jnp.where(first, other, own)
+    grad2_ref[:, 0, :] = jnp.where(first, own, other)
+    grad2_ref[:, 1, :] = jnp.where(first, other, own)
     loss_ref[...] = loss * inverse
-
-
-def first_out_kernel(classes, total_ref, own_ref, *refs):
-    _, norm = scalars(total_ref[...], classes)
-    out_ref = refs[-1]
-    summed = tree_sum([own_ref[...]] + [r[...].astype(F32) for r in refs[:-1]]) * (1.0 / norm)
-    rows = out_ref.shape[1]
-    out_ref[0] = summed[:rows]
-    out_ref[1] = summed[rows:]
+    rows = grad1_ref.shape[1]
+    grad1_ref[0] = first_ref[:rows] * inverse
+    grad1_ref[1] = first_ref[rows:] * inverse
 
 
 def exchange(value, axis, step):
@@ -248,14 +248,11 @@
     mine_own = jnp.where(core[0] == 0, w1_self, w1_neigh)
     mine = [exchange(mine_own, "feat", s) for s in range(1, feat_count)]
     limit = 12 + 6 * nodes * nodes // (1024 * 1024)
-    at, labels, loss_weight = call(
+    passing = [labels.reshape(1, nodes), loss_weight.reshape(1, nodes), w2_self.T, w2_neigh.T]
+    at, labels, loss_weight, w2s, w2n = call(
         functools.partial(count_kernel, fanout),
-        [
-            shape((nodes, nodes), BF16),
-            shape((1, nodes), jnp.int32),
-            shape((1, nodes), F32),
-        ],
-        [neighbors.T, labels.reshape(1, nodes), loss_weight.reshape(1, nodes)],
+        [shape((nodes, nodes), BF16)] + [shape(p.shape, p.dtype) for p in passing],
+        [neighbors.T] + passing,
         flops=nodes * nodes * fanout,
     )
     mine_proj, *joined = call(
@@ -269,7 +266,6 @@
     rest = iter(joined)
     whole = [block[0] if len(block) == 1 else next(rest) for block in wide]
     partner = [exchange(block, "dp", 1) for block in mine]
-    w2s, w2n = w2_self.T, w2_neigh.T
     padded = (classes + 3 + 15) // 16 * 16
     send2, keep2, grad, hidden = call(
         functools.partial(forward_kernel, feat_count, fanout),
@@ -310,17 +306,11 @@
     far1 = [exchange(chunks[s - 1], "dp", 2 * s) for s in range(1, groups)]
     (total2,) = call(second_sum_kernel, [shape((padded, hid), F32)], [own2] + far2)
     other2 = exchange(total2, "dp", 1)
-    (grad_w1,) = call(
-        functools.partial(first_out_kernel, classes),
-        [shape((2, rows // dp_count, hid), F32)],
-        [total2, own1] + far1,
-        flops=300 * rows * nodes * hid,
-        final=True,
-    )
-    grad_w2, loss = call(
-        functools.partial(second_out_kernel, classes),
-        [shape((classes, 2, hid), F32), shape((1, 1), F32)],
-        [core, total2, other2],
+    (sum1,) = call(first_sum_kernel, [shape((chunk, hid), F32)], [own1] + far1, flops=300 * rows * nodes * hid)
+    grad_w1, grad_w2, loss = call(
+        functools.partial(out_kernel, classes),
+        [shape((2, rows // dp_count, hid), F32), shape((classes, 2, hid), F32), shape((1, 1), F32)],
+        [core, total2, other2, sum1],
         smem=(0,),
         final=True,
     )

time: 41 us -> 40 us (0.976)
  local copies, waits for them, and re-layouts: 1.15 us -> 0.06 us
  waiting for transfers between devices: 6.85 us -> 7.77 us
  Pallas kernels: 6.31 us -> 5.58 us
    unnamed x16, local copies, waits for them, and re-layouts: 1.13 us -> 0.04 us
    ppermute x19, waiting for transfers between devices: 6.85 us -> 7.77 us  [exchange(): return lax.ppermute(value, axis, [(i, i ^ step) for i in range(size)])]
    pallas_call x9, Pallas kernels: 6.31 us -> 5.58 us  [call(): pl.pallas_call(kernel, out_shape=outs if final else [pltpu.VMEM(o.shape,...]
  transfers between devices with their start and end apart: 19 -> 19, of which waited for: 6 -> 7; matrix products, arithmetic and copies ran while one was open for 2% -> 2% of each run, Pallas kernels for 9% -> 7%
where the time goes in v5:
time: 40 us; the launch traced here: 39.9 us
  starting transfers between devices  24.7 us (62%)
  waiting for transfers between devices  7.77 us (19%)
  Pallas kernels  5.58 us (14%)
  other arithmetic  0.92 us (2%)
  between operations  0.82 us (2%)
    ppermute x19, starting transfers between devices, exchange(): return lax.ppermute(value, axis, [(i, i ^ step) for i in range(size)])  24.7 us
    ppermute x19, waiting for transfers between devices, exchange(): return lax.ppermute(value, axis, [(i, i ^ step) for i in range(size)])  7.77 us
    pallas_call x9, Pallas kernels, call(): pl.pallas_call(kernel, out_shape=outs if final else [pltpu.VMEM(o.shape,...  5.58 us
    select_n x1, other arithmetic, on_device(): mine_own = jnp.where(core[0] == 0, w1_self, w1_neigh)  0.92 us
  transfers between devices with their start and end apart: 19, of which 7 were waited for; matrix products, arithmetic and copies ran while one was open for 2% of the time, Pallas kernels for 7%

profile of v5, /device:TPU:0, one launch (start us, length us, event | category | flops | bytes accessed | tf_op | source)
XLA Modules:
  0.0 39.9 jit_solution(10340406947141388118)
XLA Ops:
  0.6 3.0 %collective-permute-start.1 = (bf16[256,512]{1,0:T(8,128)(2,1)}, bf16[256,512]{1,0:T(8,128)(2,1)S(1)}, u32[]{:S(2)}, u32[]{:S(2)}) collective-permute-start(bf16[256,512]{1,0:T(8,128)(2,1)} %f_ref.1), channel_id=1, source_target_pairs={{0,16},{8,24},{16,0},{24,8},{1,17},{9,25},{17,1},{25,9},{2,18},{10... | collective-permute-start | bytes 786440 | tf_op jit(solution)/shard_map/ppermute | solution.py:217
  3.7 1.5 %collective-permute-start = (bf16[256,512]{1,0:T(8,128)(2,1)}, bf16[256,512]{1,0:T(8,128)(2,1)S(1)}, u32[]{:S(2)}, u32[]{:S(2)}) collective-permute-start(bf16[256,512]{1,0:T(8,128)(2,1)} %f_ref.1), channel_id=1, source_target_pairs={{0,8},{8,0},{16,24},{24,16},{1,9},{9,1},{17,25},{25,17},{2,10},{10... | collective-permute-start | bytes 786440 | tf_op jit(solution)/shard_map/ppermute | solution.py:217
  5.2 0.9 %broadcast_select_fusion = bf16[256,256]{1,0:T(8,128)(2,1)S(1)} fusion(bf16[256,256]{1,0:T(8,128)(2,1)} %refs_10_.1, bf16[256,256]{1,0:T(8,128)(2,1)} %refs_11_.1, pred[]{:T(512)S(6)} %eq.5), kind=kLoop, calls=%fused_computation | loop fusion | flops 65536 | bytes 393217 | tf_op jit(solution)/shard_map/jit(_where)/select_n | solution.py:248
  6.1 0.1 collective-permute-start.4
  6.2 1.9 %collective-permute-start.3 = (bf16[256,256]{1,0:T(8,128)(2,1)S(1)}, bf16[256,256]{1,0:T(8,128)(2,1)S(1)}, u32[]{:S(2)}, u32[]{:S(2)}) collective-permute-start(bf16[256,256]{1,0:T(8,128)(2,1)S(1)} %broadcast_select_fusion), channel_id=1, source_target_pairs={{0,16},{8,24},{16,0},{24,8},{1,17},{9,25},{17,1},{25,9},{2,18},{10... | collective-permute-start | bytes 393224 | tf_op jit(solution)/shard_map/ppermute | solution.py:217
  8.1 1.5 %collective-permute-start.2 = (bf16[256,256]{1,0:T(8,128)(2,1)S(1)}, bf16[256,256]{1,0:T(8,128)(2,1)S(1)}, u32[]{:S(2)}, u32[]{:S(2)}) collective-permute-start(bf16[256,256]{1,0:T(8,128)(2,1)S(1)} %broadcast_select_fusion), channel_id=1, source_target_pairs={{0,8},{8,0},{16,24},{24,16},{1,9},{9,1},{17,25},{25,17},{2,10},{10... | collective-permute-start | bytes 393224 | tf_op jit(solution)/shard_map/ppermute | solution.py:217
  9.6 2.1 %collective-permute-done.1.refs_5_.refs_2_ = bf16[256,512]{1,0:T(8,128)(2,1)S(1)} collective-permute-done((bf16[256,512]{1,0:T(8,128)(2,1)}, bf16[256,512]{1,0:T(8,128)(2,1)S(1)}, u32[]{:S(2)}, u32[]{:S(2)}) %collective-permute-start.1) | collective-permute-done | bytes 262176 | tf_op jit(solution)/shard_map/ppermute | solution.py:217
  11.7 0.0 copy-start.5
  11.7 0.0 copy-start.6
  11.7 0.0 copy-start.7
  11.7 0.0 copy-start.2
  11.8 0.0 copy-start.3
  11.8 0.0 copy-start.4
  11.8 2.8 %collective-permute-start.5 = (bf16[128,512]{1,0:T(8,128)(2,1)S(1)}, bf16[128,512]{1,0:T(8,128)(2,1)S(1)}, u32[]{:S(2)}, u32[]{:S(2)}) collective-permute-start(bf16[128,512]{1,0:T(8,128)(2,1)S(1)} %slice.8), channel_id=1, source_target_pairs={{0,8},{8,0},{16,24},{24,16},{1,9},{9,1},{17,25},{25,17},{2,10},{10... | collective-permute-start | bytes 393224 | tf_op jit(solution)/shard_map/ppermute | solution.py:217
  14.6 0.0 collective-permute-done.refs_4_.refs_1_
  14.6 0.0 copy-start.1
  14.6 0.0 copy-start
  14.6 1.6 %collective-permute-start.6 = (bf16[128,512]{1,0:T(8,128)(2,1)S(1)}, bf16[128,512]{1,0:T(8,128)(2,1)S(1)}, u32[]{:S(2)}, u32[]{:S(2)}) collective-permute-start(bf16[128,512]{1,0:T(8,128)(2,1)S(1)} %slice.9), channel_id=1, source_target_pairs={{0,16},{8,24},{16,0},{24,8},{1,17},{9,25},{17,1},{25,9},{2,18},{10... | collective-permute-start | bytes 393224 | tf_op jit(solution)/shard_map/ppermute | solution.py:217
  16.2 0.0 copy-done.5
  16.2 0.0 copy-done.6
  16.2 0.0 copy-done.2
  16.2 0.0 copy-done.3
  16.2 0.0 copy-done.4
  16.2 1.1 %shard_map.104 = (bf16[512,512]{1,0:T(8,128)(2,1)S(1)}, s32[1,512]{1,0:T(1,128)S(1)}, f32[1,512]{1,0:T(1,128)S(1)}, bf16[172,256]{1,0:T(8,128)(2,1)S(1)}, bf16[172,256]{1,0:T(8,128)(2,1)S(1)}) custom-call(s32[10,512]{1,0:T(8,128)S(1)} %bitcast.11, s32[1,512]{1,0:T(1,128)S(1)} %bitcast.12, f32[1,512]{1,0:T(1,128)S(1)} %bitcast.13, ...), custom_call_target="tpu_custom_call" | custom-call | flops 2621440 | bytes 905216 | tf_op jit(solution)/shard_map/pallas_call | solution.py:38
  17.3 0.0 collective-permute-done.4.refs_2_
  17.3 0.1 collective-permute-start.9
  17.4 0.0 collective-permute-done.3.refs_1_
  17.4 0.5 %collective-permute-start.8 = (bf16[256,256]{1,0:T(8,128)(2,1)S(1)}, bf16[256,256]{1,0:T(8,128)(2,1)S(1)}, u32[]{:S(2)}, u32[]{:S(2)}) collective-permute-start(bf16[256,256]{1,0:T(8,128)(2,1)S(1)} %collective-permute-done.3.refs_1_), channel_id=1, source_target_pairs={{0,1},{1,0},{2,3},{3,2},{4,5},{5,4},{6,7},{7,6},{8,9},{9,8},{10,11... | collective-permute-start | bytes 393224 | tf_op jit(solution)/shard_map/ppermute | solution.py:217
  17.9 0.7 %collective-permute-done.2.refs_0_ = bf16[256,256]{1,0:T(8,128)(2,1)S(1)} collective-permute-done((bf16[256,256]{1,0:T(8,128)(2,1)S(1)}, bf16[256,256]{1,0:T(8,128)(2,1)S(1)}, u32[]{:S(2)}, u32[]{:S(2)}) %collective-permute-start.2) | collective-permute-done | bytes 131104 | tf_op jit(solution)/shard_map/ppermute | solution.py:217
  18.7 0.0 collective-permute-start.7
  18.7 1.4 %collective-permute-done.5.refs_6_ = bf16[128,512]{1,0:T(8,128)(2,1)S(1)} collective-permute-done((bf16[128,512]{1,0:T(8,128)(2,1)S(1)}, bf16[128,512]{1,0:T(8,128)(2,1)S(1)}, u32[]{:S(2)}, u32[]{:S(2)}) %collective-permute-start.5) | collective-permute-done | bytes 131104 | tf_op jit(solution)/shard_map/ppermute | solution.py:217
  20.1 0.0 collective-permute-done.6.refs_7_
  20.1 0.0 copy-done.7
  20.1 0.0 copy-done.1
  20.1 0.0 copy-done
  20.1 0.5 %shard_map.103 = (f32[256,512]{1,0:T(8,128)S(1)}, bf16[256,512]{1,0:T(8,128)(2,1)S(1)}) custom-call(s32[1]{0:T(128)} %bitcast.core_ref.refs_4_, bf16[256,256]{1,0:T(8,128)(2,1)S(1)} %copy-done, bf16[256,256]{1,0:T(8,128)(2,1)S(1)} %copy-done.1, bf16[256,256]{1,0:T(8,128)(2,1)S(1)} %collective-permute-done.2.refs_0_, ...), custom_call_target="tpu_custom_call" | custom-call | flops 4026531840 | bytes 2490372 | tf_op jit(solution)/shard_map/pallas_call | solution.py:38
  20.6 0.0 collective-permute-done.9.refs_15_
  20.6 0.0 collective-permute-done.8.refs_14_
  20.6 0.0 collective-permute-done.7.refs_13_
  20.6 1.7 %shard_map.105 = (f32[176,256]{1,0:T(8,128)S(1)}, f32[176,256]{1,0:T(8,128)S(1)}, bf16[172,512]{1,0:T(8,128)(2,1)S(1)}, bf16[256,512]{1,0:T(8,128)(2,1)S(1)}) custom-call(bf16[256,512]{1,0:T(8,128)(2,1)S(1)} %copy-done.7, bf16[256,512]{1,0:T(8,128)(2,1)S(1)} %collective-permute-done.refs_4_.refs_1_, ...), custom_call_target="tpu_custom_call" | custom-call | flops 805306368 | bytes 3731460 | tf_op jit(solution)/shard_map/pallas_call | solution.py:38
  22.3 0.1 collective-permute-start.10
  22.4 1.1 %shard_map.108 = (f32[4,64,256]{2,1,0:T(8,128)S(1)}, f32[4,64,256]{2,1,0:T(8,128)S(1)}) custom-call(s32[1]{0:T(128)} %bitcast.core_ref.refs_4_, bf16[172,512]{1,0:T(8,128)(2,1)S(1)} %get-tuple-element.32.g_ref, bf16[256,512]{1,0:T(8,128)(2,1)S(1)} %get-tuple-element.33.hidden_ref, bf16[512,512]{1,0:T(8,128)(2,1)S(1)} %get-tuple-element.26.refs_7_.at_ref, ...), custom_call_target="tpu_custom_call" | custom-call | flops 402653184 | bytes 1925124 | tf_op jit(solution)/shard_map/pallas_call | solution.py:38
  23.5 0.6 %collective-permute-start.15 = (f32[4,64,256]{2,1,0:T(8,128)S(1)}, f32[4,64,256]{2,1,0:T(8,128)S(1)}, u32[]{:S(2)}, u32[]{:S(2)}) collective-permute-start(f32[4,64,256]{2,1,0:T(8,128)S(1)} %get-tuple-element.35), channel_id=1, source_target_pairs={{0,1},{1,0},{2,3},{3,2},{4,5},{5,4},{6,7},{7,6},{8,9},{9,8},{10,11... | collective-permute-start | bytes 786440 | tf_op jit(solution)/shard_map/ppermute | solution.py:217
  24.1 0.0 collective-permute-done.10.recv_ref
  24.1 3.7 %collective-permute-start.13 = (bf16[176,256]{1,0:T(8,128)(2,1)S(1)}, bf16[176,256]{1,0:T(8,128)(2,1)S(1)}, u32[]{:S(2)}, u32[]{:S(2)}) collective-permute-start(bf16[176,256]{1,0:T(8,128)(2,1)S(1)} %shard_map.106.refs_0_), channel_id=1, source_target_pairs={{0,6},{1,7},{2,4},{3,5},{4,2},{5,3},{6,0},{7,1},{8,14},{9,15},{10,... | collective-permute-start | bytes 270344 | tf_op jit(solution)/shard_map/ppermute | solution.py:217
  27.8 0.0 collective-permute-start.12
  27.8 0.8 %collective-permute-start.11 = (bf16[176,256]{1,0:T(8,128)(2,1)S(1)}, bf16[176,256]{1,0:T(8,128)(2,1)S(1)}, u32[]{:S(2)}, u32[]{:S(2)}) collective-permute-start(bf16[176,256]{1,0:T(8,128)(2,1)S(1)} %shard_map.106.refs_0_), channel_id=1, source_target_pairs={{0,2},{1,3},{2,0},{3,1},{4,6},{5,7},{6,4},{7,5},{8,10},{9,11},{10,... | collective-permute-start | bytes 270344 | tf_op jit(solution)/shard_map/ppermute | solution.py:217
  28.6 0.0 collective-permute-done.15.recv_ref
  28.6 1.3 %collective-permute-start.16 = (bf16[64,256]{1,0:T(8,128)(2,1)S(1)}, bf16[64,256]{1,0:T(8,128)(2,1)S(1)}, u32[]{:S(2)}, u32[]{:S(2)}) collective-permute-start(bf16[64,256]{1,0:T(8,128)(2,1)S(1)} %get-tuple-element.37), channel_id=1, source_target_pairs={{0,2},{1,3},{2,0},{3,1},{4,6},{5,7},{6,4},{7,5},{8,10},{9,11},{10,... | collective-permute-start | bytes 98312 | tf_op jit(solution)/shard_map/ppermute | solution.py:217
  29.9 2.9 %collective-permute-start.17 = (bf16[64,256]{1,0:T(8,128)(2,1)S(1)}, bf16[64,256]{1,0:T(8,128)(2,1)S(1)}, u32[]{:S(2)}, u32[]{:S(2)}) collective-permute-start(bf16[64,256]{1,0:T(8,128)(2,1)S(1)} %get-tuple-element.38), channel_id=1, source_target_pairs={{0,4},{1,5},{2,6},{3,7},{4,0},{5,1},{6,2},{7,3},{8,12},{9,13},{10,... | collective-permute-start | bytes 98312 | tf_op jit(solution)/shard_map/ppermute | solution.py:217
  32.8 0.0 collective-permute-done.13.refs_3_
  32.8 2.3 %collective-permute-start.18 = (bf16[64,256]{1,0:T(8,128)(2,1)S(1)}, bf16[64,256]{1,0:T(8,128)(2,1)S(1)}, u32[]{:S(2)}, u32[]{:S(2)}) collective-permute-start(bf16[64,256]{1,0:T(8,128)(2,1)S(1)} %get-tuple-element.39), channel_id=1, source_target_pairs={{0,6},{1,7},{2,4},{3,5},{4,2},{5,3},{6,0},{7,1},{8,14},{9,15},{10,... | collective-permute-start | bytes 98312 | tf_op jit(solution)/shard_map/ppermute | solution.py:217
  35.2 2.1 %collective-permute-done.12.refs_2_ = bf16[176,256]{1,0:T(8,128)(2,1)S(1)} collective-permute-done((bf16[176,256]{1,0:T(8,128)(2,1)S(1)}, bf16[176,256]{1,0:T(8,128)(2,1)S(1)}, u32[]{:S(2)}, u32[]{:S(2)}) %collective-permute-start.12) | collective-permute-done | bytes 90144 | tf_op jit(solution)/shard_map/ppermute | solution.py:217
  37.3 0.0 collective-permute-done.11.refs_1_
  37.3 0.1 collective-permute-start.14
  37.4 0.0 collective-permute-done.16.refs_0_
  37.4 0.2 collective-permute-done.17.refs_1_
  37.6 0.9 %collective-permute-done.18.refs_2_ = bf16[64,256]{1,0:T(8,128)(2,1)S(1)} collective-permute-done((bf16[64,256]{1,0:T(8,128)(2,1)S(1)}, bf16[64,256]{1,0:T(8,128)(2,1)S(1)}, u32[]{:S(2)}, u32[]{:S(2)}) %collective-permute-start.18) | collective-permute-done | bytes 32800 | tf_op jit(solution)/shard_map/ppermute | solution.py:217
  38.6 0.3 collective-permute-done.14.other_ref
  38.8 1.0 %shard_map.111 = (f32[2,32,256]{2,1,0:T(8,128)}, f32[172,2,256]{2,1,0:T(2,128)}, f32[1,1]{1,0:T(1,128)}) custom-call(s32[1]{0:T(128)} %bitcast.core_ref.refs_4_, f32[176,256]{1,0:T(8,128)S(1)} %shard_map.107.own_ref, f32[176,256]{1,0:T(8,128)S(1)} %collective-permute-done.14.other_ref, f32[64,256]{1,0:T(8,128)S(1)} %shard_map.110.first_ref), custom_call_target="tpu_custom_call" | custom-call | bytes 843784 | tf_op jit(solution)/shard_map/pallas_call | solution.py:38
  (6 shorter events, 0.1 us)
Async XLA Ops:
  0.6 11.1 %collective-permute-start.1 = (bf16[256,512]{1,0:T(8,128)(2,1)}, bf16[256,512]{1,0:T(8,128)(2,1)S(1)}, u32[]{:S(2)}, u32[]{:S(2)}) collective-permute-start(bf16[256,512]{1,0:T(8,128)(2,1)} %f_ref.1), channel_id=1, source_target_pairs={{0,16},{8,24},{16,0},{24,8},{1,17},{9,25},{17,1},{25,9},{2,18},{10... | collective-permute-start | bytes 786440 | tf_op jit(solution)/shard_map/ppermute | solution.py:217
  3.7 10.9 %collective-permute-start = (bf16[256,512]{1,0:T(8,128)(2,1)}, bf16[256,512]{1,0:T(8,128)(2,1)S(1)}, u32[]{:S(2)}, u32[]{:S(2)}) collective-permute-start(bf16[256,512]{1,0:T(8,128)(2,1)} %f_ref.1), channel_id=1, source_target_pairs={{0,8},{8,0},{16,24},{24,16},{1,9},{9,1},{17,25},{25,17},{2,10},{10... | collective-permute-start | bytes 786440 | tf_op jit(solution)/shard_map/ppermute | solution.py:217
  6.1 11.2 %collective-permute-start.4 = (bf16[256,256]{1,0:T(8,128)(2,1)S(1)}, bf16[256,256]{1,0:T(8,128)(2,1)S(1)}, u32[]{:S(2)}, u32[]{:S(2)}) collective-permute-start(bf16[256,256]{1,0:T(8,128)(2,1)S(1)} %broadcast_select_fusion), channel_id=1, source_target_pairs={{0,24},{8,16},{16,8},{24,0},{1,25},{9,17},{17,9},{25,1},{2,26},{10... | collective-permute-start | bytes 393224 | tf_op jit(solution)/shard_map/ppermute | solution.py:217
  6.2 11.2 %collective-permute-start.3 = (bf16[256,256]{1,0:T(8,128)(2,1)S(1)}, bf16[256,256]{1,0:T(8,128)(2,1)S(1)}, u32[]{:S(2)}, u32[]{:S(2)}) collective-permute-start(bf16[256,256]{1,0:T(8,128)(2,1)S(1)} %broadcast_select_fusion), channel_id=1, source_target_pairs={{0,16},{8,24},{16,0},{24,8},{1,17},{9,25},{17,1},{25,9},{2,18},{10... | collective-permute-start | bytes 393224 | tf_op jit(solution)/shard_map/ppermute | solution.py:217
  8.1 10.5 %collective-permute-start.2 = (bf16[256,256]{1,0:T(8,128)(2,1)S(1)}, bf16[256,256]{1,0:T(8,128)(2,1)S(1)}, u32[]{:S(2)}, u32[]{:S(2)}) collective-permute-start(bf16[256,256]{1,0:T(8,128)(2,1)S(1)} %broadcast_select_fusion), channel_id=1, source_target_pairs={{0,8},{8,0},{16,24},{24,16},{1,9},{9,1},{17,25},{25,17},{2,10},{10... | collective-permute-start | bytes 393224 | tf_op jit(solution)/shard_map/ppermute | solution.py:217
  11.7 4.5 %copy-start.5 = (s32[512]{0:T(512)S(1)}, s32[512]{0:T(512)}, u32[]{:S(2)}) copy-start(s32[512]{0:T(512)} %param.10) | copy-start | bytes 6148
  11.7 4.5 %copy-start.6 = (f32[512]{0:T(512)S(1)}, f32[512]{0:T(512)}, u32[]{:S(2)}) copy-start(f32[512]{0:T(512)} %param.11) | copy-start | bytes 6148
  11.7 8.3 %copy-start.7 = (bf16[256,512]{1,0:T(8,128)(2,1)S(1)}, bf16[256,512]{1,0:T(8,128)(2,1)}, u32[]{:S(2)}) copy-start(bf16[256,512]{1,0:T(8,128)(2,1)} %f_ref.1) | copy-start | bytes 786436
  11.7 4.4 %copy-start.2 = (bf16[256,172]{0,1:T(8,128)(2,1)S(1)}, bf16[256,172]{0,1:T(8,128)(2,1)}, u32[]{:S(2)}) copy-start(bf16[256,172]{0,1:T(8,128)(2,1)} %param.14) | copy-start | bytes 264196
  11.8 4.4 %copy-start.3 = (bf16[256,172]{0,1:T(8,128)(2,1)S(1)}, bf16[256,172]{0,1:T(8,128)(2,1)}, u32[]{:S(2)}) copy-start(bf16[256,172]{0,1:T(8,128)(2,1)} %param.15) | copy-start | bytes 264196
  11.8 4.4 %copy-start.4 = (s32[512,10]{0,1:T(8,128)S(1)}, s32[512,10]{0,1:T(8,128)}, u32[]{:S(2)}) copy-start(s32[512,10]{0,1:T(8,128)} %param.9) | copy-start | bytes 61444
  11.8 8.3 %collective-permute-start.5 = (bf16[128,512]{1,0:T(8,128)(2,1)S(1)}, bf16[128,512]{1,0:T(8,128)(2,1)S(1)}, u32[]{:S(2)}, u32[]{:S(2)}) collective-permute-start(bf16[128,512]{1,0:T(8,128)(2,1)S(1)} %slice.8), channel_id=1, source_target_pairs={{0,8},{8,0},{16,24},{24,16},{1,9},{9,1},{17,25},{25,17},{2,10},{10... | collective-permute-start | bytes 393224 | tf_op jit(solution)/shard_map/ppermute | solution.py:217
  14.6 5.5 %copy-start.1 = (bf16[256,256]{1,0:T(8,128)(2,1)S(1)}, bf16[256,256]{1,0:T(8,128)(2,1)}, u32[]{:S(2)}) copy-start(bf16[256,256]{1,0:T(8,128)(2,1)} %refs_11_.1) | copy-start | bytes 393220
  14.6 5.5 %copy-start = (bf16[256,256]{1,0:T(8,128)(2,1)S(1)}, bf16[256,256]{1,0:T(8,128)(2,1)}, u32[]{:S(2)}) copy-start(bf16[256,256]{1,0:T(8,128)(2,1)} %refs_10_.1) | copy-start | bytes 393220
  14.6 5.5 %collective-permute-start.6 = (bf16[128,512]{1,0:T(8,128)(2,1)S(1)}, bf16[128,512]{1,0:T(8,128)(2,1)S(1)}, u32[]{:S(2)}, u32[]{:S(2)}) collective-permute-start(bf16[128,512]{1,0:T(8,128)(2,1)S(1)} %slice.9), channel_id=1, source_target_pairs={{0,16},{8,24},{16,0},{24,8},{1,17},{9,25},{17,1},{25,9},{2,18},{10... | collective-permute-start | bytes 393224 | tf_op jit(solution)/shard_map/ppermute | solution.py:217
  17.3 3.2 %collective-permute-start.9 = (bf16[256,256]{1,0:T(8,128)(2,1)S(1)}, bf16[256,256]{1,0:T(8,128)(2,1)S(1)}, u32[]{:S(2)}, u32[]{:S(2)}) collective-permute-start(bf16[256,256]{1,0:T(8,128)(2,1)S(1)} %collective-permute-done.4.refs_2_), channel_id=1, source_target_pairs={{0,1},{1,0},{2,3},{3,2},{4,5},{5,4},{6,7},{7,6},{8,9},{9,8},{10,11... | collective-permute-start | bytes 393224 | tf_op jit(solution)/shard_map/ppermute | solution.py:217
  17.4 3.1 %collective-permute-start.8 = (bf16[256,256]{1,0:T(8,128)(2,1)S(1)}, bf16[256,256]{1,0:T(8,128)(2,1)S(1)}, u32[]{:S(2)}, u32[]{:S(2)}) collective-permute-start(bf16[256,256]{1,0:T(8,128)(2,1)S(1)} %collective-permute-done.3.refs_1_), channel_id=1, source_target_pairs={{0,1},{1,0},{2,3},{3,2},{4,5},{5,4},{6,7},{7,6},{8,9},{9,8},{10,11... | collective-permute-start | bytes 393224 | tf_op jit(solution)/shard_map/ppermute | solution.py:217
  18.7 1.9 %collective-permute-start.7 = (bf16[256,256]{1,0:T(8,128)(2,1)S(1)}, bf16[256,256]{1,0:T(8,128)(2,1)S(1)}, u32[]{:S(2)}, u32[]{:S(2)}) collective-permute-start(bf16[256,256]{1,0:T(8,128)(2,1)S(1)} %collective-permute-done.2.refs_0_), channel_id=1, source_target_pairs={{0,1},{1,0},{2,3},{3,2},{4,5},{5,4},{6,7},{7,6},{8,9},{9,8},{10,11... | collective-permute-start | bytes 393224 | tf_op jit(solution)/shard_map/ppermute | solution.py:217
  22.3 1.8 %collective-permute-start.10 = (f32[176,256]{1,0:T(8,128)S(1)}, f32[176,256]{1,0:T(8,128)S(1)}, u32[]{:S(2)}, u32[]{:S(2)}) collective-permute-start(f32[176,256]{1,0:T(8,128)S(1)} %get-tuple-element.31), channel_id=1, source_target_pairs={{0,1},{1,0},{2,3},{3,2},{4,5},{5,4},{6,7},{7,6},{8,9},{9,8},{10,11... | collective-permute-start | bytes 540680 | tf_op jit(solution)/shard_map/ppermute | solution.py:217
  23.5 5.1 %collective-permute-start.15 = (f32[4,64,256]{2,1,0:T(8,128)S(1)}, f32[4,64,256]{2,1,0:T(8,128)S(1)}, u32[]{:S(2)}, u32[]{:S(2)}) collective-permute-start(f32[4,64,256]{2,1,0:T(8,128)S(1)} %get-tuple-element.35), channel_id=1, source_target_pairs={{0,1},{1,0},{2,3},{3,2},{4,5},{5,4},{6,7},{7,6},{8,9},{9,8},{10,11... | collective-permute-start | bytes 786440 | tf_op jit(solution)/shard_map/ppermute | solution.py:217
  24.1 8.7 %collective-permute-start.13 = (bf16[176,256]{1,0:T(8,128)(2,1)S(1)}, bf16[176,256]{1,0:T(8,128)(2,1)S(1)}, u32[]{:S(2)}, u32[]{:S(2)}) collective-permute-start(bf16[176,256]{1,0:T(8,128)(2,1)S(1)} %shard_map.106.refs_0_), channel_id=1, source_target_pairs={{0,6},{1,7},{2,4},{3,5},{4,2},{5,3},{6,0},{7,1},{8,14},{9,15},{10,... | collective-permute-start | bytes 270344 | tf_op jit(solution)/shard_map/ppermute | solution.py:217
  27.8 9.5 %collective-permute-start.12 = (bf16[176,256]{1,0:T(8,128)(2,1)S(1)}, bf16[176,256]{1,0:T(8,128)(2,1)S(1)}, u32[]{:S(2)}, u32[]{:S(2)}) collective-permute-start(bf16[176,256]{1,0:T(8,128)(2,1)S(1)} %shard_map.106.refs_0_), channel_id=1, source_target_pairs={{0,4},{1,5},{2,6},{3,7},{4,0},{5,1},{6,2},{7,3},{8,12},{9,13},{10,... | collective-permute-start | bytes 270344 | tf_op jit(solution)/shard_map/ppermute | solution.py:217
  27.8 9.5 %collective-permute-start.11 = (bf16[176,256]{1,0:T(8,128)(2,1)S(1)}, bf16[176,256]{1,0:T(8,128)(2,1)S(1)}, u32[]{:S(2)}, u32[]{:S(2)}) collective-permute-start(bf16[176,256]{1,0:T(8,128)(2,1)S(1)} %shard_map.106.refs_0_), channel_id=1, source_target_pairs={{0,2},{1,3},{2,0},{3,1},{4,6},{5,7},{6,4},{7,5},{8,10},{9,11},{10,... | collective-permute-start | bytes 270344 | tf_op jit(solution)/shard_map/ppermute | solution.py:217
  28.6 8.8 %collective-permute-start.16 = (bf16[64,256]{1,0:T(8,128)(2,1)S(1)}, bf16[64,256]{1,0:T(8,128)(2,1)S(1)}, u32[]{:S(2)}, u32[]{:S(2)}) collective-permute-start(bf16[64,256]{1,0:T(8,128)(2,1)S(1)} %get-tuple-element.37), channel_id=1, source_target_pairs={{0,2},{1,3},{2,0},{3,1},{4,6},{5,7},{6,4},{7,5},{8,10},{9,11},{10,... | collective-permute-start | bytes 98312 | tf_op jit(solution)/shard_map/ppermute | solution.py:217
  29.9 7.7 %collective-permute-start.17 = (bf16[64,256]{1,0:T(8,128)(2,1)S(1)}, bf16[64,256]{1,0:T(8,128)(2,1)S(1)}, u32[]{:S(2)}, u32[]{:S(2)}) collective-permute-start(bf16[64,256]{1,0:T(8,128)(2,1)S(1)} %get-tuple-element.38), channel_id=1, source_target_pairs={{0,4},{1,5},{2,6},{3,7},{4,0},{5,1},{6,2},{7,3},{8,12},{9,13},{10,... | collective-permute-start | bytes 98312 | tf_op jit(solution)/shard_map/ppermute | solution.py:217
  32.8 5.7 %collective-permute-start.18 = (bf16[64,256]{1,0:T(8,128)(2,1)S(1)}, bf16[64,256]{1,0:T(8,128)(2,1)S(1)}, u32[]{:S(2)}, u32[]{:S(2)}) collective-permute-start(bf16[64,256]{1,0:T(8,128)(2,1)S(1)} %get-tuple-element.39), channel_id=1, source_target_pairs={{0,6},{1,7},{2,4},{3,5},{4,2},{5,3},{6,0},{7,1},{8,14},{9,15},{10,... | collective-permute-start | bytes 98312 | tf_op jit(solution)/shard_map/ppermute | solution.py:217
  37.3 1.5 %collective-permute-start.14 = (f32[176,256]{1,0:T(8,128)S(1)}, f32[176,256]{1,0:T(8,128)S(1)}, u32[]{:S(2)}, u32[]{:S(2)}) collective-permute-start(f32[176,256]{1,0:T(8,128)S(1)} %shard_map.107.own_ref), channel_id=1, source_target_pairs={{0,1},{1,0},{2,3},{3,2},{4,5},{5,4},{6,7},{7,6},{8,9},{9,8},{10,11... | collective-permute-start | bytes 540680 | tf_op jit(solution)/shard_map/ppermute | solution.py:217

commit v6 on v5

--- a/solution.py
+++ b/solution.py
@@ -69,43 +69,64 @@
     lax.fori_loop(0, nodes // step, body, 0)
 
 
-def project(own, others_refs, f_refs):
-    products = [dot_tn(own, f_refs[0][...])]
-    for s in range(1, len(f_refs)):
-        products.append(dot_tn(others_refs[s - 1][...], f_refs[s][...]))
-    return tree_sum(products)
-
-
-def mine_kernel(parts, core_ref, ws_ref, wn_ref, *refs):
-    mine_refs, refs = refs[: len(parts) - 1], refs[len(parts) - 1 :]
-    out_ref, joined_refs = refs[sum(parts)], refs[sum(parts) + 1 :]
-    own = jnp.where(core_ref[0] == 0, ws_ref[...], wn_ref[...])
-    blocks, at, done = [], 0, 0
-    for count in parts:
-        block = refs[at]
-        if count > 1:
-            block, start = joined_refs[done], 0
-            for ref in refs[at : at + count]:
-                block[start : start + ref.shape[0]] = ref[...]
-                start += ref.shape[0]
-            done += 1
-        blocks.append(block)
-        at += count
-    out_ref[...] = project(own, mine_refs, blocks)
+def early_nodes(early, first, last):
+    if all(s in early for s in range(first, last)):
+        return [(first, last)]
+    if last - first == 1:
+        return []
+    middle = (first + last) // 2
+    return early_nodes(early, first, middle) + early_nodes(early, middle, last)
+
+
+def tree_product(first, last, known, leaf):
+    if (first, last) in known:
+        return known[(first, last)][...]
+    if last - first == 1:
+        return leaf(first)
+    middle = (first + last) // 2
+    return tree_product(first, middle, known, leaf) + tree_product(middle, last, known, leaf)
+
+
+def early_kernel(nodes_mine, early, core_ref, ws_ref, wn_ref, *refs):
+    f_refs = dict(zip(early, refs))
+    w_refs = dict(zip(early[1:], refs[len(early) :]))
+    outs = refs[2 * len(early) - 1 :]
+    first = core_ref[0] == 0
+    own = jnp.where(first, ws_ref[...], wn_ref[...])
+    other = jnp.where(first, wn_ref[...], ws_ref[...])
+    for (begin, end), out_ref in zip(nodes_mine, outs):
+        leaf = lambda s: dot_tn(own if s == 0 else w_refs[s][...], f_refs[s][...])
+        out_ref[...] = tree_product(begin, end, {}, leaf)
+    outs[-1][...] = dot_tn(other, f_refs[0][...])
+
+
+def mine_kernel(nodes_mine, late, feat_count, *refs):
+    known = dict(zip(nodes_mine, refs))
+    refs = refs[len(nodes_mine) :]
+    w_refs = dict(zip(late, refs))
+    halves = refs[len(late) : 3 * len(late)]
+    out_ref, joined = refs[3 * len(late)], refs[3 * len(late) + 1 :]
+    for i, block in enumerate(joined):
+        low, high = halves[2 * i : 2 * i + 2]
+        block[: low.shape[0]] = low[...]
+        block[low.shape[0] :] = high[...]
+    f_refs = dict(zip(late, joined))
+    out_ref[...] = tree_product(0, feat_count, known, lambda s: dot_tn(w_refs[s][...], f_refs[s][...]))
 
 
 def forward_kernel(feat_count, fanout, *refs):
-    f_refs, refs = refs[:feat_count], refs[feat_count:]
-    core_ref, labels_ref, weight_ref, at_ref, w2s_ref, w2n_ref, ws_ref, wn_ref, mine_ref = refs[:9]
-    partner_refs = refs[9 : 8 + feat_count]
-    send_ref, keep_ref, g_ref, hidden_ref, proj, pair = refs[8 + feat_count :]
+    f_refs, refs = refs[: feat_count - 1], refs[feat_count - 1 :]
+    core_ref, labels_ref, weight_ref, at_ref, w2s_ref, w2n_ref, mine_ref, other_ref = refs[:8]
+    partner_refs = refs[8 : 7 + feat_count]
+    send_ref, keep_ref, g_ref, hidden_ref, proj, pair = refs[7 + feat_count :]
     core = core_ref[0]
     classes = w2s_ref.shape[0]
     nodes = at_ref.shape[1]
     scale = 1.0 / fanout
-    own = jnp.where(core == 0, wn_ref[...], ws_ref[...])
     proj[core] = mine_ref[...]
-    proj[1 - core] = project(own, partner_refs, f_refs)
+    proj[1 - core] = tree_product(
+        0, feat_count, {(0, 1): other_ref}, lambda s: dot_tn(partner_refs[s - 1][...], f_refs[s - 1][...])
+    )
     at = at_ref[...]
     pre = proj[0] + dot_nn(proj[1].astype(BF16), at) * scale
     hidden = jnp.maximum(pre, 0.0).astype(BF16)
@@ -113,15 +134,16 @@
     second = (dot_nn(hidden, at) * scale).astype(BF16)
     logits = dot_nn(w2s_ref[...], hidden) + dot_nn(w2n_ref[...], second)
     shifted = logits - jnp.max(logits, axis=0, keepdims=True)
-    logprob = shifted - jnp.log(jnp.sum(jnp.exp(shifted), axis=0, keepdims=True))
+    powers = jnp.exp(shifted)
+    total = jnp.sum(powers, axis=0, keepdims=True)
     hot = lax.broadcasted_iota(jnp.int32, (classes, nodes), 0) == labels_ref[...]
-    picked = jnp.sum(jnp.where(hot, logprob, 0.0), axis=0, keepdims=True)
+    picked = jnp.sum(jnp.where(hot, shifted, 0.0), axis=0, keepdims=True) - jnp.log(total)
     chance = jnp.exp(picked)
     rest = 1.0 - chance
     weight = weight_ref[...]
     terms = -rest * rest * picked
     slope = weight * (2.0 * rest * chance * picked - rest * rest)
-    grad = (slope * (jnp.where(hot, 1.0, 0.0) - jnp.exp(logprob))).astype(BF16)
+    grad = (jnp.where(hot, slope, 0.0) - (slope / total) * powers).astype(BF16)
     g_ref[...] = grad
     pair[0] = hidden
     pair[1] = second
@@ -204,8 +226,10 @@
     inverse = 1.0 / norm
     own = own_ref[:classes, :] * inverse
     other = other_ref[:classes, :] * inverse
-    grad2_ref[:, 0, :] = jnp.where(first, own, other)
-    grad2_ref[:, 1, :] = jnp.where(first, other, own)
+    for slot, half in enumerate((jnp.where(first, own, other), jnp.where(first, other, own))):
+        lanes = half.shape[1] // 128
+        for j in range(lanes):
+            grad2_ref[pl.ds(2 * j + slot, classes, stride=2 * lanes), :] = half[:, 128 * j : 128 * (j + 1)]
     loss_ref[...] = loss * inverse
     rows = grad1_ref.shape[1]
     grad1_ref[0] = first_ref[:rows] * inverse
@@ -244,7 +268,9 @@
     z = (place // 2).reshape(1)
 
     wide = gather_parts(features, feat_count)
-    parts = tuple(len(block) for block in wide)
+    early = [s for s in range(feat_count) if len(wide[s]) == 1]
+    late = [s for s in range(feat_count) if len(wide[s]) > 1]
+    nodes_mine = early_nodes(early, 0, feat_count)
     mine_own = jnp.where(core[0] == 0, w1_self, w1_neigh)
     mine = [exchange(mine_own, "feat", s) for s in range(1, feat_count)]
     limit = 12 + 6 * nodes * nodes // (1024 * 1024)
@@ -255,12 +281,19 @@
         [neighbors.T] + passing,
         flops=nodes * nodes * fanout,
     )
+    *known, other_proj = call(
+        functools.partial(early_kernel, nodes_mine, early),
+        [shape((hid, nodes), F32)] * (len(nodes_mine) + 1),
+        [core, w1_self, w1_neigh] + [wide[s][0] for s in early] + [mine[s - 1] for s in early[1:]],
+        flops=2 * nodes * hid * rows * (len(early) + 1),
+        smem=(0,),
+        limit=limit,
+    )
     mine_proj, *joined = call(
-        functools.partial(mine_kernel, parts),
-        [shape((hid, nodes), F32)] + [shape((rows, nodes), BF16)] * sum(count > 1 for count in parts),
-        [core, w1_self, w1_neigh] + mine + [part for block in wide for part in block],
+        functools.partial(mine_kernel, nodes_mine, late, feat_count),
+        [shape((hid, nodes), F32)] + [shape((rows, nodes), BF16)] * len(late),
+        known + [mine[s - 1] for s in late] + [part for s in late for part in wide[s]],
         flops=30 * nodes * hid * rows * feat_count,
-        smem=(0,),
         limit=limit,
     )
     rest = iter(joined)
@@ -275,13 +308,13 @@
             shape((classes, nodes), BF16),
             shape((hid, nodes), BF16),
         ],
-        whole + [core, labels, loss_weight, at, w2s, w2n, w1_self, w1_neigh, mine_proj] + partner,
+        whole[1:] + [core, labels, loss_weight, at, w2s, w2n, mine_proj, other_proj] + partner,
         scratch=[
             pltpu.VMEM((2, hid, nodes), F32),
             pltpu.VMEM((2, hid, nodes), BF16),
         ],
         flops=2 * nodes * hid * 2 * (rows * feat_count + nodes),
-        smem=(feat_count,),
+        smem=(feat_count - 1,),
         limit=limit,
     )
     recv2 = exchange(send2, "dp", 1)
@@ -304,17 +337,18 @@
         smem=(0,),
     )
     far1 = [exchange(chunks[s - 1], "dp", 2 * s) for s in range(1, groups)]
-    (total2,) = call(second_sum_kernel, [shape((padded, hid), F32)], [own2] + far2)
+    (total2,) = call(second_sum_kernel, [shape((padded, hid), F32)], far2[::-1] + [own2])
     other2 = exchange(total2, "dp", 1)
     (sum1,) = call(first_sum_kernel, [shape((chunk, hid), F32)], [own1] + far1, flops=300 * rows * nodes * hid)
     grad_w1, grad_w2, loss = call(
         functools.partial(out_kernel, classes),
-        [shape((2, rows // dp_count, hid), F32), shape((classes, 2, hid), F32), shape((1, 1), F32)],
+        [shape((2, rows // dp_count, hid), F32), shape((classes * 2 * (hid // 128), 128), F32), shape((1, 1), F32)],
         [core, total2, other2, sum1],
         smem=(0,),
         final=True,
     )
-    return loss[0, 0], grad_w1, grad_w2.transpose(1, 2, 0)
+    grad_w2 = grad_w2.reshape(classes, hid // 128, 2, 128).transpose(2, 1, 3, 0).reshape(2, hid, classes)
+    return loss[0, 0], grad_w1, grad_w2
 
 
 def solution(mesh):

time: 40 us -> 39.5 us (0.988)
  starting transfers between devices: 24.7 us -> 24 us
    ppermute x19, starting transfers between devices: 24.7 us -> 24 us  [exchange(): return lax.ppermute(value, axis, [(i, i ^ step) for i in range(size)])]
    pallas_call x9 -> x10, Pallas kernels: 5.58 us -> 5.57 us  [call(): pl.pallas_call(kernel, out_shape=outs if final else [pltpu.VMEM(o.shape,...]
  transfers between devices with their start and end apart: 19 -> 19, of which waited for: 7 -> 7; matrix products, arithmetic and copies ran while one was open for 2% -> 2% of each run, Pallas kernels for 7% -> 8%
where the time goes in v6:
time: 39.5 us; the launch traced here: 39.4 us
  starting transfers between devices  24 us (61%)
  waiting for transfers between devices  7.97 us (20%)
  Pallas kernels  5.57 us (14%)
  other arithmetic  0.92 us (2%)
  between operations  0.83 us (2%)
    ppermute x19, starting transfers between devices, exchange(): return lax.ppermute(value, axis, [(i, i ^ step) for i in range(size)])  24 us
    ppermute x19, waiting for transfers between devices, exchange(): return lax.ppermute(value, axis, [(i, i ^ step) for i in range(size)])  7.97 us
    pallas_call x10, Pallas kernels, call(): pl.pallas_call(kernel, out_shape=outs if final else [pltpu.VMEM(o.shape,...  5.57 us
    select_n x1, other arithmetic, on_device(): mine_own = jnp.where(core[0] == 0, w1_self, w1_neigh)  0.92 us
  transfers between devices with their start and end apart: 19, of which 7 were waited for; matrix products, arithmetic and copies ran while one was open for 2% of the time, Pallas kernels for 8%

profile of v6, /device:TPU:0, one launch (start us, length us, event | category | flops | bytes accessed | tf_op | source)
XLA Modules:
  0.0 39.4 jit_solution(3813317273658801728)
XLA Ops:
  0.6 3.0 %collective-permute-start.1 = (bf16[256,512]{1,0:T(8,128)(2,1)}, bf16[256,512]{1,0:T(8,128)(2,1)S(1)}, u32[]{:S(2)}, u32[]{:S(2)}) collective-permute-start(bf16[256,512]{1,0:T(8,128)(2,1)} %f_ref.1), channel_id=1, source_target_pairs={{0,16},{8,24},{16,0},{24,8},{1,17},{9,25},{17,1},{25,9},{2,18},{10... | collective-permute-start | bytes 786440 | tf_op jit(solution)/shard_map/ppermute | solution.py:241
  3.7 1.5 %collective-permute-start = (bf16[256,512]{1,0:T(8,128)(2,1)}, bf16[256,512]{1,0:T(8,128)(2,1)S(1)}, u32[]{:S(2)}, u32[]{:S(2)}) collective-permute-start(bf16[256,512]{1,0:T(8,128)(2,1)} %f_ref.1), channel_id=1, source_target_pairs={{0,8},{8,0},{16,24},{24,16},{1,9},{9,1},{17,25},{25,17},{2,10},{10... | collective-permute-start | bytes 786440 | tf_op jit(solution)/shard_map/ppermute | solution.py:241
  5.2 0.9 %broadcast_select_fusion = bf16[256,256]{1,0:T(8,128)(2,1)S(1)} fusion(bf16[256,256]{1,0:T(8,128)(2,1)} %ws_ref.1, bf16[256,256]{1,0:T(8,128)(2,1)} %wn_ref.1, pred[]{:T(512)S(6)} %eq.5), kind=kLoop, calls=%fused_computation | loop fusion | flops 65536 | bytes 393217 | tf_op jit(solution)/shard_map/jit(_where)/select_n | solution.py:274
  6.1 0.6 %collective-permute-start.2 = (bf16[256,256]{1,0:T(8,128)(2,1)S(1)}, bf16[256,256]{1,0:T(8,128)(2,1)S(1)}, u32[]{:S(2)}, u32[]{:S(2)}) collective-permute-start(bf16[256,256]{1,0:T(8,128)(2,1)S(1)} %broadcast_select_fusion), channel_id=1, source_target_pairs={{0,8},{8,0},{16,24},{24,16},{1,9},{9,1},{17,25},{25,17},{2,10},{10... | collective-permute-start | bytes 393224 | tf_op jit(solution)/shard_map/ppermute | solution.py:241
  6.7 0.1 collective-permute-start.3
  6.8 2.9 %collective-permute-start.4 = (bf16[256,256]{1,0:T(8,128)(2,1)S(1)}, bf16[256,256]{1,0:T(8,128)(2,1)S(1)}, u32[]{:S(2)}, u32[]{:S(2)}) collective-permute-start(bf16[256,256]{1,0:T(8,128)(2,1)S(1)} %broadcast_select_fusion), channel_id=1, source_target_pairs={{0,24},{8,16},{16,8},{24,0},{1,25},{9,17},{17,9},{25,1},{2,26},{10... | collective-permute-start | bytes 393224 | tf_op jit(solution)/shard_map/ppermute | solution.py:241
  9.6 1.4 %collective-permute-done.1.refs_2_.refs_1_ = bf16[256,512]{1,0:T(8,128)(2,1)S(1)} collective-permute-done((bf16[256,512]{1,0:T(8,128)(2,1)}, bf16[256,512]{1,0:T(8,128)(2,1)S(1)}, u32[]{:S(2)}, u32[]{:S(2)}) %collective-permute-start.1) | collective-permute-done | bytes 262176 | tf_op jit(solution)/shard_map/ppermute | solution.py:241
  11.0 0.0 copy-start.6
  11.0 0.0 copy-start.7
  11.0 0.0 copy-start.2
  11.0 0.0 copy-start.3
  11.0 0.0 copy-start.4
  11.1 0.0 copy-start.5
  11.1 2.1 %collective-permute-start.5 = (bf16[128,512]{1,0:T(8,128)(2,1)S(1)}, bf16[128,512]{1,0:T(8,128)(2,1)S(1)}, u32[]{:S(2)}, u32[]{:S(2)}) collective-permute-start(bf16[128,512]{1,0:T(8,128)(2,1)S(1)} %slice.8), channel_id=1, source_target_pairs={{0,8},{8,0},{16,24},{24,16},{1,9},{9,1},{17,25},{25,17},{2,10},{10... | collective-permute-start | bytes 393224 | tf_op jit(solution)/shard_map/ppermute | solution.py:241
  13.2 0.0 collective-permute-done.refs_1_.refs_0_
  13.2 0.0 copy-start.1
  13.2 0.0 copy-start
  13.2 1.6 %collective-permute-start.6 = (bf16[128,512]{1,0:T(8,128)(2,1)S(1)}, bf16[128,512]{1,0:T(8,128)(2,1)S(1)}, u32[]{:S(2)}, u32[]{:S(2)}) collective-permute-start(bf16[128,512]{1,0:T(8,128)(2,1)S(1)} %slice.9), channel_id=1, source_target_pairs={{0,16},{8,24},{16,0},{24,8},{1,17},{9,25},{17,1},{25,9},{2,18},{10... | collective-permute-start | bytes 393224 | tf_op jit(solution)/shard_map/ppermute | solution.py:241
  14.8 0.0 copy-done.6
  14.8 0.0 copy-done.7
  14.8 0.0 copy-done.3
  14.8 0.0 copy-done.4
  14.8 0.0 copy-done.5
  14.8 1.1 %shard_map.105 = (bf16[512,512]{1,0:T(8,128)(2,1)S(1)}, s32[1,512]{1,0:T(1,128)S(1)}, f32[1,512]{1,0:T(1,128)S(1)}, bf16[172,256]{1,0:T(8,128)(2,1)S(1)}, bf16[172,256]{1,0:T(8,128)(2,1)S(1)}) custom-call(s32[10,512]{1,0:T(8,128)S(1)} %bitcast.15, s32[1,512]{1,0:T(1,128)S(1)} %bitcast.16, f32[1,512]{1,0:T(1,128)S(1)} %bitcast.17, ...), custom_call_target="tpu_custom_call" | custom-call | flops 2621440 | bytes 905216 | tf_op jit(solution)/shard_map/pallas_call | solution.py:38
  15.9 0.0 collective-permute-done.2.refs_3_
  15.9 0.1 collective-permute-start.7
  16.0 0.0 collective-permute-done.3.refs_4_
  16.0 0.5 %collective-permute-start.8 = (bf16[256,256]{1,0:T(8,128)(2,1)S(1)}, bf16[256,256]{1,0:T(8,128)(2,1)S(1)}, u32[]{:S(2)}, u32[]{:S(2)}) collective-permute-start(bf16[256,256]{1,0:T(8,128)(2,1)S(1)} %collective-permute-done.3.refs_4_), channel_id=1, source_target_pairs={{0,1},{1,0},{2,3},{3,2},{4,5},{5,4},{6,7},{7,6},{8,9},{9,8},{10,11... | collective-permute-start | bytes 393224 | tf_op jit(solution)/shard_map/ppermute | solution.py:241
  16.5 1.7 %collective-permute-done.4.refs_2_ = bf16[256,256]{1,0:T(8,128)(2,1)S(1)} collective-permute-done((bf16[256,256]{1,0:T(8,128)(2,1)S(1)}, bf16[256,256]{1,0:T(8,128)(2,1)S(1)}, u32[]{:S(2)}, u32[]{:S(2)}) %collective-permute-start.4) | collective-permute-done | bytes 131104 | tf_op jit(solution)/shard_map/ppermute | solution.py:241
  18.2 0.0 collective-permute-start.9
  18.2 0.0 copy-done.2
  18.2 0.0 copy-done.1
  18.2 0.0 copy-done
  18.2 0.5 %shard_map.103 = (f32[256,512]{1,0:T(8,128)S(1)}, f32[256,512]{1,0:T(8,128)S(1)}, f32[256,512]{1,0:T(8,128)S(1)}) custom-call(s32[1]{0:T(128)} %bitcast.core_ref.refs_3_, bf16[256,256]{1,0:T(8,128)(2,1)S(1)} %copy-done, bf16[256,256]{1,0:T(8,128)(2,1)S(1)} %copy-done.1, bf16[256,512]{1,0:T(8,128)(2,1)S(1)} %copy-done.2, ...), custom_call_target="tpu_custom_call" | custom-call | flops 268435456 | bytes 2883588 | tf_op jit(solution)/shard_map/pallas_call | solution.py:38
  18.7 1.4 %collective-permute-done.5.refs_3_ = bf16[128,512]{1,0:T(8,128)(2,1)S(1)} collective-permute-done((bf16[128,512]{1,0:T(8,128)(2,1)S(1)}, bf16[128,512]{1,0:T(8,128)(2,1)S(1)}, u32[]{:S(2)}, u32[]{:S(2)}) %collective-permute-start.5) | collective-permute-done | bytes 131104 | tf_op jit(solution)/shard_map/ppermute | solution.py:241
  20.1 0.0 collective-permute-done.6.refs_4_
  20.1 0.2 shard_map.104
  20.3 0.0 collective-permute-done.7.refs_11_
  20.3 0.0 collective-permute-done.8.refs_12_
  20.3 0.0 collective-permute-done.9.refs_13_
  20.4 1.6 %shard_map.106 = (f32[176,256]{1,0:T(8,128)S(1)}, f32[176,256]{1,0:T(8,128)S(1)}, bf16[172,512]{1,0:T(8,128)(2,1)S(1)}, bf16[256,512]{1,0:T(8,128)(2,1)S(1)}) custom-call(bf16[256,512]{1,0:T(8,128)(2,1)S(1)} %collective-permute-done.refs_1_.refs_0_, bf16[256,512]{1,0:T(8,128)(2,1)S(1)} %collective-permute-done.1.refs_2_.refs_1_, ...), custom_call_target="tpu_custom_call" | custom-call | flops 805306368 | bytes 3731460 | tf_op jit(solution)/shard_map/pallas_call | solution.py:38
  21.9 0.1 collective-permute-start.10
  22.0 1.1 %shard_map.109 = (f32[4,64,256]{2,1,0:T(8,128)S(1)}, f32[4,64,256]{2,1,0:T(8,128)S(1)}) custom-call(s32[1]{0:T(128)} %bitcast.core_ref.refs_3_, bf16[172,512]{1,0:T(8,128)(2,1)S(1)} %get-tuple-element.38.g_ref, bf16[256,512]{1,0:T(8,128)(2,1)S(1)} %get-tuple-element.39.hidden_ref, bf16[512,512]{1,0:T(8,128)(2,1)S(1)} %get-tuple-element.31.refs_6_.at_ref, ...), custom_call_target="tpu_custom_call" | custom-call | flops 402653184 | bytes 1925124 | tf_op jit(solution)/shard_map/pallas_call | solution.py:38
  23.1 0.6 %collective-permute-start.15 = (f32[4,64,256]{2,1,0:T(8,128)S(1)}, f32[4,64,256]{2,1,0:T(8,128)S(1)}, u32[]{:S(2)}, u32[]{:S(2)}) collective-permute-start(f32[4,64,256]{2,1,0:T(8,128)S(1)} %get-tuple-element.41), channel_id=1, source_target_pairs={{0,1},{1,0},{2,3},{3,2},{4,5},{5,4},{6,7},{7,6},{8,9},{9,8},{10,11... | collective-permute-start | bytes 786440 | tf_op jit(solution)/shard_map/ppermute | solution.py:241
  23.7 0.0 collective-permute-done.10.recv_ref
  23.7 3.7 %collective-permute-start.11 = (bf16[176,256]{1,0:T(8,128)(2,1)S(1)}, bf16[176,256]{1,0:T(8,128)(2,1)S(1)}, u32[]{:S(2)}, u32[]{:S(2)}) collective-permute-start(bf16[176,256]{1,0:T(8,128)(2,1)S(1)} %shard_map.107.refs_3_), channel_id=1, source_target_pairs={{0,6},{1,7},{2,4},{3,5},{4,2},{5,3},{6,0},{7,1},{8,14},{9,15},{10,... | collective-permute-start | bytes 270344 | tf_op jit(solution)/shard_map/ppermute | solution.py:241
  27.4 0.0 collective-permute-start.12
  27.4 0.8 %collective-permute-start.13 = (bf16[176,256]{1,0:T(8,128)(2,1)S(1)}, bf16[176,256]{1,0:T(8,128)(2,1)S(1)}, u32[]{:S(2)}, u32[]{:S(2)}) collective-permute-start(bf16[176,256]{1,0:T(8,128)(2,1)S(1)} %shard_map.107.refs_3_), channel_id=1, source_target_pairs={{0,2},{1,3},{2,0},{3,1},{4,6},{5,7},{6,4},{7,5},{8,10},{9,11},{10,... | collective-permute-start | bytes 270344 | tf_op jit(solution)/shard_map/ppermute | solution.py:241
  28.2 0.0 collective-permute-done.15.recv_ref
  28.2 1.3 %collective-permute-start.16 = (bf16[64,256]{1,0:T(8,128)(2,1)S(1)}, bf16[64,256]{1,0:T(8,128)(2,1)S(1)}, u32[]{:S(2)}, u32[]{:S(2)}) collective-permute-start(bf16[64,256]{1,0:T(8,128)(2,1)S(1)} %get-tuple-element.43), channel_id=1, source_target_pairs={{0,2},{1,3},{2,0},{3,1},{4,6},{5,7},{6,4},{7,5},{8,10},{9,11},{10,... | collective-permute-start | bytes 98312 | tf_op jit(solution)/shard_map/ppermute | solution.py:241
  29.6 2.9 %collective-permute-start.17 = (bf16[64,256]{1,0:T(8,128)(2,1)S(1)}, bf16[64,256]{1,0:T(8,128)(2,1)S(1)}, u32[]{:S(2)}, u32[]{:S(2)}) collective-permute-start(bf16[64,256]{1,0:T(8,128)(2,1)S(1)} %get-tuple-element.44), channel_id=1, source_target_pairs={{0,4},{1,5},{2,6},{3,7},{4,0},{5,1},{6,2},{7,3},{8,12},{9,13},{10,... | collective-permute-start | bytes 98312 | tf_op jit(solution)/shard_map/ppermute | solution.py:241
  32.5 0.0 collective-permute-done.11.refs_0_
  32.5 2.3 %collective-permute-start.18 = (bf16[64,256]{1,0:T(8,128)(2,1)S(1)}, bf16[64,256]{1,0:T(8,128)(2,1)S(1)}, u32[]{:S(2)}, u32[]{:S(2)}) collective-permute-start(bf16[64,256]{1,0:T(8,128)(2,1)S(1)} %get-tuple-element.45), channel_id=1, source_target_pairs={{0,6},{1,7},{2,4},{3,5},{4,2},{5,3},{6,0},{7,1},{8,14},{9,15},{10,... | collective-permute-start | bytes 98312 | tf_op jit(solution)/shard_map/ppermute | solution.py:241
  34.8 2.1 %collective-permute-done.12.refs_1_ = bf16[176,256]{1,0:T(8,128)(2,1)S(1)} collective-permute-done((bf16[176,256]{1,0:T(8,128)(2,1)S(1)}, bf16[176,256]{1,0:T(8,128)(2,1)S(1)}, u32[]{:S(2)}, u32[]{:S(2)}) %collective-permute-start.12) | collective-permute-done | bytes 90144 | tf_op jit(solution)/shard_map/ppermute | solution.py:241
  36.9 0.0 collective-permute-done.13.refs_2_
  37.0 0.1 collective-permute-start.14
  37.1 0.0 collective-permute-done.16.refs_0_
  37.1 0.2 collective-permute-done.17.refs_1_
  37.3 0.9 %collective-permute-done.18.refs_2_ = bf16[64,256]{1,0:T(8,128)(2,1)S(1)} collective-permute-done((bf16[64,256]{1,0:T(8,128)(2,1)S(1)}, bf16[64,256]{1,0:T(8,128)(2,1)S(1)}, u32[]{:S(2)}, u32[]{:S(2)}) %collective-permute-start.18) | collective-permute-done | bytes 32800 | tf_op jit(solution)/shard_map/ppermute | solution.py:241
  38.2 0.2 collective-permute-done.14.other_ref
  38.5 0.9 %shard_map.112 = (f32[2,32,256]{2,1,0:T(8,128)}, f32[688,128]{1,0:T(8,128)}, f32[1,1]{1,0:T(1,128)}) custom-call(s32[1]{0:T(128)} %bitcast.core_ref.refs_3_, f32[176,256]{1,0:T(8,128)S(1)} %shard_map.108.own_ref, f32[176,256]{1,0:T(8,128)S(1)} %collective-permute-done.14.other_ref, f32[64,256]{1,0:T(8,128)S(1)} %shard_map.111.first_ref), custom_call_target="tpu_custom_call" | custom-call | bytes 843784 | tf_op jit(solution)/shard_map/pallas_call | solution.py:38
  (6 shorter events, 0.1 us)
Async XLA Ops:
  0.6 10.4 %collective-permute-start.1 = (bf16[256,512]{1,0:T(8,128)(2,1)}, bf16[256,512]{1,0:T(8,128)(2,1)S(1)}, u32[]{:S(2)}, u32[]{:S(2)}) collective-permute-start(bf16[256,512]{1,0:T(8,128)(2,1)} %f_ref.1), channel_id=1, source_target_pairs={{0,16},{8,24},{16,0},{24,8},{1,17},{9,25},{17,1},{25,9},{2,18},{10... | collective-permute-start | bytes 786440 | tf_op jit(solution)/shard_map/ppermute | solution.py:241
  3.7 9.5 %collective-permute-start = (bf16[256,512]{1,0:T(8,128)(2,1)}, bf16[256,512]{1,0:T(8,128)(2,1)S(1)}, u32[]{:S(2)}, u32[]{:S(2)}) collective-permute-start(bf16[256,512]{1,0:T(8,128)(2,1)} %f_ref.1), channel_id=1, source_target_pairs={{0,8},{8,0},{16,24},{24,16},{1,9},{9,1},{17,25},{25,17},{2,10},{10... | collective-permute-start | bytes 786440 | tf_op jit(solution)/shard_map/ppermute | solution.py:241
  6.1 9.8 %collective-permute-start.2 = (bf16[256,256]{1,0:T(8,128)(2,1)S(1)}, bf16[256,256]{1,0:T(8,128)(2,1)S(1)}, u32[]{:S(2)}, u32[]{:S(2)}) collective-permute-start(bf16[256,256]{1,0:T(8,128)(2,1)S(1)} %broadcast_select_fusion), channel_id=1, source_target_pairs={{0,8},{8,0},{16,24},{24,16},{1,9},{9,1},{17,25},{25,17},{2,10},{10... | collective-permute-start | bytes 393224 | tf_op jit(solution)/shard_map/ppermute | solution.py:241
  6.7 9.3 %collective-permute-start.3 = (bf16[256,256]{1,0:T(8,128)(2,1)S(1)}, bf16[256,256]{1,0:T(8,128)(2,1)S(1)}, u32[]{:S(2)}, u32[]{:S(2)}) collective-permute-start(bf16[256,256]{1,0:T(8,128)(2,1)S(1)} %broadcast_select_fusion), channel_id=1, source_target_pairs={{0,16},{8,24},{16,0},{24,8},{1,17},{9,25},{17,1},{25,9},{2,18},{10... | collective-permute-start | bytes 393224 | tf_op jit(solution)/shard_map/ppermute | solution.py:241
  6.8 11.4 %collective-permute-start.4 = (bf16[256,256]{1,0:T(8,128)(2,1)S(1)}, bf16[256,256]{1,0:T(8,128)(2,1)S(1)}, u32[]{:S(2)}, u32[]{:S(2)}) collective-permute-start(bf16[256,256]{1,0:T(8,128)(2,1)S(1)} %broadcast_select_fusion), channel_id=1, source_target_pairs={{0,24},{8,16},{16,8},{24,0},{1,25},{9,17},{17,9},{25,1},{2,26},{10... | collective-permute-start | bytes 393224 | tf_op jit(solution)/shard_map/ppermute | solution.py:241
  11.0 3.8 %copy-start.6 = (s32[512]{0:T(512)S(1)}, s32[512]{0:T(512)}, u32[]{:S(2)}) copy-start(s32[512]{0:T(512)} %param.10) | copy-start | bytes 6148
  11.0 3.8 %copy-start.7 = (f32[512]{0:T(512)S(1)}, f32[512]{0:T(512)}, u32[]{:S(2)}) copy-start(f32[512]{0:T(512)} %param.11) | copy-start | bytes 6148
  11.0 7.2 %copy-start.2 = (bf16[256,512]{1,0:T(8,128)(2,1)S(1)}, bf16[256,512]{1,0:T(8,128)(2,1)}, u32[]{:S(2)}) copy-start(bf16[256,512]{1,0:T(8,128)(2,1)} %f_ref.1) | copy-start | bytes 786436
  11.0 3.8 %copy-start.3 = (bf16[256,172]{0,1:T(8,128)(2,1)S(1)}, bf16[256,172]{0,1:T(8,128)(2,1)}, u32[]{:S(2)}) copy-start(bf16[256,172]{0,1:T(8,128)(2,1)} %param.14) | copy-start | bytes 264196
  11.0 3.7 %copy-start.4 = (bf16[256,172]{0,1:T(8,128)(2,1)S(1)}, bf16[256,172]{0,1:T(8,128)(2,1)}, u32[]{:S(2)}) copy-start(bf16[256,172]{0,1:T(8,128)(2,1)} %param.15) | copy-start | bytes 264196
  11.1 3.7 %copy-start.5 = (s32[512,10]{0,1:T(8,128)S(1)}, s32[512,10]{0,1:T(8,128)}, u32[]{:S(2)}) copy-start(s32[512,10]{0,1:T(8,128)} %param.9) | copy-start | bytes 61444
  11.1 9.0 %collective-permute-start.5 = (bf16[128,512]{1,0:T(8,128)(2,1)S(1)}, bf16[128,512]{1,0:T(8,128)(2,1)S(1)}, u32[]{:S(2)}, u32[]{:S(2)}) collective-permute-start(bf16[128,512]{1,0:T(8,128)(2,1)S(1)} %slice.8), channel_id=1, source_target_pairs={{0,8},{8,0},{16,24},{24,16},{1,9},{9,1},{17,25},{25,17},{2,10},{10... | collective-permute-start | bytes 393224 | tf_op jit(solution)/shard_map/ppermute | solution.py:241
  13.2 5.0 %copy-start.1 = (bf16[256,256]{1,0:T(8,128)(2,1)S(1)}, bf16[256,256]{1,0:T(8,128)(2,1)}, u32[]{:S(2)}) copy-start(bf16[256,256]{1,0:T(8,128)(2,1)} %wn_ref.1) | copy-start | bytes 393220
  13.2 5.0 %copy-start = (bf16[256,256]{1,0:T(8,128)(2,1)S(1)}, bf16[256,256]{1,0:T(8,128)(2,1)}, u32[]{:S(2)}) copy-start(bf16[256,256]{1,0:T(8,128)(2,1)} %ws_ref.1) | copy-start | bytes 393220
  13.2 6.9 %collective-permute-start.6 = (bf16[128,512]{1,0:T(8,128)(2,1)S(1)}, bf16[128,512]{1,0:T(8,128)(2,1)S(1)}, u32[]{:S(2)}, u32[]{:S(2)}) collective-permute-start(bf16[128,512]{1,0:T(8,128)(2,1)S(1)} %slice.9), channel_id=1, source_target_pairs={{0,16},{8,24},{16,0},{24,8},{1,17},{9,25},{17,1},{25,9},{2,18},{10... | collective-permute-start | bytes 393224 | tf_op jit(solution)/shard_map/ppermute | solution.py:241
  15.9 4.4 %collective-permute-start.7 = (bf16[256,256]{1,0:T(8,128)(2,1)S(1)}, bf16[256,256]{1,0:T(8,128)(2,1)S(1)}, u32[]{:S(2)}, u32[]{:S(2)}) collective-permute-start(bf16[256,256]{1,0:T(8,128)(2,1)S(1)} %collective-permute-done.2.refs_3_), channel_id=1, source_target_pairs={{0,1},{1,0},{2,3},{3,2},{4,5},{5,4},{6,7},{7,6},{8,9},{9,8},{10,11... | collective-permute-start | bytes 393224 | tf_op jit(solution)/shard_map/ppermute | solution.py:241
  16.0 4.3 %collective-permute-start.8 = (bf16[256,256]{1,0:T(8,128)(2,1)S(1)}, bf16[256,256]{1,0:T(8,128)(2,1)S(1)}, u32[]{:S(2)}, u32[]{:S(2)}) collective-permute-start(bf16[256,256]{1,0:T(8,128)(2,1)S(1)} %collective-permute-done.3.refs_4_), channel_id=1, source_target_pairs={{0,1},{1,0},{2,3},{3,2},{4,5},{5,4},{6,7},{7,6},{8,9},{9,8},{10,11... | collective-permute-start | bytes 393224 | tf_op jit(solution)/shard_map/ppermute | solution.py:241
  18.2 2.1 %collective-permute-start.9 = (bf16[256,256]{1,0:T(8,128)(2,1)S(1)}, bf16[256,256]{1,0:T(8,128)(2,1)S(1)}, u32[]{:S(2)}, u32[]{:S(2)}) collective-permute-start(bf16[256,256]{1,0:T(8,128)(2,1)S(1)} %collective-permute-done.4.refs_2_), channel_id=1, source_target_pairs={{0,1},{1,0},{2,3},{3,2},{4,5},{5,4},{6,7},{7,6},{8,9},{9,8},{10,11... | collective-permute-start | bytes 393224 | tf_op jit(solution)/shard_map/ppermute | solution.py:241
  21.9 1.8 %collective-permute-start.10 = (f32[176,256]{1,0:T(8,128)S(1)}, f32[176,256]{1,0:T(8,128)S(1)}, u32[]{:S(2)}, u32[]{:S(2)}) collective-permute-start(f32[176,256]{1,0:T(8,128)S(1)} %get-tuple-element.37), channel_id=1, source_target_pairs={{0,1},{1,0},{2,3},{3,2},{4,5},{5,4},{6,7},{7,6},{8,9},{9,8},{10,11... | collective-permute-start | bytes 540680 | tf_op jit(solution)/shard_map/ppermute | solution.py:241
  23.1 5.1 %collective-permute-start.15 = (f32[4,64,256]{2,1,0:T(8,128)S(1)}, f32[4,64,256]{2,1,0:T(8,128)S(1)}, u32[]{:S(2)}, u32[]{:S(2)}) collective-permute-start(f32[4,64,256]{2,1,0:T(8,128)S(1)} %get-tuple-element.41), channel_id=1, source_target_pairs={{0,1},{1,0},{2,3},{3,2},{4,5},{5,4},{6,7},{7,6},{8,9},{9,8},{10,11... | collective-permute-start | bytes 786440 | tf_op jit(solution)/shard_map/ppermute | solution.py:241
  23.7 8.7 %collective-permute-start.11 = (bf16[176,256]{1,0:T(8,128)(2,1)S(1)}, bf16[176,256]{1,0:T(8,128)(2,1)S(1)}, u32[]{:S(2)}, u32[]{:S(2)}) collective-permute-start(bf16[176,256]{1,0:T(8,128)(2,1)S(1)} %shard_map.107.refs_3_), channel_id=1, source_target_pairs={{0,6},{1,7},{2,4},{3,5},{4,2},{5,3},{6,0},{7,1},{8,14},{9,15},{10,... | collective-permute-start | bytes 270344 | tf_op jit(solution)/shard_map/ppermute | solution.py:241
  27.4 9.5 %collective-permute-start.12 = (bf16[176,256]{1,0:T(8,128)(2,1)S(1)}, bf16[176,256]{1,0:T(8,128)(2,1)S(1)}, u32[]{:S(2)}, u32[]{:S(2)}) collective-permute-start(bf16[176,256]{1,0:T(8,128)(2,1)S(1)} %shard_map.107.refs_3_), channel_id=1, source_target_pairs={{0,4},{1,5},{2,6},{3,7},{4,0},{5,1},{6,2},{7,3},{8,12},{9,13},{10,... | collective-permute-start | bytes 270344 | tf_op jit(solution)/shard_map/ppermute | solution.py:241
  27.4 9.5 %collective-permute-start.13 = (bf16[176,256]{1,0:T(8,128)(2,1)S(1)}, bf16[176,256]{1,0:T(8,128)(2,1)S(1)}, u32[]{:S(2)}, u32[]{:S(2)}) collective-permute-start(bf16[176,256]{1,0:T(8,128)(2,1)S(1)} %shard_map.107.refs_3_), channel_id=1, source_target_pairs={{0,2},{1,3},{2,0},{3,1},{4,6},{5,7},{6,4},{7,5},{8,10},{9,11},{10,... | collective-permute-start | bytes 270344 | tf_op jit(solution)/shard_map/ppermute | solution.py:241
  28.2 8.8 %collective-permute-start.16 = (bf16[64,256]{1,0:T(8,128)(2,1)S(1)}, bf16[64,256]{1,0:T(8,128)(2,1)S(1)}, u32[]{:S(2)}, u32[]{:S(2)}) collective-permute-start(bf16[64,256]{1,0:T(8,128)(2,1)S(1)} %get-tuple-element.43), channel_id=1, source_target_pairs={{0,2},{1,3},{2,0},{3,1},{4,6},{5,7},{6,4},{7,5},{8,10},{9,11},{10,... | collective-permute-start | bytes 98312 | tf_op jit(solution)/shard_map/ppermute | solution.py:241
  29.6 7.7 %collective-permute-start.17 = (bf16[64,256]{1,0:T(8,128)(2,1)S(1)}, bf16[64,256]{1,0:T(8,128)(2,1)S(1)}, u32[]{:S(2)}, u32[]{:S(2)}) collective-permute-start(bf16[64,256]{1,0:T(8,128)(2,1)S(1)} %get-tuple-element.44), channel_id=1, source_target_pairs={{0,4},{1,5},{2,6},{3,7},{4,0},{5,1},{6,2},{7,3},{8,12},{9,13},{10,... | collective-permute-start | bytes 98312 | tf_op jit(solution)/shard_map/ppermute | solution.py:241
  32.5 5.7 %collective-permute-start.18 = (bf16[64,256]{1,0:T(8,128)(2,1)S(1)}, bf16[64,256]{1,0:T(8,128)(2,1)S(1)}, u32[]{:S(2)}, u32[]{:S(2)}) collective-permute-start(bf16[64,256]{1,0:T(8,128)(2,1)S(1)} %get-tuple-element.45), channel_id=1, source_target_pairs={{0,6},{1,7},{2,4},{3,5},{4,2},{5,3},{6,0},{7,1},{8,14},{9,15},{10,... | collective-permute-start | bytes 98312 | tf_op jit(solution)/shard_map/ppermute | solution.py:241
  37.0 1.5 %collective-permute-start.14 = (f32[176,256]{1,0:T(8,128)S(1)}, f32[176,256]{1,0:T(8,128)S(1)}, u32[]{:S(2)}, u32[]{:S(2)}) collective-permute-start(f32[176,256]{1,0:T(8,128)S(1)} %shard_map.108.own_ref), channel_id=1, source_target_pairs={{0,1},{1,0},{2,3},{3,2},{4,5},{5,4},{6,7},{7,6},{8,9},{9,8},{10,11... | collective-permute-start | bytes 540680 | tf_op jit(solution)/shard_map/ppermute | solution.py:241

commit v7 on v6

--- a/solution.py
+++ b/solution.py
@@ -125,7 +125,7 @@
     scale = 1.0 / fanout
     proj[core] = mine_ref[...]
     proj[1 - core] = tree_product(
-        0, feat_count, {(0, 1): other_ref}, lambda s: dot_tn(partner_refs[s - 1][...], f_refs[s - 1][...])
+        0, feat_count, {(0, 1): other_ref}, lambda s: dot_tn(partner_refs[swapped(s, feat_count) - 1][...], f_refs[s - 1][...])
     )
     at = at_ref[...]
     pre = proj[0] + dot_nn(proj[1].astype(BF16), at) * scale
@@ -241,6 +241,24 @@
     return lax.ppermute(value, axis, [(i, i ^ step) for i in range(size)])
 
 
+def swapped(step, count):
+    bits = count.bit_length() - 1
+    if bits % 2:
+        return step
+    half = bits // 2
+    return (step & ((1 << half) - 1)) << half | step >> half
+
+
+def hop(value, step):
+    count, wide = lax.axis_size("feat"), lax.axis_size("dp")
+    pairs = []
+    for f in range(count):
+        for d in range(wide):
+            other = f ^ (step if d % 2 == 0 else swapped(step, count))
+            pairs.append((f * wide + d, other * wide + d))
+    return lax.ppermute(value, ("feat", "dp"), pairs)
+
+
 def gather_parts(block, count):
     half = block.shape[0] // 2
     parts = [[block]]
@@ -248,11 +266,11 @@
         low_bit = s & -s
         rest = s ^ low_bit
         if rest == 0:
-            parts.append([exchange(block, "feat", s)])
+            parts.append([hop(block, s)])
         else:
             low = parts[rest][0][:half] if len(parts[rest]) == 1 else parts[rest][0]
             high = parts[low_bit][0][half:]
-            parts.append([exchange(low, "feat", low_bit), exchange(high, "feat", rest)])
+            parts.append([hop(low, low_bit), hop(high, rest)])
     return parts
 
 
@@ -272,7 +290,7 @@
     late = [s for s in range(feat_count) if len(wide[s]) > 1]
     nodes_mine = early_nodes(early, 0, feat_count)
     mine_own = jnp.where(core[0] == 0, w1_self, w1_neigh)
-    mine = [exchange(mine_own, "feat", s) for s in range(1, feat_count)]
+    mine = [hop(mine_own, s) for s in range(1, feat_count)]
     limit = 12 + 6 * nodes * nodes // (1024 * 1024)
     passing = [labels.reshape(1, nodes), loss_weight.reshape(1, nodes), w2_self.T, w2_neigh.T]
     at, labels, loss_weight, w2s, w2n = call(

time: 39.5 us -> 39.4 us (level)
  waiting for transfers between devices: 7.97 us -> 5.89 us
  starting transfers between devices: 24 us -> 26 us
    ppermute x0 -> x7, starting transfers between devices: none -> 13.2 us  [hop(): return lax.ppermute(value, ('feat', 'dp'), pairs)]
    ppermute x19 -> x12, starting transfers between devices: 24 us -> 12.8 us  [exchange(): return lax.ppermute(value, axis, [(i, i ^ step) for i in range(size)])]
    ppermute x19 -> x12, waiting for transfers between devices: 7.97 us -> 3.51 us  [exchange(): return lax.ppermute(value, axis, [(i, i ^ step) for i in range(size)])]
    ppermute x0 -> x7, waiting for transfers between devices: none -> 2.38 us  [hop(): return lax.ppermute(value, ('feat', 'dp'), pairs)]
  transfers between devices with their start and end apart: 19 -> 19, of which waited for: 7 -> 8; matrix products, arithmetic and copies ran while one was open for 2% -> 2% of each run, Pallas kernels for 8% -> 8%
where the time goes in v7:
time: 39.4 us; the launch traced here: 39.3 us
  starting transfers between devices  26 us (66%)
  waiting for transfers between devices  5.89 us (15%)
  Pallas kernels  5.58 us (14%)
  other arithmetic  0.92 us (2%)
  between operations  0.82 us (2%)
    ppermute x7, starting transfers between devices, hop(): return lax.ppermute(value, ('feat', 'dp'), pairs)  13.2 us
    ppermute x12, starting transfers between devices, exchange(): return lax.ppermute(value, axis, [(i, i ^ step) for i in range(size)])  12.8 us
    pallas_call x10, Pallas kernels, call(): pl.pallas_call(kernel, out_shape=outs if final else [pltpu.VMEM(o.shape,...  5.58 us
    ppermute x12, waiting for transfers between devices, exchange(): return lax.ppermute(value, axis, [(i, i ^ step) for i in range(size)])  3.51 us
    ppermute x7, waiting for transfers between devices, hop(): return lax.ppermute(value, ('feat', 'dp'), pairs)  2.38 us
    select_n x1, other arithmetic, on_device(): mine_own = jnp.where(core[0] == 0, w1_self, w1_neigh)  0.92 us
  transfers between devices with their start and end apart: 19, of which 8 were waited for; matrix products, arithmetic and copies ran while one was open for 2% of the time, Pallas kernels for 8%

profile of v7, /device:TPU:0, one launch (start us, length us, event | category | flops | bytes accessed | tf_op | source)
XLA Modules:
  0.0 39.3 jit_solution(8200380567201367416)
XLA Ops:
  0.6 3.0 %collective-permute-start.1 = (bf16[256,512]{1,0:T(8,128)(2,1)}, bf16[256,512]{1,0:T(8,128)(2,1)S(1)}, u32[]{:S(2)}, u32[]{:S(2)}) collective-permute-start(bf16[256,512]{1,0:T(8,128)(2,1)} %f_ref.1), channel_id=1, source_target_pairs={{0,16},{1,9},{2,18},{3,11},{4,20},{5,13},{6,22},{7,15},{8,24},{9,1... | collective-permute-start | bytes 786440 | tf_op jit(solution)/shard_map/ppermute | solution.py:259
  3.7 1.5 %collective-permute-start = (bf16[256,512]{1,0:T(8,128)(2,1)}, bf16[256,512]{1,0:T(8,128)(2,1)S(1)}, u32[]{:S(2)}, u32[]{:S(2)}) collective-permute-start(bf16[256,512]{1,0:T(8,128)(2,1)} %f_ref.1), channel_id=1, source_target_pairs={{0,8},{1,17},{2,10},{3,19},{4,12},{5,21},{6,14},{7,23},{8,0},{9,25... | collective-permute-start | bytes 786440 | tf_op jit(solution)/shard_map/ppermute | solution.py:259
  5.2 0.9 %broadcast_select_fusion = bf16[256,256]{1,0:T(8,128)(2,1)S(1)} fusion(bf16[256,256]{1,0:T(8,128)(2,1)} %ws_ref.1, bf16[256,256]{1,0:T(8,128)(2,1)} %wn_ref.1, pred[]{:T(512)S(6)} %eq.5), kind=kLoop, calls=%fused_computation | loop fusion | flops 65536 | bytes 393217 | tf_op jit(solution)/shard_map/jit(_where)/select_n | solution.py:292
  6.1 0.6 %collective-permute-start.2 = (bf16[256,256]{1,0:T(8,128)(2,1)S(1)}, bf16[256,256]{1,0:T(8,128)(2,1)S(1)}, u32[]{:S(2)}, u32[]{:S(2)}) collective-permute-start(bf16[256,256]{1,0:T(8,128)(2,1)S(1)} %broadcast_select_fusion), channel_id=1, source_target_pairs={{0,8},{1,17},{2,10},{3,19},{4,12},{5,21},{6,14},{7,23},{8,0},{9,25... | collective-permute-start | bytes 393224 | tf_op jit(solution)/shard_map/ppermute | solution.py:259
  6.7 0.1 collective-permute-start.3
  6.8 2.9 %collective-permute-start.4 = (bf16[256,256]{1,0:T(8,128)(2,1)S(1)}, bf16[256,256]{1,0:T(8,128)(2,1)S(1)}, u32[]{:S(2)}, u32[]{:S(2)}) collective-permute-start(bf16[256,256]{1,0:T(8,128)(2,1)S(1)} %broadcast_select_fusion), channel_id=1, source_target_pairs={{0,24},{1,25},{2,26},{3,27},{4,28},{5,29},{6,30},{7,31},{8,16},{9,... | collective-permute-start | bytes 393224 | tf_op jit(solution)/shard_map/ppermute | solution.py:259
  9.6 1.0 %collective-permute-done.1.refs_2_.refs_1_ = bf16[256,512]{1,0:T(8,128)(2,1)S(1)} collective-permute-done((bf16[256,512]{1,0:T(8,128)(2,1)}, bf16[256,512]{1,0:T(8,128)(2,1)S(1)}, u32[]{:S(2)}, u32[]{:S(2)}) %collective-permute-start.1) | collective-permute-done | bytes 262176 | tf_op jit(solution)/shard_map/ppermute | solution.py:259
  10.6 0.0 copy-start.6
  10.6 0.0 copy-start.7
  10.6 0.0 copy-start.2
  10.6 0.0 copy-start.3
  10.6 0.0 copy-start.4
  10.6 0.0 copy-start.5
  10.7 2.5 %collective-permute-start.5 = (bf16[128,512]{1,0:T(8,128)(2,1)S(1)}, bf16[128,512]{1,0:T(8,128)(2,1)S(1)}, u32[]{:S(2)}, u32[]{:S(2)}) collective-permute-start(bf16[128,512]{1,0:T(8,128)(2,1)S(1)} %slice.8), channel_id=1, source_target_pairs={{0,8},{1,17},{2,10},{3,19},{4,12},{5,21},{6,14},{7,23},{8,0},{9,25... | collective-permute-start | bytes 393224 | tf_op jit(solution)/shard_map/ppermute | solution.py:259
  13.1 0.0 collective-permute-done.refs_1_.refs_0_
  13.1 0.0 copy-start.1
  13.2 0.0 copy-start
  13.2 2.6 %collective-permute-start.6 = (bf16[128,512]{1,0:T(8,128)(2,1)S(1)}, bf16[128,512]{1,0:T(8,128)(2,1)S(1)}, u32[]{:S(2)}, u32[]{:S(2)}) collective-permute-start(bf16[128,512]{1,0:T(8,128)(2,1)S(1)} %slice.9), channel_id=1, source_target_pairs={{0,16},{1,9},{2,18},{3,11},{4,20},{5,13},{6,22},{7,15},{8,24},{9,1... | collective-permute-start | bytes 393224 | tf_op jit(solution)/shard_map/ppermute | solution.py:259
  15.8 0.0 copy-done.6
  15.8 0.0 copy-done.7
  15.8 0.0 copy-done.3
  15.8 0.0 copy-done.4
  15.8 0.0 copy-done.5
  15.8 1.1 %shard_map.105 = (bf16[512,512]{1,0:T(8,128)(2,1)S(1)}, s32[1,512]{1,0:T(1,128)S(1)}, f32[1,512]{1,0:T(1,128)S(1)}, bf16[172,256]{1,0:T(8,128)(2,1)S(1)}, bf16[172,256]{1,0:T(8,128)(2,1)S(1)}) custom-call(s32[10,512]{1,0:T(8,128)S(1)} %bitcast.15, s32[1,512]{1,0:T(1,128)S(1)} %bitcast.16, f32[1,512]{1,0:T(1,128)S(1)} %bitcast.17, ...), custom_call_target="tpu_custom_call" | custom-call | flops 2621440 | bytes 905216 | tf_op jit(solution)/shard_map/pallas_call | solution.py:38
  17.0 0.0 collective-permute-done.2.refs_3_
  17.0 0.1 collective-permute-start.7
  17.1 0.0 collective-permute-done.3.refs_4_
  17.1 0.5 %collective-permute-start.8 = (bf16[256,256]{1,0:T(8,128)(2,1)S(1)}, bf16[256,256]{1,0:T(8,128)(2,1)S(1)}, u32[]{:S(2)}, u32[]{:S(2)}) collective-permute-start(bf16[256,256]{1,0:T(8,128)(2,1)S(1)} %collective-permute-done.3.refs_4_), channel_id=1, source_target_pairs={{0,1},{1,0},{2,3},{3,2},{4,5},{5,4},{6,7},{7,6},{8,9},{9,8},{10,11... | collective-permute-start | bytes 393224 | tf_op jit(solution)/shard_map/ppermute | solution.py:241
  17.6 0.3 collective-permute-done.4.refs_2_
  17.9 0.0 collective-permute-start.9
  17.9 0.0 copy-done.2
  17.9 0.0 copy-done.1
  17.9 0.0 copy-done
  17.9 0.5 %shard_map.103 = (f32[256,512]{1,0:T(8,128)S(1)}, f32[256,512]{1,0:T(8,128)S(1)}, f32[256,512]{1,0:T(8,128)S(1)}) custom-call(s32[1]{0:T(128)} %bitcast.core_ref.refs_3_, bf16[256,256]{1,0:T(8,128)(2,1)S(1)} %copy-done, bf16[256,256]{1,0:T(8,128)(2,1)S(1)} %copy-done.1, bf16[256,512]{1,0:T(8,128)(2,1)S(1)} %copy-done.2, ...), custom_call_target="tpu_custom_call" | custom-call | flops 268435456 | bytes 2883588 | tf_op jit(solution)/shard_map/pallas_call | solution.py:38
  18.4 0.3 collective-permute-done.5.refs_3_
  18.7 0.8 %collective-permute-done.6.refs_4_ = bf16[128,512]{1,0:T(8,128)(2,1)S(1)} collective-permute-done((bf16[128,512]{1,0:T(8,128)(2,1)S(1)}, bf16[128,512]{1,0:T(8,128)(2,1)S(1)}, u32[]{:S(2)}, u32[]{:S(2)}) %collective-permute-start.6) | collective-permute-done | bytes 131104 | tf_op jit(solution)/shard_map/ppermute | solution.py:259
  19.5 0.2 shard_map.104
  19.7 0.0 collective-permute-done.7.refs_11_
  19.7 0.0 collective-permute-done.8.refs_12_
  19.7 0.0 collective-permute-done.9.refs_13_
  19.7 1.6 %shard_map.106 = (f32[176,256]{1,0:T(8,128)S(1)}, f32[176,256]{1,0:T(8,128)S(1)}, bf16[172,512]{1,0:T(8,128)(2,1)S(1)}, bf16[256,512]{1,0:T(8,128)(2,1)S(1)}) custom-call(bf16[256,512]{1,0:T(8,128)(2,1)S(1)} %collective-permute-done.refs_1_.refs_0_, bf16[256,512]{1,0:T(8,128)(2,1)S(1)} %collective-permute-done.1.refs_2_.refs_1_, ...), custom_call_target="tpu_custom_call" | custom-call | flops 805306368 | bytes 3731460 | tf_op jit(solution)/shard_map/pallas_call | solution.py:38
  21.3 0.1 collective-permute-start.10
  21.4 1.1 %shard_map.109 = (f32[4,64,256]{2,1,0:T(8,128)S(1)}, f32[4,64,256]{2,1,0:T(8,128)S(1)}) custom-call(s32[1]{0:T(128)} %bitcast.core_ref.refs_3_, bf16[172,512]{1,0:T(8,128)(2,1)S(1)} %get-tuple-element.38.g_ref, bf16[256,512]{1,0:T(8,128)(2,1)S(1)} %get-tuple-element.39.hidden_ref, bf16[512,512]{1,0:T(8,128)(2,1)S(1)} %get-tuple-element.31.refs_6_.at_ref, ...), custom_call_target="tpu_custom_call" | custom-call | flops 402653184 | bytes 1925124 | tf_op jit(solution)/shard_map/pallas_call | solution.py:38
  22.5 0.6 %collective-permute-start.15 = (f32[4,64,256]{2,1,0:T(8,128)S(1)}, f32[4,64,256]{2,1,0:T(8,128)S(1)}, u32[]{:S(2)}, u32[]{:S(2)}) collective-permute-start(f32[4,64,256]{2,1,0:T(8,128)S(1)} %get-tuple-element.41), channel_id=1, source_target_pairs={{0,1},{1,0},{2,3},{3,2},{4,5},{5,4},{6,7},{7,6},{8,9},{9,8},{10,11... | collective-permute-start | bytes 786440 | tf_op jit(solution)/shard_map/ppermute | solution.py:241
  23.1 0.0 collective-permute-done.10.recv_ref
  23.1 4.2 %collective-permute-start.11 = (bf16[176,256]{1,0:T(8,128)(2,1)S(1)}, bf16[176,256]{1,0:T(8,128)(2,1)S(1)}, u32[]{:S(2)}, u32[]{:S(2)}) collective-permute-start(bf16[176,256]{1,0:T(8,128)(2,1)S(1)} %shard_map.107.refs_3_), channel_id=1, source_target_pairs={{0,6},{1,7},{2,4},{3,5},{4,2},{5,3},{6,0},{7,1},{8,14},{9,15},{10,... | collective-permute-start | bytes 270344 | tf_op jit(solution)/shard_map/ppermute | solution.py:241
  27.3 0.0 collective-permute-start.12
  27.3 0.6 %collective-permute-start.13 = (bf16[176,256]{1,0:T(8,128)(2,1)S(1)}, bf16[176,256]{1,0:T(8,128)(2,1)S(1)}, u32[]{:S(2)}, u32[]{:S(2)}) collective-permute-start(bf16[176,256]{1,0:T(8,128)(2,1)S(1)} %shard_map.107.refs_3_), channel_id=1, source_target_pairs={{0,2},{1,3},{2,0},{3,1},{4,6},{5,7},{6,4},{7,5},{8,10},{9,11},{10,... | collective-permute-start | bytes 270344 | tf_op jit(solution)/shard_map/ppermute | solution.py:241
  28.0 0.0 collective-permute-done.15.recv_ref
  28.0 1.5 %collective-permute-start.16 = (bf16[64,256]{1,0:T(8,128)(2,1)S(1)}, bf16[64,256]{1,0:T(8,128)(2,1)S(1)}, u32[]{:S(2)}, u32[]{:S(2)}) collective-permute-start(bf16[64,256]{1,0:T(8,128)(2,1)S(1)} %get-tuple-element.43), channel_id=1, source_target_pairs={{0,2},{1,3},{2,0},{3,1},{4,6},{5,7},{6,4},{7,5},{8,10},{9,11},{10,... | collective-permute-start | bytes 98312 | tf_op jit(solution)/shard_map/ppermute | solution.py:241
  29.4 2.9 %collective-permute-start.17 = (bf16[64,256]{1,0:T(8,128)(2,1)S(1)}, bf16[64,256]{1,0:T(8,128)(2,1)S(1)}, u32[]{:S(2)}, u32[]{:S(2)}) collective-permute-start(bf16[64,256]{1,0:T(8,128)(2,1)S(1)} %get-tuple-element.44), channel_id=1, source_target_pairs={{0,4},{1,5},{2,6},{3,7},{4,0},{5,1},{6,2},{7,3},{8,12},{9,13},{10,... | collective-permute-start | bytes 98312 | tf_op jit(solution)/shard_map/ppermute | solution.py:241
  32.4 0.0 collective-permute-done.11.refs_0_
  32.4 2.3 %collective-permute-start.18 = (bf16[64,256]{1,0:T(8,128)(2,1)S(1)}, bf16[64,256]{1,0:T(8,128)(2,1)S(1)}, u32[]{:S(2)}, u32[]{:S(2)}) collective-permute-start(bf16[64,256]{1,0:T(8,128)(2,1)S(1)} %get-tuple-element.45), channel_id=1, source_target_pairs={{0,6},{1,7},{2,4},{3,5},{4,2},{5,3},{6,0},{7,1},{8,14},{9,15},{10,... | collective-permute-start | bytes 98312 | tf_op jit(solution)/shard_map/ppermute | solution.py:241
  34.7 2.1 %collective-permute-done.12.refs_1_ = bf16[176,256]{1,0:T(8,128)(2,1)S(1)} collective-permute-done((bf16[176,256]{1,0:T(8,128)(2,1)S(1)}, bf16[176,256]{1,0:T(8,128)(2,1)S(1)}, u32[]{:S(2)}, u32[]{:S(2)}) %collective-permute-start.12) | collective-permute-done | bytes 90144 | tf_op jit(solution)/shard_map/ppermute | solution.py:241
  36.8 0.0 collective-permute-done.13.refs_2_
  36.9 0.1 collective-permute-start.14
  36.9 0.0 collective-permute-done.16.refs_0_
  36.9 0.2 collective-permute-done.17.refs_1_
  37.2 0.9 %collective-permute-done.18.refs_2_ = bf16[64,256]{1,0:T(8,128)(2,1)S(1)} collective-permute-done((bf16[64,256]{1,0:T(8,128)(2,1)S(1)}, bf16[64,256]{1,0:T(8,128)(2,1)S(1)}, u32[]{:S(2)}, u32[]{:S(2)}) %collective-permute-start.18) | collective-permute-done | bytes 32800 | tf_op jit(solution)/shard_map/ppermute | solution.py:241
  38.1 0.2 collective-permute-done.14.other_ref
  38.3 0.9 %shard_map.112 = (f32[2,32,256]{2,1,0:T(8,128)}, f32[688,128]{1,0:T(8,128)}, f32[1,1]{1,0:T(1,128)}) custom-call(s32[1]{0:T(128)} %bitcast.core_ref.refs_3_, f32[176,256]{1,0:T(8,128)S(1)} %shard_map.108.own_ref, f32[176,256]{1,0:T(8,128)S(1)} %collective-permute-done.14.other_ref, f32[64,256]{1,0:T(8,128)S(1)} %shard_map.111.first_ref), custom_call_target="tpu_custom_call" | custom-call | bytes 843784 | tf_op jit(solution)/shard_map/pallas_call | solution.py:38
  (6 shorter events, 0.1 us)
Async XLA Ops:
  0.6 10.0 %collective-permute-start.1 = (bf16[256,512]{1,0:T(8,128)(2,1)}, bf16[256,512]{1,0:T(8,128)(2,1)S(1)}, u32[]{:S(2)}, u32[]{:S(2)}) collective-permute-start(bf16[256,512]{1,0:T(8,128)(2,1)} %f_ref.1), channel_id=1, source_target_pairs={{0,16},{1,9},{2,18},{3,11},{4,20},{5,13},{6,22},{7,15},{8,24},{9,1... | collective-permute-start | bytes 786440 | tf_op jit(solution)/shard_map/ppermute | solution.py:259
  3.7 9.5 %collective-permute-start = (bf16[256,512]{1,0:T(8,128)(2,1)}, bf16[256,512]{1,0:T(8,128)(2,1)S(1)}, u32[]{:S(2)}, u32[]{:S(2)}) collective-permute-start(bf16[256,512]{1,0:T(8,128)(2,1)} %f_ref.1), channel_id=1, source_target_pairs={{0,8},{1,17},{2,10},{3,19},{4,12},{5,21},{6,14},{7,23},{8,0},{9,25... | collective-permute-start | bytes 786440 | tf_op jit(solution)/shard_map/ppermute | solution.py:259
  6.1 10.9 %collective-permute-start.2 = (bf16[256,256]{1,0:T(8,128)(2,1)S(1)}, bf16[256,256]{1,0:T(8,128)(2,1)S(1)}, u32[]{:S(2)}, u32[]{:S(2)}) collective-permute-start(bf16[256,256]{1,0:T(8,128)(2,1)S(1)} %broadcast_select_fusion), channel_id=1, source_target_pairs={{0,8},{1,17},{2,10},{3,19},{4,12},{5,21},{6,14},{7,23},{8,0},{9,25... | collective-permute-start | bytes 393224 | tf_op jit(solution)/shard_map/ppermute | solution.py:259
  6.7 10.4 %collective-permute-start.3 = (bf16[256,256]{1,0:T(8,128)(2,1)S(1)}, bf16[256,256]{1,0:T(8,128)(2,1)S(1)}, u32[]{:S(2)}, u32[]{:S(2)}) collective-permute-start(bf16[256,256]{1,0:T(8,128)(2,1)S(1)} %broadcast_select_fusion), channel_id=1, source_target_pairs={{0,16},{1,9},{2,18},{3,11},{4,20},{5,13},{6,22},{7,15},{8,24},{9,1... | collective-permute-start | bytes 393224 | tf_op jit(solution)/shard_map/ppermute | solution.py:259
  6.8 11.1 %collective-permute-start.4 = (bf16[256,256]{1,0:T(8,128)(2,1)S(1)}, bf16[256,256]{1,0:T(8,128)(2,1)S(1)}, u32[]{:S(2)}, u32[]{:S(2)}) collective-permute-start(bf16[256,256]{1,0:T(8,128)(2,1)S(1)} %broadcast_select_fusion), channel_id=1, source_target_pairs={{0,24},{1,25},{2,26},{3,27},{4,28},{5,29},{6,30},{7,31},{8,16},{9,... | collective-permute-start | bytes 393224 | tf_op jit(solution)/shard_map/ppermute | solution.py:259
  10.6 5.2 %copy-start.6 = (s32[512]{0:T(512)S(1)}, s32[512]{0:T(512)}, u32[]{:S(2)}) copy-start(s32[512]{0:T(512)} %param.10) | copy-start | bytes 6148
  10.6 5.2 %copy-start.7 = (f32[512]{0:T(512)S(1)}, f32[512]{0:T(512)}, u32[]{:S(2)}) copy-start(f32[512]{0:T(512)} %param.11) | copy-start | bytes 6148
  10.6 7.3 %copy-start.2 = (bf16[256,512]{1,0:T(8,128)(2,1)S(1)}, bf16[256,512]{1,0:T(8,128)(2,1)}, u32[]{:S(2)}) copy-start(bf16[256,512]{1,0:T(8,128)(2,1)} %f_ref.1) | copy-start | bytes 786436
  10.6 5.2 %copy-start.3 = (bf16[256,172]{0,1:T(8,128)(2,1)S(1)}, bf16[256,172]{0,1:T(8,128)(2,1)}, u32[]{:S(2)}) copy-start(bf16[256,172]{0,1:T(8,128)(2,1)} %param.14) | copy-start | bytes 264196
  10.6 5.2 %copy-start.4 = (bf16[256,172]{0,1:T(8,128)(2,1)S(1)}, bf16[256,172]{0,1:T(8,128)(2,1)}, u32[]{:S(2)}) copy-start(bf16[256,172]{0,1:T(8,128)(2,1)} %param.15) | copy-start | bytes 264196
  10.6 5.2 %copy-start.5 = (s32[512,10]{0,1:T(8,128)S(1)}, s32[512,10]{0,1:T(8,128)}, u32[]{:S(2)}) copy-start(s32[512,10]{0,1:T(8,128)} %param.9) | copy-start | bytes 61444
  10.7 8.0 %collective-permute-start.5 = (bf16[128,512]{1,0:T(8,128)(2,1)S(1)}, bf16[128,512]{1,0:T(8,128)(2,1)S(1)}, u32[]{:S(2)}, u32[]{:S(2)}) collective-permute-start(bf16[128,512]{1,0:T(8,128)(2,1)S(1)} %slice.8), channel_id=1, source_target_pairs={{0,8},{1,17},{2,10},{3,19},{4,12},{5,21},{6,14},{7,23},{8,0},{9,25... | collective-permute-start | bytes 393224 | tf_op jit(solution)/shard_map/ppermute | solution.py:259
  13.1 4.7 %copy-start.1 = (bf16[256,256]{1,0:T(8,128)(2,1)S(1)}, bf16[256,256]{1,0:T(8,128)(2,1)}, u32[]{:S(2)}) copy-start(bf16[256,256]{1,0:T(8,128)(2,1)} %wn_ref.1) | copy-start | bytes 393220
  13.2 4.7 %copy-start = (bf16[256,256]{1,0:T(8,128)(2,1)S(1)}, bf16[256,256]{1,0:T(8,128)(2,1)}, u32[]{:S(2)}) copy-start(bf16[256,256]{1,0:T(8,128)(2,1)} %ws_ref.1) | copy-start | bytes 393220
  13.2 6.3 %collective-permute-start.6 = (bf16[128,512]{1,0:T(8,128)(2,1)S(1)}, bf16[128,512]{1,0:T(8,128)(2,1)S(1)}, u32[]{:S(2)}, u32[]{:S(2)}) collective-permute-start(bf16[128,512]{1,0:T(8,128)(2,1)S(1)} %slice.9), channel_id=1, source_target_pairs={{0,16},{1,9},{2,18},{3,11},{4,20},{5,13},{6,22},{7,15},{8,24},{9,1... | collective-permute-start | bytes 393224 | tf_op jit(solution)/shard_map/ppermute | solution.py:259
  17.0 2.7 %collective-permute-start.7 = (bf16[256,256]{1,0:T(8,128)(2,1)S(1)}, bf16[256,256]{1,0:T(8,128)(2,1)S(1)}, u32[]{:S(2)}, u32[]{:S(2)}) collective-permute-start(bf16[256,256]{1,0:T(8,128)(2,1)S(1)} %collective-permute-done.2.refs_3_), channel_id=1, source_target_pairs={{0,1},{1,0},{2,3},{3,2},{4,5},{5,4},{6,7},{7,6},{8,9},{9,8},{10,11... | collective-permute-start | bytes 393224 | tf_op jit(solution)/shard_map/ppermute | solution.py:241
  17.1 2.7 %collective-permute-start.8 = (bf16[256,256]{1,0:T(8,128)(2,1)S(1)}, bf16[256,256]{1,0:T(8,128)(2,1)S(1)}, u32[]{:S(2)}, u32[]{:S(2)}) collective-permute-start(bf16[256,256]{1,0:T(8,128)(2,1)S(1)} %collective-permute-done.3.refs_4_), channel_id=1, source_target_pairs={{0,1},{1,0},{2,3},{3,2},{4,5},{5,4},{6,7},{7,6},{8,9},{9,8},{10,11... | collective-permute-start | bytes 393224 | tf_op jit(solution)/shard_map/ppermute | solution.py:241
  17.9 1.9 %collective-permute-start.9 = (bf16[256,256]{1,0:T(8,128)(2,1)S(1)}, bf16[256,256]{1,0:T(8,128)(2,1)S(1)}, u32[]{:S(2)}, u32[]{:S(2)}) collective-permute-start(bf16[256,256]{1,0:T(8,128)(2,1)S(1)} %collective-permute-done.4.refs_2_), channel_id=1, source_target_pairs={{0,1},{1,0},{2,3},{3,2},{4,5},{5,4},{6,7},{7,6},{8,9},{9,8},{10,11... | collective-permute-start | bytes 393224 | tf_op jit(solution)/shard_map/ppermute | solution.py:241
  21.3 1.8 %collective-permute-start.10 = (f32[176,256]{1,0:T(8,128)S(1)}, f32[176,256]{1,0:T(8,128)S(1)}, u32[]{:S(2)}, u32[]{:S(2)}) collective-permute-start(f32[176,256]{1,0:T(8,128)S(1)} %get-tuple-element.37), channel_id=1, source_target_pairs={{0,1},{1,0},{2,3},{3,2},{4,5},{5,4},{6,7},{7,6},{8,9},{9,8},{10,11... | collective-permute-start | bytes 540680 | tf_op jit(solution)/shard_map/ppermute | solution.py:241
  22.5 5.4 %collective-permute-start.15 = (f32[4,64,256]{2,1,0:T(8,128)S(1)}, f32[4,64,256]{2,1,0:T(8,128)S(1)}, u32[]{:S(2)}, u32[]{:S(2)}) collective-permute-start(f32[4,64,256]{2,1,0:T(8,128)S(1)} %get-tuple-element.41), channel_id=1, source_target_pairs={{0,1},{1,0},{2,3},{3,2},{4,5},{5,4},{6,7},{7,6},{8,9},{9,8},{10,11... | collective-permute-start | bytes 786440 | tf_op jit(solution)/shard_map/ppermute | solution.py:241
  23.1 9.2 %collective-permute-start.11 = (bf16[176,256]{1,0:T(8,128)(2,1)S(1)}, bf16[176,256]{1,0:T(8,128)(2,1)S(1)}, u32[]{:S(2)}, u32[]{:S(2)}) collective-permute-start(bf16[176,256]{1,0:T(8,128)(2,1)S(1)} %shard_map.107.refs_3_), channel_id=1, source_target_pairs={{0,6},{1,7},{2,4},{3,5},{4,2},{5,3},{6,0},{7,1},{8,14},{9,15},{10,... | collective-permute-start | bytes 270344 | tf_op jit(solution)/shard_map/ppermute | solution.py:241
  27.3 9.5 %collective-permute-start.12 = (bf16[176,256]{1,0:T(8,128)(2,1)S(1)}, bf16[176,256]{1,0:T(8,128)(2,1)S(1)}, u32[]{:S(2)}, u32[]{:S(2)}) collective-permute-start(bf16[176,256]{1,0:T(8,128)(2,1)S(1)} %shard_map.107.refs_3_), channel_id=1, source_target_pairs={{0,4},{1,5},{2,6},{3,7},{4,0},{5,1},{6,2},{7,3},{8,12},{9,13},{10,... | collective-permute-start | bytes 270344 | tf_op jit(solution)/shard_map/ppermute | solution.py:241
  27.3 9.5 %collective-permute-start.13 = (bf16[176,256]{1,0:T(8,128)(2,1)S(1)}, bf16[176,256]{1,0:T(8,128)(2,1)S(1)}, u32[]{:S(2)}, u32[]{:S(2)}) collective-permute-start(bf16[176,256]{1,0:T(8,128)(2,1)S(1)} %shard_map.107.refs_3_), channel_id=1, source_target_pairs={{0,2},{1,3},{2,0},{3,1},{4,6},{5,7},{6,4},{7,5},{8,10},{9,11},{10,... | collective-permute-start | bytes 270344 | tf_op jit(solution)/shard_map/ppermute | solution.py:241
  28.0 9.0 %collective-permute-start.16 = (bf16[64,256]{1,0:T(8,128)(2,1)S(1)}, bf16[64,256]{1,0:T(8,128)(2,1)S(1)}, u32[]{:S(2)}, u32[]{:S(2)}) collective-permute-start(bf16[64,256]{1,0:T(8,128)(2,1)S(1)} %get-tuple-element.43), channel_id=1, source_target_pairs={{0,2},{1,3},{2,0},{3,1},{4,6},{5,7},{6,4},{7,5},{8,10},{9,11},{10,... | collective-permute-start | bytes 98312 | tf_op jit(solution)/shard_map/ppermute | solution.py:241
  29.4 7.7 %collective-permute-start.17 = (bf16[64,256]{1,0:T(8,128)(2,1)S(1)}, bf16[64,256]{1,0:T(8,128)(2,1)S(1)}, u32[]{:S(2)}, u32[]{:S(2)}) collective-permute-start(bf16[64,256]{1,0:T(8,128)(2,1)S(1)} %get-tuple-element.44), channel_id=1, source_target_pairs={{0,4},{1,5},{2,6},{3,7},{4,0},{5,1},{6,2},{7,3},{8,12},{9,13},{10,... | collective-permute-start | bytes 98312 | tf_op jit(solution)/shard_map/ppermute | solution.py:241
  32.4 5.7 %collective-permute-start.18 = (bf16[64,256]{1,0:T(8,128)(2,1)S(1)}, bf16[64,256]{1,0:T(8,128)(2,1)S(1)}, u32[]{:S(2)}, u32[]{:S(2)}) collective-permute-start(bf16[64,256]{1,0:T(8,128)(2,1)S(1)} %get-tuple-element.45), channel_id=1, source_target_pairs={{0,6},{1,7},{2,4},{3,5},{4,2},{5,3},{6,0},{7,1},{8,14},{9,15},{10,... | collective-permute-start | bytes 98312 | tf_op jit(solution)/shard_map/ppermute | solution.py:241
  36.9 1.5 %collective-permute-start.14 = (f32[176,256]{1,0:T(8,128)S(1)}, f32[176,256]{1,0:T(8,128)S(1)}, u32[]{:S(2)}, u32[]{:S(2)}) collective-permute-start(f32[176,256]{1,0:T(8,128)S(1)} %shard_map.108.own_ref), channel_id=1, source_target_pairs={{0,1},{1,0},{2,3},{3,2},{4,5},{5,4},{6,7},{7,6},{8,9},{9,8},{10,11... | collective-permute-start | bytes 540680 | tf_op jit(solution)/shard_map/ppermute | solution.py:241

commit v8 on v7

--- a/solution.py
+++ b/solution.py
@@ -184,22 +184,41 @@
             keep_ref[z, part * rows : (part + 1) * rows] = jnp.where(first, low_rows, high_rows)
 
 
-def pair_kernel(classes, keep_ref, recv_ref, out_ref):
-    total = keep_ref[...] + recv_ref[...]
+def split_rows(total, classes):
     high = total.astype(BF16).astype(F32)
     rest = total - high
     middle = rest.astype(BF16).astype(F32)
     low = rest - middle
     row = lax.broadcasted_iota(jnp.int32, total.shape, 0)
-    out_ref[...] = jnp.where(row == classes + 1, middle, jnp.where(row == classes + 2, low, high)).astype(BF16)
-
-
-def chunk_kernel(groups, z_ref, keep_ref, recv_ref, own_ref, *out_refs):
-    z = z_ref[0]
-    own_ref[...] = keep_ref[z] + recv_ref[z]
-    for s in range(1, groups):
-        other = jnp.bitwise_xor(z, s)
-        out_refs[s - 1][...] = (keep_ref[other] + recv_ref[other]).astype(BF16)
+    return jnp.where(row == classes + 1, middle, jnp.where(row == classes + 2, low, high)).astype(BF16)
+
+
+def pair_kernel(classes, keep_ref, recv_ref, out_ref):
+    out_ref[...] = split_rows(keep_ref[...] + recv_ref[...], classes)
+
+
+def fold_second_kernel(classes, order_ref, own_ref, recv_ref, out_ref):
+    total = own_ref[...].astype(F32) + recv_ref[...].astype(F32)
+    row = lax.broadcasted_iota(jnp.int32, total.shape, 0)
+    inside = jnp.logical_and(row >= classes, row < classes + 3)
+    whole = jnp.sum(jnp.where(inside, total, 0.0), axis=0, keepdims=True)
+    out_ref[...] = split_rows(jnp.where(row >= classes, whole, total), classes)
+
+
+def chunk_kernel(groups, z_ref, keep_ref, recv_ref, kept_ref, send_ref):
+    z, chunk = z_ref[0], keep_ref.shape[1]
+    for i in range(groups // 2):
+        here, there = jnp.bitwise_xor(z, 2 * i), jnp.bitwise_xor(z, 2 * i + 1)
+        kept_ref[i] = keep_ref[here] + recv_ref[here]
+        send_ref[i * chunk : (i + 1) * chunk] = (keep_ref[there] + recv_ref[there]).astype(BF16)
+
+
+def fold_first_kernel(own_ref, recv_ref, kept_ref, send_ref):
+    chunk = own_ref.shape[1]
+    for i in range(own_ref.shape[0] // 2):
+        kept_ref[i] = own_ref[2 * i] + recv_ref[2 * i * chunk : (2 * i + 1) * chunk].astype(F32)
+        other = own_ref[2 * i + 1] + recv_ref[(2 * i + 1) * chunk : (2 * i + 2) * chunk].astype(F32)
+        send_ref[i * chunk : (i + 1) * chunk] = other.astype(BF16)
 
 
 def second_sum_kernel(*refs):
@@ -217,23 +236,22 @@
 
 
 def first_sum_kernel(own_ref, *refs):
-    refs[-1][...] = tree_sum([own_ref[...]] + [r[...].astype(F32) for r in refs[:-1]])
+    refs[-1][...] = own_ref[0] + refs[0][...].astype(F32)
 
 
 def out_kernel(classes, core_ref, own_ref, other_ref, first_ref, grad1_ref, grad2_ref, loss_ref):
     first = core_ref[0] == 0
     loss, norm = scalars(own_ref[...], classes)
-    inverse = 1.0 / norm
-    own = own_ref[:classes, :] * inverse
-    other = other_ref[:classes, :] * inverse
+    own = own_ref[:classes, :] / norm
+    other = other_ref[:classes, :] / norm
     for slot, half in enumerate((jnp.where(first, own, other), jnp.where(first, other, own))):
         lanes = half.shape[1] // 128
         for j in range(lanes):
             grad2_ref[pl.ds(2 * j + slot, classes, stride=2 * lanes), :] = half[:, 128 * j : 128 * (j + 1)]
-    loss_ref[...] = loss * inverse
+    loss_ref[...] = loss / norm
     rows = grad1_ref.shape[1]
-    grad1_ref[0] = first_ref[:rows] * inverse
-    grad1_ref[1] = first_ref[rows:] * inverse
+    grad1_ref[0] = first_ref[:rows] / norm
+    grad1_ref[1] = first_ref[rows:] / norm
 
 
 def exchange(value, axis, step):
@@ -347,17 +365,29 @@
     )
     recv1 = exchange(send1, "dp", 1)
     (own2,) = call(functools.partial(pair_kernel, classes), [shape((padded, hid), BF16)], [keep2, recv2])
-    far2 = [exchange(own2, "dp", 2 * s) for s in range(1, groups)]
-    own1, *chunks = call(
+    left = groups // 2
+    kept1, send1 = call(
         functools.partial(chunk_kernel, groups),
-        [shape((chunk, hid), F32)] + [shape((chunk, hid), BF16)] * (groups - 1),
+        [shape((left, chunk, hid), F32), shape((left * chunk, hid), BF16)],
         [z, keep1, recv1],
         smem=(0,),
     )
-    far1 = [exchange(chunks[s - 1], "dp", 2 * s) for s in range(1, groups)]
-    (total2,) = call(second_sum_kernel, [shape((padded, hid), F32)], far2[::-1] + [own2])
+    step = 2
+    while left > 1:
+        far2, far1 = exchange(own2, "dp", step), exchange(send1, "dp", step)
+        left, step = left // 2, 2 * step
+        (own2,) = call(
+            functools.partial(fold_second_kernel, classes), [shape((padded, hid), BF16)], [kept1, own2, far2]
+        )
+        kept1, send1 = call(
+            fold_first_kernel,
+            [shape((left, chunk, hid), F32), shape((left * chunk, hid), BF16)],
+            [kept1, far1],
+        )
+    far2, far1 = exchange(own2, "dp", step), exchange(send1, "dp", step)
+    (total2,) = call(second_sum_kernel, [shape((padded, hid), F32)], [own2, far2])
     other2 = exchange(total2, "dp", 1)
-    (sum1,) = call(first_sum_kernel, [shape((chunk, hid), F32)], [own1] + far1, flops=300 * rows * nodes * hid)
+    (sum1,) = call(first_sum_kernel, [shape((chunk, hid), F32)], [kept1, far1], flops=300 * rows * nodes * hid)
     grad_w1, grad_w2, loss = call(
         functools.partial(out_kernel, classes),
         [shape((2, rows // dp_count, hid), F32), shape((classes * 2 * (hid // 128), 128), F32), shape((1, 1), F32)],

time: 39.4 us -> 37.4 us (0.949)
  starting transfers between devices: 26 us -> 21.5 us
  waiting for transfers between devices: 5.89 us -> 8.34 us
    ppermute x12 -> x10, starting transfers between devices: 12.8 us -> 8.32 us  [exchange(): return lax.ppermute(value, axis, [(i, i ^ step) for i in range(size)])]
    ppermute x12 -> x10, waiting for transfers between devices: 3.51 us -> 5.95 us  [exchange(): return lax.ppermute(value, axis, [(i, i ^ step) for i in range(size)])]
    pallas_call x10 -> x12, Pallas kernels: 5.58 us -> 5.61 us  [call(): pl.pallas_call(kernel, out_shape=outs if final else [pltpu.VMEM(o.shape,...]
  transfers between devices with their start and end apart: 19 -> 17, of which waited for: 8 -> 7; matrix products, arithmetic and copies ran while one was open for 2% -> 3% of each run, Pallas kernels for 8% -> 8%
where the time goes in v8:
time: 37.4 us; the launch traced here: 37.3 us
  starting transfers between devices  21.5 us (57%)
  waiting for transfers between devices  8.34 us (22%)
  Pallas kernels  5.61 us (15%)
  other arithmetic  0.92 us (2%)
  between operations  0.83 us (2%)
    ppermute x7, starting transfers between devices, hop(): return lax.ppermute(value, ('feat', 'dp'), pairs)  13.2 us
    ppermute x10, starting transfers between devices, exchange(): return lax.ppermute(value, axis, [(i, i ^ step) for i in range(size)])  8.32 us
    ppermute x10, waiting for transfers between devices, exchange(): return lax.ppermute(value, axis, [(i, i ^ step) for i in range(size)])  5.95 us
    pallas_call x12, Pallas kernels, call(): pl.pallas_call(kernel, out_shape=outs if final else [pltpu.VMEM(o.shape,...  5.61 us
    ppermute x7, waiting for transfers between devices, hop(): return lax.ppermute(value, ('feat', 'dp'), pairs)  2.38 us
    select_n x1, other arithmetic, on_device(): mine_own = jnp.where(core[0] == 0, w1_self, w1_neigh)  0.92 us
  transfers between devices with their start and end apart: 17, of which 7 were waited for; matrix products, arithmetic and copies ran while one was open for 3% of the time, Pallas kernels for 8%

profile of v8, /device:TPU:0, one launch (start us, length us, event | category | flops | bytes accessed | tf_op | source)
XLA Modules:
  0.0 37.3 jit_solution(662122163270894353)
XLA Ops:
  0.6 3.0 %collective-permute-start.1 = (bf16[256,512]{1,0:T(8,128)(2,1)}, bf16[256,512]{1,0:T(8,128)(2,1)S(1)}, u32[]{:S(2)}, u32[]{:S(2)}) collective-permute-start(bf16[256,512]{1,0:T(8,128)(2,1)} %f_ref.1), channel_id=1, source_target_pairs={{0,16},{1,9},{2,18},{3,11},{4,20},{5,13},{6,22},{7,15},{8,24},{9,1... | collective-permute-start | bytes 786440 | tf_op jit(solution)/shard_map/ppermute | solution.py:277
  3.7 1.5 %collective-permute-start = (bf16[256,512]{1,0:T(8,128)(2,1)}, bf16[256,512]{1,0:T(8,128)(2,1)S(1)}, u32[]{:S(2)}, u32[]{:S(2)}) collective-permute-start(bf16[256,512]{1,0:T(8,128)(2,1)} %f_ref.1), channel_id=1, source_target_pairs={{0,8},{1,17},{2,10},{3,19},{4,12},{5,21},{6,14},{7,23},{8,0},{9,25... | collective-permute-start | bytes 786440 | tf_op jit(solution)/shard_map/ppermute | solution.py:277
  5.2 0.9 %broadcast_select_fusion = bf16[256,256]{1,0:T(8,128)(2,1)S(1)} fusion(bf16[256,256]{1,0:T(8,128)(2,1)} %ws_ref.1, bf16[256,256]{1,0:T(8,128)(2,1)} %wn_ref.1, pred[]{:T(512)S(6)} %eq.5), kind=kLoop, calls=%fused_computation | loop fusion | flops 65536 | bytes 393217 | tf_op jit(solution)/shard_map/jit(_where)/select_n | solution.py:310
  6.1 0.6 %collective-permute-start.2 = (bf16[256,256]{1,0:T(8,128)(2,1)S(1)}, bf16[256,256]{1,0:T(8,128)(2,1)S(1)}, u32[]{:S(2)}, u32[]{:S(2)}) collective-permute-start(bf16[256,256]{1,0:T(8,128)(2,1)S(1)} %broadcast_select_fusion), channel_id=1, source_target_pairs={{0,8},{1,17},{2,10},{3,19},{4,12},{5,21},{6,14},{7,23},{8,0},{9,25... | collective-permute-start | bytes 393224 | tf_op jit(solution)/shard_map/ppermute | solution.py:277
  6.7 0.1 collective-permute-start.3
  6.8 2.9 %collective-permute-start.4 = (bf16[256,256]{1,0:T(8,128)(2,1)S(1)}, bf16[256,256]{1,0:T(8,128)(2,1)S(1)}, u32[]{:S(2)}, u32[]{:S(2)}) collective-permute-start(bf16[256,256]{1,0:T(8,128)(2,1)S(1)} %broadcast_select_fusion), channel_id=1, source_target_pairs={{0,24},{1,25},{2,26},{3,27},{4,28},{5,29},{6,30},{7,31},{8,16},{9,... | collective-permute-start | bytes 393224 | tf_op jit(solution)/shard_map/ppermute | solution.py:277
  9.6 1.0 %collective-permute-done.1.refs_2_.refs_1_ = bf16[256,512]{1,0:T(8,128)(2,1)S(1)} collective-permute-done((bf16[256,512]{1,0:T(8,128)(2,1)}, bf16[256,512]{1,0:T(8,128)(2,1)S(1)}, u32[]{:S(2)}, u32[]{:S(2)}) %collective-permute-start.1) | collective-permute-done | bytes 262176 | tf_op jit(solution)/shard_map/ppermute | solution.py:277
  10.6 0.0 copy-start.6
  10.6 0.0 copy-start.7
  10.6 0.0 copy-start.2
  10.6 0.0 copy-start.3
  10.6 0.0 copy-start.4
  10.6 0.0 copy-start.5
  10.7 2.5 %collective-permute-start.5 = (bf16[128,512]{1,0:T(8,128)(2,1)S(1)}, bf16[128,512]{1,0:T(8,128)(2,1)S(1)}, u32[]{:S(2)}, u32[]{:S(2)}) collective-permute-start(bf16[128,512]{1,0:T(8,128)(2,1)S(1)} %slice.8), channel_id=1, source_target_pairs={{0,8},{1,17},{2,10},{3,19},{4,12},{5,21},{6,14},{7,23},{8,0},{9,25... | collective-permute-start | bytes 393224 | tf_op jit(solution)/shard_map/ppermute | solution.py:277
  13.1 0.0 collective-permute-done.refs_1_.refs_0_
  13.1 0.0 copy-start.1
  13.2 0.0 copy-start
  13.2 2.6 %collective-permute-start.6 = (bf16[128,512]{1,0:T(8,128)(2,1)S(1)}, bf16[128,512]{1,0:T(8,128)(2,1)S(1)}, u32[]{:S(2)}, u32[]{:S(2)}) collective-permute-start(bf16[128,512]{1,0:T(8,128)(2,1)S(1)} %slice.9), channel_id=1, source_target_pairs={{0,16},{1,9},{2,18},{3,11},{4,20},{5,13},{6,22},{7,15},{8,24},{9,1... | collective-permute-start | bytes 393224 | tf_op jit(solution)/shard_map/ppermute | solution.py:277
  15.8 0.0 copy-done.6
  15.8 0.0 copy-done.7
  15.8 0.0 copy-done.3
  15.8 0.0 copy-done.4
  15.8 0.0 copy-done.5
  15.8 1.1 %shard_map.105 = (bf16[512,512]{1,0:T(8,128)(2,1)S(1)}, s32[1,512]{1,0:T(1,128)S(1)}, f32[1,512]{1,0:T(1,128)S(1)}, bf16[172,256]{1,0:T(8,128)(2,1)S(1)}, bf16[172,256]{1,0:T(8,128)(2,1)S(1)}) custom-call(s32[10,512]{1,0:T(8,128)S(1)} %bitcast.15, s32[1,512]{1,0:T(1,128)S(1)} %bitcast.16, f32[1,512]{1,0:T(1,128)S(1)} %bitcast.17, ...), custom_call_target="tpu_custom_call" | custom-call | flops 2621440 | bytes 905216 | tf_op jit(solution)/shard_map/pallas_call | solution.py:38
  17.0 0.0 collective-permute-done.2.refs_3_
  17.0 0.1 collective-permute-start.7
  17.1 0.0 collective-permute-done.3.refs_4_
  17.1 0.5 %collective-permute-start.8 = (bf16[256,256]{1,0:T(8,128)(2,1)S(1)}, bf16[256,256]{1,0:T(8,128)(2,1)S(1)}, u32[]{:S(2)}, u32[]{:S(2)}) collective-permute-start(bf16[256,256]{1,0:T(8,128)(2,1)S(1)} %collective-permute-done.3.refs_4_), channel_id=1, source_target_pairs={{0,1},{1,0},{2,3},{3,2},{4,5},{5,4},{6,7},{7,6},{8,9},{9,8},{10,11... | collective-permute-start | bytes 393224 | tf_op jit(solution)/shard_map/ppermute | solution.py:259
  17.6 0.3 collective-permute-done.4.refs_2_
  17.9 0.0 collective-permute-start.9
  17.9 0.0 copy-done.2
  17.9 0.0 copy-done.1
  17.9 0.0 copy-done
  17.9 0.5 %shard_map.103 = (f32[256,512]{1,0:T(8,128)S(1)}, f32[256,512]{1,0:T(8,128)S(1)}, f32[256,512]{1,0:T(8,128)S(1)}) custom-call(s32[1]{0:T(128)} %bitcast.core_ref.refs_3_, bf16[256,256]{1,0:T(8,128)(2,1)S(1)} %copy-done, bf16[256,256]{1,0:T(8,128)(2,1)S(1)} %copy-done.1, bf16[256,512]{1,0:T(8,128)(2,1)S(1)} %copy-done.2, ...), custom_call_target="tpu_custom_call" | custom-call | flops 268435456 | bytes 2883588 | tf_op jit(solution)/shard_map/pallas_call | solution.py:38
  18.4 0.3 collective-permute-done.5.refs_3_
  18.7 0.8 %collective-permute-done.6.refs_4_ = bf16[128,512]{1,0:T(8,128)(2,1)S(1)} collective-permute-done((bf16[128,512]{1,0:T(8,128)(2,1)S(1)}, bf16[128,512]{1,0:T(8,128)(2,1)S(1)}, u32[]{:S(2)}, u32[]{:S(2)}) %collective-permute-start.6) | collective-permute-done | bytes 131104 | tf_op jit(solution)/shard_map/ppermute | solution.py:277
  19.5 0.2 shard_map.104
  19.7 0.0 collective-permute-done.7.refs_11_
  19.7 0.0 collective-permute-done.8.refs_12_
  19.7 0.0 collective-permute-done.9.refs_13_
  19.7 1.6 %shard_map.106 = (f32[176,256]{1,0:T(8,128)S(1)}, f32[176,256]{1,0:T(8,128)S(1)}, bf16[172,512]{1,0:T(8,128)(2,1)S(1)}, bf16[256,512]{1,0:T(8,128)(2,1)S(1)}) custom-call(bf16[256,512]{1,0:T(8,128)(2,1)S(1)} %collective-permute-done.refs_1_.refs_0_, bf16[256,512]{1,0:T(8,128)(2,1)S(1)} %collective-permute-done.1.refs_2_.refs_1_, ...), custom_call_target="tpu_custom_call" | custom-call | flops 805306368 | bytes 3731460 | tf_op jit(solution)/shard_map/pallas_call | solution.py:38
  21.3 0.1 collective-permute-start.11
  21.4 1.1 %shard_map.107 = (f32[4,64,256]{2,1,0:T(8,128)S(1)}, f32[4,64,256]{2,1,0:T(8,128)S(1)}) custom-call(s32[1]{0:T(128)} %bitcast.core_ref.refs_3_, bf16[172,512]{1,0:T(8,128)(2,1)S(1)} %get-tuple-element.36.g_ref, bf16[256,512]{1,0:T(8,128)(2,1)S(1)} %get-tuple-element.37.hidden_ref, bf16[512,512]{1,0:T(8,128)(2,1)S(1)} %get-tuple-element.31.refs_6_.at_ref, ...), custom_call_target="tpu_custom_call" | custom-call | flops 402653184 | bytes 1925124 | tf_op jit(solution)/shard_map/pallas_call | solution.py:38
  22.5 0.6 %collective-permute-start.10 = (f32[4,64,256]{2,1,0:T(8,128)S(1)}, f32[4,64,256]{2,1,0:T(8,128)S(1)}, u32[]{:S(2)}, u32[]{:S(2)}) collective-permute-start(f32[4,64,256]{2,1,0:T(8,128)S(1)} %get-tuple-element.39), channel_id=1, source_target_pairs={{0,1},{1,0},{2,3},{3,2},{4,5},{5,4},{6,7},{7,6},{8,9},{9,8},{10,11... | collective-permute-start | bytes 786440 | tf_op jit(solution)/shard_map/ppermute | solution.py:259
  23.1 0.0 collective-permute-done.11.recv_ref
  23.1 2.1 %collective-permute-start.12 = (bf16[176,256]{1,0:T(8,128)(2,1)S(1)}, bf16[176,256]{1,0:T(8,128)(2,1)S(1)}, u32[]{:S(2)}, u32[]{:S(2)}) collective-permute-start(bf16[176,256]{1,0:T(8,128)(2,1)S(1)} %shard_map.109.own_ref), channel_id=1, source_target_pairs={{0,2},{1,3},{2,0},{3,1},{4,6},{5,7},{6,4},{7,5},{8,10},{9,11},{10,... | collective-permute-start | bytes 270344 | tf_op jit(solution)/shard_map/ppermute | solution.py:259
  25.3 0.0 collective-permute-done.10.recv_ref
  25.3 1.1 %collective-permute-start.15 = (bf16[128,256]{1,0:T(8,128)(2,1)S(1)}, bf16[128,256]{1,0:T(8,128)(2,1)S(1)}, u32[]{:S(2)}, u32[]{:S(2)}) collective-permute-start(bf16[128,256]{1,0:T(8,128)(2,1)S(1)} %get-tuple-element.43), channel_id=1, source_target_pairs={{0,2},{1,3},{2,0},{3,1},{4,6},{5,7},{6,4},{7,5},{8,10},{9,11},{10,... | collective-permute-start | bytes 196616 | tf_op jit(solution)/shard_map/ppermute | solution.py:259
  26.4 2.0 %collective-permute-done.12.recv_ref = bf16[176,256]{1,0:T(8,128)(2,1)S(1)} collective-permute-done((bf16[176,256]{1,0:T(8,128)(2,1)S(1)}, bf16[176,256]{1,0:T(8,128)(2,1)S(1)}, u32[]{:S(2)}, u32[]{:S(2)}) %collective-permute-start.12) | collective-permute-done | bytes 90144 | tf_op jit(solution)/shard_map/ppermute | solution.py:259
  28.5 2.9 %collective-permute-start.13 = (bf16[176,256]{1,0:T(8,128)(2,1)S(1)}, bf16[176,256]{1,0:T(8,128)(2,1)S(1)}, u32[]{:S(2)}, u32[]{:S(2)}) collective-permute-start(bf16[176,256]{1,0:T(8,128)(2,1)S(1)} %shard_map.110.refs_0_), channel_id=1, source_target_pairs={{0,4},{1,5},{2,6},{3,7},{4,0},{5,1},{6,2},{7,3},{8,12},{9,13},{10,... | collective-permute-start | bytes 270344 | tf_op jit(solution)/shard_map/ppermute | solution.py:259
  31.4 0.0 collective-permute-done.15.recv_ref
  31.5 0.9 %collective-permute-start.16 = (bf16[64,256]{1,0:T(8,128)(2,1)S(1)}, bf16[64,256]{1,0:T(8,128)(2,1)S(1)}, u32[]{:S(2)}, u32[]{:S(2)}) collective-permute-start(bf16[64,256]{1,0:T(8,128)(2,1)S(1)} %get-tuple-element.45), channel_id=1, source_target_pairs={{0,4},{1,5},{2,6},{3,7},{4,0},{5,1},{6,2},{7,3},{8,12},{9,13},{10,... | collective-permute-start | bytes 98312 | tf_op jit(solution)/shard_map/ppermute | solution.py:259
  32.3 2.1 %collective-permute-done.13.refs_1_ = bf16[176,256]{1,0:T(8,128)(2,1)S(1)} collective-permute-done((bf16[176,256]{1,0:T(8,128)(2,1)S(1)}, bf16[176,256]{1,0:T(8,128)(2,1)S(1)}, u32[]{:S(2)}, u32[]{:S(2)}) %collective-permute-start.13) | collective-permute-done | bytes 90144 | tf_op jit(solution)/shard_map/ppermute | solution.py:259
  34.5 0.1 collective-permute-start.14
  34.5 1.8 %collective-permute-done.16.refs_0_ = bf16[64,256]{1,0:T(8,128)(2,1)S(1)} collective-permute-done((bf16[64,256]{1,0:T(8,128)(2,1)S(1)}, bf16[64,256]{1,0:T(8,128)(2,1)S(1)}, u32[]{:S(2)}, u32[]{:S(2)}) %collective-permute-start.16) | collective-permute-done | bytes 32800 | tf_op jit(solution)/shard_map/ppermute | solution.py:259
  36.4 0.0 collective-permute-done.14.other_ref
  36.4 0.9 %shard_map.114 = (f32[2,32,256]{2,1,0:T(8,128)}, f32[688,128]{1,0:T(8,128)}, f32[1,1]{1,0:T(1,128)}) custom-call(s32[1]{0:T(128)} %bitcast.core_ref.refs_3_, f32[176,256]{1,0:T(8,128)S(1)} %shard_map.111.own_ref, f32[176,256]{1,0:T(8,128)S(1)} %collective-permute-done.14.other_ref, f32[64,256]{1,0:T(8,128)S(1)} %shard_map.113.first_ref), custom_call_target="tpu_custom_call" | custom-call | bytes 843784 | tf_op jit(solution)/shard_map/pallas_call | solution.py:38
  (8 shorter events, 0.2 us)
Async XLA Ops:
  0.6 10.0 %collective-permute-start.1 = (bf16[256,512]{1,0:T(8,128)(2,1)}, bf16[256,512]{1,0:T(8,128)(2,1)S(1)}, u32[]{:S(2)}, u32[]{:S(2)}) collective-permute-start(bf16[256,512]{1,0:T(8,128)(2,1)} %f_ref.1), channel_id=1, source_target_pairs={{0,16},{1,9},{2,18},{3,11},{4,20},{5,13},{6,22},{7,15},{8,24},{9,1... | collective-permute-start | bytes 786440 | tf_op jit(solution)/shard_map/ppermute | solution.py:277
  3.7 9.5 %collective-permute-start = (bf16[256,512]{1,0:T(8,128)(2,1)}, bf16[256,512]{1,0:T(8,128)(2,1)S(1)}, u32[]{:S(2)}, u32[]{:S(2)}) collective-permute-start(bf16[256,512]{1,0:T(8,128)(2,1)} %f_ref.1), channel_id=1, source_target_pairs={{0,8},{1,17},{2,10},{3,19},{4,12},{5,21},{6,14},{7,23},{8,0},{9,25... | collective-permute-start | bytes 786440 | tf_op jit(solution)/shard_map/ppermute | solution.py:277
  6.1 10.9 %collective-permute-start.2 = (bf16[256,256]{1,0:T(8,128)(2,1)S(1)}, bf16[256,256]{1,0:T(8,128)(2,1)S(1)}, u32[]{:S(2)}, u32[]{:S(2)}) collective-permute-start(bf16[256,256]{1,0:T(8,128)(2,1)S(1)} %broadcast_select_fusion), channel_id=1, source_target_pairs={{0,8},{1,17},{2,10},{3,19},{4,12},{5,21},{6,14},{7,23},{8,0},{9,25... | collective-permute-start | bytes 393224 | tf_op jit(solution)/shard_map/ppermute | solution.py:277
  6.7 10.4 %collective-permute-start.3 = (bf16[256,256]{1,0:T(8,128)(2,1)S(1)}, bf16[256,256]{1,0:T(8,128)(2,1)S(1)}, u32[]{:S(2)}, u32[]{:S(2)}) collective-permute-start(bf16[256,256]{1,0:T(8,128)(2,1)S(1)} %broadcast_select_fusion), channel_id=1, source_target_pairs={{0,16},{1,9},{2,18},{3,11},{4,20},{5,13},{6,22},{7,15},{8,24},{9,1... | collective-permute-start | bytes 393224 | tf_op jit(solution)/shard_map/ppermute | solution.py:277
  6.8 11.1 %collective-permute-start.4 = (bf16[256,256]{1,0:T(8,128)(2,1)S(1)}, bf16[256,256]{1,0:T(8,128)(2,1)S(1)}, u32[]{:S(2)}, u32[]{:S(2)}) collective-permute-start(bf16[256,256]{1,0:T(8,128)(2,1)S(1)} %broadcast_select_fusion), channel_id=1, source_target_pairs={{0,24},{1,25},{2,26},{3,27},{4,28},{5,29},{6,30},{7,31},{8,16},{9,... | collective-permute-start | bytes 393224 | tf_op jit(solution)/shard_map/ppermute | solution.py:277
  10.6 5.2 %copy-start.6 = (s32[512]{0:T(512)S(1)}, s32[512]{0:T(512)}, u32[]{:S(2)}) copy-start(s32[512]{0:T(512)} %param.10) | copy-start | bytes 6148
  10.6 5.2 %copy-start.7 = (f32[512]{0:T(512)S(1)}, f32[512]{0:T(512)}, u32[]{:S(2)}) copy-start(f32[512]{0:T(512)} %param.11) | copy-start | bytes 6148
  10.6 7.3 %copy-start.2 = (bf16[256,512]{1,0:T(8,128)(2,1)S(1)}, bf16[256,512]{1,0:T(8,128)(2,1)}, u32[]{:S(2)}) copy-start(bf16[256,512]{1,0:T(8,128)(2,1)} %f_ref.1) | copy-start | bytes 786436
  10.6 5.2 %copy-start.3 = (bf16[256,172]{0,1:T(8,128)(2,1)S(1)}, bf16[256,172]{0,1:T(8,128)(2,1)}, u32[]{:S(2)}) copy-start(bf16[256,172]{0,1:T(8,128)(2,1)} %param.14) | copy-start | bytes 264196
  10.6 5.2 %copy-start.4 = (bf16[256,172]{0,1:T(8,128)(2,1)S(1)}, bf16[256,172]{0,1:T(8,128)(2,1)}, u32[]{:S(2)}) copy-start(bf16[256,172]{0,1:T(8,128)(2,1)} %param.15) | copy-start | bytes 264196
  10.6 5.2 %copy-start.5 = (s32[512,10]{0,1:T(8,128)S(1)}, s32[512,10]{0,1:T(8,128)}, u32[]{:S(2)}) copy-start(s32[512,10]{0,1:T(8,128)} %param.9) | copy-start | bytes 61444
  10.7 8.0 %collective-permute-start.5 = (bf16[128,512]{1,0:T(8,128)(2,1)S(1)}, bf16[128,512]{1,0:T(8,128)(2,1)S(1)}, u32[]{:S(2)}, u32[]{:S(2)}) collective-permute-start(bf16[128,512]{1,0:T(8,128)(2,1)S(1)} %slice.8), channel_id=1, source_target_pairs={{0,8},{1,17},{2,10},{3,19},{4,12},{5,21},{6,14},{7,23},{8,0},{9,25... | collective-permute-start | bytes 393224 | tf_op jit(solution)/shard_map/ppermute | solution.py:277
  13.1 4.7 %copy-start.1 = (bf16[256,256]{1,0:T(8,128)(2,1)S(1)}, bf16[256,256]{1,0:T(8,128)(2,1)}, u32[]{:S(2)}) copy-start(bf16[256,256]{1,0:T(8,128)(2,1)} %wn_ref.1) | copy-start | bytes 393220
  13.2 4.7 %copy-start = (bf16[256,256]{1,0:T(8,128)(2,1)S(1)}, bf16[256,256]{1,0:T(8,128)(2,1)}, u32[]{:S(2)}) copy-start(bf16[256,256]{1,0:T(8,128)(2,1)} %ws_ref.1) | copy-start | bytes 393220
  13.2 6.3 %collective-permute-start.6 = (bf16[128,512]{1,0:T(8,128)(2,1)S(1)}, bf16[128,512]{1,0:T(8,128)(2,1)S(1)}, u32[]{:S(2)}, u32[]{:S(2)}) collective-permute-start(bf16[128,512]{1,0:T(8,128)(2,1)S(1)} %slice.9), channel_id=1, source_target_pairs={{0,16},{1,9},{2,18},{3,11},{4,20},{5,13},{6,22},{7,15},{8,24},{9,1... | collective-permute-start | bytes 393224 | tf_op jit(solution)/shard_map/ppermute | solution.py:277
  17.0 2.7 %collective-permute-start.7 = (bf16[256,256]{1,0:T(8,128)(2,1)S(1)}, bf16[256,256]{1,0:T(8,128)(2,1)S(1)}, u32[]{:S(2)}, u32[]{:S(2)}) collective-permute-start(bf16[256,256]{1,0:T(8,128)(2,1)S(1)} %collective-permute-done.2.refs_3_), channel_id=1, source_target_pairs={{0,1},{1,0},{2,3},{3,2},{4,5},{5,4},{6,7},{7,6},{8,9},{9,8},{10,11... | collective-permute-start | bytes 393224 | tf_op jit(solution)/shard_map/ppermute | solution.py:259
  17.1 2.7 %collective-permute-start.8 = (bf16[256,256]{1,0:T(8,128)(2,1)S(1)}, bf16[256,256]{1,0:T(8,128)(2,1)S(1)}, u32[]{:S(2)}, u32[]{:S(2)}) collective-permute-start(bf16[256,256]{1,0:T(8,128)(2,1)S(1)} %collective-permute-done.3.refs_4_), channel_id=1, source_target_pairs={{0,1},{1,0},{2,3},{3,2},{4,5},{5,4},{6,7},{7,6},{8,9},{9,8},{10,11... | collective-permute-start | bytes 393224 | tf_op jit(solution)/shard_map/ppermute | solution.py:259
  17.9 1.9 %collective-permute-start.9 = (bf16[256,256]{1,0:T(8,128)(2,1)S(1)}, bf16[256,256]{1,0:T(8,128)(2,1)S(1)}, u32[]{:S(2)}, u32[]{:S(2)}) collective-permute-start(bf16[256,256]{1,0:T(8,128)(2,1)S(1)} %collective-permute-done.4.refs_2_), channel_id=1, source_target_pairs={{0,1},{1,0},{2,3},{3,2},{4,5},{5,4},{6,7},{7,6},{8,9},{9,8},{10,11... | collective-permute-start | bytes 393224 | tf_op jit(solution)/shard_map/ppermute | solution.py:259
  21.3 1.8 %collective-permute-start.11 = (f32[176,256]{1,0:T(8,128)S(1)}, f32[176,256]{1,0:T(8,128)S(1)}, u32[]{:S(2)}, u32[]{:S(2)}) collective-permute-start(f32[176,256]{1,0:T(8,128)S(1)} %get-tuple-element.42), channel_id=1, source_target_pairs={{0,1},{1,0},{2,3},{3,2},{4,5},{5,4},{6,7},{7,6},{8,9},{9,8},{10,11... | collective-permute-start | bytes 540680 | tf_op jit(solution)/shard_map/ppermute | solution.py:259
  22.5 2.7 %collective-permute-start.10 = (f32[4,64,256]{2,1,0:T(8,128)S(1)}, f32[4,64,256]{2,1,0:T(8,128)S(1)}, u32[]{:S(2)}, u32[]{:S(2)}) collective-permute-start(f32[4,64,256]{2,1,0:T(8,128)S(1)} %get-tuple-element.39), channel_id=1, source_target_pairs={{0,1},{1,0},{2,3},{3,2},{4,5},{5,4},{6,7},{7,6},{8,9},{9,8},{10,11... | collective-permute-start | bytes 786440 | tf_op jit(solution)/shard_map/ppermute | solution.py:259
  23.1 5.3 %collective-permute-start.12 = (bf16[176,256]{1,0:T(8,128)(2,1)S(1)}, bf16[176,256]{1,0:T(8,128)(2,1)S(1)}, u32[]{:S(2)}, u32[]{:S(2)}) collective-permute-start(bf16[176,256]{1,0:T(8,128)(2,1)S(1)} %shard_map.109.own_ref), channel_id=1, source_target_pairs={{0,2},{1,3},{2,0},{3,1},{4,6},{5,7},{6,4},{7,5},{8,10},{9,11},{10,... | collective-permute-start | bytes 270344 | tf_op jit(solution)/shard_map/ppermute | solution.py:259
  25.3 6.1 %collective-permute-start.15 = (bf16[128,256]{1,0:T(8,128)(2,1)S(1)}, bf16[128,256]{1,0:T(8,128)(2,1)S(1)}, u32[]{:S(2)}, u32[]{:S(2)}) collective-permute-start(bf16[128,256]{1,0:T(8,128)(2,1)S(1)} %get-tuple-element.43), channel_id=1, source_target_pairs={{0,2},{1,3},{2,0},{3,1},{4,6},{5,7},{6,4},{7,5},{8,10},{9,11},{10,... | collective-permute-start | bytes 196616 | tf_op jit(solution)/shard_map/ppermute | solution.py:259
  28.5 5.9 %collective-permute-start.13 = (bf16[176,256]{1,0:T(8,128)(2,1)S(1)}, bf16[176,256]{1,0:T(8,128)(2,1)S(1)}, u32[]{:S(2)}, u32[]{:S(2)}) collective-permute-start(bf16[176,256]{1,0:T(8,128)(2,1)S(1)} %shard_map.110.refs_0_), channel_id=1, source_target_pairs={{0,4},{1,5},{2,6},{3,7},{4,0},{5,1},{6,2},{7,3},{8,12},{9,13},{10,... | collective-permute-start | bytes 270344 | tf_op jit(solution)/shard_map/ppermute | solution.py:259
  31.5 4.9 %collective-permute-start.16 = (bf16[64,256]{1,0:T(8,128)(2,1)S(1)}, bf16[64,256]{1,0:T(8,128)(2,1)S(1)}, u32[]{:S(2)}, u32[]{:S(2)}) collective-permute-start(bf16[64,256]{1,0:T(8,128)(2,1)S(1)} %get-tuple-element.45), channel_id=1, source_target_pairs={{0,4},{1,5},{2,6},{3,7},{4,0},{5,1},{6,2},{7,3},{8,12},{9,13},{10,... | collective-permute-start | bytes 98312 | tf_op jit(solution)/shard_map/ppermute | solution.py:259
  34.5 1.9 %collective-permute-start.14 = (f32[176,256]{1,0:T(8,128)S(1)}, f32[176,256]{1,0:T(8,128)S(1)}, u32[]{:S(2)}, u32[]{:S(2)}) collective-permute-start(f32[176,256]{1,0:T(8,128)S(1)} %shard_map.111.own_ref), channel_id=1, source_target_pairs={{0,1},{1,0},{2,3},{3,2},{4,5},{5,4},{6,7},{7,6},{8,9},{9,8},{10,11... | collective-permute-start | bytes 540680 | tf_op jit(solution)/shard_map/ppermute | solution.py:259

commit v9 on v8

--- a/solution.py
+++ b/solution.py
@@ -205,12 +205,16 @@
     out_ref[...] = split_rows(jnp.where(row >= classes, whole, total), classes)
 
 
-def chunk_kernel(groups, z_ref, keep_ref, recv_ref, kept_ref, send_ref):
-    z, chunk = z_ref[0], keep_ref.shape[1]
+def chunk_kernel(groups, z_ref, core_ref, keep_ref, recv_ref, kept_ref, send_ref):
+    z, core, chunk = z_ref[0], core_ref[0], keep_ref.shape[1]
+
+    def total(step):
+        group = jnp.bitwise_xor(z, step + core * (swapped(step, groups) - step))
+        return keep_ref[group] + recv_ref[group]
+
     for i in range(groups // 2):
-        here, there = jnp.bitwise_xor(z, 2 * i), jnp.bitwise_xor(z, 2 * i + 1)
-        kept_ref[i] = keep_ref[here] + recv_ref[here]
-        send_ref[i * chunk : (i + 1) * chunk] = (keep_ref[there] + recv_ref[there]).astype(BF16)
+        kept_ref[i] = total(2 * i)
+        send_ref[i * chunk : (i + 1) * chunk] = total(2 * i + 1).astype(BF16)
 
 
 def fold_first_kernel(own_ref, recv_ref, kept_ref, send_ref):
@@ -241,10 +245,10 @@
 
 def out_kernel(classes, core_ref, own_ref, other_ref, first_ref, grad1_ref, grad2_ref, loss_ref):
     first = core_ref[0] == 0
-    loss, norm = scalars(own_ref[...], classes)
-    own = own_ref[:classes, :] / norm
-    other = other_ref[:classes, :] / norm
-    for slot, half in enumerate((jnp.where(first, own, other), jnp.where(first, other, own))):
+    halves = jnp.where(first, own_ref[...], other_ref[...]), jnp.where(first, other_ref[...], own_ref[...])
+    loss, norm = scalars(halves[0], classes)
+    for slot, half in enumerate(halves):
+        half = half[:classes] / norm
         lanes = half.shape[1] // 128
         for j in range(lanes):
             grad2_ref[pl.ds(2 * j + slot, classes, stride=2 * lanes), :] = half[:, 128 * j : 128 * (j + 1)]
@@ -275,6 +279,15 @@
             other = f ^ (step if d % 2 == 0 else swapped(step, count))
             pairs.append((f * wide + d, other * wide + d))
     return lax.ppermute(value, ("feat", "dp"), pairs)
+
+
+def fold_hop(value, step):
+    count = lax.axis_size("dp")
+    pairs = []
+    for d in range(count):
+        z = d // 2 ^ (step if d % 2 == 0 else swapped(step, count // 2))
+        pairs.append((d, 2 * z + d % 2))
+    return lax.ppermute(value, "dp", pairs)
 
 
 def gather_parts(block, count):
@@ -369,12 +382,12 @@
     kept1, send1 = call(
         functools.partial(chunk_kernel, groups),
         [shape((left, chunk, hid), F32), shape((left * chunk, hid), BF16)],
-        [z, keep1, recv1],
-        smem=(0,),
-    )
-    step = 2
+        [z, core, keep1, recv1],
+        smem=(0, 1),
+    )
+    step = 1
     while left > 1:
-        far2, far1 = exchange(own2, "dp", step), exchange(send1, "dp", step)
+        far2, far1 = fold_hop(own2, step), fold_hop(send1, step)
         left, step = left // 2, 2 * step
         (own2,) = call(
             functools.partial(fold_second_kernel, classes), [shape((padded, hid), BF16)], [kept1, own2, far2]
@@ -384,7 +397,7 @@
             [shape((left, chunk, hid), F32), shape((left * chunk, hid), BF16)],
             [kept1, far1],
         )
-    far2, far1 = exchange(own2, "dp", step), exchange(send1, "dp", step)
+    far2, far1 = fold_hop(own2, step), fold_hop(send1, step)
     (total2,) = call(second_sum_kernel, [shape((padded, hid), F32)], [own2, far2])
     other2 = exchange(total2, "dp", 1)
     (sum1,) = call(first_sum_kernel, [shape((chunk, hid), F32)], [kept1, far1], flops=300 * rows * nodes * hid)

time: 37.4 us -> 37.3 us (level)
    ppermute x0 -> x4, starting transfers between devices: none -> 7.13 us  [fold_hop(): return lax.ppermute(value, 'dp', pairs)]
    ppermute x10 -> x6, starting transfers between devices: 8.32 us -> 1.26 us  [exchange(): return lax.ppermute(value, axis, [(i, i ^ step) for i in range(size)])]
    ppermute x10 -> x6, waiting for transfers between devices: 5.95 us -> 0.02 us  [exchange(): return lax.ppermute(value, axis, [(i, i ^ step) for i in range(size)])]
    ppermute x0 -> x4, waiting for transfers between devices: none -> 5.76 us  [fold_hop(): return lax.ppermute(value, 'dp', pairs)]
where the time goes in v9:
time: 37.3 us; the launch traced here: 37.2 us
  starting transfers between devices  21.6 us (58%)
  waiting for transfers between devices  8.16 us (22%)
  Pallas kernels  5.59 us (15%)
  other arithmetic  0.92 us (2%)
  between operations  0.83 us (2%)
    ppermute x7, starting transfers between devices, hop(): return lax.ppermute(value, ('feat', 'dp'), pairs)  13.2 us
    ppermute x4, starting transfers between devices, fold_hop(): return lax.ppermute(value, 'dp', pairs)  7.13 us
    ppermute x4, waiting for transfers between devices, fold_hop(): return lax.ppermute(value, 'dp', pairs)  5.76 us
    pallas_call x12, Pallas kernels, call(): pl.pallas_call(kernel, out_shape=outs if final else [pltpu.VMEM(o.shape,...  5.59 us
    ppermute x7, waiting for transfers between devices, hop(): return lax.ppermute(value, ('feat', 'dp'), pairs)  2.38 us
    ppermute x6, starting transfers between devices, exchange(): return lax.ppermute(value, axis, [(i, i ^ step) for i in range(size)])  1.26 us
    select_n x1, other arithmetic, on_device(): mine_own = jnp.where(core[0] == 0, w1_self, w1_neigh)  0.92 us
  transfers between devices with their start and end apart: 17, of which 7 were waited for; matrix products, arithmetic and copies ran while one was open for 3% of the time, Pallas kernels for 8%

profile of v9, /device:TPU:0, one launch (start us, length us, event | category | flops | bytes accessed | tf_op | source)
XLA Modules:
  0.0 37.2 jit_solution(5279252392324779250)
XLA Ops:
  0.6 3.0 %collective-permute-start.1 = (bf16[256,512]{1,0:T(8,128)(2,1)}, bf16[256,512]{1,0:T(8,128)(2,1)S(1)}, u32[]{:S(2)}, u32[]{:S(2)}) collective-permute-start(bf16[256,512]{1,0:T(8,128)(2,1)} %f_ref.1), channel_id=1, source_target_pairs={{0,16},{1,9},{2,18},{3,11},{4,20},{5,13},{6,22},{7,15},{8,24},{9,1... | collective-permute-start | bytes 786440 | tf_op jit(solution)/shard_map/ppermute | solution.py:281
  3.7 1.5 %collective-permute-start = (bf16[256,512]{1,0:T(8,128)(2,1)}, bf16[256,512]{1,0:T(8,128)(2,1)S(1)}, u32[]{:S(2)}, u32[]{:S(2)}) collective-permute-start(bf16[256,512]{1,0:T(8,128)(2,1)} %f_ref.1), channel_id=1, source_target_pairs={{0,8},{1,17},{2,10},{3,19},{4,12},{5,21},{6,14},{7,23},{8,0},{9,25... | collective-permute-start | bytes 786440 | tf_op jit(solution)/shard_map/ppermute | solution.py:281
  5.2 0.9 %broadcast_select_fusion = bf16[256,256]{1,0:T(8,128)(2,1)S(1)} fusion(bf16[256,256]{1,0:T(8,128)(2,1)} %ws_ref.1, bf16[256,256]{1,0:T(8,128)(2,1)} %wn_ref.1, pred[]{:T(512)S(6)} %eq.5), kind=kLoop, calls=%fused_computation | loop fusion | flops 65536 | bytes 393217 | tf_op jit(solution)/shard_map/jit(_where)/select_n | solution.py:323
  6.1 0.6 %collective-permute-start.2 = (bf16[256,256]{1,0:T(8,128)(2,1)S(1)}, bf16[256,256]{1,0:T(8,128)(2,1)S(1)}, u32[]{:S(2)}, u32[]{:S(2)}) collective-permute-start(bf16[256,256]{1,0:T(8,128)(2,1)S(1)} %broadcast_select_fusion), channel_id=1, source_target_pairs={{0,8},{1,17},{2,10},{3,19},{4,12},{5,21},{6,14},{7,23},{8,0},{9,25... | collective-permute-start | bytes 393224 | tf_op jit(solution)/shard_map/ppermute | solution.py:281
  6.7 0.1 collective-permute-start.3
  6.8 2.9 %collective-permute-start.4 = (bf16[256,256]{1,0:T(8,128)(2,1)S(1)}, bf16[256,256]{1,0:T(8,128)(2,1)S(1)}, u32[]{:S(2)}, u32[]{:S(2)}) collective-permute-start(bf16[256,256]{1,0:T(8,128)(2,1)S(1)} %broadcast_select_fusion), channel_id=1, source_target_pairs={{0,24},{1,25},{2,26},{3,27},{4,28},{5,29},{6,30},{7,31},{8,16},{9,... | collective-permute-start | bytes 393224 | tf_op jit(solution)/shard_map/ppermute | solution.py:281
  9.6 1.0 %collective-permute-done.1.refs_2_.refs_1_ = bf16[256,512]{1,0:T(8,128)(2,1)S(1)} collective-permute-done((bf16[256,512]{1,0:T(8,128)(2,1)}, bf16[256,512]{1,0:T(8,128)(2,1)S(1)}, u32[]{:S(2)}, u32[]{:S(2)}) %collective-permute-start.1) | collective-permute-done | bytes 262176 | tf_op jit(solution)/shard_map/ppermute | solution.py:281
  10.6 0.0 copy-start.6
  10.6 0.0 copy-start.7
  10.6 0.0 copy-start.2
  10.6 0.0 copy-start.3
  10.6 0.0 copy-start.4
  10.6 0.0 copy-start.5
  10.7 2.5 %collective-permute-start.5 = (bf16[128,512]{1,0:T(8,128)(2,1)S(1)}, bf16[128,512]{1,0:T(8,128)(2,1)S(1)}, u32[]{:S(2)}, u32[]{:S(2)}) collective-permute-start(bf16[128,512]{1,0:T(8,128)(2,1)S(1)} %slice.8), channel_id=1, source_target_pairs={{0,8},{1,17},{2,10},{3,19},{4,12},{5,21},{6,14},{7,23},{8,0},{9,25... | collective-permute-start | bytes 393224 | tf_op jit(solution)/shard_map/ppermute | solution.py:281
  13.1 0.0 collective-permute-done.refs_1_.refs_0_
  13.1 0.0 copy-start.1
  13.2 0.0 copy-start
  13.2 2.6 %collective-permute-start.6 = (bf16[128,512]{1,0:T(8,128)(2,1)S(1)}, bf16[128,512]{1,0:T(8,128)(2,1)S(1)}, u32[]{:S(2)}, u32[]{:S(2)}) collective-permute-start(bf16[128,512]{1,0:T(8,128)(2,1)S(1)} %slice.9), channel_id=1, source_target_pairs={{0,16},{1,9},{2,18},{3,11},{4,20},{5,13},{6,22},{7,15},{8,24},{9,1... | collective-permute-start | bytes 393224 | tf_op jit(solution)/shard_map/ppermute | solution.py:281
  15.8 0.0 copy-done.6
  15.8 0.0 copy-done.7
  15.8 0.0 copy-done.3
  15.8 0.0 copy-done.4
  15.8 0.0 copy-done.5
  15.8 1.1 %shard_map.105 = (bf16[512,512]{1,0:T(8,128)(2,1)S(1)}, s32[1,512]{1,0:T(1,128)S(1)}, f32[1,512]{1,0:T(1,128)S(1)}, bf16[172,256]{1,0:T(8,128)(2,1)S(1)}, bf16[172,256]{1,0:T(8,128)(2,1)S(1)}) custom-call(s32[10,512]{1,0:T(8,128)S(1)} %bitcast.15, s32[1,512]{1,0:T(1,128)S(1)} %bitcast.16, f32[1,512]{1,0:T(1,128)S(1)} %bitcast.17, ...), custom_call_target="tpu_custom_call" | custom-call | flops 2621440 | bytes 905216 | tf_op jit(solution)/shard_map/pallas_call | solution.py:38
  17.0 0.0 collective-permute-done.2.refs_3_
  17.0 0.1 collective-permute-start.7
  17.1 0.0 collective-permute-done.3.refs_4_
  17.1 0.5 %collective-permute-start.8 = (bf16[256,256]{1,0:T(8,128)(2,1)S(1)}, bf16[256,256]{1,0:T(8,128)(2,1)S(1)}, u32[]{:S(2)}, u32[]{:S(2)}) collective-permute-start(bf16[256,256]{1,0:T(8,128)(2,1)S(1)} %collective-permute-done.3.refs_4_), channel_id=1, source_target_pairs={{0,1},{1,0},{2,3},{3,2},{4,5},{5,4},{6,7},{7,6},{8,9},{9,8},{10,11... | collective-permute-start | bytes 393224 | tf_op jit(solution)/shard_map/ppermute | solution.py:263
  17.6 0.3 collective-permute-done.4.refs_2_
  17.9 0.0 collective-permute-start.9
  17.9 0.0 copy-done.2
  17.9 0.0 copy-done.1
  17.9 0.0 copy-done
  17.9 0.5 %shard_map.103 = (f32[256,512]{1,0:T(8,128)S(1)}, f32[256,512]{1,0:T(8,128)S(1)}, f32[256,512]{1,0:T(8,128)S(1)}) custom-call(s32[1]{0:T(128)} %bitcast.core_ref.refs_3_, bf16[256,256]{1,0:T(8,128)(2,1)S(1)} %copy-done, bf16[256,256]{1,0:T(8,128)(2,1)S(1)} %copy-done.1, bf16[256,512]{1,0:T(8,128)(2,1)S(1)} %copy-done.2, ...), custom_call_target="tpu_custom_call" | custom-call | flops 268435456 | bytes 2883588 | tf_op jit(solution)/shard_map/pallas_call | solution.py:38
  18.4 0.3 collective-permute-done.5.refs_3_
  18.7 0.8 %collective-permute-done.6.refs_4_ = bf16[128,512]{1,0:T(8,128)(2,1)S(1)} collective-permute-done((bf16[128,512]{1,0:T(8,128)(2,1)S(1)}, bf16[128,512]{1,0:T(8,128)(2,1)S(1)}, u32[]{:S(2)}, u32[]{:S(2)}) %collective-permute-start.6) | collective-permute-done | bytes 131104 | tf_op jit(solution)/shard_map/ppermute | solution.py:281
  19.5 0.2 shard_map.104
  19.7 0.0 collective-permute-done.7.refs_11_
  19.7 0.0 collective-permute-done.8.refs_12_
  19.7 0.0 collective-permute-done.9.refs_13_
  19.7 1.6 %shard_map.106 = (f32[176,256]{1,0:T(8,128)S(1)}, f32[176,256]{1,0:T(8,128)S(1)}, bf16[172,512]{1,0:T(8,128)(2,1)S(1)}, bf16[256,512]{1,0:T(8,128)(2,1)S(1)}) custom-call(bf16[256,512]{1,0:T(8,128)(2,1)S(1)} %collective-permute-done.refs_1_.refs_0_, bf16[256,512]{1,0:T(8,128)(2,1)S(1)} %collective-permute-done.1.refs_2_.refs_1_, ...), custom_call_target="tpu_custom_call" | custom-call | flops 805306368 | bytes 3731460 | tf_op jit(solution)/shard_map/pallas_call | solution.py:38
  21.3 0.1 collective-permute-start.11
  21.4 1.1 %shard_map.107 = (f32[4,64,256]{2,1,0:T(8,128)S(1)}, f32[4,64,256]{2,1,0:T(8,128)S(1)}) custom-call(s32[1]{0:T(128)} %bitcast.core_ref.refs_3_, bf16[172,512]{1,0:T(8,128)(2,1)S(1)} %get-tuple-element.36.g_ref, bf16[256,512]{1,0:T(8,128)(2,1)S(1)} %get-tuple-element.37.hidden_ref, bf16[512,512]{1,0:T(8,128)(2,1)S(1)} %get-tuple-element.31.refs_6_.at_ref, ...), custom_call_target="tpu_custom_call" | custom-call | flops 402653184 | bytes 1925124 | tf_op jit(solution)/shard_map/pallas_call | solution.py:38
  22.5 0.6 %collective-permute-start.10 = (f32[4,64,256]{2,1,0:T(8,128)S(1)}, f32[4,64,256]{2,1,0:T(8,128)S(1)}, u32[]{:S(2)}, u32[]{:S(2)}) collective-permute-start(f32[4,64,256]{2,1,0:T(8,128)S(1)} %get-tuple-element.39), channel_id=1, source_target_pairs={{0,1},{1,0},{2,3},{3,2},{4,5},{5,4},{6,7},{7,6},{8,9},{9,8},{10,11... | collective-permute-start | bytes 786440 | tf_op jit(solution)/shard_map/ppermute | solution.py:263
  23.1 0.0 collective-permute-done.11.recv_ref
  23.1 2.1 %collective-permute-start.12 = (bf16[176,256]{1,0:T(8,128)(2,1)S(1)}, bf16[176,256]{1,0:T(8,128)(2,1)S(1)}, u32[]{:S(2)}, u32[]{:S(2)}) collective-permute-start(bf16[176,256]{1,0:T(8,128)(2,1)S(1)} %shard_map.109.own_ref), channel_id=1, source_target_pairs={{0,2},{1,5},{2,0},{3,7},{4,6},{5,1},{6,4},{7,3},{8,10},{9,13},{10,... | collective-permute-start | bytes 270344 | tf_op jit(solution)/shard_map/ppermute | solution.py:290
  25.3 0.0 collective-permute-done.10.recv_ref
  25.3 1.1 %collective-permute-start.15 = (bf16[128,256]{1,0:T(8,128)(2,1)S(1)}, bf16[128,256]{1,0:T(8,128)(2,1)S(1)}, u32[]{:S(2)}, u32[]{:S(2)}) collective-permute-start(bf16[128,256]{1,0:T(8,128)(2,1)S(1)} %get-tuple-element.43), channel_id=1, source_target_pairs={{0,2},{1,5},{2,0},{3,7},{4,6},{5,1},{6,4},{7,3},{8,10},{9,13},{10,... | collective-permute-start | bytes 196616 | tf_op jit(solution)/shard_map/ppermute | solution.py:290
  26.4 2.3 %collective-permute-done.12.recv_ref = bf16[176,256]{1,0:T(8,128)(2,1)S(1)} collective-permute-done((bf16[176,256]{1,0:T(8,128)(2,1)S(1)}, bf16[176,256]{1,0:T(8,128)(2,1)S(1)}, u32[]{:S(2)}, u32[]{:S(2)}) %collective-permute-start.12) | collective-permute-done | bytes 90144 | tf_op jit(solution)/shard_map/ppermute | solution.py:290
  28.8 2.1 %collective-permute-start.13 = (bf16[176,256]{1,0:T(8,128)(2,1)S(1)}, bf16[176,256]{1,0:T(8,128)(2,1)S(1)}, u32[]{:S(2)}, u32[]{:S(2)}) collective-permute-start(bf16[176,256]{1,0:T(8,128)(2,1)S(1)} %shard_map.110.refs_0_), channel_id=1, source_target_pairs={{0,4},{1,3},{2,6},{3,1},{4,0},{5,7},{6,2},{7,5},{8,12},{9,11},{10,... | collective-permute-start | bytes 270344 | tf_op jit(solution)/shard_map/ppermute | solution.py:290
  30.9 0.0 collective-permute-done.15.recv_ref
  31.0 1.7 %collective-permute-start.16 = (bf16[64,256]{1,0:T(8,128)(2,1)S(1)}, bf16[64,256]{1,0:T(8,128)(2,1)S(1)}, u32[]{:S(2)}, u32[]{:S(2)}) collective-permute-start(bf16[64,256]{1,0:T(8,128)(2,1)S(1)} %get-tuple-element.45), channel_id=1, source_target_pairs={{0,4},{1,3},{2,6},{3,1},{4,0},{5,7},{6,2},{7,5},{8,12},{9,11},{10,... | collective-permute-start | bytes 98312 | tf_op jit(solution)/shard_map/ppermute | solution.py:290
  32.7 1.7 %collective-permute-done.13.refs_1_ = bf16[176,256]{1,0:T(8,128)(2,1)S(1)} collective-permute-done((bf16[176,256]{1,0:T(8,128)(2,1)S(1)}, bf16[176,256]{1,0:T(8,128)(2,1)S(1)}, u32[]{:S(2)}, u32[]{:S(2)}) %collective-permute-start.13) | collective-permute-done | bytes 90144 | tf_op jit(solution)/shard_map/ppermute | solution.py:290
  34.4 0.1 collective-permute-start.14
  34.5 1.8 %collective-permute-done.16.refs_0_ = bf16[64,256]{1,0:T(8,128)(2,1)S(1)} collective-permute-done((bf16[64,256]{1,0:T(8,128)(2,1)S(1)}, bf16[64,256]{1,0:T(8,128)(2,1)S(1)}, u32[]{:S(2)}, u32[]{:S(2)}) %collective-permute-start.16) | collective-permute-done | bytes 32800 | tf_op jit(solution)/shard_map/ppermute | solution.py:290
  36.2 0.0 collective-permute-done.14.other_ref
  36.3 0.9 %shard_map.114 = (f32[2,32,256]{2,1,0:T(8,128)}, f32[688,128]{1,0:T(8,128)}, f32[1,1]{1,0:T(1,128)}) custom-call(s32[1]{0:T(128)} %bitcast.core_ref.refs_3_, f32[176,256]{1,0:T(8,128)S(1)} %shard_map.111.own_ref, f32[176,256]{1,0:T(8,128)S(1)} %collective-permute-done.14.other_ref, f32[64,256]{1,0:T(8,128)S(1)} %shard_map.113.first_ref), custom_call_target="tpu_custom_call" | custom-call | bytes 843784 | tf_op jit(solution)/shard_map/pallas_call | solution.py:38
  (8 shorter events, 0.2 us)
Async XLA Ops:
  0.6 10.0 %collective-permute-start.1 = (bf16[256,512]{1,0:T(8,128)(2,1)}, bf16[256,512]{1,0:T(8,128)(2,1)S(1)}, u32[]{:S(2)}, u32[]{:S(2)}) collective-permute-start(bf16[256,512]{1,0:T(8,128)(2,1)} %f_ref.1), channel_id=1, source_target_pairs={{0,16},{1,9},{2,18},{3,11},{4,20},{5,13},{6,22},{7,15},{8,24},{9,1... | collective-permute-start | bytes 786440 | tf_op jit(solution)/shard_map/ppermute | solution.py:281
  3.7 9.5 %collective-permute-start = (bf16[256,512]{1,0:T(8,128)(2,1)}, bf16[256,512]{1,0:T(8,128)(2,1)S(1)}, u32[]{:S(2)}, u32[]{:S(2)}) collective-permute-start(bf16[256,512]{1,0:T(8,128)(2,1)} %f_ref.1), channel_id=1, source_target_pairs={{0,8},{1,17},{2,10},{3,19},{4,12},{5,21},{6,14},{7,23},{8,0},{9,25... | collective-permute-start | bytes 786440 | tf_op jit(solution)/shard_map/ppermute | solution.py:281
  6.1 10.9 %collective-permute-start.2 = (bf16[256,256]{1,0:T(8,128)(2,1)S(1)}, bf16[256,256]{1,0:T(8,128)(2,1)S(1)}, u32[]{:S(2)}, u32[]{:S(2)}) collective-permute-start(bf16[256,256]{1,0:T(8,128)(2,1)S(1)} %broadcast_select_fusion), channel_id=1, source_target_pairs={{0,8},{1,17},{2,10},{3,19},{4,12},{5,21},{6,14},{7,23},{8,0},{9,25... | collective-permute-start | bytes 393224 | tf_op jit(solution)/shard_map/ppermute | solution.py:281
  6.7 10.4 %collective-permute-start.3 = (bf16[256,256]{1,0:T(8,128)(2,1)S(1)}, bf16[256,256]{1,0:T(8,128)(2,1)S(1)}, u32[]{:S(2)}, u32[]{:S(2)}) collective-permute-start(bf16[256,256]{1,0:T(8,128)(2,1)S(1)} %broadcast_select_fusion), channel_id=1, source_target_pairs={{0,16},{1,9},{2,18},{3,11},{4,20},{5,13},{6,22},{7,15},{8,24},{9,1... | collective-permute-start | bytes 393224 | tf_op jit(solution)/shard_map/ppermute | solution.py:281
  6.8 11.1 %collective-permute-start.4 = (bf16[256,256]{1,0:T(8,128)(2,1)S(1)}, bf16[256,256]{1,0:T(8,128)(2,1)S(1)}, u32[]{:S(2)}, u32[]{:S(2)}) collective-permute-start(bf16[256,256]{1,0:T(8,128)(2,1)S(1)} %broadcast_select_fusion), channel_id=1, source_target_pairs={{0,24},{1,25},{2,26},{3,27},{4,28},{5,29},{6,30},{7,31},{8,16},{9,... | collective-permute-start | bytes 393224 | tf_op jit(solution)/shard_map/ppermute | solution.py:281
  10.6 5.2 %copy-start.6 = (s32[512]{0:T(512)S(1)}, s32[512]{0:T(512)}, u32[]{:S(2)}) copy-start(s32[512]{0:T(512)} %param.10) | copy-start | bytes 6148
  10.6 5.2 %copy-start.7 = (f32[512]{0:T(512)S(1)}, f32[512]{0:T(512)}, u32[]{:S(2)}) copy-start(f32[512]{0:T(512)} %param.11) | copy-start | bytes 6148
  10.6 7.3 %copy-start.2 = (bf16[256,512]{1,0:T(8,128)(2,1)S(1)}, bf16[256,512]{1,0:T(8,128)(2,1)}, u32[]{:S(2)}) copy-start(bf16[256,512]{1,0:T(8,128)(2,1)} %f_ref.1) | copy-start | bytes 786436
  10.6 5.2 %copy-start.3 = (bf16[256,172]{0,1:T(8,128)(2,1)S(1)}, bf16[256,172]{0,1:T(8,128)(2,1)}, u32[]{:S(2)}) copy-start(bf16[256,172]{0,1:T(8,128)(2,1)} %param.14) | copy-start | bytes 264196
  10.6 5.2 %copy-start.4 = (bf16[256,172]{0,1:T(8,128)(2,1)S(1)}, bf16[256,172]{0,1:T(8,128)(2,1)}, u32[]{:S(2)}) copy-start(bf16[256,172]{0,1:T(8,128)(2,1)} %param.15) | copy-start | bytes 264196
  10.6 5.2 %copy-start.5 = (s32[512,10]{0,1:T(8,128)S(1)}, s32[512,10]{0,1:T(8,128)}, u32[]{:S(2)}) copy-start(s32[512,10]{0,1:T(8,128)} %param.9) | copy-start | bytes 61444
  10.7 8.0 %collective-permute-start.5 = (bf16[128,512]{1,0:T(8,128)(2,1)S(1)}, bf16[128,512]{1,0:T(8,128)(2,1)S(1)}, u32[]{:S(2)}, u32[]{:S(2)}) collective-permute-start(bf16[128,512]{1,0:T(8,128)(2,1)S(1)} %slice.8), channel_id=1, source_target_pairs={{0,8},{1,17},{2,10},{3,19},{4,12},{5,21},{6,14},{7,23},{8,0},{9,25... | collective-permute-start | bytes 393224 | tf_op jit(solution)/shard_map/ppermute | solution.py:281
  13.1 4.7 %copy-start.1 = (bf16[256,256]{1,0:T(8,128)(2,1)S(1)}, bf16[256,256]{1,0:T(8,128)(2,1)}, u32[]{:S(2)}) copy-start(bf16[256,256]{1,0:T(8,128)(2,1)} %wn_ref.1) | copy-start | bytes 393220
  13.2 4.7 %copy-start = (bf16[256,256]{1,0:T(8,128)(2,1)S(1)}, bf16[256,256]{1,0:T(8,128)(2,1)}, u32[]{:S(2)}) copy-start(bf16[256,256]{1,0:T(8,128)(2,1)} %ws_ref.1) | copy-start | bytes 393220
  13.2 6.3 %collective-permute-start.6 = (bf16[128,512]{1,0:T(8,128)(2,1)S(1)}, bf16[128,512]{1,0:T(8,128)(2,1)S(1)}, u32[]{:S(2)}, u32[]{:S(2)}) collective-permute-start(bf16[128,512]{1,0:T(8,128)(2,1)S(1)} %slice.9), channel_id=1, source_target_pairs={{0,16},{1,9},{2,18},{3,11},{4,20},{5,13},{6,22},{7,15},{8,24},{9,1... | collective-permute-start | bytes 393224 | tf_op jit(solution)/shard_map/ppermute | solution.py:281
  17.0 2.7 %collective-permute-start.7 = (bf16[256,256]{1,0:T(8,128)(2,1)S(1)}, bf16[256,256]{1,0:T(8,128)(2,1)S(1)}, u32[]{:S(2)}, u32[]{:S(2)}) collective-permute-start(bf16[256,256]{1,0:T(8,128)(2,1)S(1)} %collective-permute-done.2.refs_3_), channel_id=1, source_target_pairs={{0,1},{1,0},{2,3},{3,2},{4,5},{5,4},{6,7},{7,6},{8,9},{9,8},{10,11... | collective-permute-start | bytes 393224 | tf_op jit(solution)/shard_map/ppermute | solution.py:263
  17.1 2.7 %collective-permute-start.8 = (bf16[256,256]{1,0:T(8,128)(2,1)S(1)}, bf16[256,256]{1,0:T(8,128)(2,1)S(1)}, u32[]{:S(2)}, u32[]{:S(2)}) collective-permute-start(bf16[256,256]{1,0:T(8,128)(2,1)S(1)} %collective-permute-done.3.refs_4_), channel_id=1, source_target_pairs={{0,1},{1,0},{2,3},{3,2},{4,5},{5,4},{6,7},{7,6},{8,9},{9,8},{10,11... | collective-permute-start | bytes 393224 | tf_op jit(solution)/shard_map/ppermute | solution.py:263
  17.9 1.9 %collective-permute-start.9 = (bf16[256,256]{1,0:T(8,128)(2,1)S(1)}, bf16[256,256]{1,0:T(8,128)(2,1)S(1)}, u32[]{:S(2)}, u32[]{:S(2)}) collective-permute-start(bf16[256,256]{1,0:T(8,128)(2,1)S(1)} %collective-permute-done.4.refs_2_), channel_id=1, source_target_pairs={{0,1},{1,0},{2,3},{3,2},{4,5},{5,4},{6,7},{7,6},{8,9},{9,8},{10,11... | collective-permute-start | bytes 393224 | tf_op jit(solution)/shard_map/ppermute | solution.py:263
  21.3 1.8 %collective-permute-start.11 = (f32[176,256]{1,0:T(8,128)S(1)}, f32[176,256]{1,0:T(8,128)S(1)}, u32[]{:S(2)}, u32[]{:S(2)}) collective-permute-start(f32[176,256]{1,0:T(8,128)S(1)} %get-tuple-element.42), channel_id=1, source_target_pairs={{0,1},{1,0},{2,3},{3,2},{4,5},{5,4},{6,7},{7,6},{8,9},{9,8},{10,11... | collective-permute-start | bytes 540680 | tf_op jit(solution)/shard_map/ppermute | solution.py:263
  22.5 2.7 %collective-permute-start.10 = (f32[4,64,256]{2,1,0:T(8,128)S(1)}, f32[4,64,256]{2,1,0:T(8,128)S(1)}, u32[]{:S(2)}, u32[]{:S(2)}) collective-permute-start(f32[4,64,256]{2,1,0:T(8,128)S(1)} %get-tuple-element.39), channel_id=1, source_target_pairs={{0,1},{1,0},{2,3},{3,2},{4,5},{5,4},{6,7},{7,6},{8,9},{9,8},{10,11... | collective-permute-start | bytes 786440 | tf_op jit(solution)/shard_map/ppermute | solution.py:263
  23.1 5.6 %collective-permute-start.12 = (bf16[176,256]{1,0:T(8,128)(2,1)S(1)}, bf16[176,256]{1,0:T(8,128)(2,1)S(1)}, u32[]{:S(2)}, u32[]{:S(2)}) collective-permute-start(bf16[176,256]{1,0:T(8,128)(2,1)S(1)} %shard_map.109.own_ref), channel_id=1, source_target_pairs={{0,2},{1,5},{2,0},{3,7},{4,6},{5,1},{6,4},{7,3},{8,10},{9,13},{10,... | collective-permute-start | bytes 270344 | tf_op jit(solution)/shard_map/ppermute | solution.py:290
  25.3 5.6 %collective-permute-start.15 = (bf16[128,256]{1,0:T(8,128)(2,1)S(1)}, bf16[128,256]{1,0:T(8,128)(2,1)S(1)}, u32[]{:S(2)}, u32[]{:S(2)}) collective-permute-start(bf16[128,256]{1,0:T(8,128)(2,1)S(1)} %get-tuple-element.43), channel_id=1, source_target_pairs={{0,2},{1,5},{2,0},{3,7},{4,6},{5,1},{6,4},{7,3},{8,10},{9,13},{10,... | collective-permute-start | bytes 196616 | tf_op jit(solution)/shard_map/ppermute | solution.py:290
  28.8 5.6 %collective-permute-start.13 = (bf16[176,256]{1,0:T(8,128)(2,1)S(1)}, bf16[176,256]{1,0:T(8,128)(2,1)S(1)}, u32[]{:S(2)}, u32[]{:S(2)}) collective-permute-start(bf16[176,256]{1,0:T(8,128)(2,1)S(1)} %shard_map.110.refs_0_), channel_id=1, source_target_pairs={{0,4},{1,3},{2,6},{3,1},{4,0},{5,7},{6,2},{7,5},{8,12},{9,11},{10,... | collective-permute-start | bytes 270344 | tf_op jit(solution)/shard_map/ppermute | solution.py:290
  31.0 5.3 %collective-permute-start.16 = (bf16[64,256]{1,0:T(8,128)(2,1)S(1)}, bf16[64,256]{1,0:T(8,128)(2,1)S(1)}, u32[]{:S(2)}, u32[]{:S(2)}) collective-permute-start(bf16[64,256]{1,0:T(8,128)(2,1)S(1)} %get-tuple-element.45), channel_id=1, source_target_pairs={{0,4},{1,3},{2,6},{3,1},{4,0},{5,7},{6,2},{7,5},{8,12},{9,11},{10,... | collective-permute-start | bytes 98312 | tf_op jit(solution)/shard_map/ppermute | solution.py:290
  34.4 1.9 %collective-permute-start.14 = (f32[176,256]{1,0:T(8,128)S(1)}, f32[176,256]{1,0:T(8,128)S(1)}, u32[]{:S(2)}, u32[]{:S(2)}) collective-permute-start(f32[176,256]{1,0:T(8,128)S(1)} %shard_map.111.own_ref), channel_id=1, source_target_pairs={{0,1},{1,0},{2,3},{3,2},{4,5},{5,4},{6,7},{7,6},{8,9},{9,8},{10,11... | collective-permute-start | bytes 540680 | tf_op jit(solution)/shard_map/ppermute | solution.py:263

commit v10 on v9

--- a/solution.py
+++ b/solution.py
@@ -30,15 +30,16 @@
     return terms[0]
 
 
-def call(kernel, outs, args, flops=0, scratch=(), smem=(), limit=16, final=False):
+def call(kernel, outs, args, flops=0, scratch=(), smem=(), limit=16, final=False, place=True):
     size = sum(a.size * a.dtype.itemsize for a in args)
     size += sum(o.dtype.itemsize * o.size for o in outs)
     spaces = [pltpu.SMEM if i in smem else pltpu.VMEM for i in range(len(args))]
-    placed = [a if i in smem else pltpu.with_memory_space_constraint(a, pltpu.VMEM) for i, a in enumerate(args)]
+    space = pltpu.VMEM if place else pltpu.HBM
+    placed = [a if i in smem else pltpu.with_memory_space_constraint(a, space) for i, a in enumerate(args)]
     return pl.pallas_call(
         kernel,
         out_shape=outs if final else [pltpu.VMEM(o.shape, o.dtype) for o in outs],
-        in_specs=[pl.BlockSpec(memory_space=space) for space in spaces],
+        in_specs=[pl.BlockSpec(memory_space=kind) for kind in spaces],
         out_specs=[pl.BlockSpec(memory_space=pltpu.VMEM)] * len(outs),
         scratch_shapes=list(scratch),
         cost_estimate=pl.CostEstimate(flops=flops, bytes_accessed=size, transcendentals=0),
@@ -50,11 +51,14 @@
     return jax.ShapeDtypeStruct(dims, dtype)
 
 
-def count_kernel(fanout, nbr_ref, *refs):
-    passing = len(refs) // 2
-    at_ref = refs[passing]
+def count_kernel(fanout, core_ref, nbr_ref, ws_ref, wn_ref, *refs):
+    passing = (len(refs) - 3) // 2
+    at_ref, mine_ref, other_ref = refs[passing : passing + 3]
+    first = core_ref[0] == 0
+    mine_ref[...] = jnp.where(first, ws_ref[...], wn_ref[...])
+    other_ref[...] = jnp.where(first, wn_ref[...], ws_ref[...])
     for i in range(passing):
-        refs[passing + 1 + i][...] = refs[i][...]
+        refs[passing + 3 + i][...] = refs[i][...]
     nodes = at_ref.shape[1]
     step = 32
 
@@ -87,31 +91,21 @@
     return tree_product(first, middle, known, leaf) + tree_product(middle, last, known, leaf)
 
 
-def early_kernel(nodes_mine, early, core_ref, ws_ref, wn_ref, *refs):
+def early_kernel(nodes_mine, early, own_ref, other_ref, *refs):
     f_refs = dict(zip(early, refs))
     w_refs = dict(zip(early[1:], refs[len(early) :]))
     outs = refs[2 * len(early) - 1 :]
-    first = core_ref[0] == 0
-    own = jnp.where(first, ws_ref[...], wn_ref[...])
-    other = jnp.where(first, wn_ref[...], ws_ref[...])
     for (begin, end), out_ref in zip(nodes_mine, outs):
-        leaf = lambda s: dot_tn(own if s == 0 else w_refs[s][...], f_refs[s][...])
+        leaf = lambda s: dot_tn(own_ref[...] if s == 0 else w_refs[s][...], f_refs[s][...])
         out_ref[...] = tree_product(begin, end, {}, leaf)
-    outs[-1][...] = dot_tn(other, f_refs[0][...])
+    outs[-1][...] = dot_tn(other_ref[...], f_refs[0][...])
 
 
 def mine_kernel(nodes_mine, late, feat_count, *refs):
     known = dict(zip(nodes_mine, refs))
     refs = refs[len(nodes_mine) :]
-    w_refs = dict(zip(late, refs))
-    halves = refs[len(late) : 3 * len(late)]
-    out_ref, joined = refs[3 * len(late)], refs[3 * len(late) + 1 :]
-    for i, block in enumerate(joined):
-        low, high = halves[2 * i : 2 * i + 2]
-        block[: low.shape[0]] = low[...]
-        block[low.shape[0] :] = high[...]
-    f_refs = dict(zip(late, joined))
-    out_ref[...] = tree_product(0, feat_count, known, lambda s: dot_tn(w_refs[s][...], f_refs[s][...]))
+    w_refs, f_refs = dict(zip(late, refs)), dict(zip(late, refs[len(late) :]))
+    refs[-1][...] = tree_product(0, feat_count, known, lambda s: dot_tn(w_refs[s][...], f_refs[s][...]))
 
 
 def forward_kernel(feat_count, fanout, *refs):
@@ -290,19 +284,12 @@
     return lax.ppermute(value, "dp", pairs)
 
 
-def gather_parts(block, count):
-    half = block.shape[0] // 2
-    parts = [[block]]
+def gather_blocks(block, count):
+    blocks = [block]
     for s in range(1, count):
         low_bit = s & -s
-        rest = s ^ low_bit
-        if rest == 0:
-            parts.append([hop(block, s)])
-        else:
-            low = parts[rest][0][:half] if len(parts[rest]) == 1 else parts[rest][0]
-            high = parts[low_bit][0][half:]
-            parts.append([hop(low, low_bit), hop(high, rest)])
-    return parts
+        blocks.append(hop(blocks[low_bit] if s != low_bit else block, s ^ low_bit if s != low_bit else s))
+    return blocks
 
 
 def on_device(features, neighbors, labels, loss_weight, w1_self, w1_neigh, w2_self, w2_neigh):
@@ -316,37 +303,37 @@
     core = (place % 2).reshape(1)
     z = (place // 2).reshape(1)
 
-    wide = gather_parts(features, feat_count)
-    early = [s for s in range(feat_count) if len(wide[s]) == 1]
-    late = [s for s in range(feat_count) if len(wide[s]) > 1]
+    wide = gather_blocks(features, feat_count)
+    early = [s for s in range(feat_count) if s & (s - 1) == 0]
+    late = [s for s in range(feat_count) if s & (s - 1)]
     nodes_mine = early_nodes(early, 0, feat_count)
-    mine_own = jnp.where(core[0] == 0, w1_self, w1_neigh)
-    mine = [hop(mine_own, s) for s in range(1, feat_count)]
     limit = 12 + 6 * nodes * nodes // (1024 * 1024)
     passing = [labels.reshape(1, nodes), loss_weight.reshape(1, nodes), w2_self.T, w2_neigh.T]
-    at, labels, loss_weight, w2s, w2n = call(
+    at, mine_own, other_own, labels, loss_weight, w2s, w2n = call(
         functools.partial(count_kernel, fanout),
-        [shape((nodes, nodes), BF16)] + [shape(p.shape, p.dtype) for p in passing],
-        [neighbors.T] + passing,
+        [shape((nodes, nodes), BF16)]
+        + [shape((rows, hid), BF16)] * 2
+        + [shape(p.shape, p.dtype) for p in passing],
+        [core, neighbors.T, w1_self, w1_neigh] + passing,
         flops=nodes * nodes * fanout,
-    )
+        smem=(0,),
+        place=False,
+    )
+    mine = gather_blocks(mine_own, feat_count)[1:]
     *known, other_proj = call(
         functools.partial(early_kernel, nodes_mine, early),
         [shape((hid, nodes), F32)] * (len(nodes_mine) + 1),
-        [core, w1_self, w1_neigh] + [wide[s][0] for s in early] + [mine[s - 1] for s in early[1:]],
+        [mine_own, other_own] + [wide[s] for s in early] + [mine[s - 1] for s in early[1:]],
         flops=2 * nodes * hid * rows * (len(early) + 1),
-        smem=(0,),
         limit=limit,
     )
-    mine_proj, *joined = call(
+    (mine_proj,) = call(
         functools.partial(mine_kernel, nodes_mine, late, feat_count),
-        [shape((hid, nodes), F32)] + [shape((rows, nodes), BF16)] * len(late),
-        known + [mine[s - 1] for s in late] + [part for s in late for part in wide[s]],
+        [shape((hid, nodes), F32)],
+        known + [mine[s - 1] for s in late] + [wide[s] for s in late],
         flops=30 * nodes * hid * rows * feat_count,
         limit=limit,
     )
-    rest = iter(joined)
-    whole = [block[0] if len(block) == 1 else next(rest) for block in wide]
     partner = [exchange(block, "dp", 1) for block in mine]
     padded = (classes + 3 + 15) // 16 * 16
     send2, keep2, grad, hidden = call(
@@ -357,7 +344,7 @@
             shape((classes, nodes), BF16),
             shape((hid, nodes), BF16),
         ],
-        whole[1:] + [core, labels, loss_weight, at, w2s, w2n, mine_proj, other_proj] + partner,
+        wide[1:] + [core, labels, loss_weight, at, w2s, w2n, mine_proj, other_proj] + partner,
         scratch=[
             pltpu.VMEM((2, hid, nodes), F32),
             pltpu.VMEM((2, hid, nodes), BF16),

time: 37.3 us -> 37 us (level)
  starting transfers between devices: 21.6 us -> 17.2 us
  waiting for transfers between devices: 8.16 us -> 12.2 us
  Pallas kernels: 5.59 us -> 6.74 us
  other arithmetic: 0.92 us -> 0 us
    ppermute x7 -> x6, starting transfers between devices: 13.2 us -> 9.01 us  [hop(): return lax.ppermute(value, ('feat', 'dp'), pairs)]
    ppermute x7 -> x6, waiting for transfers between devices: 2.38 us -> 6 us  [hop(): return lax.ppermute(value, ('feat', 'dp'), pairs)]
    pallas_call x12, Pallas kernels: 5.59 us -> 6.74 us  [call(): pl.pallas_call(kernel, out_shape=outs if final else [pltpu.VMEM(o.shape,...]
    select_n x1 -> x0, other arithmetic: 0.92 us -> none  [on_device(): mine_own = jnp.where(core[0] == 0, w1_self, w1_neigh)]
    ppermute x6, waiting for transfers between devices: 0.02 us -> 0.48 us  [exchange(): return lax.ppermute(value, axis, [(i, i ^ step) for i in range(size)])]
  transfers between devices with their start and end apart: 17 -> 16, of which waited for: 7 -> 8; matrix products, arithmetic and copies ran while one was open for 3% -> 0% of each run, Pallas kernels for 8% -> 12%
where the time goes in v10:
time: 37 us; the launch traced here: 36.8 us
  starting transfers between devices  17.2 us (46%)
  waiting for transfers between devices  12.2 us (33%)
  Pallas kernels  6.74 us (18%)
  between operations  0.74 us (2%)
    ppermute x6, starting transfers between devices, hop(): return lax.ppermute(value, ('feat', 'dp'), pairs)  9.01 us
    ppermute x4, starting transfers between devices, fold_hop(): return lax.ppermute(value, 'dp', pairs)  7.21 us
    pallas_call x12, Pallas kernels, call(): pl.pallas_call(kernel, out_shape=outs if final else [pltpu.VMEM(o.shape,...  6.74 us
    ppermute x6, waiting for transfers between devices, hop(): return lax.ppermute(value, ('feat', 'dp'), pairs)  6 us
    ppermute x4, waiting for transfers between devices, fold_hop(): return lax.ppermute(value, 'dp', pairs)  5.67 us
    ppermute x6, starting transfers between devices, exchange(): return lax.ppermute(value, axis, [(i, i ^ step) for i in range(size)])  0.96 us
  transfers between devices with their start and end apart: 16, of which 8 were waited for; matrix products, arithmetic and copies ran while one was open for 0% of the time, Pallas kernels for 12%

profile of v10, /device:TPU:0, one launch (start us, length us, event | category | flops | bytes accessed | tf_op | source)
XLA Modules:
  0.0 36.8 jit_solution(10440077362520017282)
XLA Ops:
  0.6 0.0 copy-start
  0.6 3.0 %collective-permute-start = (bf16[256,512]{1,0:T(8,128)(2,1)}, bf16[256,512]{1,0:T(8,128)(2,1)S(1)}, u32[]{:S(2)}, u32[]{:S(2)}) collective-permute-start(bf16[256,512]{1,0:T(8,128)(2,1)} %f_ref.1), channel_id=1, source_target_pairs={{0,8},{1,17},{2,10},{3,19},{4,12},{5,21},{6,14},{7,23},{8,0},{9,25... | collective-permute-start | bytes 786440 | tf_op jit(solution)/shard_map/ppermute | solution.py:275
  3.6 2.2 %shard_map.103 = (bf16[512,512]{1,0:T(8,128)(2,1)S(1)}, bf16[256,256]{1,0:T(8,128)(2,1)S(1)}, bf16[256,256]{1,0:T(8,128)(2,1)S(1)}, s32[1,512]{1,0:T(1,128)S(1)}...) custom-call(s32[1]{0:T(128)} %bitcast.core_ref.refs_3_, s32[10,512]{1,0:T(8,128)} %bitcast.15, ...), custom_call_target="tpu_custom_call" | custom-call | flops 2621440 | bytes 1429508 | tf_op jit(solution)/shard_map/pallas_call | solution.py:39
  5.9 0.1 collective-permute-start.3
  6.0 0.0 copy-done
  6.0 2.0 %collective-permute-start.1 = (bf16[256,512]{1,0:T(8,128)(2,1)S(1)}, bf16[256,512]{1,0:T(8,128)(2,1)S(1)}, u32[]{:S(2)}, u32[]{:S(2)}) collective-permute-start(bf16[256,512]{1,0:T(8,128)(2,1)S(1)} %copy-done), channel_id=1, source_target_pairs={{0,16},{1,9},{2,18},{3,11},{4,20},{5,13},{6,22},{7,15},{8,24},{9,1... | collective-permute-start | bytes 786440 | tf_op jit(solution)/shard_map/ppermute | solution.py:275
  8.0 0.2 collective-permute-done.refs_1_.refs_0_
  8.2 2.4 %collective-permute-start.2 = (bf16[256,512]{1,0:T(8,128)(2,1)S(1)}, bf16[256,512]{1,0:T(8,128)(2,1)S(1)}, u32[]{:S(2)}, u32[]{:S(2)}) collective-permute-start(bf16[256,512]{1,0:T(8,128)(2,1)S(1)} %collective-permute-done.refs_1_.refs_0_), channel_id=1, source_target_pairs={{0,16},{1,9},{2,18},{3,11},{4,20},{5,13},{6,22},{7,15},{8,24},{9,1... | collective-permute-start | bytes 786440 | tf_op jit(solution)/shard_map/ppermute | solution.py:275
  10.6 0.0 collective-permute-start.4
  10.6 1.8 %collective-permute-done.3.refs_3_ = bf16[256,256]{1,0:T(8,128)(2,1)S(1)} collective-permute-done((bf16[256,256]{1,0:T(8,128)(2,1)S(1)}, bf16[256,256]{1,0:T(8,128)(2,1)S(1)}, u32[]{:S(2)}, u32[]{:S(2)}) %collective-permute-start.3) | collective-permute-done | bytes 131104 | tf_op jit(solution)/shard_map/ppermute | solution.py:275
  12.4 1.5 %collective-permute-start.5 = (bf16[256,256]{1,0:T(8,128)(2,1)S(1)}, bf16[256,256]{1,0:T(8,128)(2,1)S(1)}, u32[]{:S(2)}, u32[]{:S(2)}) collective-permute-start(bf16[256,256]{1,0:T(8,128)(2,1)S(1)} %collective-permute-done.3.refs_3_), channel_id=1, source_target_pairs={{0,16},{1,9},{2,18},{3,11},{4,20},{5,13},{6,22},{7,15},{8,24},{9,1... | collective-permute-start | bytes 393224 | tf_op jit(solution)/shard_map/ppermute | solution.py:275
  13.9 0.0 collective-permute-start.6
  13.9 2.8 %collective-permute-done.4.refs_4_ = bf16[256,256]{1,0:T(8,128)(2,1)S(1)} collective-permute-done((bf16[256,256]{1,0:T(8,128)(2,1)S(1)}, bf16[256,256]{1,0:T(8,128)(2,1)S(1)}, u32[]{:S(2)}, u32[]{:S(2)}) %collective-permute-start.4) | collective-permute-done | bytes 131104 | tf_op jit(solution)/shard_map/ppermute | solution.py:275
  16.6 0.1 collective-permute-start.7
  16.8 1.3 %collective-permute-done.5.refs_2_ = bf16[256,256]{1,0:T(8,128)(2,1)S(1)} collective-permute-done((bf16[256,256]{1,0:T(8,128)(2,1)S(1)}, bf16[256,256]{1,0:T(8,128)(2,1)S(1)}, u32[]{:S(2)}, u32[]{:S(2)}) %collective-permute-start.5) | collective-permute-done | bytes 131104 | tf_op jit(solution)/shard_map/ppermute | solution.py:275
  18.0 0.1 collective-permute-start.8
  18.2 0.0 collective-permute-done.1.refs_2_.refs_1_
  18.2 0.5 %shard_map.104 = (f32[256,512]{1,0:T(8,128)S(1)}, f32[256,512]{1,0:T(8,128)S(1)}, f32[256,512]{1,0:T(8,128)S(1)}) custom-call(bf16[256,256]{1,0:T(8,128)(2,1)S(1)} %get-tuple-element.31.own_ref, bf16[256,256]{1,0:T(8,128)(2,1)S(1)} %get-tuple-element.32.other_ref, bf16[256,512]{1,0:T(8,128)(2,1)S(1)} %copy-done, ...), custom_call_target="tpu_custom_call" | custom-call | flops 268435456 | bytes 2883584 | tf_op jit(solution)/shard_map/pallas_call | solution.py:39
  18.6 0.0 collective-permute-done.2.refs_3_.refs_2_
  18.6 0.2 shard_map.105.refs_9_
  18.9 0.0 collective-permute-done.6.refs_11_
  18.9 0.0 collective-permute-done.7.refs_12_
  18.9 0.5 %collective-permute-done.8.refs_13_ = bf16[256,256]{1,0:T(8,128)(2,1)S(1)} collective-permute-done((bf16[256,256]{1,0:T(8,128)(2,1)S(1)}, bf16[256,256]{1,0:T(8,128)(2,1)S(1)}, u32[]{:S(2)}, u32[]{:S(2)}) %collective-permute-start.8) | collective-permute-done | bytes 131104 | tf_op jit(solution)/shard_map/ppermute | solution.py:257
  19.4 1.6 %shard_map.106 = (f32[176,256]{1,0:T(8,128)S(1)}, f32[176,256]{1,0:T(8,128)S(1)}, bf16[172,512]{1,0:T(8,128)(2,1)S(1)}, bf16[256,512]{1,0:T(8,128)(2,1)S(1)}) custom-call(bf16[256,512]{1,0:T(8,128)(2,1)S(1)} %collective-permute-done.refs_1_.refs_0_, bf16[256,512]{1,0:T(8,128)(2,1)S(1)} %collective-permute-done.1.refs_2_.refs_1_, ...), custom_call_target="tpu_custom_call" | custom-call | flops 805306368 | bytes 3731460 | tf_op jit(solution)/shard_map/pallas_call | solution.py:39
  21.0 0.2 collective-permute-start.10
  21.2 1.1 %shard_map.107 = (f32[4,64,256]{2,1,0:T(8,128)S(1)}, f32[4,64,256]{2,1,0:T(8,128)S(1)}) custom-call(s32[1]{0:T(128)} %bitcast.core_ref.refs_3_, bf16[172,512]{1,0:T(8,128)(2,1)S(1)} %get-tuple-element.36.g_ref, bf16[256,512]{1,0:T(8,128)(2,1)S(1)} %get-tuple-element.37.hidden_ref, bf16[512,512]{1,0:T(8,128)(2,1)S(1)} %get-tuple-element.28.refs_6_.at_ref, ...), custom_call_target="tpu_custom_call" | custom-call | flops 402653184 | bytes 1925124 | tf_op jit(solution)/shard_map/pallas_call | solution.py:39
  22.3 0.4 %collective-permute-start.9 = (f32[4,64,256]{2,1,0:T(8,128)S(1)}, f32[4,64,256]{2,1,0:T(8,128)S(1)}, u32[]{:S(2)}, u32[]{:S(2)}) collective-permute-start(f32[4,64,256]{2,1,0:T(8,128)S(1)} %get-tuple-element.39), channel_id=1, source_target_pairs={{0,1},{1,0},{2,3},{3,2},{4,5},{5,4},{6,7},{7,6},{8,9},{9,8},{10,11... | collective-permute-start | bytes 786440 | tf_op jit(solution)/shard_map/ppermute | solution.py:257
  22.8 0.0 collective-permute-done.10.recv_ref
  22.8 2.1 %collective-permute-start.11 = (bf16[176,256]{1,0:T(8,128)(2,1)S(1)}, bf16[176,256]{1,0:T(8,128)(2,1)S(1)}, u32[]{:S(2)}, u32[]{:S(2)}) collective-permute-start(bf16[176,256]{1,0:T(8,128)(2,1)S(1)} %shard_map.109.own_ref), channel_id=1, source_target_pairs={{0,2},{1,5},{2,0},{3,7},{4,6},{5,1},{6,4},{7,3},{8,10},{9,13},{10,... | collective-permute-start | bytes 270344 | tf_op jit(solution)/shard_map/ppermute | solution.py:284
  24.9 0.0 collective-permute-done.9.recv_ref
  24.9 1.1 %collective-permute-start.14 = (bf16[128,256]{1,0:T(8,128)(2,1)S(1)}, bf16[128,256]{1,0:T(8,128)(2,1)S(1)}, u32[]{:S(2)}, u32[]{:S(2)}) collective-permute-start(bf16[128,256]{1,0:T(8,128)(2,1)S(1)} %get-tuple-element.43), channel_id=1, source_target_pairs={{0,2},{1,5},{2,0},{3,7},{4,6},{5,1},{6,4},{7,3},{8,10},{9,13},{10,... | collective-permute-start | bytes 196616 | tf_op jit(solution)/shard_map/ppermute | solution.py:284
  26.0 2.3 %collective-permute-done.11.recv_ref = bf16[176,256]{1,0:T(8,128)(2,1)S(1)} collective-permute-done((bf16[176,256]{1,0:T(8,128)(2,1)S(1)}, bf16[176,256]{1,0:T(8,128)(2,1)S(1)}, u32[]{:S(2)}, u32[]{:S(2)}) %collective-permute-start.11) | collective-permute-done | bytes 90144 | tf_op jit(solution)/shard_map/ppermute | solution.py:284
  28.4 2.2 %collective-permute-start.12 = (bf16[176,256]{1,0:T(8,128)(2,1)S(1)}, bf16[176,256]{1,0:T(8,128)(2,1)S(1)}, u32[]{:S(2)}, u32[]{:S(2)}) collective-permute-start(bf16[176,256]{1,0:T(8,128)(2,1)S(1)} %shard_map.110.refs_0_), channel_id=1, source_target_pairs={{0,4},{1,3},{2,6},{3,1},{4,0},{5,7},{6,2},{7,5},{8,12},{9,11},{10,... | collective-permute-start | bytes 270344 | tf_op jit(solution)/shard_map/ppermute | solution.py:284
  30.6 0.0 collective-permute-done.14.recv_ref
  30.6 1.8 %collective-permute-start.15 = (bf16[64,256]{1,0:T(8,128)(2,1)S(1)}, bf16[64,256]{1,0:T(8,128)(2,1)S(1)}, u32[]{:S(2)}, u32[]{:S(2)}) collective-permute-start(bf16[64,256]{1,0:T(8,128)(2,1)S(1)} %get-tuple-element.45), channel_id=1, source_target_pairs={{0,4},{1,3},{2,6},{3,1},{4,0},{5,7},{6,2},{7,5},{8,12},{9,11},{10,... | collective-permute-start | bytes 98312 | tf_op jit(solution)/shard_map/ppermute | solution.py:284
  32.4 1.6 %collective-permute-done.12.refs_1_ = bf16[176,256]{1,0:T(8,128)(2,1)S(1)} collective-permute-done((bf16[176,256]{1,0:T(8,128)(2,1)S(1)}, bf16[176,256]{1,0:T(8,128)(2,1)S(1)}, u32[]{:S(2)}, u32[]{:S(2)}) %collective-permute-start.12) | collective-permute-done | bytes 90144 | tf_op jit(solution)/shard_map/ppermute | solution.py:284
  34.0 0.1 collective-permute-start.13
  34.1 1.8 %collective-permute-done.15.refs_0_ = bf16[64,256]{1,0:T(8,128)(2,1)S(1)} collective-permute-done((bf16[64,256]{1,0:T(8,128)(2,1)S(1)}, bf16[64,256]{1,0:T(8,128)(2,1)S(1)}, u32[]{:S(2)}, u32[]{:S(2)}) %collective-permute-start.15) | collective-permute-done | bytes 32800 | tf_op jit(solution)/shard_map/ppermute | solution.py:284
  35.9 0.0 collective-permute-done.13.other_ref
  35.9 0.9 %shard_map.114 = (f32[2,32,256]{2,1,0:T(8,128)}, f32[688,128]{1,0:T(8,128)}, f32[1,1]{1,0:T(1,128)}) custom-call(s32[1]{0:T(128)} %bitcast.core_ref.refs_3_, f32[176,256]{1,0:T(8,128)S(1)} %shard_map.111.own_ref, f32[176,256]{1,0:T(8,128)S(1)} %collective-permute-done.13.other_ref, f32[64,256]{1,0:T(8,128)S(1)} %shard_map.113.first_ref), custom_call_target="tpu_custom_call" | custom-call | bytes 843784 | tf_op jit(solution)/shard_map/pallas_call | solution.py:39
  (6 shorter events, 0.2 us)
Async XLA Ops:
  0.6 5.4 %copy-start = (bf16[256,512]{1,0:T(8,128)(2,1)S(1)}, bf16[256,512]{1,0:T(8,128)(2,1)}, u32[]{:S(2)}) copy-start(bf16[256,512]{1,0:T(8,128)(2,1)} %f_ref.1) | copy-start | bytes 786436
  0.6 7.6 %collective-permute-start = (bf16[256,512]{1,0:T(8,128)(2,1)}, bf16[256,512]{1,0:T(8,128)(2,1)S(1)}, u32[]{:S(2)}, u32[]{:S(2)}) collective-permute-start(bf16[256,512]{1,0:T(8,128)(2,1)} %f_ref.1), channel_id=1, source_target_pairs={{0,8},{1,17},{2,10},{3,19},{4,12},{5,21},{6,14},{7,23},{8,0},{9,25... | collective-permute-start | bytes 786440 | tf_op jit(solution)/shard_map/ppermute | solution.py:275
  5.9 6.5 %collective-permute-start.3 = (bf16[256,256]{1,0:T(8,128)(2,1)S(1)}, bf16[256,256]{1,0:T(8,128)(2,1)S(1)}, u32[]{:S(2)}, u32[]{:S(2)}) collective-permute-start(bf16[256,256]{1,0:T(8,128)(2,1)S(1)} %get-tuple-element.31.own_ref), channel_id=1, source_target_pairs={{0,8},{1,17},{2,10},{3,19},{4,12},{5,21},{6,14},{7,23},{8,0},{9,25... | collective-permute-start | bytes 393224 | tf_op jit(solution)/shard_map/ppermute | solution.py:275
  6.0 12.2 %collective-permute-start.1 = (bf16[256,512]{1,0:T(8,128)(2,1)S(1)}, bf16[256,512]{1,0:T(8,128)(2,1)S(1)}, u32[]{:S(2)}, u32[]{:S(2)}) collective-permute-start(bf16[256,512]{1,0:T(8,128)(2,1)S(1)} %copy-done), channel_id=1, source_target_pairs={{0,16},{1,9},{2,18},{3,11},{4,20},{5,13},{6,22},{7,15},{8,24},{9,1... | collective-permute-start | bytes 786440 | tf_op jit(solution)/shard_map/ppermute | solution.py:275
  8.2 10.4 %collective-permute-start.2 = (bf16[256,512]{1,0:T(8,128)(2,1)S(1)}, bf16[256,512]{1,0:T(8,128)(2,1)S(1)}, u32[]{:S(2)}, u32[]{:S(2)}) collective-permute-start(bf16[256,512]{1,0:T(8,128)(2,1)S(1)} %collective-permute-done.refs_1_.refs_0_), channel_id=1, source_target_pairs={{0,16},{1,9},{2,18},{3,11},{4,20},{5,13},{6,22},{7,15},{8,24},{9,1... | collective-permute-start | bytes 786440 | tf_op jit(solution)/shard_map/ppermute | solution.py:275
  10.6 6.1 %collective-permute-start.4 = (bf16[256,256]{1,0:T(8,128)(2,1)S(1)}, bf16[256,256]{1,0:T(8,128)(2,1)S(1)}, u32[]{:S(2)}, u32[]{:S(2)}) collective-permute-start(bf16[256,256]{1,0:T(8,128)(2,1)S(1)} %get-tuple-element.31.own_ref), channel_id=1, source_target_pairs={{0,16},{1,9},{2,18},{3,11},{4,20},{5,13},{6,22},{7,15},{8,24},{9,1... | collective-permute-start | bytes 393224 | tf_op jit(solution)/shard_map/ppermute | solution.py:275
  12.4 5.7 %collective-permute-start.5 = (bf16[256,256]{1,0:T(8,128)(2,1)S(1)}, bf16[256,256]{1,0:T(8,128)(2,1)S(1)}, u32[]{:S(2)}, u32[]{:S(2)}) collective-permute-start(bf16[256,256]{1,0:T(8,128)(2,1)S(1)} %collective-permute-done.3.refs_3_), channel_id=1, source_target_pairs={{0,16},{1,9},{2,18},{3,11},{4,20},{5,13},{6,22},{7,15},{8,24},{9,1... | collective-permute-start | bytes 393224 | tf_op jit(solution)/shard_map/ppermute | solution.py:275
  13.9 5.0 %collective-permute-start.6 = (bf16[256,256]{1,0:T(8,128)(2,1)S(1)}, bf16[256,256]{1,0:T(8,128)(2,1)S(1)}, u32[]{:S(2)}, u32[]{:S(2)}) collective-permute-start(bf16[256,256]{1,0:T(8,128)(2,1)S(1)} %collective-permute-done.3.refs_3_), channel_id=1, source_target_pairs={{0,1},{1,0},{2,3},{3,2},{4,5},{5,4},{6,7},{7,6},{8,9},{9,8},{10,11... | collective-permute-start | bytes 393224 | tf_op jit(solution)/shard_map/ppermute | solution.py:257
  16.6 2.3 %collective-permute-start.7 = (bf16[256,256]{1,0:T(8,128)(2,1)S(1)}, bf16[256,256]{1,0:T(8,128)(2,1)S(1)}, u32[]{:S(2)}, u32[]{:S(2)}) collective-permute-start(bf16[256,256]{1,0:T(8,128)(2,1)S(1)} %collective-permute-done.4.refs_4_), channel_id=1, source_target_pairs={{0,1},{1,0},{2,3},{3,2},{4,5},{5,4},{6,7},{7,6},{8,9},{9,8},{10,11... | collective-permute-start | bytes 393224 | tf_op jit(solution)/shard_map/ppermute | solution.py:257
  18.0 1.3 %collective-permute-start.8 = (bf16[256,256]{1,0:T(8,128)(2,1)S(1)}, bf16[256,256]{1,0:T(8,128)(2,1)S(1)}, u32[]{:S(2)}, u32[]{:S(2)}) collective-permute-start(bf16[256,256]{1,0:T(8,128)(2,1)S(1)} %collective-permute-done.5.refs_2_), channel_id=1, source_target_pairs={{0,1},{1,0},{2,3},{3,2},{4,5},{5,4},{6,7},{7,6},{8,9},{9,8},{10,11... | collective-permute-start | bytes 393224 | tf_op jit(solution)/shard_map/ppermute | solution.py:257
  21.0 1.8 %collective-permute-start.10 = (f32[176,256]{1,0:T(8,128)S(1)}, f32[176,256]{1,0:T(8,128)S(1)}, u32[]{:S(2)}, u32[]{:S(2)}) collective-permute-start(f32[176,256]{1,0:T(8,128)S(1)} %get-tuple-element.42), channel_id=1, source_target_pairs={{0,1},{1,0},{2,3},{3,2},{4,5},{5,4},{6,7},{7,6},{8,9},{9,8},{10,11... | collective-permute-start | bytes 540680 | tf_op jit(solution)/shard_map/ppermute | solution.py:257
  22.3 2.6 %collective-permute-start.9 = (f32[4,64,256]{2,1,0:T(8,128)S(1)}, f32[4,64,256]{2,1,0:T(8,128)S(1)}, u32[]{:S(2)}, u32[]{:S(2)}) collective-permute-start(f32[4,64,256]{2,1,0:T(8,128)S(1)} %get-tuple-element.39), channel_id=1, source_target_pairs={{0,1},{1,0},{2,3},{3,2},{4,5},{5,4},{6,7},{7,6},{8,9},{9,8},{10,11... | collective-permute-start | bytes 786440 | tf_op jit(solution)/shard_map/ppermute | solution.py:257
  22.8 5.6 %collective-permute-start.11 = (bf16[176,256]{1,0:T(8,128)(2,1)S(1)}, bf16[176,256]{1,0:T(8,128)(2,1)S(1)}, u32[]{:S(2)}, u32[]{:S(2)}) collective-permute-start(bf16[176,256]{1,0:T(8,128)(2,1)S(1)} %shard_map.109.own_ref), channel_id=1, source_target_pairs={{0,2},{1,5},{2,0},{3,7},{4,6},{5,1},{6,4},{7,3},{8,10},{9,13},{10,... | collective-permute-start | bytes 270344 | tf_op jit(solution)/shard_map/ppermute | solution.py:284
  24.9 5.6 %collective-permute-start.14 = (bf16[128,256]{1,0:T(8,128)(2,1)S(1)}, bf16[128,256]{1,0:T(8,128)(2,1)S(1)}, u32[]{:S(2)}, u32[]{:S(2)}) collective-permute-start(bf16[128,256]{1,0:T(8,128)(2,1)S(1)} %get-tuple-element.43), channel_id=1, source_target_pairs={{0,2},{1,5},{2,0},{3,7},{4,6},{5,1},{6,4},{7,3},{8,10},{9,13},{10,... | collective-permute-start | bytes 196616 | tf_op jit(solution)/shard_map/ppermute | solution.py:284
  28.4 5.6 %collective-permute-start.12 = (bf16[176,256]{1,0:T(8,128)(2,1)S(1)}, bf16[176,256]{1,0:T(8,128)(2,1)S(1)}, u32[]{:S(2)}, u32[]{:S(2)}) collective-permute-start(bf16[176,256]{1,0:T(8,128)(2,1)S(1)} %shard_map.110.refs_0_), channel_id=1, source_target_pairs={{0,4},{1,3},{2,6},{3,1},{4,0},{5,7},{6,2},{7,5},{8,12},{9,11},{10,... | collective-permute-start | bytes 270344 | tf_op jit(solution)/shard_map/ppermute | solution.py:284
  30.6 5.3 %collective-permute-start.15 = (bf16[64,256]{1,0:T(8,128)(2,1)S(1)}, bf16[64,256]{1,0:T(8,128)(2,1)S(1)}, u32[]{:S(2)}, u32[]{:S(2)}) collective-permute-start(bf16[64,256]{1,0:T(8,128)(2,1)S(1)} %get-tuple-element.45), channel_id=1, source_target_pairs={{0,4},{1,3},{2,6},{3,1},{4,0},{5,7},{6,2},{7,5},{8,12},{9,11},{10,... | collective-permute-start | bytes 98312 | tf_op jit(solution)/shard_map/ppermute | solution.py:284
  34.0 1.9 %collective-permute-start.13 = (f32[176,256]{1,0:T(8,128)S(1)}, f32[176,256]{1,0:T(8,128)S(1)}, u32[]{:S(2)}, u32[]{:S(2)}) collective-permute-start(f32[176,256]{1,0:T(8,128)S(1)} %shard_map.111.own_ref), channel_id=1, source_target_pairs={{0,1},{1,0},{2,3},{3,2},{4,5},{5,4},{6,7},{7,6},{8,9},{9,8},{10,11... | collective-permute-start | bytes 540680 | tf_op jit(solution)/shard_map/ppermute | solution.py:257

commit v11 on v10

--- a/solution.py
+++ b/solution.py
@@ -101,6 +101,14 @@
     outs[-1][...] = dot_tn(other_ref[...], f_refs[0][...])
 
 
+def partner_kernel(tree_nodes, early, own_ref, *refs):
+    f_refs = dict(zip(early[1:], refs))
+    w_refs = dict(zip(early[1:], refs[len(early) - 1 :]))
+    for (begin, end), out_ref in zip(tree_nodes, refs[2 * len(early) - 2 :]):
+        leaf = lambda s: dot_tn(w_refs[s][...], f_refs[s][...])
+        out_ref[...] = tree_product(begin, end, {(0, 1): own_ref}, leaf)
+
+
 def mine_kernel(nodes_mine, late, feat_count, *refs):
     known = dict(zip(nodes_mine, refs))
     refs = refs[len(nodes_mine) :]
@@ -108,19 +116,18 @@
     refs[-1][...] = tree_product(0, feat_count, known, lambda s: dot_tn(w_refs[s][...], f_refs[s][...]))
 
 
-def forward_kernel(feat_count, fanout, *refs):
-    f_refs, refs = refs[: feat_count - 1], refs[feat_count - 1 :]
-    core_ref, labels_ref, weight_ref, at_ref, w2s_ref, w2n_ref, mine_ref, other_ref = refs[:8]
-    partner_refs = refs[8 : 7 + feat_count]
-    send_ref, keep_ref, g_ref, hidden_ref, proj, pair = refs[7 + feat_count :]
+def forward_kernel(tree_nodes, late, feat_count, fanout, *refs):
+    core_ref, labels_ref, weight_ref, at_ref, w2s_ref, w2n_ref, mine_ref = refs[:7]
+    known = dict(zip(tree_nodes, refs[7:]))
+    refs = refs[7 + len(tree_nodes) :]
+    f_refs, w_refs = dict(zip(late, refs)), dict(zip(late, refs[len(late) :]))
+    send_ref, keep_ref, g_ref, hidden_ref, proj, pair = refs[2 * len(late) :]
     core = core_ref[0]
     classes = w2s_ref.shape[0]
     nodes = at_ref.shape[1]
     scale = 1.0 / fanout
     proj[core] = mine_ref[...]
-    proj[1 - core] = tree_product(
-        0, feat_count, {(0, 1): other_ref}, lambda s: dot_tn(partner_refs[swapped(s, feat_count) - 1][...], f_refs[s - 1][...])
-    )
+    proj[1 - core] = tree_product(0, feat_count, known, lambda s: dot_tn(w_refs[s][...], f_refs[s][...]))
     at = at_ref[...]
     pre = proj[0] + dot_nn(proj[1].astype(BF16), at) * scale
     hidden = jnp.maximum(pre, 0.0).astype(BF16)
@@ -335,22 +342,33 @@
         limit=limit,
     )
     partner = [exchange(block, "dp", 1) for block in mine]
+    partner = [partner[swapped(s, feat_count) - 1] for s in range(1, feat_count)]
+    known_other = call(
+        functools.partial(partner_kernel, nodes_mine, early),
+        [shape((hid, nodes), F32)] * len(nodes_mine),
+        [other_proj] + [wide[s] for s in early[1:]] + [partner[s - 1] for s in early[1:]],
+        flops=2 * nodes * hid * rows * (len(early) - 1),
+        limit=limit,
+    )
     padded = (classes + 3 + 15) // 16 * 16
     send2, keep2, grad, hidden = call(
-        functools.partial(forward_kernel, feat_count, fanout),
+        functools.partial(forward_kernel, nodes_mine, late, feat_count, fanout),
         [
             shape((padded, hid), F32),
             shape((padded, hid), F32),
             shape((classes, nodes), BF16),
             shape((hid, nodes), BF16),
         ],
-        wide[1:] + [core, labels, loss_weight, at, w2s, w2n, mine_proj, other_proj] + partner,
+        [core, labels, loss_weight, at, w2s, w2n, mine_proj]
+        + list(known_other)
+        + [wide[s] for s in late]
+        + [partner[s - 1] for s in late],
         scratch=[
             pltpu.VMEM((2, hid, nodes), F32),
             pltpu.VMEM((2, hid, nodes), BF16),
         ],
         flops=2 * nodes * hid * 2 * (rows * feat_count + nodes),
-        smem=(feat_count - 1,),
+        smem=(0,),
         limit=limit,
     )
     recv2 = exchange(send2, "dp", 1)

time: 37 us -> 36.9 us (level)
  waiting for transfers between devices: 12.2 us -> 11.2 us
  starting transfers between devices: 17.2 us -> 17.8 us
    ppermute x6, waiting for transfers between devices: 6 us -> 5.6 us  [hop(): return lax.ppermute(value, ('feat', 'dp'), pairs)]
    ppermute x6, starting transfers between devices: 0.96 us -> 1.34 us  [exchange(): return lax.ppermute(value, axis, [(i, i ^ step) for i in range(size)])]
    pallas_call x12 -> x13, Pallas kernels: 6.74 us -> 6.94 us  [call(): pl.pallas_call(kernel, out_shape=outs if final else [pltpu.VMEM(o.shape,...]
  transfers between devices with their start and end apart: 16 -> 16, of which waited for: 8 -> 7; matrix products, arithmetic and copies ran while one was open for 0% -> 0% of each run, Pallas kernels for 12% -> 12%
where the time goes in v11:
time: 36.9 us; the launch traced here: 36.7 us
  starting transfers between devices  17.8 us (48%)
  waiting for transfers between devices  11.2 us (30%)
  Pallas kernels  6.94 us (19%)
  between operations  0.74 us (2%)
    ppermute x6, starting transfers between devices, hop(): return lax.ppermute(value, ('feat', 'dp'), pairs)  9.04 us
    ppermute x4, starting transfers between devices, fold_hop(): return lax.ppermute(value, 'dp', pairs)  7.47 us
    pallas_call x13, Pallas kernels, call(): pl.pallas_call(kernel, out_shape=outs if final else [pltpu.VMEM(o.shape,...  6.94 us
    ppermute x6, waiting for transfers between devices, hop(): return lax.ppermute(value, ('feat', 'dp'), pairs)  5.6 us
    ppermute x4, waiting for transfers between devices, fold_hop(): return lax.ppermute(value, 'dp', pairs)  5.45 us
    ppermute x6, starting transfers between devices, exchange(): return lax.ppermute(value, axis, [(i, i ^ step) for i in range(size)])  1.34 us
  transfers between devices with their start and end apart: 16, of which 7 were waited for; matrix products, arithmetic and copies ran while one was open for 0% of the time, Pallas kernels for 12%

profile of v11, /device:TPU:0, one launch (start us, length us, event | category | flops | bytes accessed | tf_op | source)
XLA Modules:
  0.0 36.7 jit_solution(15276619061150694165)
XLA Ops:
  0.6 0.0 copy-start
  0.6 3.0 %collective-permute-start = (bf16[256,512]{1,0:T(8,128)(2,1)}, bf16[256,512]{1,0:T(8,128)(2,1)S(1)}, u32[]{:S(2)}, u32[]{:S(2)}) collective-permute-start(bf16[256,512]{1,0:T(8,128)(2,1)} %f_ref.1), channel_id=1, source_target_pairs={{0,8},{1,17},{2,10},{3,19},{4,12},{5,21},{6,14},{7,23},{8,0},{9,25... | collective-permute-start | bytes 786440 | tf_op jit(solution)/shard_map/ppermute | solution.py:282
  3.6 2.2 %shard_map.103 = (bf16[512,512]{1,0:T(8,128)(2,1)S(1)}, bf16[256,256]{1,0:T(8,128)(2,1)S(1)}, bf16[256,256]{1,0:T(8,128)(2,1)S(1)}, s32[1,512]{1,0:T(1,128)S(1)}...) custom-call(s32[1]{0:T(128)} %bitcast.core_ref.refs_0_, s32[10,512]{1,0:T(8,128)} %bitcast.15, ...), custom_call_target="tpu_custom_call" | custom-call | flops 2621440 | bytes 1429508 | tf_op jit(solution)/shard_map/pallas_call | solution.py:39
  5.9 0.1 collective-permute-start.2
  6.0 0.0 copy-done
  6.0 2.0 %collective-permute-start.1 = (bf16[256,512]{1,0:T(8,128)(2,1)S(1)}, bf16[256,512]{1,0:T(8,128)(2,1)S(1)}, u32[]{:S(2)}, u32[]{:S(2)}) collective-permute-start(bf16[256,512]{1,0:T(8,128)(2,1)S(1)} %copy-done), channel_id=1, source_target_pairs={{0,16},{1,9},{2,18},{3,11},{4,20},{5,13},{6,22},{7,15},{8,24},{9,1... | collective-permute-start | bytes 786440 | tf_op jit(solution)/shard_map/ppermute | solution.py:282
  8.0 0.1 collective-permute-start.3
  8.1 0.1 collective-permute-done.refs_1_.refs_0_
  8.2 2.4 %collective-permute-start.5 = (bf16[256,512]{1,0:T(8,128)(2,1)S(1)}, bf16[256,512]{1,0:T(8,128)(2,1)S(1)}, u32[]{:S(2)}, u32[]{:S(2)}) collective-permute-start(bf16[256,512]{1,0:T(8,128)(2,1)S(1)} %collective-permute-done.refs_1_.refs_0_), channel_id=1, source_target_pairs={{0,16},{1,9},{2,18},{3,11},{4,20},{5,13},{6,22},{7,15},{8,24},{9,1... | collective-permute-start | bytes 786440 | tf_op jit(solution)/shard_map/ppermute | solution.py:282
  10.6 1.8 %collective-permute-done.2.refs_3_ = bf16[256,256]{1,0:T(8,128)(2,1)S(1)} collective-permute-done((bf16[256,256]{1,0:T(8,128)(2,1)S(1)}, bf16[256,256]{1,0:T(8,128)(2,1)S(1)}, u32[]{:S(2)}, u32[]{:S(2)}) %collective-permute-start.2) | collective-permute-done | bytes 131104 | tf_op jit(solution)/shard_map/ppermute | solution.py:282
  12.4 1.5 %collective-permute-start.4 = (bf16[256,256]{1,0:T(8,128)(2,1)S(1)}, bf16[256,256]{1,0:T(8,128)(2,1)S(1)}, u32[]{:S(2)}, u32[]{:S(2)}) collective-permute-start(bf16[256,256]{1,0:T(8,128)(2,1)S(1)} %collective-permute-done.2.refs_3_), channel_id=1, source_target_pairs={{0,16},{1,9},{2,18},{3,11},{4,20},{5,13},{6,22},{7,15},{8,24},{9,1... | collective-permute-start | bytes 393224 | tf_op jit(solution)/shard_map/ppermute | solution.py:282
  13.9 0.0 collective-permute-done.3.refs_4_
  13.9 0.1 collective-permute-start.6
  14.0 0.4 %collective-permute-start.7 = (bf16[256,256]{1,0:T(8,128)(2,1)S(1)}, bf16[256,256]{1,0:T(8,128)(2,1)S(1)}, u32[]{:S(2)}, u32[]{:S(2)}) collective-permute-start(bf16[256,256]{1,0:T(8,128)(2,1)S(1)} %collective-permute-done.2.refs_3_), channel_id=1, source_target_pairs={{0,1},{1,0},{2,3},{3,2},{4,5},{5,4},{6,7},{7,6},{8,9},{9,8},{10,11... | collective-permute-start | bytes 393224 | tf_op jit(solution)/shard_map/ppermute | solution.py:264
  14.4 3.7 %collective-permute-done.4.refs_2_ = bf16[256,256]{1,0:T(8,128)(2,1)S(1)} collective-permute-done((bf16[256,256]{1,0:T(8,128)(2,1)S(1)}, bf16[256,256]{1,0:T(8,128)(2,1)S(1)}, u32[]{:S(2)}, u32[]{:S(2)}) %collective-permute-start.4) | collective-permute-done | bytes 131104 | tf_op jit(solution)/shard_map/ppermute | solution.py:282
  18.0 0.1 collective-permute-start.8
  18.2 0.0 collective-permute-done.1.refs_2_.refs_1_
  18.2 0.5 %shard_map.104 = (f32[256,512]{1,0:T(8,128)S(1)}, f32[256,512]{1,0:T(8,128)S(1)}, f32[256,512]{1,0:T(8,128)S(1)}) custom-call(bf16[256,256]{1,0:T(8,128)(2,1)S(1)} %get-tuple-element.33.own_ref, bf16[256,256]{1,0:T(8,128)(2,1)S(1)} %get-tuple-element.34.other_ref, bf16[256,512]{1,0:T(8,128)(2,1)S(1)} %copy-done, ...), custom_call_target="tpu_custom_call" | custom-call | flops 268435456 | bytes 2883584 | tf_op jit(solution)/shard_map/pallas_call | solution.py:39
  18.6 0.0 collective-permute-done.6.refs_2_
  18.6 0.0 collective-permute-done.7.refs_3_
  18.7 0.3 shard_map.106
  19.0 0.0 collective-permute-done.5.refs_3_.refs_9_
  19.0 0.3 shard_map.105.refs_6_
  19.2 0.1 collective-permute-done.8.refs_10_
  19.4 1.4 %shard_map.107 = (f32[176,256]{1,0:T(8,128)S(1)}, f32[176,256]{1,0:T(8,128)S(1)}, bf16[172,512]{1,0:T(8,128)(2,1)S(1)}, bf16[256,512]{1,0:T(8,128)(2,1)S(1)}) custom-call(s32[1]{0:T(128)} %bitcast.core_ref.refs_0_, s32[1,512]{1,0:T(1,128)S(1)} %get-tuple-element.28.refs_1_, f32[1,512]{1,0:T(1,128)S(1)} %get-tuple-element.29.refs_2_, ...), custom_call_target="tpu_custom_call" | custom-call | flops 805306368 | bytes 3469316 | tf_op jit(solution)/shard_map/pallas_call | solution.py:39
  20.8 0.3 collective-permute-start.10
  21.2 1.1 %shard_map.108 = (f32[4,64,256]{2,1,0:T(8,128)S(1)}, f32[4,64,256]{2,1,0:T(8,128)S(1)}) custom-call(s32[1]{0:T(128)} %bitcast.core_ref.refs_0_, bf16[172,512]{1,0:T(8,128)(2,1)S(1)} %get-tuple-element.40.g_ref, bf16[256,512]{1,0:T(8,128)(2,1)S(1)} %get-tuple-element.41.hidden_ref, bf16[512,512]{1,0:T(8,128)(2,1)S(1)} %get-tuple-element.30.refs_3_.at_ref, ...), custom_call_target="tpu_custom_call" | custom-call | flops 402653184 | bytes 1925124 | tf_op jit(solution)/shard_map/pallas_call | solution.py:39
  22.3 0.3 collective-permute-start.9
  22.6 0.0 collective-permute-done.10.recv_ref
  22.7 2.1 %collective-permute-start.11 = (bf16[176,256]{1,0:T(8,128)(2,1)S(1)}, bf16[176,256]{1,0:T(8,128)(2,1)S(1)}, u32[]{:S(2)}, u32[]{:S(2)}) collective-permute-start(bf16[176,256]{1,0:T(8,128)(2,1)S(1)} %shard_map.110.own_ref), channel_id=1, source_target_pairs={{0,2},{1,5},{2,0},{3,7},{4,6},{5,1},{6,4},{7,3},{8,10},{9,13},{10,... | collective-permute-start | bytes 270344 | tf_op jit(solution)/shard_map/ppermute | solution.py:291
  24.7 0.0 collective-permute-done.9.recv_ref
  24.8 1.3 %collective-permute-start.14 = (bf16[128,256]{1,0:T(8,128)(2,1)S(1)}, bf16[128,256]{1,0:T(8,128)(2,1)S(1)}, u32[]{:S(2)}, u32[]{:S(2)}) collective-permute-start(bf16[128,256]{1,0:T(8,128)(2,1)S(1)} %get-tuple-element.47), channel_id=1, source_target_pairs={{0,2},{1,5},{2,0},{3,7},{4,6},{5,1},{6,4},{7,3},{8,10},{9,13},{10,... | collective-permute-start | bytes 196616 | tf_op jit(solution)/shard_map/ppermute | solution.py:291
  26.0 2.2 %collective-permute-done.11.recv_ref = bf16[176,256]{1,0:T(8,128)(2,1)S(1)} collective-permute-done((bf16[176,256]{1,0:T(8,128)(2,1)S(1)}, bf16[176,256]{1,0:T(8,128)(2,1)S(1)}, u32[]{:S(2)}, u32[]{:S(2)}) %collective-permute-start.11) | collective-permute-done | bytes 90144 | tf_op jit(solution)/shard_map/ppermute | solution.py:291
  28.3 2.3 %collective-permute-start.12 = (bf16[176,256]{1,0:T(8,128)(2,1)S(1)}, bf16[176,256]{1,0:T(8,128)(2,1)S(1)}, u32[]{:S(2)}, u32[]{:S(2)}) collective-permute-start(bf16[176,256]{1,0:T(8,128)(2,1)S(1)} %shard_map.111.refs_0_), channel_id=1, source_target_pairs={{0,4},{1,3},{2,6},{3,1},{4,0},{5,7},{6,2},{7,5},{8,12},{9,11},{10,... | collective-permute-start | bytes 270344 | tf_op jit(solution)/shard_map/ppermute | solution.py:291
  30.5 0.0 collective-permute-done.14.recv_ref
  30.6 1.8 %collective-permute-start.15 = (bf16[64,256]{1,0:T(8,128)(2,1)S(1)}, bf16[64,256]{1,0:T(8,128)(2,1)S(1)}, u32[]{:S(2)}, u32[]{:S(2)}) collective-permute-start(bf16[64,256]{1,0:T(8,128)(2,1)S(1)} %get-tuple-element.49), channel_id=1, source_target_pairs={{0,4},{1,3},{2,6},{3,1},{4,0},{5,7},{6,2},{7,5},{8,12},{9,11},{10,... | collective-permute-start | bytes 98312 | tf_op jit(solution)/shard_map/ppermute | solution.py:291
  32.4 1.4 %collective-permute-done.12.refs_1_ = bf16[176,256]{1,0:T(8,128)(2,1)S(1)} collective-permute-done((bf16[176,256]{1,0:T(8,128)(2,1)S(1)}, bf16[176,256]{1,0:T(8,128)(2,1)S(1)}, u32[]{:S(2)}, u32[]{:S(2)}) %collective-permute-start.12) | collective-permute-done | bytes 90144 | tf_op jit(solution)/shard_map/ppermute | solution.py:291
  33.9 0.1 collective-permute-start.13
  33.9 1.9 %collective-permute-done.15.refs_0_ = bf16[64,256]{1,0:T(8,128)(2,1)S(1)} collective-permute-done((bf16[64,256]{1,0:T(8,128)(2,1)S(1)}, bf16[64,256]{1,0:T(8,128)(2,1)S(1)}, u32[]{:S(2)}, u32[]{:S(2)}) %collective-permute-start.15) | collective-permute-done | bytes 32800 | tf_op jit(solution)/shard_map/ppermute | solution.py:291
  35.8 0.0 collective-permute-done.13.other_ref
  35.8 0.9 %shard_map.115 = (f32[2,32,256]{2,1,0:T(8,128)}, f32[688,128]{1,0:T(8,128)}, f32[1,1]{1,0:T(1,128)}) custom-call(s32[1]{0:T(128)} %bitcast.core_ref.refs_0_, f32[176,256]{1,0:T(8,128)S(1)} %shard_map.112.own_ref, f32[176,256]{1,0:T(8,128)S(1)} %collective-permute-done.13.other_ref, f32[64,256]{1,0:T(8,128)S(1)} %shard_map.114.first_ref), custom_call_target="tpu_custom_call" | custom-call | bytes 843784 | tf_op jit(solution)/shard_map/pallas_call | solution.py:39
  (6 shorter events, 0.2 us)
Async XLA Ops:
  0.6 5.4 %copy-start = (bf16[256,512]{1,0:T(8,128)(2,1)S(1)}, bf16[256,512]{1,0:T(8,128)(2,1)}, u32[]{:S(2)}) copy-start(bf16[256,512]{1,0:T(8,128)(2,1)} %f_ref.1) | copy-start | bytes 786436
  0.6 7.6 %collective-permute-start = (bf16[256,512]{1,0:T(8,128)(2,1)}, bf16[256,512]{1,0:T(8,128)(2,1)S(1)}, u32[]{:S(2)}, u32[]{:S(2)}) collective-permute-start(bf16[256,512]{1,0:T(8,128)(2,1)} %f_ref.1), channel_id=1, source_target_pairs={{0,8},{1,17},{2,10},{3,19},{4,12},{5,21},{6,14},{7,23},{8,0},{9,25... | collective-permute-start | bytes 786440 | tf_op jit(solution)/shard_map/ppermute | solution.py:282
  5.9 6.5 %collective-permute-start.2 = (bf16[256,256]{1,0:T(8,128)(2,1)S(1)}, bf16[256,256]{1,0:T(8,128)(2,1)S(1)}, u32[]{:S(2)}, u32[]{:S(2)}) collective-permute-start(bf16[256,256]{1,0:T(8,128)(2,1)S(1)} %get-tuple-element.33.own_ref), channel_id=1, source_target_pairs={{0,8},{1,17},{2,10},{3,19},{4,12},{5,21},{6,14},{7,23},{8,0},{9,25... | collective-permute-start | bytes 393224 | tf_op jit(solution)/shard_map/ppermute | solution.py:282
  6.0 12.2 %collective-permute-start.1 = (bf16[256,512]{1,0:T(8,128)(2,1)S(1)}, bf16[256,512]{1,0:T(8,128)(2,1)S(1)}, u32[]{:S(2)}, u32[]{:S(2)}) collective-permute-start(bf16[256,512]{1,0:T(8,128)(2,1)S(1)} %copy-done), channel_id=1, source_target_pairs={{0,16},{1,9},{2,18},{3,11},{4,20},{5,13},{6,22},{7,15},{8,24},{9,1... | collective-permute-start | bytes 786440 | tf_op jit(solution)/shard_map/ppermute | solution.py:282
  8.0 5.9 %collective-permute-start.3 = (bf16[256,256]{1,0:T(8,128)(2,1)S(1)}, bf16[256,256]{1,0:T(8,128)(2,1)S(1)}, u32[]{:S(2)}, u32[]{:S(2)}) collective-permute-start(bf16[256,256]{1,0:T(8,128)(2,1)S(1)} %get-tuple-element.33.own_ref), channel_id=1, source_target_pairs={{0,16},{1,9},{2,18},{3,11},{4,20},{5,13},{6,22},{7,15},{8,24},{9,1... | collective-permute-start | bytes 393224 | tf_op jit(solution)/shard_map/ppermute | solution.py:282
  8.2 10.8 %collective-permute-start.5 = (bf16[256,512]{1,0:T(8,128)(2,1)S(1)}, bf16[256,512]{1,0:T(8,128)(2,1)S(1)}, u32[]{:S(2)}, u32[]{:S(2)}) collective-permute-start(bf16[256,512]{1,0:T(8,128)(2,1)S(1)} %collective-permute-done.refs_1_.refs_0_), channel_id=1, source_target_pairs={{0,16},{1,9},{2,18},{3,11},{4,20},{5,13},{6,22},{7,15},{8,24},{9,1... | collective-permute-start | bytes 786440 | tf_op jit(solution)/shard_map/ppermute | solution.py:282
  12.4 5.7 %collective-permute-start.4 = (bf16[256,256]{1,0:T(8,128)(2,1)S(1)}, bf16[256,256]{1,0:T(8,128)(2,1)S(1)}, u32[]{:S(2)}, u32[]{:S(2)}) collective-permute-start(bf16[256,256]{1,0:T(8,128)(2,1)S(1)} %collective-permute-done.2.refs_3_), channel_id=1, source_target_pairs={{0,16},{1,9},{2,18},{3,11},{4,20},{5,13},{6,22},{7,15},{8,24},{9,1... | collective-permute-start | bytes 393224 | tf_op jit(solution)/shard_map/ppermute | solution.py:282
  13.9 4.8 %collective-permute-start.6 = (bf16[256,256]{1,0:T(8,128)(2,1)S(1)}, bf16[256,256]{1,0:T(8,128)(2,1)S(1)}, u32[]{:S(2)}, u32[]{:S(2)}) collective-permute-start(bf16[256,256]{1,0:T(8,128)(2,1)S(1)} %collective-permute-done.3.refs_4_), channel_id=1, source_target_pairs={{0,1},{1,0},{2,3},{3,2},{4,5},{5,4},{6,7},{7,6},{8,9},{9,8},{10,11... | collective-permute-start | bytes 393224 | tf_op jit(solution)/shard_map/ppermute | solution.py:264
  14.0 4.7 %collective-permute-start.7 = (bf16[256,256]{1,0:T(8,128)(2,1)S(1)}, bf16[256,256]{1,0:T(8,128)(2,1)S(1)}, u32[]{:S(2)}, u32[]{:S(2)}) collective-permute-start(bf16[256,256]{1,0:T(8,128)(2,1)S(1)} %collective-permute-done.2.refs_3_), channel_id=1, source_target_pairs={{0,1},{1,0},{2,3},{3,2},{4,5},{5,4},{6,7},{7,6},{8,9},{9,8},{10,11... | collective-permute-start | bytes 393224 | tf_op jit(solution)/shard_map/ppermute | solution.py:264
  18.0 1.3 %collective-permute-start.8 = (bf16[256,256]{1,0:T(8,128)(2,1)S(1)}, bf16[256,256]{1,0:T(8,128)(2,1)S(1)}, u32[]{:S(2)}, u32[]{:S(2)}) collective-permute-start(bf16[256,256]{1,0:T(8,128)(2,1)S(1)} %collective-permute-done.4.refs_2_), channel_id=1, source_target_pairs={{0,1},{1,0},{2,3},{3,2},{4,5},{5,4},{6,7},{7,6},{8,9},{9,8},{10,11... | collective-permute-start | bytes 393224 | tf_op jit(solution)/shard_map/ppermute | solution.py:264
  20.8 1.8 %collective-permute-start.10 = (f32[176,256]{1,0:T(8,128)S(1)}, f32[176,256]{1,0:T(8,128)S(1)}, u32[]{:S(2)}, u32[]{:S(2)}) collective-permute-start(f32[176,256]{1,0:T(8,128)S(1)} %get-tuple-element.46), channel_id=1, source_target_pairs={{0,1},{1,0},{2,3},{3,2},{4,5},{5,4},{6,7},{7,6},{8,9},{9,8},{10,11... | collective-permute-start | bytes 540680 | tf_op jit(solution)/shard_map/ppermute | solution.py:264
  22.3 2.4 %collective-permute-start.9 = (f32[4,64,256]{2,1,0:T(8,128)S(1)}, f32[4,64,256]{2,1,0:T(8,128)S(1)}, u32[]{:S(2)}, u32[]{:S(2)}) collective-permute-start(f32[4,64,256]{2,1,0:T(8,128)S(1)} %get-tuple-element.43), channel_id=1, source_target_pairs={{0,1},{1,0},{2,3},{3,2},{4,5},{5,4},{6,7},{7,6},{8,9},{9,8},{10,11... | collective-permute-start | bytes 786440 | tf_op jit(solution)/shard_map/ppermute | solution.py:264
  22.7 5.6 %collective-permute-start.11 = (bf16[176,256]{1,0:T(8,128)(2,1)S(1)}, bf16[176,256]{1,0:T(8,128)(2,1)S(1)}, u32[]{:S(2)}, u32[]{:S(2)}) collective-permute-start(bf16[176,256]{1,0:T(8,128)(2,1)S(1)} %shard_map.110.own_ref), channel_id=1, source_target_pairs={{0,2},{1,5},{2,0},{3,7},{4,6},{5,1},{6,4},{7,3},{8,10},{9,13},{10,... | collective-permute-start | bytes 270344 | tf_op jit(solution)/shard_map/ppermute | solution.py:291
  24.8 5.8 %collective-permute-start.14 = (bf16[128,256]{1,0:T(8,128)(2,1)S(1)}, bf16[128,256]{1,0:T(8,128)(2,1)S(1)}, u32[]{:S(2)}, u32[]{:S(2)}) collective-permute-start(bf16[128,256]{1,0:T(8,128)(2,1)S(1)} %get-tuple-element.47), channel_id=1, source_target_pairs={{0,2},{1,5},{2,0},{3,7},{4,6},{5,1},{6,4},{7,3},{8,10},{9,13},{10,... | collective-permute-start | bytes 196616 | tf_op jit(solution)/shard_map/ppermute | solution.py:291
  28.3 5.6 %collective-permute-start.12 = (bf16[176,256]{1,0:T(8,128)(2,1)S(1)}, bf16[176,256]{1,0:T(8,128)(2,1)S(1)}, u32[]{:S(2)}, u32[]{:S(2)}) collective-permute-start(bf16[176,256]{1,0:T(8,128)(2,1)S(1)} %shard_map.111.refs_0_), channel_id=1, source_target_pairs={{0,4},{1,3},{2,6},{3,1},{4,0},{5,7},{6,2},{7,5},{8,12},{9,11},{10,... | collective-permute-start | bytes 270344 | tf_op jit(solution)/shard_map/ppermute | solution.py:291
  30.6 5.2 %collective-permute-start.15 = (bf16[64,256]{1,0:T(8,128)(2,1)S(1)}, bf16[64,256]{1,0:T(8,128)(2,1)S(1)}, u32[]{:S(2)}, u32[]{:S(2)}) collective-permute-start(bf16[64,256]{1,0:T(8,128)(2,1)S(1)} %get-tuple-element.49), channel_id=1, source_target_pairs={{0,4},{1,3},{2,6},{3,1},{4,0},{5,7},{6,2},{7,5},{8,12},{9,11},{10,... | collective-permute-start | bytes 98312 | tf_op jit(solution)/shard_map/ppermute | solution.py:291
  33.9 1.9 %collective-permute-start.13 = (f32[176,256]{1,0:T(8,128)S(1)}, f32[176,256]{1,0:T(8,128)S(1)}, u32[]{:S(2)}, u32[]{:S(2)}) collective-permute-start(f32[176,256]{1,0:T(8,128)S(1)} %shard_map.112.own_ref), channel_id=1, source_target_pairs={{0,1},{1,0},{2,3},{3,2},{4,5},{5,4},{6,7},{7,6},{8,9},{9,8},{10,11... | collective-permute-start | bytes 540680 | tf_op jit(solution)/shard_map/ppermute | solution.py:264

commit v12 on v10

--- a/solution.py
+++ b/solution.py
@@ -112,17 +112,17 @@
     f_refs, refs = refs[: feat_count - 1], refs[feat_count - 1 :]
     core_ref, labels_ref, weight_ref, at_ref, w2s_ref, w2n_ref, mine_ref, other_ref = refs[:8]
     partner_refs = refs[8 : 7 + feat_count]
-    send_ref, keep_ref, g_ref, hidden_ref, proj, pair = refs[7 + feat_count :]
+    send_ref, keep_ref, g_ref, hidden_ref, pair = refs[7 + feat_count :]
     core = core_ref[0]
     classes = w2s_ref.shape[0]
     nodes = at_ref.shape[1]
     scale = 1.0 / fanout
-    proj[core] = mine_ref[...]
-    proj[1 - core] = tree_product(
+    first, mine = core == 0, mine_ref[...]
+    other = tree_product(
         0, feat_count, {(0, 1): other_ref}, lambda s: dot_tn(partner_refs[swapped(s, feat_count) - 1][...], f_refs[s - 1][...])
     )
     at = at_ref[...]
-    pre = proj[0] + dot_nn(proj[1].astype(BF16), at) * scale
+    pre = jnp.where(first, mine, other) + dot_nn(jnp.where(first, other, mine).astype(BF16), at) * scale
     hidden = jnp.maximum(pre, 0.0).astype(BF16)
     hidden_ref[...] = hidden
     second = (dot_nn(hidden, at) * scale).astype(BF16)
@@ -145,10 +145,8 @@
     norm_part = jnp.sum(weight)
     for out_ref, which in ((send_ref, 1 - core), (keep_ref, core)):
         rows, cols = out_ref.shape
-        row = lax.broadcasted_iota(jnp.int32, (rows, cols), 0)
-        col = lax.broadcasted_iota(jnp.int32, (rows, cols), 1)
-        extra = jnp.where(col == 0, loss_part, jnp.where(col == 1, norm_part, 0.0))
-        out_ref[...] = jnp.where(row >= classes, extra, 0.0)
+        col = lax.broadcasted_iota(jnp.int32, (rows - classes, cols), 1)
+        out_ref[classes:, :] = jnp.where(col == 0, loss_part, jnp.where(col == 1, norm_part, 0.0))
         out_ref[:classes, :] = dot_nt(grad, pair[which])
 
 
@@ -346,7 +344,6 @@
         ],
         wide[1:] + [core, labels, loss_weight, at, w2s, w2n, mine_proj, other_proj] + partner,
         scratch=[
-            pltpu.VMEM((2, hid, nodes), F32),
             pltpu.VMEM((2, hid, nodes), BF16),
         ],
         flops=2 * nodes * hid * 2 * (rows * feat_count + nodes),

time: 37 us -> 36.9 us (level)
  no operation moved by 1% of the time
where the time goes in v12:
time: 36.9 us; the launch traced here: 36.8 us
  starting transfers between devices  17.2 us (47%)
  waiting for transfers between devices  12.2 us (33%)
  Pallas kernels  6.71 us (18%)
  between operations  0.74 us (2%)
    ppermute x6, starting transfers between devices, hop(): return lax.ppermute(value, ('feat', 'dp'), pairs)  9.01 us
    ppermute x4, starting transfers between devices, fold_hop(): return lax.ppermute(value, 'dp', pairs)  7.2 us
    pallas_call x12, Pallas kernels, call(): pl.pallas_call(kernel, out_shape=outs if final else [pltpu.VMEM(o.shape,...  6.71 us
    ppermute x6, waiting for transfers between devices, hop(): return lax.ppermute(value, ('feat', 'dp'), pairs)  6 us
    ppermute x4, waiting for transfers between devices, fold_hop(): return lax.ppermute(value, 'dp', pairs)  5.67 us
    ppermute x6, starting transfers between devices, exchange(): return lax.ppermute(value, axis, [(i, i ^ step) for i in range(size)])  0.97 us
  transfers between devices with their start and end apart: 16, of which 8 were waited for; matrix products, arithmetic and copies ran while one was open for 0% of the time, Pallas kernels for 12%

profile of v12, /device:TPU:0, one launch (start us, length us, event | category | flops | bytes accessed | tf_op | source)
XLA Modules:
  0.0 36.8 jit_solution(14629615664897520402)
XLA Ops:
  0.6 0.0 copy-start
  0.6 3.0 %collective-permute-start = (bf16[256,512]{1,0:T(8,128)(2,1)}, bf16[256,512]{1,0:T(8,128)(2,1)S(1)}, u32[]{:S(2)}, u32[]{:S(2)}) collective-permute-start(bf16[256,512]{1,0:T(8,128)(2,1)} %f_ref.1), channel_id=1, source_target_pairs={{0,8},{1,17},{2,10},{3,19},{4,12},{5,21},{6,14},{7,23},{8,0},{9,25... | collective-permute-start | bytes 786440 | tf_op jit(solution)/shard_map/ppermute | solution.py:273
  3.6 2.2 %shard_map.103 = (bf16[512,512]{1,0:T(8,128)(2,1)S(1)}, bf16[256,256]{1,0:T(8,128)(2,1)S(1)}, bf16[256,256]{1,0:T(8,128)(2,1)S(1)}, s32[1,512]{1,0:T(1,128)S(1)}...) custom-call(s32[1]{0:T(128)} %bitcast.core_ref.refs_3_, s32[10,512]{1,0:T(8,128)} %bitcast.15, ...), custom_call_target="tpu_custom_call" | custom-call | flops 2621440 | bytes 1429508 | tf_op jit(solution)/shard_map/pallas_call | solution.py:39
  5.9 0.1 collective-permute-start.3
  6.0 0.0 copy-done
  6.0 2.0 %collective-permute-start.1 = (bf16[256,512]{1,0:T(8,128)(2,1)S(1)}, bf16[256,512]{1,0:T(8,128)(2,1)S(1)}, u32[]{:S(2)}, u32[]{:S(2)}) collective-permute-start(bf16[256,512]{1,0:T(8,128)(2,1)S(1)} %copy-done), channel_id=1, source_target_pairs={{0,16},{1,9},{2,18},{3,11},{4,20},{5,13},{6,22},{7,15},{8,24},{9,1... | collective-permute-start | bytes 786440 | tf_op jit(solution)/shard_map/ppermute | solution.py:273
  8.0 0.2 collective-permute-done.refs_1_.refs_0_
  8.2 2.4 %collective-permute-start.2 = (bf16[256,512]{1,0:T(8,128)(2,1)S(1)}, bf16[256,512]{1,0:T(8,128)(2,1)S(1)}, u32[]{:S(2)}, u32[]{:S(2)}) collective-permute-start(bf16[256,512]{1,0:T(8,128)(2,1)S(1)} %collective-permute-done.refs_1_.refs_0_), channel_id=1, source_target_pairs={{0,16},{1,9},{2,18},{3,11},{4,20},{5,13},{6,22},{7,15},{8,24},{9,1... | collective-permute-start | bytes 786440 | tf_op jit(solution)/shard_map/ppermute | solution.py:273
  10.6 0.0 collective-permute-start.4
  10.6 1.8 %collective-permute-done.3.refs_3_ = bf16[256,256]{1,0:T(8,128)(2,1)S(1)} collective-permute-done((bf16[256,256]{1,0:T(8,128)(2,1)S(1)}, bf16[256,256]{1,0:T(8,128)(2,1)S(1)}, u32[]{:S(2)}, u32[]{:S(2)}) %collective-permute-start.3) | collective-permute-done | bytes 131104 | tf_op jit(solution)/shard_map/ppermute | solution.py:273
  12.4 1.5 %collective-permute-start.5 = (bf16[256,256]{1,0:T(8,128)(2,1)S(1)}, bf16[256,256]{1,0:T(8,128)(2,1)S(1)}, u32[]{:S(2)}, u32[]{:S(2)}) collective-permute-start(bf16[256,256]{1,0:T(8,128)(2,1)S(1)} %collective-permute-done.3.refs_3_), channel_id=1, source_target_pairs={{0,16},{1,9},{2,18},{3,11},{4,20},{5,13},{6,22},{7,15},{8,24},{9,1... | collective-permute-start | bytes 393224 | tf_op jit(solution)/shard_map/ppermute | solution.py:273
  13.9 0.0 collective-permute-start.6
  13.9 2.8 %collective-permute-done.4.refs_4_ = bf16[256,256]{1,0:T(8,128)(2,1)S(1)} collective-permute-done((bf16[256,256]{1,0:T(8,128)(2,1)S(1)}, bf16[256,256]{1,0:T(8,128)(2,1)S(1)}, u32[]{:S(2)}, u32[]{:S(2)}) %collective-permute-start.4) | collective-permute-done | bytes 131104 | tf_op jit(solution)/shard_map/ppermute | solution.py:273
  16.6 0.1 collective-permute-start.7
  16.8 1.3 %collective-permute-done.5.refs_2_ = bf16[256,256]{1,0:T(8,128)(2,1)S(1)} collective-permute-done((bf16[256,256]{1,0:T(8,128)(2,1)S(1)}, bf16[256,256]{1,0:T(8,128)(2,1)S(1)}, u32[]{:S(2)}, u32[]{:S(2)}) %collective-permute-start.5) | collective-permute-done | bytes 131104 | tf_op jit(solution)/shard_map/ppermute | solution.py:273
  18.0 0.1 collective-permute-start.8
  18.2 0.0 collective-permute-done.1.refs_2_.refs_1_
  18.2 0.5 %shard_map.104 = (f32[256,512]{1,0:T(8,128)S(1)}, f32[256,512]{1,0:T(8,128)S(1)}, f32[256,512]{1,0:T(8,128)S(1)}) custom-call(bf16[256,256]{1,0:T(8,128)(2,1)S(1)} %get-tuple-element.31.own_ref, bf16[256,256]{1,0:T(8,128)(2,1)S(1)} %get-tuple-element.32.other_ref, bf16[256,512]{1,0:T(8,128)(2,1)S(1)} %copy-done, ...), custom_call_target="tpu_custom_call" | custom-call | flops 268435456 | bytes 2883584 | tf_op jit(solution)/shard_map/pallas_call | solution.py:39
  18.6 0.0 collective-permute-done.2.refs_3_.refs_2_
  18.6 0.2 shard_map.105.refs_9_
  18.9 0.0 collective-permute-done.6.refs_11_
  18.9 0.0 collective-permute-done.7.refs_12_
  18.9 0.5 %collective-permute-done.8.refs_13_ = bf16[256,256]{1,0:T(8,128)(2,1)S(1)} collective-permute-done((bf16[256,256]{1,0:T(8,128)(2,1)S(1)}, bf16[256,256]{1,0:T(8,128)(2,1)S(1)}, u32[]{:S(2)}, u32[]{:S(2)}) %collective-permute-start.8) | collective-permute-done | bytes 131104 | tf_op jit(solution)/shard_map/ppermute | solution.py:255
  19.4 1.5 %shard_map.106 = (f32[176,256]{1,0:T(8,128)S(1)}, f32[176,256]{1,0:T(8,128)S(1)}, bf16[172,512]{1,0:T(8,128)(2,1)S(1)}, bf16[256,512]{1,0:T(8,128)(2,1)S(1)}) custom-call(bf16[256,512]{1,0:T(8,128)(2,1)S(1)} %collective-permute-done.refs_1_.refs_0_, bf16[256,512]{1,0:T(8,128)(2,1)S(1)} %collective-permute-done.1.refs_2_.refs_1_, ...), custom_call_target="tpu_custom_call" | custom-call | flops 805306368 | bytes 3731460 | tf_op jit(solution)/shard_map/pallas_call | solution.py:39
  20.9 0.2 collective-permute-start.10
  21.1 1.1 %shard_map.107 = (f32[4,64,256]{2,1,0:T(8,128)S(1)}, f32[4,64,256]{2,1,0:T(8,128)S(1)}) custom-call(s32[1]{0:T(128)} %bitcast.core_ref.refs_3_, bf16[172,512]{1,0:T(8,128)(2,1)S(1)} %get-tuple-element.36.g_ref, bf16[256,512]{1,0:T(8,128)(2,1)S(1)} %get-tuple-element.37.hidden_ref, bf16[512,512]{1,0:T(8,128)(2,1)S(1)} %get-tuple-element.28.refs_6_.at_ref, ...), custom_call_target="tpu_custom_call" | custom-call | flops 402653184 | bytes 1925124 | tf_op jit(solution)/shard_map/pallas_call | solution.py:39
  22.3 0.4 %collective-permute-start.9 = (f32[4,64,256]{2,1,0:T(8,128)S(1)}, f32[4,64,256]{2,1,0:T(8,128)S(1)}, u32[]{:S(2)}, u32[]{:S(2)}) collective-permute-start(f32[4,64,256]{2,1,0:T(8,128)S(1)} %get-tuple-element.39), channel_id=1, source_target_pairs={{0,1},{1,0},{2,3},{3,2},{4,5},{5,4},{6,7},{7,6},{8,9},{9,8},{10,11... | collective-permute-start | bytes 786440 | tf_op jit(solution)/shard_map/ppermute | solution.py:255
  22.7 0.0 collective-permute-done.10.recv_ref
  22.8 2.1 %collective-permute-start.11 = (bf16[176,256]{1,0:T(8,128)(2,1)S(1)}, bf16[176,256]{1,0:T(8,128)(2,1)S(1)}, u32[]{:S(2)}, u32[]{:S(2)}) collective-permute-start(bf16[176,256]{1,0:T(8,128)(2,1)S(1)} %shard_map.109.own_ref), channel_id=1, source_target_pairs={{0,2},{1,5},{2,0},{3,7},{4,6},{5,1},{6,4},{7,3},{8,10},{9,13},{10,... | collective-permute-start | bytes 270344 | tf_op jit(solution)/shard_map/ppermute | solution.py:282
  24.9 0.0 collective-permute-done.9.recv_ref
  24.9 1.1 %collective-permute-start.14 = (bf16[128,256]{1,0:T(8,128)(2,1)S(1)}, bf16[128,256]{1,0:T(8,128)(2,1)S(1)}, u32[]{:S(2)}, u32[]{:S(2)}) collective-permute-start(bf16[128,256]{1,0:T(8,128)(2,1)S(1)} %get-tuple-element.43), channel_id=1, source_target_pairs={{0,2},{1,5},{2,0},{3,7},{4,6},{5,1},{6,4},{7,3},{8,10},{9,13},{10,... | collective-permute-start | bytes 196616 | tf_op jit(solution)/shard_map/ppermute | solution.py:282
  26.0 2.3 %collective-permute-done.11.recv_ref = bf16[176,256]{1,0:T(8,128)(2,1)S(1)} collective-permute-done((bf16[176,256]{1,0:T(8,128)(2,1)S(1)}, bf16[176,256]{1,0:T(8,128)(2,1)S(1)}, u32[]{:S(2)}, u32[]{:S(2)}) %collective-permute-start.11) | collective-permute-done | bytes 90144 | tf_op jit(solution)/shard_map/ppermute | solution.py:282
  28.4 2.2 %collective-permute-start.12 = (bf16[176,256]{1,0:T(8,128)(2,1)S(1)}, bf16[176,256]{1,0:T(8,128)(2,1)S(1)}, u32[]{:S(2)}, u32[]{:S(2)}) collective-permute-start(bf16[176,256]{1,0:T(8,128)(2,1)S(1)} %shard_map.110.refs_0_), channel_id=1, source_target_pairs={{0,4},{1,3},{2,6},{3,1},{4,0},{5,7},{6,2},{7,5},{8,12},{9,11},{10,... | collective-permute-start | bytes 270344 | tf_op jit(solution)/shard_map/ppermute | solution.py:282
  30.5 0.0 collective-permute-done.14.recv_ref
  30.5 1.8 %collective-permute-start.15 = (bf16[64,256]{1,0:T(8,128)(2,1)S(1)}, bf16[64,256]{1,0:T(8,128)(2,1)S(1)}, u32[]{:S(2)}, u32[]{:S(2)}) collective-permute-start(bf16[64,256]{1,0:T(8,128)(2,1)S(1)} %get-tuple-element.45), channel_id=1, source_target_pairs={{0,4},{1,3},{2,6},{3,1},{4,0},{5,7},{6,2},{7,5},{8,12},{9,11},{10,... | collective-permute-start | bytes 98312 | tf_op jit(solution)/shard_map/ppermute | solution.py:282
  32.4 1.6 %collective-permute-done.12.refs_1_ = bf16[176,256]{1,0:T(8,128)(2,1)S(1)} collective-permute-done((bf16[176,256]{1,0:T(8,128)(2,1)S(1)}, bf16[176,256]{1,0:T(8,128)(2,1)S(1)}, u32[]{:S(2)}, u32[]{:S(2)}) %collective-permute-start.12) | collective-permute-done | bytes 90144 | tf_op jit(solution)/shard_map/ppermute | solution.py:282
  34.0 0.1 collective-permute-start.13
  34.1 1.8 %collective-permute-done.15.refs_0_ = bf16[64,256]{1,0:T(8,128)(2,1)S(1)} collective-permute-done((bf16[64,256]{1,0:T(8,128)(2,1)S(1)}, bf16[64,256]{1,0:T(8,128)(2,1)S(1)}, u32[]{:S(2)}, u32[]{:S(2)}) %collective-permute-start.15) | collective-permute-done | bytes 32800 | tf_op jit(solution)/shard_map/ppermute | solution.py:282
  35.9 0.0 collective-permute-done.13.other_ref
  35.9 0.9 %shard_map.114 = (f32[2,32,256]{2,1,0:T(8,128)}, f32[688,128]{1,0:T(8,128)}, f32[1,1]{1,0:T(1,128)}) custom-call(s32[1]{0:T(128)} %bitcast.core_ref.refs_3_, f32[176,256]{1,0:T(8,128)S(1)} %shard_map.111.own_ref, f32[176,256]{1,0:T(8,128)S(1)} %collective-permute-done.13.other_ref, f32[64,256]{1,0:T(8,128)S(1)} %shard_map.113.first_ref), custom_call_target="tpu_custom_call" | custom-call | bytes 843784 | tf_op jit(solution)/shard_map/pallas_call | solution.py:39
  (6 shorter events, 0.2 us)
Async XLA Ops:
  0.6 5.4 %copy-start = (bf16[256,512]{1,0:T(8,128)(2,1)S(1)}, bf16[256,512]{1,0:T(8,128)(2,1)}, u32[]{:S(2)}) copy-start(bf16[256,512]{1,0:T(8,128)(2,1)} %f_ref.1) | copy-start | bytes 786436
  0.6 7.6 %collective-permute-start = (bf16[256,512]{1,0:T(8,128)(2,1)}, bf16[256,512]{1,0:T(8,128)(2,1)S(1)}, u32[]{:S(2)}, u32[]{:S(2)}) collective-permute-start(bf16[256,512]{1,0:T(8,128)(2,1)} %f_ref.1), channel_id=1, source_target_pairs={{0,8},{1,17},{2,10},{3,19},{4,12},{5,21},{6,14},{7,23},{8,0},{9,25... | collective-permute-start | bytes 786440 | tf_op jit(solution)/shard_map/ppermute | solution.py:273
  5.9 6.5 %collective-permute-start.3 = (bf16[256,256]{1,0:T(8,128)(2,1)S(1)}, bf16[256,256]{1,0:T(8,128)(2,1)S(1)}, u32[]{:S(2)}, u32[]{:S(2)}) collective-permute-start(bf16[256,256]{1,0:T(8,128)(2,1)S(1)} %get-tuple-element.31.own_ref), channel_id=1, source_target_pairs={{0,8},{1,17},{2,10},{3,19},{4,12},{5,21},{6,14},{7,23},{8,0},{9,25... | collective-permute-start | bytes 393224 | tf_op jit(solution)/shard_map/ppermute | solution.py:273
  6.0 12.2 %collective-permute-start.1 = (bf16[256,512]{1,0:T(8,128)(2,1)S(1)}, bf16[256,512]{1,0:T(8,128)(2,1)S(1)}, u32[]{:S(2)}, u32[]{:S(2)}) collective-permute-start(bf16[256,512]{1,0:T(8,128)(2,1)S(1)} %copy-done), channel_id=1, source_target_pairs={{0,16},{1,9},{2,18},{3,11},{4,20},{5,13},{6,22},{7,15},{8,24},{9,1... | collective-permute-start | bytes 786440 | tf_op jit(solution)/shard_map/ppermute | solution.py:273
  8.2 10.4 %collective-permute-start.2 = (bf16[256,512]{1,0:T(8,128)(2,1)S(1)}, bf16[256,512]{1,0:T(8,128)(2,1)S(1)}, u32[]{:S(2)}, u32[]{:S(2)}) collective-permute-start(bf16[256,512]{1,0:T(8,128)(2,1)S(1)} %collective-permute-done.refs_1_.refs_0_), channel_id=1, source_target_pairs={{0,16},{1,9},{2,18},{3,11},{4,20},{5,13},{6,22},{7,15},{8,24},{9,1... | collective-permute-start | bytes 786440 | tf_op jit(solution)/shard_map/ppermute | solution.py:273
  10.6 6.1 %collective-permute-start.4 = (bf16[256,256]{1,0:T(8,128)(2,1)S(1)}, bf16[256,256]{1,0:T(8,128)(2,1)S(1)}, u32[]{:S(2)}, u32[]{:S(2)}) collective-permute-start(bf16[256,256]{1,0:T(8,128)(2,1)S(1)} %get-tuple-element.31.own_ref), channel_id=1, source_target_pairs={{0,16},{1,9},{2,18},{3,11},{4,20},{5,13},{6,22},{7,15},{8,24},{9,1... | collective-permute-start | bytes 393224 | tf_op jit(solution)/shard_map/ppermute | solution.py:273
  12.4 5.7 %collective-permute-start.5 = (bf16[256,256]{1,0:T(8,128)(2,1)S(1)}, bf16[256,256]{1,0:T(8,128)(2,1)S(1)}, u32[]{:S(2)}, u32[]{:S(2)}) collective-permute-start(bf16[256,256]{1,0:T(8,128)(2,1)S(1)} %collective-permute-done.3.refs_3_), channel_id=1, source_target_pairs={{0,16},{1,9},{2,18},{3,11},{4,20},{5,13},{6,22},{7,15},{8,24},{9,1... | collective-permute-start | bytes 393224 | tf_op jit(solution)/shard_map/ppermute | solution.py:273
  13.9 5.0 %collective-permute-start.6 = (bf16[256,256]{1,0:T(8,128)(2,1)S(1)}, bf16[256,256]{1,0:T(8,128)(2,1)S(1)}, u32[]{:S(2)}, u32[]{:S(2)}) collective-permute-start(bf16[256,256]{1,0:T(8,128)(2,1)S(1)} %collective-permute-done.3.refs_3_), channel_id=1, source_target_pairs={{0,1},{1,0},{2,3},{3,2},{4,5},{5,4},{6,7},{7,6},{8,9},{9,8},{10,11... | collective-permute-start | bytes 393224 | tf_op jit(solution)/shard_map/ppermute | solution.py:255
  16.6 2.3 %collective-permute-start.7 = (bf16[256,256]{1,0:T(8,128)(2,1)S(1)}, bf16[256,256]{1,0:T(8,128)(2,1)S(1)}, u32[]{:S(2)}, u32[]{:S(2)}) collective-permute-start(bf16[256,256]{1,0:T(8,128)(2,1)S(1)} %collective-permute-done.4.refs_4_), channel_id=1, source_target_pairs={{0,1},{1,0},{2,3},{3,2},{4,5},{5,4},{6,7},{7,6},{8,9},{9,8},{10,11... | collective-permute-start | bytes 393224 | tf_op jit(solution)/shard_map/ppermute | solution.py:255
  18.0 1.3 %collective-permute-start.8 = (bf16[256,256]{1,0:T(8,128)(2,1)S(1)}, bf16[256,256]{1,0:T(8,128)(2,1)S(1)}, u32[]{:S(2)}, u32[]{:S(2)}) collective-permute-start(bf16[256,256]{1,0:T(8,128)(2,1)S(1)} %collective-permute-done.5.refs_2_), channel_id=1, source_target_pairs={{0,1},{1,0},{2,3},{3,2},{4,5},{5,4},{6,7},{7,6},{8,9},{9,8},{10,11... | collective-permute-start | bytes 393224 | tf_op jit(solution)/shard_map/ppermute | solution.py:255
  20.9 1.8 %collective-permute-start.10 = (f32[176,256]{1,0:T(8,128)S(1)}, f32[176,256]{1,0:T(8,128)S(1)}, u32[]{:S(2)}, u32[]{:S(2)}) collective-permute-start(f32[176,256]{1,0:T(8,128)S(1)} %get-tuple-element.42), channel_id=1, source_target_pairs={{0,1},{1,0},{2,3},{3,2},{4,5},{5,4},{6,7},{7,6},{8,9},{9,8},{10,11... | collective-permute-start | bytes 540680 | tf_op jit(solution)/shard_map/ppermute | solution.py:255
  22.3 2.6 %collective-permute-start.9 = (f32[4,64,256]{2,1,0:T(8,128)S(1)}, f32[4,64,256]{2,1,0:T(8,128)S(1)}, u32[]{:S(2)}, u32[]{:S(2)}) collective-permute-start(f32[4,64,256]{2,1,0:T(8,128)S(1)} %get-tuple-element.39), channel_id=1, source_target_pairs={{0,1},{1,0},{2,3},{3,2},{4,5},{5,4},{6,7},{7,6},{8,9},{9,8},{10,11... | collective-permute-start | bytes 786440 | tf_op jit(solution)/shard_map/ppermute | solution.py:255
  22.8 5.6 %collective-permute-start.11 = (bf16[176,256]{1,0:T(8,128)(2,1)S(1)}, bf16[176,256]{1,0:T(8,128)(2,1)S(1)}, u32[]{:S(2)}, u32[]{:S(2)}) collective-permute-start(bf16[176,256]{1,0:T(8,128)(2,1)S(1)} %shard_map.109.own_ref), channel_id=1, source_target_pairs={{0,2},{1,5},{2,0},{3,7},{4,6},{5,1},{6,4},{7,3},{8,10},{9,13},{10,... | collective-permute-start | bytes 270344 | tf_op jit(solution)/shard_map/ppermute | solution.py:282
  24.9 5.6 %collective-permute-start.14 = (bf16[128,256]{1,0:T(8,128)(2,1)S(1)}, bf16[128,256]{1,0:T(8,128)(2,1)S(1)}, u32[]{:S(2)}, u32[]{:S(2)}) collective-permute-start(bf16[128,256]{1,0:T(8,128)(2,1)S(1)} %get-tuple-element.43), channel_id=1, source_target_pairs={{0,2},{1,5},{2,0},{3,7},{4,6},{5,1},{6,4},{7,3},{8,10},{9,13},{10,... | collective-permute-start | bytes 196616 | tf_op jit(solution)/shard_map/ppermute | solution.py:282
  28.4 5.6 %collective-permute-start.12 = (bf16[176,256]{1,0:T(8,128)(2,1)S(1)}, bf16[176,256]{1,0:T(8,128)(2,1)S(1)}, u32[]{:S(2)}, u32[]{:S(2)}) collective-permute-start(bf16[176,256]{1,0:T(8,128)(2,1)S(1)} %shard_map.110.refs_0_), channel_id=1, source_target_pairs={{0,4},{1,3},{2,6},{3,1},{4,0},{5,7},{6,2},{7,5},{8,12},{9,11},{10,... | collective-permute-start | bytes 270344 | tf_op jit(solution)/shard_map/ppermute | solution.py:282
  30.5 5.3 %collective-permute-start.15 = (bf16[64,256]{1,0:T(8,128)(2,1)S(1)}, bf16[64,256]{1,0:T(8,128)(2,1)S(1)}, u32[]{:S(2)}, u32[]{:S(2)}) collective-permute-start(bf16[64,256]{1,0:T(8,128)(2,1)S(1)} %get-tuple-element.45), channel_id=1, source_target_pairs={{0,4},{1,3},{2,6},{3,1},{4,0},{5,7},{6,2},{7,5},{8,12},{9,11},{10,... | collective-permute-start | bytes 98312 | tf_op jit(solution)/shard_map/ppermute | solution.py:282
  34.0 1.9 %collective-permute-start.13 = (f32[176,256]{1,0:T(8,128)S(1)}, f32[176,256]{1,0:T(8,128)S(1)}, u32[]{:S(2)}, u32[]{:S(2)}) collective-permute-start(f32[176,256]{1,0:T(8,128)S(1)} %shard_map.111.own_ref), channel_id=1, source_target_pairs={{0,1},{1,0},{2,3},{3,2},{4,5},{5,4},{6,7},{7,6},{8,9},{9,8},{10,11... | collective-permute-start | bytes 540680 | tf_op jit(solution)/shard_map/ppermute | solution.py:255

commit v13 on v10

--- a/solution.py
+++ b/solution.py
@@ -63,11 +63,12 @@
     step = 32
 
     def body(i, carry):
-        row = lax.broadcasted_iota(jnp.int32, (step, nodes), 0) + i * step
-        total = jnp.zeros((step, nodes), F32)
+        row = (lax.broadcasted_iota(jnp.int32, (step, nodes), 0) + i * step).astype(jnp.int16)
+        total = jnp.zeros((step, nodes), BF16)
         for k in range(fanout):
-            total = total + jnp.where(nbr_ref[k : k + 1, :] == row, 1.0, 0.0)
-        at_ref[pl.ds(pl.multiple_of(i * step, step), step), :] = total.astype(BF16)
+            hit = jnp.broadcast_to(nbr_ref[k : k + 1, :], (step, nodes)).astype(jnp.int16) == row
+            total = total + jnp.where(hit, jnp.ones((step, nodes), BF16), jnp.zeros((step, nodes), BF16))
+        at_ref[pl.ds(pl.multiple_of(i * step, step), step), :] = total
         return carry
 
     lax.fori_loop(0, nodes // step, body, 0)

time: 37 us -> 37.1 us (level)
  Pallas kernels: 6.74 us -> 6.33 us
    pallas_call x12, Pallas kernels: 6.74 us -> 6.33 us  [call(): pl.pallas_call(kernel, out_shape=outs if final else [pltpu.VMEM(o.shape,...]
  transfers between devices with their start and end apart: 16 -> 16, of which waited for: 8 -> 8; matrix products, arithmetic and copies ran while one was open for 0% -> 0% of each run, Pallas kernels for 12% -> 10%
where the time goes in v13:
time: 37.1 us; the launch traced here: 37 us
  starting transfers between devices  17.4 us (47%)
  waiting for transfers between devices  12.5 us (34%)
  Pallas kernels  6.33 us (17%)
  between operations  0.74 us (2%)
    ppermute x6, starting transfers between devices, hop(): return lax.ppermute(value, ('feat', 'dp'), pairs)  9.37 us
    ppermute x4, starting transfers between devices, fold_hop(): return lax.ppermute(value, 'dp', pairs)  7.28 us
    pallas_call x12, Pallas kernels, call(): pl.pallas_call(kernel, out_shape=outs if final else [pltpu.VMEM(o.shape,...  6.33 us
    ppermute x6, waiting for transfers between devices, hop(): return lax.ppermute(value, ('feat', 'dp'), pairs)  6.23 us
    ppermute x4, waiting for transfers between devices, fold_hop(): return lax.ppermute(value, 'dp', pairs)  5.66 us
    ppermute x6, starting transfers between devices, exchange(): return lax.ppermute(value, axis, [(i, i ^ step) for i in range(size)])  0.77 us
  transfers between devices with their start and end apart: 16, of which 8 were waited for; matrix products, arithmetic and copies ran while one was open for 0% of the time, Pallas kernels for 10%

profile of v13, /device:TPU:0, one launch (start us, length us, event | category | flops | bytes accessed | tf_op | source)
XLA Modules:
  0.0 37.0 jit_solution(16512249463954922636)
XLA Ops:
  0.6 0.0 copy-start
  0.6 3.0 %collective-permute-start = (bf16[256,512]{1,0:T(8,128)(2,1)}, bf16[256,512]{1,0:T(8,128)(2,1)S(1)}, u32[]{:S(2)}, u32[]{:S(2)}) collective-permute-start(bf16[256,512]{1,0:T(8,128)(2,1)} %f_ref.1), channel_id=1, source_target_pairs={{0,8},{1,17},{2,10},{3,19},{4,12},{5,21},{6,14},{7,23},{8,0},{9,25... | collective-permute-start | bytes 786440 | tf_op jit(solution)/shard_map/ppermute | solution.py:276
  3.6 1.8 %shard_map.103 = (bf16[512,512]{1,0:T(8,128)(2,1)S(1)}, bf16[256,256]{1,0:T(8,128)(2,1)S(1)}, bf16[256,256]{1,0:T(8,128)(2,1)S(1)}, s32[1,512]{1,0:T(1,128)S(1)}...) custom-call(s32[1]{0:T(128)} %bitcast.core_ref.refs_3_, s32[10,512]{1,0:T(8,128)} %bitcast.15, ...), custom_call_target="tpu_custom_call" | custom-call | flops 2621440 | bytes 1429508 | tf_op jit(solution)/shard_map/pallas_call | solution.py:39
  5.5 0.1 collective-permute-start.3
  5.6 0.0 copy-done
  5.6 2.0 %collective-permute-start.1 = (bf16[256,512]{1,0:T(8,128)(2,1)S(1)}, bf16[256,512]{1,0:T(8,128)(2,1)S(1)}, u32[]{:S(2)}, u32[]{:S(2)}) collective-permute-start(bf16[256,512]{1,0:T(8,128)(2,1)S(1)} %copy-done), channel_id=1, source_target_pairs={{0,16},{1,9},{2,18},{3,11},{4,20},{5,13},{6,22},{7,15},{8,24},{9,1... | collective-permute-start | bytes 786440 | tf_op jit(solution)/shard_map/ppermute | solution.py:276
  7.6 0.9 %collective-permute-done.refs_1_.refs_0_ = bf16[256,512]{1,0:T(8,128)(2,1)S(1)} collective-permute-done((bf16[256,512]{1,0:T(8,128)(2,1)}, bf16[256,512]{1,0:T(8,128)(2,1)S(1)}, u32[]{:S(2)}, u32[]{:S(2)}) %collective-permute-start) | collective-permute-done | bytes 262176 | tf_op jit(solution)/shard_map/ppermute | solution.py:276
  8.6 2.4 %collective-permute-start.2 = (bf16[256,512]{1,0:T(8,128)(2,1)S(1)}, bf16[256,512]{1,0:T(8,128)(2,1)S(1)}, u32[]{:S(2)}, u32[]{:S(2)}) collective-permute-start(bf16[256,512]{1,0:T(8,128)(2,1)S(1)} %collective-permute-done.refs_1_.refs_0_), channel_id=1, source_target_pairs={{0,16},{1,9},{2,18},{3,11},{4,20},{5,13},{6,22},{7,15},{8,24},{9,1... | collective-permute-start | bytes 786440 | tf_op jit(solution)/shard_map/ppermute | solution.py:276
  11.0 0.0 collective-permute-start.4
  11.0 1.0 %collective-permute-done.3.refs_3_ = bf16[256,256]{1,0:T(8,128)(2,1)S(1)} collective-permute-done((bf16[256,256]{1,0:T(8,128)(2,1)S(1)}, bf16[256,256]{1,0:T(8,128)(2,1)S(1)}, u32[]{:S(2)}, u32[]{:S(2)}) %collective-permute-start.3) | collective-permute-done | bytes 131104 | tf_op jit(solution)/shard_map/ppermute | solution.py:276
  12.0 1.8 %collective-permute-start.5 = (bf16[256,256]{1,0:T(8,128)(2,1)S(1)}, bf16[256,256]{1,0:T(8,128)(2,1)S(1)}, u32[]{:S(2)}, u32[]{:S(2)}) collective-permute-start(bf16[256,256]{1,0:T(8,128)(2,1)S(1)} %collective-permute-done.3.refs_3_), channel_id=1, source_target_pairs={{0,16},{1,9},{2,18},{3,11},{4,20},{5,13},{6,22},{7,15},{8,24},{9,1... | collective-permute-start | bytes 393224 | tf_op jit(solution)/shard_map/ppermute | solution.py:276
  13.8 0.0 collective-permute-start.6
  13.8 2.9 %collective-permute-done.4.refs_4_ = bf16[256,256]{1,0:T(8,128)(2,1)S(1)} collective-permute-done((bf16[256,256]{1,0:T(8,128)(2,1)S(1)}, bf16[256,256]{1,0:T(8,128)(2,1)S(1)}, u32[]{:S(2)}, u32[]{:S(2)}) %collective-permute-start.4) | collective-permute-done | bytes 131104 | tf_op jit(solution)/shard_map/ppermute | solution.py:276
  16.7 0.0 collective-permute-start.7
  16.8 1.4 %collective-permute-done.5.refs_2_ = bf16[256,256]{1,0:T(8,128)(2,1)S(1)} collective-permute-done((bf16[256,256]{1,0:T(8,128)(2,1)S(1)}, bf16[256,256]{1,0:T(8,128)(2,1)S(1)}, u32[]{:S(2)}, u32[]{:S(2)}) %collective-permute-start.5) | collective-permute-done | bytes 131104 | tf_op jit(solution)/shard_map/ppermute | solution.py:276
  18.1 0.0 collective-permute-start.8
  18.2 0.0 collective-permute-done.1.refs_2_.refs_1_
  18.2 0.5 %shard_map.104 = (f32[256,512]{1,0:T(8,128)S(1)}, f32[256,512]{1,0:T(8,128)S(1)}, f32[256,512]{1,0:T(8,128)S(1)}) custom-call(bf16[256,256]{1,0:T(8,128)(2,1)S(1)} %get-tuple-element.31.own_ref, bf16[256,256]{1,0:T(8,128)(2,1)S(1)} %get-tuple-element.32.other_ref, bf16[256,512]{1,0:T(8,128)(2,1)S(1)} %copy-done, ...), custom_call_target="tpu_custom_call" | custom-call | flops 268435456 | bytes 2883584 | tf_op jit(solution)/shard_map/pallas_call | solution.py:39
  18.6 0.0 collective-permute-done.2.refs_3_.refs_2_
  18.6 0.2 shard_map.105.refs_9_
  18.9 0.0 collective-permute-done.6.refs_11_
  18.9 0.0 collective-permute-done.7.refs_12_
  18.9 0.6 %collective-permute-done.8.refs_13_ = bf16[256,256]{1,0:T(8,128)(2,1)S(1)} collective-permute-done((bf16[256,256]{1,0:T(8,128)(2,1)S(1)}, bf16[256,256]{1,0:T(8,128)(2,1)S(1)}, u32[]{:S(2)}, u32[]{:S(2)}) %collective-permute-start.8) | collective-permute-done | bytes 131104 | tf_op jit(solution)/shard_map/ppermute | solution.py:258
  19.5 1.6 %shard_map.106 = (f32[176,256]{1,0:T(8,128)S(1)}, f32[176,256]{1,0:T(8,128)S(1)}, bf16[172,512]{1,0:T(8,128)(2,1)S(1)}, bf16[256,512]{1,0:T(8,128)(2,1)S(1)}) custom-call(bf16[256,512]{1,0:T(8,128)(2,1)S(1)} %collective-permute-done.refs_1_.refs_0_, bf16[256,512]{1,0:T(8,128)(2,1)S(1)} %collective-permute-done.1.refs_2_.refs_1_, ...), custom_call_target="tpu_custom_call" | custom-call | flops 805306368 | bytes 3731460 | tf_op jit(solution)/shard_map/pallas_call | solution.py:39
  21.0 0.2 collective-permute-start.10
  21.3 1.1 %shard_map.107 = (f32[4,64,256]{2,1,0:T(8,128)S(1)}, f32[4,64,256]{2,1,0:T(8,128)S(1)}) custom-call(s32[1]{0:T(128)} %bitcast.core_ref.refs_3_, bf16[172,512]{1,0:T(8,128)(2,1)S(1)} %get-tuple-element.36.g_ref, bf16[256,512]{1,0:T(8,128)(2,1)S(1)} %get-tuple-element.37.hidden_ref, bf16[512,512]{1,0:T(8,128)(2,1)S(1)} %get-tuple-element.28.refs_6_.at_ref, ...), custom_call_target="tpu_custom_call" | custom-call | flops 402653184 | bytes 1925124 | tf_op jit(solution)/shard_map/pallas_call | solution.py:39
  22.4 0.4 %collective-permute-start.9 = (f32[4,64,256]{2,1,0:T(8,128)S(1)}, f32[4,64,256]{2,1,0:T(8,128)S(1)}, u32[]{:S(2)}, u32[]{:S(2)}) collective-permute-start(f32[4,64,256]{2,1,0:T(8,128)S(1)} %get-tuple-element.39), channel_id=1, source_target_pairs={{0,1},{1,0},{2,3},{3,2},{4,5},{5,4},{6,7},{7,6},{8,9},{9,8},{10,11... | collective-permute-start | bytes 786440 | tf_op jit(solution)/shard_map/ppermute | solution.py:258
  22.8 0.0 collective-permute-done.10.recv_ref
  22.9 2.1 %collective-permute-start.11 = (bf16[176,256]{1,0:T(8,128)(2,1)S(1)}, bf16[176,256]{1,0:T(8,128)(2,1)S(1)}, u32[]{:S(2)}, u32[]{:S(2)}) collective-permute-start(bf16[176,256]{1,0:T(8,128)(2,1)S(1)} %shard_map.109.own_ref), channel_id=1, source_target_pairs={{0,2},{1,5},{2,0},{3,7},{4,6},{5,1},{6,4},{7,3},{8,10},{9,13},{10,... | collective-permute-start | bytes 270344 | tf_op jit(solution)/shard_map/ppermute | solution.py:285
  25.0 0.0 collective-permute-done.9.recv_ref
  25.1 1.1 %collective-permute-start.14 = (bf16[128,256]{1,0:T(8,128)(2,1)S(1)}, bf16[128,256]{1,0:T(8,128)(2,1)S(1)}, u32[]{:S(2)}, u32[]{:S(2)}) collective-permute-start(bf16[128,256]{1,0:T(8,128)(2,1)S(1)} %get-tuple-element.43), channel_id=1, source_target_pairs={{0,2},{1,5},{2,0},{3,7},{4,6},{5,1},{6,4},{7,3},{8,10},{9,13},{10,... | collective-permute-start | bytes 196616 | tf_op jit(solution)/shard_map/ppermute | solution.py:285
  26.2 2.3 %collective-permute-done.11.recv_ref = bf16[176,256]{1,0:T(8,128)(2,1)S(1)} collective-permute-done((bf16[176,256]{1,0:T(8,128)(2,1)S(1)}, bf16[176,256]{1,0:T(8,128)(2,1)S(1)}, u32[]{:S(2)}, u32[]{:S(2)}) %collective-permute-start.11) | collective-permute-done | bytes 90144 | tf_op jit(solution)/shard_map/ppermute | solution.py:285
  28.5 2.2 %collective-permute-start.12 = (bf16[176,256]{1,0:T(8,128)(2,1)S(1)}, bf16[176,256]{1,0:T(8,128)(2,1)S(1)}, u32[]{:S(2)}, u32[]{:S(2)}) collective-permute-start(bf16[176,256]{1,0:T(8,128)(2,1)S(1)} %shard_map.110.refs_0_), channel_id=1, source_target_pairs={{0,4},{1,3},{2,6},{3,1},{4,0},{5,7},{6,2},{7,5},{8,12},{9,11},{10,... | collective-permute-start | bytes 270344 | tf_op jit(solution)/shard_map/ppermute | solution.py:285
  30.7 0.0 collective-permute-done.14.recv_ref
  30.7 1.8 %collective-permute-start.15 = (bf16[64,256]{1,0:T(8,128)(2,1)S(1)}, bf16[64,256]{1,0:T(8,128)(2,1)S(1)}, u32[]{:S(2)}, u32[]{:S(2)}) collective-permute-start(bf16[64,256]{1,0:T(8,128)(2,1)S(1)} %get-tuple-element.45), channel_id=1, source_target_pairs={{0,4},{1,3},{2,6},{3,1},{4,0},{5,7},{6,2},{7,5},{8,12},{9,11},{10,... | collective-permute-start | bytes 98312 | tf_op jit(solution)/shard_map/ppermute | solution.py:285
  32.6 1.6 %collective-permute-done.12.refs_1_ = bf16[176,256]{1,0:T(8,128)(2,1)S(1)} collective-permute-done((bf16[176,256]{1,0:T(8,128)(2,1)S(1)}, bf16[176,256]{1,0:T(8,128)(2,1)S(1)}, u32[]{:S(2)}, u32[]{:S(2)}) %collective-permute-start.12) | collective-permute-done | bytes 90144 | tf_op jit(solution)/shard_map/ppermute | solution.py:285
  34.2 0.1 collective-permute-start.13
  34.2 1.8 %collective-permute-done.15.refs_0_ = bf16[64,256]{1,0:T(8,128)(2,1)S(1)} collective-permute-done((bf16[64,256]{1,0:T(8,128)(2,1)S(1)}, bf16[64,256]{1,0:T(8,128)(2,1)S(1)}, u32[]{:S(2)}, u32[]{:S(2)}) %collective-permute-start.15) | collective-permute-done | bytes 32800 | tf_op jit(solution)/shard_map/ppermute | solution.py:285
  36.0 0.0 collective-permute-done.13.other_ref
  36.0 0.9 %shard_map.114 = (f32[2,32,256]{2,1,0:T(8,128)}, f32[688,128]{1,0:T(8,128)}, f32[1,1]{1,0:T(1,128)}) custom-call(s32[1]{0:T(128)} %bitcast.core_ref.refs_3_, f32[176,256]{1,0:T(8,128)S(1)} %shard_map.111.own_ref, f32[176,256]{1,0:T(8,128)S(1)} %collective-permute-done.13.other_ref, f32[64,256]{1,0:T(8,128)S(1)} %shard_map.113.first_ref), custom_call_target="tpu_custom_call" | custom-call | bytes 843784 | tf_op jit(solution)/shard_map/pallas_call | solution.py:39
  (6 shorter events, 0.2 us)
Async XLA Ops:
  0.6 5.0 %copy-start = (bf16[256,512]{1,0:T(8,128)(2,1)S(1)}, bf16[256,512]{1,0:T(8,128)(2,1)}, u32[]{:S(2)}) copy-start(bf16[256,512]{1,0:T(8,128)(2,1)} %f_ref.1) | copy-start | bytes 786436
  0.6 7.9 %collective-permute-start = (bf16[256,512]{1,0:T(8,128)(2,1)}, bf16[256,512]{1,0:T(8,128)(2,1)S(1)}, u32[]{:S(2)}, u32[]{:S(2)}) collective-permute-start(bf16[256,512]{1,0:T(8,128)(2,1)} %f_ref.1), channel_id=1, source_target_pairs={{0,8},{1,17},{2,10},{3,19},{4,12},{5,21},{6,14},{7,23},{8,0},{9,25... | collective-permute-start | bytes 786440 | tf_op jit(solution)/shard_map/ppermute | solution.py:276
  5.5 6.5 %collective-permute-start.3 = (bf16[256,256]{1,0:T(8,128)(2,1)S(1)}, bf16[256,256]{1,0:T(8,128)(2,1)S(1)}, u32[]{:S(2)}, u32[]{:S(2)}) collective-permute-start(bf16[256,256]{1,0:T(8,128)(2,1)S(1)} %get-tuple-element.31.own_ref), channel_id=1, source_target_pairs={{0,8},{1,17},{2,10},{3,19},{4,12},{5,21},{6,14},{7,23},{8,0},{9,25... | collective-permute-start | bytes 393224 | tf_op jit(solution)/shard_map/ppermute | solution.py:276
  5.6 12.6 %collective-permute-start.1 = (bf16[256,512]{1,0:T(8,128)(2,1)S(1)}, bf16[256,512]{1,0:T(8,128)(2,1)S(1)}, u32[]{:S(2)}, u32[]{:S(2)}) collective-permute-start(bf16[256,512]{1,0:T(8,128)(2,1)S(1)} %copy-done), channel_id=1, source_target_pairs={{0,16},{1,9},{2,18},{3,11},{4,20},{5,13},{6,22},{7,15},{8,24},{9,1... | collective-permute-start | bytes 786440 | tf_op jit(solution)/shard_map/ppermute | solution.py:276
  8.6 10.1 %collective-permute-start.2 = (bf16[256,512]{1,0:T(8,128)(2,1)S(1)}, bf16[256,512]{1,0:T(8,128)(2,1)S(1)}, u32[]{:S(2)}, u32[]{:S(2)}) collective-permute-start(bf16[256,512]{1,0:T(8,128)(2,1)S(1)} %collective-permute-done.refs_1_.refs_0_), channel_id=1, source_target_pairs={{0,16},{1,9},{2,18},{3,11},{4,20},{5,13},{6,22},{7,15},{8,24},{9,1... | collective-permute-start | bytes 786440 | tf_op jit(solution)/shard_map/ppermute | solution.py:276
  11.0 5.8 %collective-permute-start.4 = (bf16[256,256]{1,0:T(8,128)(2,1)S(1)}, bf16[256,256]{1,0:T(8,128)(2,1)S(1)}, u32[]{:S(2)}, u32[]{:S(2)}) collective-permute-start(bf16[256,256]{1,0:T(8,128)(2,1)S(1)} %get-tuple-element.31.own_ref), channel_id=1, source_target_pairs={{0,16},{1,9},{2,18},{3,11},{4,20},{5,13},{6,22},{7,15},{8,24},{9,1... | collective-permute-start | bytes 393224 | tf_op jit(solution)/shard_map/ppermute | solution.py:276
  12.0 6.2 %collective-permute-start.5 = (bf16[256,256]{1,0:T(8,128)(2,1)S(1)}, bf16[256,256]{1,0:T(8,128)(2,1)S(1)}, u32[]{:S(2)}, u32[]{:S(2)}) collective-permute-start(bf16[256,256]{1,0:T(8,128)(2,1)S(1)} %collective-permute-done.3.refs_3_), channel_id=1, source_target_pairs={{0,16},{1,9},{2,18},{3,11},{4,20},{5,13},{6,22},{7,15},{8,24},{9,1... | collective-permute-start | bytes 393224 | tf_op jit(solution)/shard_map/ppermute | solution.py:276
  13.8 5.1 %collective-permute-start.6 = (bf16[256,256]{1,0:T(8,128)(2,1)S(1)}, bf16[256,256]{1,0:T(8,128)(2,1)S(1)}, u32[]{:S(2)}, u32[]{:S(2)}) collective-permute-start(bf16[256,256]{1,0:T(8,128)(2,1)S(1)} %collective-permute-done.3.refs_3_), channel_id=1, source_target_pairs={{0,1},{1,0},{2,3},{3,2},{4,5},{5,4},{6,7},{7,6},{8,9},{9,8},{10,11... | collective-permute-start | bytes 393224 | tf_op jit(solution)/shard_map/ppermute | solution.py:258
  16.7 2.2 %collective-permute-start.7 = (bf16[256,256]{1,0:T(8,128)(2,1)S(1)}, bf16[256,256]{1,0:T(8,128)(2,1)S(1)}, u32[]{:S(2)}, u32[]{:S(2)}) collective-permute-start(bf16[256,256]{1,0:T(8,128)(2,1)S(1)} %collective-permute-done.4.refs_4_), channel_id=1, source_target_pairs={{0,1},{1,0},{2,3},{3,2},{4,5},{5,4},{6,7},{7,6},{8,9},{9,8},{10,11... | collective-permute-start | bytes 393224 | tf_op jit(solution)/shard_map/ppermute | solution.py:258
  18.1 1.3 %collective-permute-start.8 = (bf16[256,256]{1,0:T(8,128)(2,1)S(1)}, bf16[256,256]{1,0:T(8,128)(2,1)S(1)}, u32[]{:S(2)}, u32[]{:S(2)}) collective-permute-start(bf16[256,256]{1,0:T(8,128)(2,1)S(1)} %collective-permute-done.5.refs_2_), channel_id=1, source_target_pairs={{0,1},{1,0},{2,3},{3,2},{4,5},{5,4},{6,7},{7,6},{8,9},{9,8},{10,11... | collective-permute-start | bytes 393224 | tf_op jit(solution)/shard_map/ppermute | solution.py:258
  21.0 1.8 %collective-permute-start.10 = (f32[176,256]{1,0:T(8,128)S(1)}, f32[176,256]{1,0:T(8,128)S(1)}, u32[]{:S(2)}, u32[]{:S(2)}) collective-permute-start(f32[176,256]{1,0:T(8,128)S(1)} %get-tuple-element.42), channel_id=1, source_target_pairs={{0,1},{1,0},{2,3},{3,2},{4,5},{5,4},{6,7},{7,6},{8,9},{9,8},{10,11... | collective-permute-start | bytes 540680 | tf_op jit(solution)/shard_map/ppermute | solution.py:258
  22.4 2.6 %collective-permute-start.9 = (f32[4,64,256]{2,1,0:T(8,128)S(1)}, f32[4,64,256]{2,1,0:T(8,128)S(1)}, u32[]{:S(2)}, u32[]{:S(2)}) collective-permute-start(f32[4,64,256]{2,1,0:T(8,128)S(1)} %get-tuple-element.39), channel_id=1, source_target_pairs={{0,1},{1,0},{2,3},{3,2},{4,5},{5,4},{6,7},{7,6},{8,9},{9,8},{10,11... | collective-permute-start | bytes 786440 | tf_op jit(solution)/shard_map/ppermute | solution.py:258
  22.9 5.6 %collective-permute-start.11 = (bf16[176,256]{1,0:T(8,128)(2,1)S(1)}, bf16[176,256]{1,0:T(8,128)(2,1)S(1)}, u32[]{:S(2)}, u32[]{:S(2)}) collective-permute-start(bf16[176,256]{1,0:T(8,128)(2,1)S(1)} %shard_map.109.own_ref), channel_id=1, source_target_pairs={{0,2},{1,5},{2,0},{3,7},{4,6},{5,1},{6,4},{7,3},{8,10},{9,13},{10,... | collective-permute-start | bytes 270344 | tf_op jit(solution)/shard_map/ppermute | solution.py:285
  25.1 5.6 %collective-permute-start.14 = (bf16[128,256]{1,0:T(8,128)(2,1)S(1)}, bf16[128,256]{1,0:T(8,128)(2,1)S(1)}, u32[]{:S(2)}, u32[]{:S(2)}) collective-permute-start(bf16[128,256]{1,0:T(8,128)(2,1)S(1)} %get-tuple-element.43), channel_id=1, source_target_pairs={{0,2},{1,5},{2,0},{3,7},{4,6},{5,1},{6,4},{7,3},{8,10},{9,13},{10,... | collective-permute-start | bytes 196616 | tf_op jit(solution)/shard_map/ppermute | solution.py:285
  28.5 5.6 %collective-permute-start.12 = (bf16[176,256]{1,0:T(8,128)(2,1)S(1)}, bf16[176,256]{1,0:T(8,128)(2,1)S(1)}, u32[]{:S(2)}, u32[]{:S(2)}) collective-permute-start(bf16[176,256]{1,0:T(8,128)(2,1)S(1)} %shard_map.110.refs_0_), channel_id=1, source_target_pairs={{0,4},{1,3},{2,6},{3,1},{4,0},{5,7},{6,2},{7,5},{8,12},{9,11},{10,... | collective-permute-start | bytes 270344 | tf_op jit(solution)/shard_map/ppermute | solution.py:285
  30.7 5.3 %collective-permute-start.15 = (bf16[64,256]{1,0:T(8,128)(2,1)S(1)}, bf16[64,256]{1,0:T(8,128)(2,1)S(1)}, u32[]{:S(2)}, u32[]{:S(2)}) collective-permute-start(bf16[64,256]{1,0:T(8,128)(2,1)S(1)} %get-tuple-element.45), channel_id=1, source_target_pairs={{0,4},{1,3},{2,6},{3,1},{4,0},{5,7},{6,2},{7,5},{8,12},{9,11},{10,... | collective-permute-start | bytes 98312 | tf_op jit(solution)/shard_map/ppermute | solution.py:285
  34.2 1.9 %collective-permute-start.13 = (f32[176,256]{1,0:T(8,128)S(1)}, f32[176,256]{1,0:T(8,128)S(1)}, u32[]{:S(2)}, u32[]{:S(2)}) collective-permute-start(f32[176,256]{1,0:T(8,128)S(1)} %shard_map.111.own_ref), channel_id=1, source_target_pairs={{0,1},{1,0},{2,3},{3,2},{4,5},{5,4},{6,7},{7,6},{8,9},{9,8},{10,11... | collective-permute-start | bytes 540680 | tf_op jit(solution)/shard_map/ppermute | solution.py:258
